TPU v7x, 128 devices: a whole 4x4x4 slice. The times are simulated.
128 devices in a mesh: bulk: 16 (over y, x), coarse: 8 (over z, core).
Axes of the slice: x: 4, y: 4, z: 4, core: 2. Of those that a mesh axis runs over, the one named last changes fastest.
Arguments:
- diag_blocks: bfloat16 [2048, 128, 128], P(('bulk', 'coarse')), as said below
- off_blocks: bfloat16 [2048, 3, 128, 128], P(('bulk', 'coarse')), may hold values from -0.125 to 0.125
- off_columns: int32 [2048, 3], P(('bulk', 'coarse')), may hold values from 0 to 31
- tentative: bfloat16 [2048, 128, 128], P(('bulk', 'coarse')), may hold values from -2 to 2
- aggregate: int32 [2048], P(('bulk', 'coarse')), may hold values from 0 to 1
- send_rows: int32 [512, 4], P(('bulk', 'coarse')), may hold values from 0 to 15
Outputs:
- coarse_op: float32 [256, 128, 3328], P(('bulk', 'coarse'))
Inputs may be any that keep to these rules, and one draw needn't show every extreme that they name: `diag_blocks`: every block's diagonal entries lie between 1 and 2.
All inputs are finite; a program needn't handle non-finite values.
Results may differ from a plain program's by a relative error of at most 0.0017.
Values may be sent and summed in bfloat16 or wider, within the bound.
No kernel may reach another device: no remote copies, remote signals or barrier semaphores. Data moves between devices by JAX's collectives and lax.ppermute only.
A program may use at most 256 MiB of HBM per device.

v0:
```python
import jax
import jax.numpy as jnp
from jax import lax
from jax.sharding import PartitionSpec as P

CB_DEV = 2


damping = 0.6


def from_behind(value, axis, steps):
    count = lax.axis_size(axis)
    initial, last = (max(0, -steps), min(count, count - steps))
    return lax.ppermute(value, axis, [(source, source + steps) for source in range(initial, last)])


def for_sending(x):
    return jax.tree.map(lambda a: a.astype(jnp.bfloat16) if a.dtype == jnp.float32 else a, x)


def place_slots(slot_values, slot_labels, width_blocks):
    select = (
        slot_labels[:, :, None] == jnp.arange(width_blocks, dtype=jnp.int32)[None, None, :]
    ).astype(jnp.float32)
    dense_rows = jnp.einsum("rkw,rkic->riwc", select, slot_values, precision=lax.Precision.HIGHEST)
    coarse_cols = slot_values.shape[3]
    return dense_rows.reshape(
        slot_values.shape[0], slot_values.shape[2], width_blocks * coarse_cols
    )


def band_place(row_piece, start_unit, span_units, row_span):
    return jnp.pad(
        row_piece, ((0, 0), (start_unit * row_span, (13 - start_unit - span_units) * row_span))
    )


def local(diag_blocks, off_blocks, off_columns, tentative, aggregate, send_rows):
    coarse_cols = tentative.shape[2]
    fine_rows = tentative.shape[1]
    local_blocks = tentative.shape[0]
    groups = CB_DEV
    row_span = groups * coarse_cols
    frame_blocks = 9 * groups
    offsets = (1, -1, 2, -2)
    ghost_tent = []
    ghost_labels = []
    for neighbour in range(4):
        picked = send_rows[neighbour]
        arrived = from_behind(
            (tentative[picked], aggregate[picked]), ("bulk", "coarse"), offsets[neighbour]
        )
        ghost_tent.append(arrived[0])
        ghost_labels.append(arrived[1] + (4 - offsets[neighbour]) * groups)
    own_labels = aggregate + 4 * groups
    tent_table = jnp.concatenate([tentative] + ghost_tent, axis=0)
    label_table = jnp.concatenate([own_labels] + ghost_labels, axis=0)
    inv_diag = 1.0 / jnp.diagonal(diag_blocks, axis1=1, axis2=2).astype(jnp.float32)
    near_tent = tent_table[off_columns]
    own_term = jnp.einsum(
        "rij,rjc->ric", diag_blocks, tentative, preferred_element_type=jnp.float32
    )
    off_term = jnp.einsum(
        "rkij,rkjc->rkic", off_blocks, near_tent, preferred_element_type=jnp.float32
    )
    first_slot = tentative.astype(jnp.float32) - damping * inv_diag[:, :, None] * own_term
    others = -damping * inv_diag[:, None, :, None] * off_term
    slots = jnp.concatenate([first_slot[:, None], others], axis=1).astype(jnp.bfloat16)
    slot_labels = jnp.concatenate([own_labels[:, None], label_table[off_columns]], axis=1)
    ghost_slots = []
    ghost_slot_labels = []
    for neighbour in range(4):
        shift_by = offsets[neighbour]
        picked = send_rows[neighbour]
        slot_piece, label_piece = from_behind(
            (slots[picked], for_sending(slot_labels[picked])), ("bulk", "coarse"), shift_by
        )
        ghost_slots.append(slot_piece)
        ghost_slot_labels.append(label_piece - shift_by * groups)
    slot_table = jnp.concatenate([slots] + ghost_slots, axis=0)
    slot_label_table = jnp.concatenate([slot_labels] + ghost_slot_labels, axis=0)
    near_slots = slot_table[off_columns]
    near_labels = slot_label_table[off_columns]
    own_prod = jnp.einsum("rij,rmjc->rmic", diag_blocks, slots, preferred_element_type=jnp.float32)
    off_prod = jnp.einsum(
        "rkij,rkmjc->rkmic", off_blocks, near_slots, preferred_element_type=jnp.float32
    )
    slot_count = slots.shape[1]
    all_prod = jnp.concatenate([own_prod[:, None], off_prod], axis=1).reshape(
        local_blocks, -1, fine_rows, coarse_cols
    )
    all_labels = jnp.concatenate([slot_labels[:, None], near_labels], axis=1).reshape(
        local_blocks, -1
    )
    applied = place_slots(all_prod, all_labels, frame_blocks).astype(jnp.bfloat16)
    partial_value = jnp.zeros((5 * groups, coarse_cols, frame_blocks * coarse_cols), jnp.float32)
    compact_ids = jnp.arange(5 * groups, dtype=jnp.int32)
    for member in range(slot_count):
        contrib = jnp.einsum(
            "ric,riz->rcz", slots[:, member], applied, preferred_element_type=jnp.float32
        )
        select = ((slot_labels[:, member] - 2 * groups)[:, None] == compact_ids[None, :]).astype(
            jnp.float32
        )
        partial_value = partial_value + jnp.einsum(
            "rw,rcz->wcz", select, contrib, precision=lax.Precision.HIGHEST
        )
    partial_value = partial_value.reshape(5 * row_span, frame_blocks * coarse_cols)

    def rows_at(level):
        return partial_value[level * row_span : (level + 1) * row_span]

    summed = band_place(rows_at(2), 2, 9, row_span)
    for shift_by in (1, -1, 2, -2):
        arrived = from_behind(for_sending(rows_at(shift_by + 2)), ("bulk", "coarse"), shift_by)
        summed = summed + band_place(arrived, 2 - shift_by, 9, row_span)
    return summed.reshape(groups, coarse_cols, 13 * row_span)


def solution(mesh):
    in_specs = (
        P(("bulk", "coarse"), None, None),
        P(("bulk", "coarse"), None, None, None),
        P(("bulk", "coarse"), None),
        P(("bulk", "coarse"), None, None),
        P(("bulk", "coarse")),
        P(("bulk", "coarse"), None),
    )
    out_specs = P(("bulk", "coarse"), None, None)
    return jax.shard_map(local, mesh=mesh, in_specs=in_specs, out_specs=out_specs, check_vma=False)
```

profile of v0, /device:TPU:24, one launch (start us, length us, event | category | flops | bytes accessed | tf_op | source)
XLA Modules:
  0.0 452.0 jit_solution(174642882280062078)
XLA Ops:
  0.9 2.3 gather_fusion.1
  5.1 2.3 gather_fusion.2
  7.4 7.8 %collective-permute-start.1 = (bf16[4,128,128]{2,1,0:T(8,128)(2,1)}, bf16[4,128,128]{2,1,0:T(8,128)(2,1)S(1)}, u32[]{:S(2)}, u32[]{:S(2)}) collective-permute-start(bf16[4,128,128]{2,1,0:T(8,128)(2,1)} %gather_fusion.2), channel_id=1, source_target_pairs={{1,0},{2,1},{3,2},{4,3},{5,4},{6,5},{7,6},{8,7},{9,8},{10,9},{11,1... | collective-permute-start | bytes 393224 | tf_op jit(solution)/shard_map/ppermute | solution.py:15
  15.2 2.3 gather_fusion.3
  17.5 2.0 collective-permute-start.2
  19.6 2.2 gather_fusion.4
  21.8 8.1 %collective-permute-start.3 = (bf16[4,128,128]{2,1,0:T(8,128)(2,1)}, bf16[4,128,128]{2,1,0:T(8,128)(2,1)}, u32[]{:S(2)}, u32[]{:S(2)}) collective-permute-start(bf16[4,128,128]{2,1,0:T(8,128)(2,1)} %gather_fusion.4), channel_id=1, source_target_pairs={{2,0},{3,1},{4,2},{5,3},{6,4},{7,5},{8,6},{9,7},{10,8},{11,9},{12,... | collective-permute-start | bytes 393224 | tf_op jit(solution)/shard_map/ppermute | solution.py:15
  39.2 3.2 copy.102
  42.3 2.0 gather_fusion
  45.8 3.9 collective-permute-start.10
  49.8 5.7 %collective-permute-done.10 = s32[4]{0:T(128)S(1)} collective-permute-done((s32[4]{0:T(128)S(1)}, s32[4]{0:T(128)S(1)}, u32[]{:S(2)}, u32[]{:S(2)}) %collective-permute-start.10) | collective-permute-done | bytes 48 | tf_op jit(solution)/shard_map/ppermute | solution.py:15
  60.6 7.1 %collective-permute-done.8 = s32[4]{0:T(128)S(1)} collective-permute-done((s32[4]{0:T(128)S(1)}, s32[4]{0:T(128)S(1)}, u32[]{:S(2)}, u32[]{:S(2)}) %collective-permute-start.8) | collective-permute-done | bytes 48 | tf_op jit(solution)/shard_map/ppermute | solution.py:15
  71.2 1.9 collective-permute-start.15
  73.2 3.5 collective-permute-done.15
  78.6 7.8 %collective-permute-done.14 = s32[4,4]{1,0:T(4,128)S(1)} collective-permute-done((s32[4,4]{1,0:T(4,128)S(1)}, s32[4,4]{1,0:T(4,128)S(1)}, u32[]{:S(2)}, u32[]{:S(2)}) %collective-permute-start.14) | collective-permute-done | bytes 96 | tf_op jit(solution)/shard_map/ppermute | solution.py:15
  93.5 1.9 gather_fusion.5
  95.4 2.7 fusion.11
  98.1 4.2 pad_maximum_fusion.1
  102.3 3.1 gather_fusion.6
  105.3 3.0 gather_fusion.7
  110.2 7.9 %collective-permute-start.5 = (bf16[4,4,128,128]{2,3,1,0:T(8,128)(2,1)}, bf16[4,4,128,128]{2,3,1,0:T(8,128)(2,1)}, u32[]{:S(2)}, u32[]{:S(2)}) collective-permute-start(bf16[4,4,128,128]{2,3,1,0:T(8,128)(2,1)} %gather_fusion.7), channel_id=1, source_target_pairs={{1,0},{2,1},{3,2},{4,3},{5,4},{6,5},{7,6},{8,7},{9,8},{10,9},{11,1... | collective-permute-start | bytes 1572872 | tf_op jit(solution)/shard_map/ppermute | solution.py:15
  118.9 3.0 gather_fusion.8
  123.9 3.0 gather_fusion.9
  126.9 8.6 %collective-permute-start.7 = (bf16[4,4,128,128]{2,3,1,0:T(8,128)(2,1)}, bf16[4,4,128,128]{2,3,1,0:T(8,128)(2,1)S(1)}, u32[]{:S(2)}, u32[]{:S(2)}) collective-permute-start(bf16[4,4,128,128]{2,3,1,0:T(8,128)(2,1)} %gather_fusion.9), channel_id=1, source_target_pairs={{2,0},{3,1},{4,2},{5,3},{6,4},{7,5},{8,6},{9,7},{10,8},{11,9},{12,... | collective-permute-start | bytes 1572872 | tf_op jit(solution)/shard_map/ppermute | solution.py:15
  135.5 3.9 convolution_bitcast_fusion.1
  145.9 7.2 %gather_fusion.10 = bf16[48,4,128,128]{2,3,1,0:T(8,128)(2,1)} fusion(bf16[32,4,128,128]{2,3,1,0:T(8,128)(2,1)} %constant_dynamic-update-slice_fusion.5, s32[1024]{0:T(1024)S(1)} %pad_clamp_fusion), kind=kCustom, calls=%fused_computation.10 | custom fusion | bytes 12583104 | tf_op jit(solution)/shard_map/gather | solution.py:83
  153.1 4.0 convolution_bitcast_fusion
  157.1 6.1 %pad_maximum_fusion = f32[16,4,4,128,128]{3,4,2,1,0:T(8,128)} fusion(f32[16,3,4,128,128]{3,4,2,1,0:T(8,128)S(1)} %convolution_bitcast_fusion, f32[16,1,4,128,128]{3,4,2,1,0:T(8,128)S(1)} %copy-done.3), kind=kLoop, calls=%fused_computation.30 | loop fusion | flops 4194304 | bytes 33554432 | tf_op jit(solution)/shard_map/concatenate | solution.py:90
  163.2 17.6 %copy.113 = f32[16,16,128,128]{3,1,2,0:T(8,128)} copy(f32[16,16,128,128]{2,3,1,0:T(8,128)} %bitcast.102) | data formatting | bytes 33554432 | tf_op jit(solution)/shard_map/reshape | solution.py:90
  180.9 17.9 %convert_bitcast_fusion = bf16[16,128,18,128]{3,2,1,0:T(8,128)(2,1)} fusion(f32[16,16,128,128]{3,1,2,0:T(8,128)} %copy.113, s32[16,16]{1,0:T(8,128)S(1)} %copy.112), kind=kOutput, calls=%fused_computation.31 | convolution fusion | flops 910692864 | bytes 26215424 | tf_op jit(solution)/shard_map/rkw,rkic->riwc/dot_general | solution.py:26
  198.8 15.3 %copy.114 = bf16[16,128,18,128]{1,3,2,0:T(8,128)(2,1)} copy(bf16[16,128,18,128]{3,2,1,0:T(8,128)(2,1)} %convert_bitcast_fusion) | data formatting | bytes 18874368 | tf_op jit(solution)/shard_map/convert_element_type | solution.py:96
  214.1 12.8 %fusion.15 = f32[16,128,2304]{2,1,0:T(8,128)} fusion(bf16[16,128,2304]{1,2,0:T(8,128)(2,1)} %bitcast.98, bf16[16,3,128,128]{2,3,1,0:T(8,128)(2,1)S(1)} %fusion.11), kind=kOutput, calls=%fused_computation.45 | convolution fusion | flops 1207959552 | bytes 28835840 | tf_op jit(solution)/shard_map/ric,riz->rcz/dot_general | solution.py:100
  226.9 12.7 %fusion.16 = f32[16,128,2304]{2,1,0:T(8,128)} fusion(bf16[16,128,2304]{1,2,0:T(8,128)(2,1)} %bitcast.99, bf16[16,3,128,128]{2,3,1,0:T(8,128)(2,1)S(1)} %fusion.11), kind=kOutput, calls=%fused_computation.47 | convolution fusion | flops 1207959552 | bytes 28835840 | tf_op jit(solution)/shard_map/ric,riz->rcz/dot_general | solution.py:100
  239.6 12.7 %fusion.14 = f32[16,128,2304]{2,1,0:T(8,128)} fusion(bf16[16,128,2304]{1,2,0:T(8,128)(2,1)} %bitcast.100, bf16[16,3,128,128]{2,3,1,0:T(8,128)(2,1)S(1)} %fusion.11), kind=kOutput, calls=%fused_computation.43 | convolution fusion | flops 1207959552 | bytes 28835840 | tf_op jit(solution)/shard_map/ric,riz->rcz/dot_general | solution.py:100
  252.3 12.8 %fusion.43 = f32[16,128,2304]{2,1,0:T(8,128)} fusion(bf16[16,128,128]{2,1,0:T(8,128)(2,1)S(1)} %copy-done.5, bf16[16,128,2304]{1,2,0:T(8,128)(2,1)} %bitcast.101), kind=kOutput, calls=%fused_computation.113 | convolution fusion | flops 1207959552 | bytes 28835840 | tf_op jit(solution)/shard_map/ric,riz->rcz/dot_general | solution.py:100
  265.1 29.0 %fusion.2 = f32[10,128,2304]{2,0,1:T(8,128)} fusion(f32[16,128,2304]{2,1,0:T(8,128)} %fusion.15, s32[16]{0:T(128)S(1)} %get-tuple-element.6), kind=kOutput, calls=%fused_computation.23 | convolution fusion | flops 566231168 | bytes 30670912 | tf_op jit(solution)/shard_map/rw,rcz->wcz/dot_general | solution.py:106
  294.1 29.2 %fusion.4 = f32[10,128,2304]{2,0,1:T(8,128)} fusion(f32[16,128,2304]{2,1,0:T(8,128)} %fusion.16, s32[16]{0:T(128)S(1)} %get-tuple-element.5), kind=kOutput, calls=%fused_computation.25 | convolution fusion | flops 566231168 | bytes 30670912 | tf_op jit(solution)/shard_map/rw,rcz->wcz/dot_general | solution.py:106
  323.2 28.9 %fusion = f32[10,128,2304]{2,0,1:T(8,128)} fusion(f32[16,128,2304]{2,1,0:T(8,128)} %fusion.14, s32[16]{0:T(128)S(1)} %get-tuple-element.7), kind=kOutput, calls=%fused_computation.21 | convolution fusion | flops 566231168 | bytes 30670912 | tf_op jit(solution)/shard_map/rw,rcz->wcz/dot_general | solution.py:106
  352.2 39.6 %fusion.42 = (bf16[10,128,2304]{2,0,1:T(8,128)(2,1)}, f32[10,128,2304]{2,0,1:T(8,128)}) fusion(f32[10,128,2304]{2,0,1:T(8,128)} %fusion, f32[10,128,2304]{2,0,1:T(8,128)} %fusion.2, f32[10,128,2304]{2,0,1:T(8,128)} %fusion.4, f32[16,128,2304]{2,1,0:T(8,128)} %fusion.43, s32[16]{0:T(128)S(1)} %get-tuple-element.20), kind=kOutput, calls=%fused_computation.112 | convolution fusion | flops 578027648 | bytes 71958592 | tf_op jit(solution)/shard_map/rw,rcz->wcz/dot_general | solution.py:106
  391.7 8.6 %fusion.41 = (bf16[2,128,2304]{2,0,1:T(2,128)(2,1)S(1)}, bf16[2,128,2304]{2,0,1:T(2,128)(2,1)S(1)}, bf16[2,128,2304]{2,0,1:T(2,128)(2,1)S(1)}, bf16[2,128,2304]{2,0,1:T(2,128)(2,1)S(1)}) fusion(bf16[10,128,2304]{2,0,1:T(8,128)(2,1)} %get-tuple-element.23), kind=kLoop, calls=%fused_computation.111 | loop fusion | bytes 9437184 | tf_op jit(solution)/shard_map/slice | solution.py:112
  400.5 1.9 collective-permute-start.16
  402.5 7.9 %collective-permute-start.17 = (bf16[256,2304]{1,0:T(8,128)(2,1)S(1)}, bf16[256,2304]{1,0:T(8,128)(2,1)S(1)}, u32[]{:S(2)}, u32[]{:S(2)}) collective-permute-start(bf16[256,2304]{1,0:T(8,128)(2,1)S(1)} %bitcast.108), channel_id=1, source_target_pairs={{1,0},{2,1},{3,2},{4,3},{5,4},{6,5},{7,6},{8,7},{9,8},{10,9},{11,1... | collective-permute-start | bytes 3538952 | tf_op jit(solution)/shard_map/ppermute | solution.py:15
  412.6 8.1 %collective-permute-start.19 = (bf16[256,2304]{1,0:T(8,128)(2,1)S(1)}, bf16[256,2304]{1,0:T(8,128)(2,1)S(1)}, u32[]{:S(2)}, u32[]{:S(2)}) collective-permute-start(bf16[256,2304]{1,0:T(8,128)(2,1)S(1)} %bitcast.110), channel_id=1, source_target_pairs={{2,0},{3,1},{4,2},{5,3},{6,4},{7,5},{8,6},{9,7},{10,8},{11,9},{12,... | collective-permute-start | bytes 3538952 | tf_op jit(solution)/shard_map/ppermute | solution.py:15
  420.7 4.7 %slice.128 = f32[2,128,2304]{2,0,1:T(2,128)S(1)} slice(f32[10,128,2304]{2,0,1:T(8,128)} %get-tuple-element.24), slice={[4:6], [0:128], [0:2304]} | slice | bytes 4718592 | tf_op jit(solution)/shard_map/slice | solution.py:112
  425.6 7.4 %collective-permute-done.17 = bf16[256,2304]{1,0:T(8,128)(2,1)S(1)} collective-permute-done((bf16[256,2304]{1,0:T(8,128)(2,1)S(1)}, bf16[256,2304]{1,0:T(8,128)(2,1)S(1)}, u32[]{:S(2)}, u32[]{:S(2)}) %collective-permute-start.17) | collective-permute-done | bytes 1179680 | tf_op jit(solution)/shard_map/ppermute | solution.py:15
  433.0 12.5 %collective-permute-done.18 = bf16[256,2304]{1,0:T(8,128)(2,1)S(1)} collective-permute-done((bf16[256,2304]{1,0:T(8,128)(2,1)S(1)}, bf16[256,2304]{1,0:T(8,128)(2,1)S(1)}, u32[]{:S(2)}, u32[]{:S(2)}) %collective-permute-start.18) | collective-permute-done | bytes 1179680 | tf_op jit(solution)/shard_map/ppermute | solution.py:15
  445.5 3.8 collective-permute-done.19
  449.4 2.4 convert_add_fusion
  (101 shorter events, 44.8 us)
Async XLA Ops:
  0.0 95.4 %copy-start = (bf16[16,3,128,128]{3,2,1,0:T(8,128)(2,1)S(1)}, bf16[16,3,128,128]{3,2,1,0:T(8,128)(2,1)}, u32[]{:S(2)}) copy-start(bf16[16,3,128,128]{3,2,1,0:T(8,128)(2,1)} %param.7) | copy-start | bytes 4718596
  0.0 38.9 %copy-start.2 = (s32[16]{0:T(128)S(1)}, s32[16]{0:T(128)}, u32[]{:S(2)}) copy-start(s32[16]{0:T(128)} %param.10) | copy-start | bytes 196
  0.0 38.9 %copy-start.9 = (s32[16,3]{0,1:T(4,128)S(1)}, s32[16,3]{0,1:T(4,128)}, u32[]{:S(2)}) copy-start(s32[16,3]{0,1:T(4,128)} %param.8) | copy-start | bytes 580
  0.0 39.1 %copy-start.7 = (bf16[16,128,128]{2,1,0:T(8,128)(2,1)S(1)}, bf16[16,128,128]{2,1,0:T(8,128)(2,1)}, u32[]{:S(2)}) copy-start(bf16[16,128,128]{2,1,0:T(8,128)(2,1)} %param.6) | copy-start | bytes 1572868
  3.2 88.3 %collective-permute-start = (bf16[4,128,128]{2,1,0:T(8,128)(2,1)}, bf16[4,128,128]{2,1,0:T(8,128)(2,1)S(1)}, u32[]{:S(2)}, u32[]{:S(2)}) collective-permute-start(bf16[4,128,128]{2,1,0:T(8,128)(2,1)} %gather_fusion.1), channel_id=1, source_target_pairs={{0,1},{1,2},{2,3},{3,4},{4,5},{5,6},{6,7},{7,8},{8,9},{9,10},{10,1... | collective-permute-start | bytes 393224 | tf_op jit(solution)/shard_map/ppermute | solution.py:15
  7.4 84.2 %collective-permute-start.1 = (bf16[4,128,128]{2,1,0:T(8,128)(2,1)}, bf16[4,128,128]{2,1,0:T(8,128)(2,1)S(1)}, u32[]{:S(2)}, u32[]{:S(2)}) collective-permute-start(bf16[4,128,128]{2,1,0:T(8,128)(2,1)} %gather_fusion.2), channel_id=1, source_target_pairs={{1,0},{2,1},{3,2},{4,3},{5,4},{6,5},{7,6},{8,7},{9,8},{10,9},{11,1... | collective-permute-start | bytes 393224 | tf_op jit(solution)/shard_map/ppermute | solution.py:15
  17.5 26.9 %copy-start.6 = (bf16[16,128,128]{2,1,0:T(8,128)(2,1)S(1)}, bf16[16,128,128]{2,1,0:T(8,128)(2,1)}, u32[]{:S(2)}) copy-start(bf16[16,128,128]{2,1,0:T(8,128)(2,1)} %param.9) | copy-start | bytes 1572868
  17.5 74.1 %collective-permute-start.2 = (bf16[4,128,128]{2,1,0:T(8,128)(2,1)}, bf16[4,128,128]{2,1,0:T(8,128)(2,1)}, u32[]{:S(2)}, u32[]{:S(2)}) collective-permute-start(bf16[4,128,128]{2,1,0:T(8,128)(2,1)} %gather_fusion.3), channel_id=1, source_target_pairs={{0,2},{1,3},{2,4},{3,5},{4,6},{5,7},{6,8},{7,9},{8,10},{9,11},{10,... | collective-permute-start | bytes 393224 | tf_op jit(solution)/shard_map/ppermute | solution.py:15
  21.8 70.7 %collective-permute-start.3 = (bf16[4,128,128]{2,1,0:T(8,128)(2,1)}, bf16[4,128,128]{2,1,0:T(8,128)(2,1)}, u32[]{:S(2)}, u32[]{:S(2)}) collective-permute-start(bf16[4,128,128]{2,1,0:T(8,128)(2,1)} %gather_fusion.4), channel_id=1, source_target_pairs={{2,0},{3,1},{4,2},{5,3},{6,4},{7,5},{8,6},{9,7},{10,8},{11,9},{12,... | collective-permute-start | bytes 393224 | tf_op jit(solution)/shard_map/ppermute | solution.py:15
  31.2 14.6 %collective-permute-start.11 = (s32[4]{0:T(128)S(1)}, s32[4]{0:T(128)S(1)}, u32[]{:S(2)}, u32[]{:S(2)}) collective-permute-start(s32[4]{0:T(128)S(1)} %gather_fusion.14), channel_id=1, source_target_pairs={{2,0},{3,1},{4,2},{5,3},{6,4},{7,5},{8,6},{9,7},{10,8},{11,9},{12,... | collective-permute-start | bytes 56 | tf_op jit(solution)/shard_map/ppermute | solution.py:15
  44.7 23.0 %copy-start.4 = (bf16[16,128,128]{2,1,0:T(8,128)(2,1)}, bf16[16,128,128]{2,1,0:T(8,128)(2,1)S(1)}, u32[]{:S(2)}) copy-start(bf16[16,128,128]{2,1,0:T(8,128)(2,1)S(1)} %fusion.13) | copy-start | bytes 1572868
  45.8 9.6 %collective-permute-start.10 = (s32[4]{0:T(128)S(1)}, s32[4]{0:T(128)S(1)}, u32[]{:S(2)}, u32[]{:S(2)}) collective-permute-start(s32[4]{0:T(128)S(1)} %gather_fusion.13), channel_id=1, source_target_pairs={{0,2},{1,3},{2,4},{3,5},{4,6},{5,7},{6,8},{7,9},{8,10},{9,11},{10,... | collective-permute-start | bytes 56 | tf_op jit(solution)/shard_map/ppermute | solution.py:15
  55.5 3.2 collective-permute-start.9
  58.7 9.1 %collective-permute-start.8 = (s32[4]{0:T(128)S(1)}, s32[4]{0:T(128)S(1)}, u32[]{:S(2)}, u32[]{:S(2)}) collective-permute-start(s32[4]{0:T(128)S(1)} %gather_fusion.11), channel_id=1, source_target_pairs={{0,1},{1,2},{2,3},{3,4},{4,5},{5,6},{6,7},{7,8},{8,9},{9,10},{10,1... | collective-permute-start | bytes 56 | tf_op jit(solution)/shard_map/ppermute | solution.py:15
  67.8 23.7 %copy-start.8 = (bf16[32,128,128]{2,1,0:T(8,128)(2,1)S(1)}, bf16[32,128,128]{2,1,0:T(8,128)(2,1)}, u32[]{:S(2)}) copy-start(bf16[32,128,128]{2,1,0:T(8,128)(2,1)} %constant_dynamic-update-slice_fusion.4) | copy-start | bytes 3145732
  71.2 5.5 %collective-permute-start.15 = (s32[4,4]{1,0:T(4,128)S(1)}, s32[4,4]{1,0:T(4,128)S(1)}, u32[]{:S(2)}, u32[]{:S(2)}) collective-permute-start(s32[4,4]{1,0:T(4,128)S(1)} %gather_fusion.19), channel_id=1, source_target_pairs={{2,0},{3,1},{4,2},{5,3},{6,4},{7,5},{8,6},{9,7},{10,8},{11,9},{12,... | collective-permute-start | bytes 200 | tf_op jit(solution)/shard_map/ppermute | solution.py:15
  76.7 9.7 %collective-permute-start.14 = (s32[4,4]{1,0:T(4,128)S(1)}, s32[4,4]{1,0:T(4,128)S(1)}, u32[]{:S(2)}, u32[]{:S(2)}) collective-permute-start(s32[4,4]{1,0:T(4,128)S(1)} %gather_fusion.18), channel_id=1, source_target_pairs={{0,2},{1,3},{2,4},{3,5},{4,6},{5,7},{6,8},{7,9},{8,10},{9,11},{10,... | collective-permute-start | bytes 200 | tf_op jit(solution)/shard_map/ppermute | solution.py:15
  86.4 3.2 collective-permute-start.13
  89.6 28.5 %collective-permute-start.12 = (s32[4,4]{1,0:T(4,128)S(1)}, s32[4,4]{1,0:T(4,128)S(1)}, u32[]{:S(2)}, u32[]{:S(2)}) collective-permute-start(s32[4,4]{1,0:T(4,128)S(1)} %gather_fusion.16), channel_id=1, source_target_pairs={{0,1},{1,2},{2,3},{3,4},{4,5},{5,6},{6,7},{7,8},{8,9},{9,10},{10,1... | collective-permute-start | bytes 200 | tf_op jit(solution)/shard_map/ppermute | solution.py:15
  108.3 31.1 %collective-permute-start.4 = (bf16[4,4,128,128]{2,3,1,0:T(8,128)(2,1)}, bf16[4,4,128,128]{2,3,1,0:T(8,128)(2,1)}, u32[]{:S(2)}, u32[]{:S(2)}) collective-permute-start(bf16[4,4,128,128]{2,3,1,0:T(8,128)(2,1)} %gather_fusion.6), channel_id=1, source_target_pairs={{0,1},{1,2},{2,3},{3,4},{4,5},{5,6},{6,7},{7,8},{8,9},{9,10},{10,1... | collective-permute-start | bytes 1572872 | tf_op jit(solution)/shard_map/ppermute | solution.py:15
  110.2 31.1 %collective-permute-start.5 = (bf16[4,4,128,128]{2,3,1,0:T(8,128)(2,1)}, bf16[4,4,128,128]{2,3,1,0:T(8,128)(2,1)}, u32[]{:S(2)}, u32[]{:S(2)}) collective-permute-start(bf16[4,4,128,128]{2,3,1,0:T(8,128)(2,1)} %gather_fusion.7), channel_id=1, source_target_pairs={{1,0},{2,1},{3,2},{4,3},{5,4},{6,5},{7,6},{8,7},{9,8},{10,9},{11,1... | collective-permute-start | bytes 1572872 | tf_op jit(solution)/shard_map/ppermute | solution.py:15
  121.9 21.3 %collective-permute-start.6 = (bf16[4,4,128,128]{2,3,1,0:T(8,128)(2,1)}, bf16[4,4,128,128]{2,3,1,0:T(8,128)(2,1)}, u32[]{:S(2)}, u32[]{:S(2)}) collective-permute-start(bf16[4,4,128,128]{2,3,1,0:T(8,128)(2,1)} %gather_fusion.8), channel_id=1, source_target_pairs={{0,2},{1,3},{2,4},{3,5},{4,6},{5,7},{6,8},{7,9},{8,10},{9,11},{10,... | collective-permute-start | bytes 1572872 | tf_op jit(solution)/shard_map/ppermute | solution.py:15
  126.9 18.2 %collective-permute-start.7 = (bf16[4,4,128,128]{2,3,1,0:T(8,128)(2,1)}, bf16[4,4,128,128]{2,3,1,0:T(8,128)(2,1)S(1)}, u32[]{:S(2)}, u32[]{:S(2)}) collective-permute-start(bf16[4,4,128,128]{2,3,1,0:T(8,128)(2,1)} %gather_fusion.9), channel_id=1, source_target_pairs={{2,0},{3,1},{4,2},{5,3},{6,4},{7,5},{8,6},{9,7},{10,8},{11,9},{12,... | collective-permute-start | bytes 1572872 | tf_op jit(solution)/shard_map/ppermute | solution.py:15
  153.1 4.0 copy-start.3
  239.6 12.7 %copy-start.5 = (bf16[16,128,128]{2,1,0:T(8,128)(2,1)S(1)}, bf16[16,128,128]{2,1,0:T(8,128)(2,1)}, u32[]{:S(2)}) copy-start(bf16[16,128,128]{2,1,0:T(8,128)(2,1)} %copy-done.4) | copy-start | bytes 1572868
  400.5 25.1 %collective-permute-start.16 = (bf16[256,2304]{1,0:T(8,128)(2,1)S(1)}, bf16[256,2304]{1,0:T(8,128)(2,1)S(1)}, u32[]{:S(2)}, u32[]{:S(2)}) collective-permute-start(bf16[256,2304]{1,0:T(8,128)(2,1)S(1)} %bitcast.107), channel_id=1, source_target_pairs={{0,1},{1,2},{2,3},{3,4},{4,5},{5,6},{6,7},{7,8},{8,9},{9,10},{10,1... | collective-permute-start | bytes 3538952 | tf_op jit(solution)/shard_map/ppermute | solution.py:15
  402.5 30.5 %collective-permute-start.17 = (bf16[256,2304]{1,0:T(8,128)(2,1)S(1)}, bf16[256,2304]{1,0:T(8,128)(2,1)S(1)}, u32[]{:S(2)}, u32[]{:S(2)}) collective-permute-start(bf16[256,2304]{1,0:T(8,128)(2,1)S(1)} %bitcast.108), channel_id=1, source_target_pairs={{1,0},{2,1},{3,2},{4,3},{5,4},{6,5},{7,6},{8,7},{9,8},{10,9},{11,1... | collective-permute-start | bytes 3538952 | tf_op jit(solution)/shard_map/ppermute | solution.py:15
  410.5 35.0 %collective-permute-start.18 = (bf16[256,2304]{1,0:T(8,128)(2,1)S(1)}, bf16[256,2304]{1,0:T(8,128)(2,1)S(1)}, u32[]{:S(2)}, u32[]{:S(2)}) collective-permute-start(bf16[256,2304]{1,0:T(8,128)(2,1)S(1)} %bitcast.109), channel_id=1, source_target_pairs={{0,2},{1,3},{2,4},{3,5},{4,6},{5,7},{6,8},{7,9},{8,10},{9,11},{10,... | collective-permute-start | bytes 3538952 | tf_op jit(solution)/shard_map/ppermute | solution.py:15
  412.6 36.8 %collective-permute-start.19 = (bf16[256,2304]{1,0:T(8,128)(2,1)S(1)}, bf16[256,2304]{1,0:T(8,128)(2,1)S(1)}, u32[]{:S(2)}, u32[]{:S(2)}) collective-permute-start(bf16[256,2304]{1,0:T(8,128)(2,1)S(1)} %bitcast.110), channel_id=1, source_target_pairs={{2,0},{3,1},{4,2},{5,3},{6,4},{7,5},{8,6},{9,7},{10,8},{11,9},{12,... | collective-permute-start | bytes 3538952 | tf_op jit(solution)/shard_map/ppermute | solution.py:15
  449.4 2.4 copy-start.1
where the time goes:
time: 459 us; the launch traced here: 452 us
  matrix products  207 us (45%)
  local copies, waits for them, and re-layouts  103 us (22%)
  starting transfers between devices  77.3 us (17%)
  waiting for transfers between devices  50.4 us (11%)
  other arithmetic  13.9 us (3%)
    dot_general x4, matrix products, local(): jnp.einsum('rw,rcz->wcz', select, contrib, precision=lax.Precision.HIGHEST)  127 us
    ppermute x20, starting transfers between devices, from_behind(): lax.ppermute(value, axis, [(source, source + steps) for source in range(i...  77.3 us
    dot_general x4, matrix products, local(): jnp.einsum('ric,riz->rcz', slots[:, member], applied, preferred_element_t...  51 us
    ppermute x20, waiting for transfers between devices, from_behind(): lax.ppermute(value, axis, [(source, source + steps) for source in range(i...  50.4 us
    dot_general x1, matrix products, place_slots(): jnp.einsum('rkw,rkic->riwc', select, slot_values, precision=lax.Precision...  17.9 us
    reshape x1, local copies, waits for them, and re-layouts, local(): jnp.concatenate([own_prod[:, None], off_prod], axis=1)  17.6 us
    convert_element_type x1, local copies, waits for them, and re-layouts, local(): place_slots(all_prod, all_labels, frame_blocks).astype(jnp.bfloat16)  15.3 us
    slice x7, local copies, waits for them, and re-layouts, rows_at(): return partial_value[level * row_span:(level + 1) * row_span]  13.9 us
  transfers between devices with their start and end apart: 20, of which 9 were waited for; matrix products, arithmetic and copies ran while one was open for 14% of the time, Pallas kernels for 0%

commit v1 on v0

v1 whole, which is shorter than its diff:
```python
import jax
import jax.numpy as jnp
from jax import lax
from jax.experimental import pallas as pl
from jax.experimental.pallas import tpu as pltpu
from jax.sharding import PartitionSpec as P

AXES = ("bulk", "coarse")
OFFSETS = (1, -1, 2, -2)
BS = 128
NB = 16
NG = 4
NT = NB + 4 * NG
FRAME = 18
WIDE = FRAME * BS
SLOTW = 4 * BS
EXTRA = 16
BF = jnp.bfloat16
F32 = jnp.float32
SMEM = pltpu.SMEM
ANY = pl.ANY
VMEM_LIMIT = 56 * 1024 * 1024


def spec(space):
    return pl.BlockSpec(memory_space=space)


def shift(value, steps):
    count = lax.axis_size(AXES)
    first, last = max(0, -steps), min(count, count - steps)
    return lax.ppermute(value, AXES, [(s, s + steps) for s in range(first, last)])


def label_rows(values, width):
    lane = lax.broadcasted_iota(jnp.int32, (EXTRA, width), 1)
    total = jnp.zeros((EXTRA, width), jnp.int32)
    for at, value in enumerate(values):
        total = jnp.where(lane == at, value, total)
    return total.astype(F32).astype(BF)


def pack_kernel(send_rows, aggregate, tent, *refs):
    outs, labels, sem = refs[:4], refs[4], refs[5]
    copies = []
    for n in range(4):
        for g in range(NG):
            copies.append(
                pltpu.make_async_copy(
                    tent.at[send_rows[n, g]], outs[n].at[pl.ds(g * BS, BS)], sem.at[n, g]
                )
            )
    for copy in copies:
        copy.start()
    for n in range(4):
        labels[n] = label_rows([aggregate[send_rows[n, g]] for g in range(NG)], BS)
        copy = pltpu.make_async_copy(labels.at[n], outs[n].at[pl.ds(NG * BS, EXTRA)], sem.at[n, NG])
        copy.start()
        copies.append(copy)
    for copy in copies:
        copy.wait()


def pack(send_rows, aggregate, tent):
    shape = jax.ShapeDtypeStruct((NG * BS + EXTRA, BS), BF)
    return pl.pallas_call(
        pack_kernel,
        out_shape=[shape] * 4,
        in_specs=[spec(SMEM), spec(SMEM), spec(ANY)],
        out_specs=[spec(ANY)] * 4,
        scratch_shapes=[pltpu.VMEM((4, EXTRA, BS), BF), pltpu.SemaphoreType.DMA((4, NG + 1))],
        name="pack",
    )(send_rows, aggregate, tent)


def slots_kernel(
    send_rows, off_columns, aggregate, diag, off, tent, g0, g1, g2, g3,
    own_labels, slots, slots_t, s0, s1, s2, s3,
    table, labels_in, labels_out, label_smem, slot_buf, sem_in, sem_lab, sem_out,
):
    ghosts, sends = (g0, g1, g2, g3), (s0, s1, s2, s3)
    copies = [pltpu.make_async_copy(tent, table.at[pl.ds(0, NB)], sem_in.at[0])]
    for n in range(4):
        for g in range(NG):
            copies.append(
                pltpu.make_async_copy(
                    ghosts[n].at[pl.ds(g * BS, BS)], table.at[NB + n * NG + g], sem_in.at[1 + n * NG + g]
                )
            )
    lab = [
        pltpu.make_async_copy(ghosts[n].at[pl.ds(NG * BS, EXTRA)], labels_out.at[n, :, pl.ds(0, BS)], sem_lab.at[n])
        for n in range(4)
    ]
    for copy in lab + copies:
        copy.start()
    for copy in lab:
        copy.wait()
    for n in range(4):
        labels_in[n] = labels_out[n, :, pl.ds(0, BS)].astype(F32).astype(jnp.int32)[:8]
    to_smem = pltpu.make_async_copy(labels_in, label_smem, sem_lab.at[0])
    to_smem.start()
    for copy in copies:
        copy.wait()
    to_smem.wait()

    eye = lax.broadcasted_iota(jnp.int32, (BS, BS), 0) == lax.broadcasted_iota(jnp.int32, (BS, BS), 1)

    def row(i, carry):
        block = diag[i]
        inv = 1.0 / jnp.sum(jnp.where(eye, block.astype(F32), 0.0), axis=1, keepdims=True)
        scale = 0.6 * inv
        own = table[i]
        first = own.astype(F32) - scale * jnp.dot(block, own, preferred_element_type=F32)
        parts = [first]
        for k in range(3):
            near = table[off_columns[i, k]]
            parts.append(-scale * jnp.dot(off[i, k], near, preferred_element_type=F32))
        for k in range(4):
            slot = parts[k].astype(BF)
            slot_buf[i, :, k * BS : (k + 1) * BS] = slot
            slots_t[i, k * BS : (k + 1) * BS, :] = slot.T
        own_labels[i, 0] = aggregate[i] + 8
        for k in range(3):
            c = off_columns[i, k]
            ghost = jnp.maximum(c - NB, 0)
            n = lax.div(ghost, NG)
            base = 8 - 2 * jnp.where(n == 0, 1, jnp.where(n == 1, -1, jnp.where(n == 2, 2, -2)))
            remote = label_smem[n, 0, lax.rem(ghost, NG)] + base
            local = aggregate[jnp.minimum(c, NB - 1)] + 8
            own_labels[i, k + 1] = jnp.where(c < NB, local, remote)
        return carry

    lax.fori_loop(0, NB, row, 0)

    outs = [pltpu.make_async_copy(slot_buf, slots, sem_out.at[0])]
    for n in range(4):
        for g in range(NG):
            outs.append(
                pltpu.make_async_copy(
                    slot_buf.at[send_rows[n, g]], sends[n].at[pl.ds(g * BS, BS)], sem_out.at[1 + n * NG + g]
                )
            )
    for copy in outs:
        copy.start()
    for n in range(4):
        values = [own_labels[send_rows[n, g], k] for g in range(NG) for k in range(4)]
        labels_out[n] = label_rows(values, SLOTW)
        copy = pltpu.make_async_copy(labels_out.at[n], sends[n].at[pl.ds(NG * BS, EXTRA)], sem_lab.at[n])
        copy.start()
        outs.append(copy)
    for copy in outs:
        copy.wait()


def make_slots(send_rows, off_columns, aggregate, diag, off, tent, ghosts):
    send = jax.ShapeDtypeStruct((NG * BS + EXTRA, SLOTW), BF)
    return pl.pallas_call(
        slots_kernel,
        out_shape=[
            jax.ShapeDtypeStruct((NB, 4), jnp.int32),
            jax.ShapeDtypeStruct((NB, BS, SLOTW), BF),
            jax.ShapeDtypeStruct((NB, SLOTW, BS), BF),
        ]
        + [send] * 4,
        in_specs=[spec(SMEM)] * 3 + [spec(pltpu.VMEM)] * 2 + [spec(ANY)] * 5,
        out_specs=[spec(SMEM), spec(ANY), spec(pltpu.VMEM)] + [spec(ANY)] * 4,
        scratch_shapes=[
            pltpu.VMEM((NT, BS, BS), BF),
            pltpu.VMEM((4, 8, BS), jnp.int32),
            pltpu.VMEM((4, EXTRA, SLOTW), BF),
            pltpu.SMEM((4, 8, BS), jnp.int32),
            pltpu.VMEM((NB, BS, SLOTW), BF),
            pltpu.SemaphoreType.DMA((1 + 4 * NG,)),
            pltpu.SemaphoreType.DMA((4,)),
            pltpu.SemaphoreType.DMA((1 + 4 * NG,)),
        ],
        compiler_params=pltpu.CompilerParams(vmem_limit_bytes=VMEM_LIMIT),
        name="slots",
    )(send_rows, off_columns, aggregate, diag, off, tent, *ghosts)


def coarse_kernel(
    off_columns, own_labels, diag, off, slots, slots_t, g0, g1, g2, g3,
    own_rows, s0, s1, s2, s3,
    table, labels_in, labels_vmem, label_smem, total, applied, coarse, sem_in, sem_lab,
):
    ghosts, sends = (g0, g1, g2, g3), (s0, s1, s2, s3)
    copies = [pltpu.make_async_copy(slots, table.at[pl.ds(0, NB)], sem_in.at[0])]
    for n in range(4):
        for g in range(NG):
            copies.append(
                pltpu.make_async_copy(
                    ghosts[n].at[pl.ds(g * BS, BS)], table.at[NB + n * NG + g], sem_in.at[1 + n * NG + g]
                )
            )
    lab = [
        pltpu.make_async_copy(ghosts[n].at[pl.ds(NG * BS, EXTRA), pl.ds(0, BS)], labels_in.at[n], sem_lab.at[n])
        for n in range(4)
    ]
    for copy in lab + copies:
        copy.start()
    coarse[...] = jnp.zeros_like(coarse)
    for copy in lab:
        copy.wait()
    for n in range(4):
        labels_vmem[n] = labels_in[n].astype(F32).astype(jnp.int32)[:8] - 2 * OFFSETS[n]
    to_smem = pltpu.make_async_copy(labels_vmem, label_smem, sem_lab.at[0])
    to_smem.start()
    for copy in copies:
        copy.wait()
    to_smem.wait()

    def label_of(j, m):
        ghost = jnp.maximum(j - NB, 0)
        remote = label_smem[lax.div(ghost, NG), 0, lax.rem(ghost, NG) * 4 + m]
        local = own_labels[jnp.minimum(j, NB - 1), m]
        return jnp.clip(jnp.where(j < NB, local, remote), 0, FRAME - 1)

    def row(i, carry):
        total[...] = jnp.zeros_like(total)
        for k in range(4):
            j = i if k == 0 else off_columns[i, k - 1]
            block = diag[i] if k == 0 else off[i, k - 1]
            prod = jnp.dot(block, table[j], preferred_element_type=F32)
            for m in range(4):
                at = label_of(j, m)
                total[at] = total[at] + prod[:, m * BS : (m + 1) * BS]
        for at in range(FRAME):
            applied[:, at * BS : (at + 1) * BS] = total[at].astype(BF)
        left = slots_t[i]
        targets = [jnp.clip(own_labels[i, s] - 4, 0, 9) for s in range(4)]
        for t in range(FRAME // 2):
            cols = slice(t * 2 * BS, (t + 1) * 2 * BS)
            res = jnp.dot(left, applied[:, cols], preferred_element_type=F32)
            for s in range(4):
                coarse[targets[s], :, cols] = coarse[targets[s], :, cols] + res[s * BS : (s + 1) * BS]
        return carry

    lax.fori_loop(0, NB, row, 0)
    own_rows[...] = coarse[4:6]
    for n in range(4):
        level = OFFSETS[n] + 2
        sends[n][...] = coarse[2 * level : 2 * level + 2].astype(BF)


def make_coarse(off_columns, own_labels, diag, off, slots, slots_t, ghosts):
    send = jax.ShapeDtypeStruct((2, BS, WIDE), BF)
    return pl.pallas_call(
        coarse_kernel,
        out_shape=[jax.ShapeDtypeStruct((2, BS, WIDE), F32)] + [send] * 4,
        in_specs=[spec(SMEM)] * 2 + [spec(pltpu.VMEM)] * 2 + [spec(ANY), spec(pltpu.VMEM)] + [spec(ANY)] * 4,
        out_specs=[spec(pltpu.VMEM)] * 5,
        scratch_shapes=[
            pltpu.VMEM((NT, BS, SLOTW), BF),
            pltpu.VMEM((4, EXTRA, BS), BF),
            pltpu.VMEM((4, 8, BS), jnp.int32),
            pltpu.SMEM((4, 8, BS), jnp.int32),
            pltpu.VMEM((FRAME, BS, BS), F32),
            pltpu.VMEM((BS, WIDE), BF),
            pltpu.VMEM((10, BS, WIDE), F32),
            pltpu.SemaphoreType.DMA((1 + 4 * NG,)),
            pltpu.SemaphoreType.DMA((4,)),
        ],
        compiler_params=pltpu.CompilerParams(vmem_limit_bytes=VMEM_LIMIT),
        name="coarse",
    )(off_columns, own_labels, diag, off, slots, slots_t, *ghosts)


def local(diag_blocks, off_blocks, off_columns, tentative, aggregate, send_rows):
    sends = pack(send_rows, aggregate, tentative)
    ghosts = [shift(value, by) for value, by in zip(sends, OFFSETS)]
    own_labels, slots, slots_t, *sends = make_slots(
        send_rows, off_columns, aggregate, diag_blocks, off_blocks, tentative, ghosts
    )
    ghosts = [shift(value, by) for value, by in zip(sends, OFFSETS)]
    own_rows, *sends = make_coarse(
        off_columns, own_labels, diag_blocks, off_blocks, slots, slots_t, ghosts
    )

    def band(piece, start):
        lead = start * 2 * BS
        return jnp.pad(piece.astype(F32), ((0, 0), (0, 0), (lead, 26 * BS - lead - WIDE)))

    summed = band(own_rows, 2)
    for value, by in zip(sends, OFFSETS):
        summed = summed + band(shift(value, by), 2 - by)
    return summed


def solution(mesh):
    in_specs = (
        P(AXES, None, None),
        P(AXES, None, None, None),
        P(AXES, None),
        P(AXES, None, None),
        P(AXES),
        P(AXES, None),
    )
    return jax.shard_map(
        local, mesh=mesh, in_specs=in_specs, out_specs=P(AXES, None, None), check_vma=False
    )
```

time: 459 us -> 164 us (0.36); the launches traced: 452 us -> 162 us
  matrix products: 207 us -> 0 us
  local copies, waits for them, and re-layouts: 103 us -> 2.82 us
  Pallas kernels: 0 us -> 56.5 us
  starting transfers between devices: 77.3 us -> 59.5 us
  waiting for transfers between devices: 50.4 us -> 39.3 us
  other arithmetic: 13.9 us -> 4.17 us
    dot_general x13 -> x0, matrix products: 207 us -> none  [the longest x4 127 us: local(): jnp.einsum('rw,rcz->wcz', select, contrib, precision=lax.Precision.HIGHEST)]
    pallas_call x0 -> x3, Pallas kernels: none -> 56.5 us  [the longest x1 27.7 us: make_coarse(): pl.pallas_call(coarse_kernel, out_shape=[jax.ShapeDtypeStruct((2, BS, WID...]
    gather x25 -> x0, local copies, waits for them, and re-layouts: 41.2 us -> none  [the longest x4 12.1 us: local(): slots[picked]]
    ppermute x20 -> x12, starting transfers between devices: 77.3 us -> 59.5 us  [shift(): lax.ppermute(value, AXES, [(s, s + steps) for s in range(first, last)])]
    reshape x1 -> x0, local copies, waits for them, and re-layouts: 17.6 us -> none  [local(): jnp.concatenate([own_prod[:, None], off_prod], axis=1)]
    convert_element_type x1 -> x0, local copies, waits for them, and re-layouts: 15.3 us -> none  [local(): place_slots(all_prod, all_labels, frame_blocks).astype(jnp.bfloat16)]
    slice x7 -> x0, local copies, waits for them, and re-layouts: 13.9 us -> none  [rows_at(): return partial_value[level * row_span:(level + 1) * row_span]]
    ppermute x20 -> x12, waiting for transfers between devices: 50.4 us -> 39.3 us  [shift(): lax.ppermute(value, AXES, [(s, s + steps) for s in range(first, last)])]
  transfers between devices with their start and end apart: 20 -> 12, of which waited for: 9 -> 7; matrix products, arithmetic and copies ran while one was open for 14% -> 1% of each run, Pallas kernels for 0% -> 0%
where the time goes in v1:
time: 164 us; the launch traced here: 162 us
  starting transfers between devices  59.5 us (36%)
  Pallas kernels  56.5 us (34%)
  waiting for transfers between devices  39.3 us (24%)
  other arithmetic  4.17 us (3%)
  local copies, waits for them, and re-layouts  2.82 us (2%)
    ppermute x12, starting transfers between devices, shift(): lax.ppermute(value, AXES, [(s, s + steps) for s in range(first, last)])  59.5 us
    ppermute x12, waiting for transfers between devices, shift(): lax.ppermute(value, AXES, [(s, s + steps) for s in range(first, last)])  39.3 us
    pallas_call x1, Pallas kernels, make_coarse(): pl.pallas_call(coarse_kernel, out_shape=[jax.ShapeDtypeStruct((2, BS, WID...  27.7 us
    pallas_call x1, Pallas kernels, pack(): pl.pallas_call(pack_kernel, out_shape=[shape] * 4, in_specs=[spec(SMEM),...  17.9 us
    pallas_call x1, Pallas kernels, make_slots(): pl.pallas_call(slots_kernel, out_shape=[jax.ShapeDtypeStruct((NB, 4), jnp...  10.9 us
    add x1, other arithmetic, local(): summed = summed + band(shift(value, by), 2 - by)  4.17 us
  transfers between devices with their start and end apart: 12, of which 7 were waited for; matrix products, arithmetic and copies ran while one was open for 1% of the time, Pallas kernels for 0%

profile of v1, /device:TPU:24, one launch (start us, length us, event | category | flops | bytes accessed | tf_op | source)
XLA Modules:
  0.0 162.5 jit_solution(15371864279925577035)
XLA Ops:
  0.0 17.9 %pack.1 = (bf16[528,128]{1,0:T(8,128)(2,1)}, bf16[528,128]{1,0:T(8,128)(2,1)}, bf16[528,128]{1,0:T(8,128)(2,1)}, bf16[528,128]{1,0:T(8,128)(2,1)}) custom-call(s32[4,4]{1,0:T(4,128)} %send_rows.3, s32[16]{0:T(128)} %aggregate.3, bf16[16,128,128]{2,1,0:T(8,128)(2,1)} %tent.3), custom_call_target="tpu_custom_call" | custom-call | tf_op jit(solution)/shard_map/pack/pallas_call | solution.py:66
  17.9 1.9 %collective-permute-start = (bf16[528,128]{1,0:T(8,128)(2,1)}, bf16[528,128]{1,0:T(8,128)(2,1)S(1)}, u32[]{:S(2)}, u32[]{:S(2)}) collective-permute-start(bf16[528,128]{1,0:T(8,128)(2,1)} %get-tuple-element.21), channel_id=1, source_target_pairs={{0,1},{1,2},{2,3},{3,4},{4,5},{5,6},{6,7},{7,8},{8,9},{9,10},{10,1... | collective-permute-start | bytes 405512 | tf_op jit(solution)/shard_map/ppermute | solution.py:32
  19.8 7.9 %collective-permute-start.1 = (bf16[528,128]{1,0:T(8,128)(2,1)}, bf16[528,128]{1,0:T(8,128)(2,1)S(1)}, u32[]{:S(2)}, u32[]{:S(2)}) collective-permute-start(bf16[528,128]{1,0:T(8,128)(2,1)} %get-tuple-element.22), channel_id=1, source_target_pairs={{1,0},{2,1},{3,2},{4,3},{5,4},{6,5},{7,6},{8,7},{9,8},{10,9},{11,1... | collective-permute-start | bytes 405512 | tf_op jit(solution)/shard_map/ppermute | solution.py:32
  27.7 1.9 %collective-permute-start.2 = (bf16[528,128]{1,0:T(8,128)(2,1)}, bf16[528,128]{1,0:T(8,128)(2,1)S(1)}, u32[]{:S(2)}, u32[]{:S(2)}) collective-permute-start(bf16[528,128]{1,0:T(8,128)(2,1)} %get-tuple-element.23), channel_id=1, source_target_pairs={{0,2},{1,3},{2,4},{3,5},{4,6},{5,7},{6,8},{7,9},{8,10},{9,11},{10,... | collective-permute-start | bytes 405512 | tf_op jit(solution)/shard_map/ppermute | solution.py:32
  29.6 8.1 %collective-permute-start.3 = (bf16[528,128]{1,0:T(8,128)(2,1)}, bf16[528,128]{1,0:T(8,128)(2,1)S(1)}, u32[]{:S(2)}, u32[]{:S(2)}) collective-permute-start(bf16[528,128]{1,0:T(8,128)(2,1)} %get-tuple-element.24), channel_id=1, source_target_pairs={{2,0},{3,1},{4,2},{5,3},{6,4},{7,5},{8,6},{9,7},{10,8},{11,9},{12,... | collective-permute-start | bytes 405512 | tf_op jit(solution)/shard_map/ppermute | solution.py:32
  37.8 1.4 copy.8.off_columns
  39.1 0.0 collective-permute-done.g0
  39.1 0.0 copy-start.4
  39.1 0.0 collective-permute-done.1.g1
  39.1 0.0 copy-start.5
  39.1 0.0 collective-permute-done.2.g2
  39.1 0.0 copy-start.6
  39.1 1.5 collective-permute-done.3.g3
  40.6 0.0 copy-done.4
  40.6 0.0 copy-done.5
  40.6 0.0 copy-done.6
  40.6 0.0 copy-start.7
  40.6 0.7 copy-done.7
  41.3 10.9 %slots.1 = (s32[16,4]{1,0:T(8,128)}, bf16[16,128,512]{2,1,0:T(8,128)(2,1)}, bf16[16,512,128]{2,1,0:T(8,128)(2,1)}, bf16[528,512]{1,0:T(8,128)(2,1)}, bf16[528,51...) custom-call(s32[4,4]{1,0:T(4,128)} %send_rows.3, s32[16,3]{1,0:T(8,128)} %copy.8.off_columns, ...), custom_call_target="tpu_custom_call" | custom-call | tf_op jit(solution)/shard_map/slots/pallas_call | solution.py:157
  52.2 1.9 %collective-permute-start.4 = (bf16[528,512]{1,0:T(8,128)(2,1)}, bf16[528,512]{1,0:T(8,128)(2,1)S(1)}, u32[]{:S(2)}, u32[]{:S(2)}) collective-permute-start(bf16[528,512]{1,0:T(8,128)(2,1)} %get-tuple-element.28), channel_id=1, source_target_pairs={{0,1},{1,2},{2,3},{3,4},{4,5},{5,6},{6,7},{7,8},{8,9},{9,10},{10,1... | collective-permute-start | bytes 1622024 | tf_op jit(solution)/shard_map/ppermute | solution.py:32
  54.1 7.9 %collective-permute-start.5 = (bf16[528,512]{1,0:T(8,128)(2,1)}, bf16[528,512]{1,0:T(8,128)(2,1)S(1)}, u32[]{:S(2)}, u32[]{:S(2)}) collective-permute-start(bf16[528,512]{1,0:T(8,128)(2,1)} %get-tuple-element.29), channel_id=1, source_target_pairs={{1,0},{2,1},{3,2},{4,3},{5,4},{6,5},{7,6},{8,7},{9,8},{10,9},{11,1... | collective-permute-start | bytes 1622024 | tf_op jit(solution)/shard_map/ppermute | solution.py:32
  62.0 1.9 %collective-permute-start.6 = (bf16[528,512]{1,0:T(8,128)(2,1)}, bf16[528,512]{1,0:T(8,128)(2,1)S(1)}, u32[]{:S(2)}, u32[]{:S(2)}) collective-permute-start(bf16[528,512]{1,0:T(8,128)(2,1)} %get-tuple-element.30), channel_id=1, source_target_pairs={{0,2},{1,3},{2,4},{3,5},{4,6},{5,7},{6,8},{7,9},{8,10},{9,11},{10,... | collective-permute-start | bytes 1622024 | tf_op jit(solution)/shard_map/ppermute | solution.py:32
  63.9 8.1 %collective-permute-start.7 = (bf16[528,512]{1,0:T(8,128)(2,1)}, bf16[528,512]{1,0:T(8,128)(2,1)S(1)}, u32[]{:S(2)}, u32[]{:S(2)}) collective-permute-start(bf16[528,512]{1,0:T(8,128)(2,1)} %get-tuple-element.31), channel_id=1, source_target_pairs={{2,0},{3,1},{4,2},{5,3},{6,4},{7,5},{8,6},{9,7},{10,8},{11,9},{12,... | collective-permute-start | bytes 1622024 | tf_op jit(solution)/shard_map/ppermute | solution.py:32
  72.0 0.0 collective-permute-done.4.g0
  72.0 0.0 copy-start
  72.0 0.0 collective-permute-done.5.g1
  72.1 0.0 copy-start.1
  72.1 6.8 %collective-permute-done.6.g2 = bf16[528,512]{1,0:T(8,128)(2,1)S(1)} collective-permute-done((bf16[528,512]{1,0:T(8,128)(2,1)}, bf16[528,512]{1,0:T(8,128)(2,1)S(1)}, u32[]{:S(2)}, u32[]{:S(2)}) %collective-permute-start.6) | collective-permute-done | bytes 540704 | tf_op jit(solution)/shard_map/ppermute | solution.py:32
  78.8 0.0 copy-start.2
  78.8 1.9 %collective-permute-done.7.g3 = bf16[528,512]{1,0:T(8,128)(2,1)S(1)} collective-permute-done((bf16[528,512]{1,0:T(8,128)(2,1)}, bf16[528,512]{1,0:T(8,128)(2,1)S(1)}, u32[]{:S(2)}, u32[]{:S(2)}) %collective-permute-start.7) | collective-permute-done | bytes 540704 | tf_op jit(solution)/shard_map/ppermute | solution.py:32
  80.7 0.0 copy-start.3
  80.7 0.0 copy-done
  80.7 0.0 copy-done.1
  80.7 0.0 copy-done.2
  80.7 0.8 copy-done.3
  81.5 27.7 %coarse.1 = (f32[2,128,2304]{2,1,0:T(8,128)}, bf16[2,128,2304]{2,1,0:T(8,128)(2,1)}, bf16[2,128,2304]{2,1,0:T(8,128)(2,1)}, bf16[2,128,2304]{2,1,0:T(8,128)(2,1)}, bf16[2,128,2304]{2,1,0:T(8,128)(2,1)}) custom-call(s32[16,3]{1,0:T(8,128)} %copy.8.off_columns, s32[16,4]{1,0:T(8,128)} %get-tuple-element.25.own_labels, bf16[16,128,128]{2,1,0:T(8,128)(2,1)} %diag.3, ...), custom_call_target="tpu_custom_call" | custom-call | tf_op jit(solution)/shard_map/coarse/pallas_call | solution.py:248
  109.2 1.9 %collective-permute-start.8 = (bf16[2,128,2304]{2,1,0:T(8,128)(2,1)}, bf16[2,128,2304]{2,1,0:T(8,128)(2,1)S(1)}, u32[]{:S(2)}, u32[]{:S(2)}) collective-permute-start(bf16[2,128,2304]{2,1,0:T(8,128)(2,1)} %get-tuple-element.33), channel_id=1, source_target_pairs={{0,1},{1,2},{2,3},{3,4},{4,5},{5,6},{6,7},{7,8},{8,9},{9,10},{10,1... | collective-permute-start | bytes 3538952 | tf_op jit(solution)/shard_map/ppermute | solution.py:32
  111.2 7.9 %collective-permute-start.9 = (bf16[2,128,2304]{2,1,0:T(8,128)(2,1)}, bf16[2,128,2304]{2,1,0:T(8,128)(2,1)S(1)}, u32[]{:S(2)}, u32[]{:S(2)}) collective-permute-start(bf16[2,128,2304]{2,1,0:T(8,128)(2,1)} %get-tuple-element.34), channel_id=1, source_target_pairs={{1,0},{2,1},{3,2},{4,3},{5,4},{6,5},{7,6},{8,7},{9,8},{10,9},{11,1... | collective-permute-start | bytes 3538952 | tf_op jit(solution)/shard_map/ppermute | solution.py:32
  119.0 1.9 %collective-permute-start.10 = (bf16[2,128,2304]{2,1,0:T(8,128)(2,1)}, bf16[2,128,2304]{2,1,0:T(8,128)(2,1)S(1)}, u32[]{:S(2)}, u32[]{:S(2)}) collective-permute-start(bf16[2,128,2304]{2,1,0:T(8,128)(2,1)} %get-tuple-element.35), channel_id=1, source_target_pairs={{0,2},{1,3},{2,4},{3,5},{4,6},{5,7},{6,8},{7,9},{8,10},{9,11},{10,... | collective-permute-start | bytes 3538952 | tf_op jit(solution)/shard_map/ppermute | solution.py:32
  121.0 8.1 %collective-permute-start.11 = (bf16[2,128,2304]{2,1,0:T(8,128)(2,1)}, bf16[2,128,2304]{2,1,0:T(8,128)(2,1)S(1)}, u32[]{:S(2)}, u32[]{:S(2)}) collective-permute-start(bf16[2,128,2304]{2,1,0:T(8,128)(2,1)} %get-tuple-element.36), channel_id=1, source_target_pairs={{2,0},{3,1},{4,2},{5,3},{6,4},{7,5},{8,6},{9,7},{10,8},{11,9},{12,... | collective-permute-start | bytes 3538952 | tf_op jit(solution)/shard_map/ppermute | solution.py:32
  129.1 4.3 %collective-permute-done.8 = bf16[2,128,2304]{2,1,0:T(8,128)(2,1)S(1)} collective-permute-done((bf16[2,128,2304]{2,1,0:T(8,128)(2,1)}, bf16[2,128,2304]{2,1,0:T(8,128)(2,1)S(1)}, u32[]{:S(2)}, u32[]{:S(2)}) %collective-permute-start.8) | collective-permute-done | bytes 1179680 | tf_op jit(solution)/shard_map/ppermute | solution.py:32
  133.4 8.1 %collective-permute-done.9 = bf16[2,128,2304]{2,1,0:T(8,128)(2,1)S(1)} collective-permute-done((bf16[2,128,2304]{2,1,0:T(8,128)(2,1)}, bf16[2,128,2304]{2,1,0:T(8,128)(2,1)S(1)}, u32[]{:S(2)}, u32[]{:S(2)}) %collective-permute-start.9) | collective-permute-done | bytes 1179680 | tf_op jit(solution)/shard_map/ppermute | solution.py:32
  141.5 12.8 %collective-permute-done.10 = bf16[2,128,2304]{2,1,0:T(8,128)(2,1)S(1)} collective-permute-done((bf16[2,128,2304]{2,1,0:T(8,128)(2,1)}, bf16[2,128,2304]{2,1,0:T(8,128)(2,1)S(1)}, u32[]{:S(2)}, u32[]{:S(2)}) %collective-permute-start.10) | collective-permute-done | bytes 1179680 | tf_op jit(solution)/shard_map/ppermute | solution.py:32
  154.3 4.1 %collective-permute-done.11 = bf16[2,128,2304]{2,1,0:T(8,128)(2,1)S(1)} collective-permute-done((bf16[2,128,2304]{2,1,0:T(8,128)(2,1)}, bf16[2,128,2304]{2,1,0:T(8,128)(2,1)S(1)}, u32[]{:S(2)}, u32[]{:S(2)}) %collective-permute-start.11) | collective-permute-done | bytes 1179680 | tf_op jit(solution)/shard_map/ppermute | solution.py:32
  158.3 4.2 %convert_add_fusion = f32[2,128,3328]{2,1,0:T(8,128)} fusion(f32[2,128,2304]{2,1,0:T(8,128)} %get-tuple-element.32, bf16[2,128,2304]{2,1,0:T(8,128)(2,1)S(1)} %collective-permute-done.11, bf16[2,128,2304]{2,1,0:T(8,128)(2,1)S(1)} %collective-permute-done.10, bf16[2,128,2304]{2,1,0:T(8,128)(2,1)S(1)} %collective-permute-done.9, ...), kind=kLoop, calls=%fused_computation | loop fusion | flops 6815744 | bytes 10485760 | tf_op jit(solution)/shard_map/add | solution.py:286
Async XLA Ops:
  17.9 21.2 %collective-permute-start = (bf16[528,128]{1,0:T(8,128)(2,1)}, bf16[528,128]{1,0:T(8,128)(2,1)S(1)}, u32[]{:S(2)}, u32[]{:S(2)}) collective-permute-start(bf16[528,128]{1,0:T(8,128)(2,1)} %get-tuple-element.21), channel_id=1, source_target_pairs={{0,1},{1,2},{2,3},{3,4},{4,5},{5,6},{6,7},{7,8},{8,9},{9,10},{10,1... | collective-permute-start | bytes 405512 | tf_op jit(solution)/shard_map/ppermute | solution.py:32
  19.8 19.3 %collective-permute-start.1 = (bf16[528,128]{1,0:T(8,128)(2,1)}, bf16[528,128]{1,0:T(8,128)(2,1)S(1)}, u32[]{:S(2)}, u32[]{:S(2)}) collective-permute-start(bf16[528,128]{1,0:T(8,128)(2,1)} %get-tuple-element.22), channel_id=1, source_target_pairs={{1,0},{2,1},{3,2},{4,3},{5,4},{6,5},{7,6},{8,7},{9,8},{10,9},{11,1... | collective-permute-start | bytes 405512 | tf_op jit(solution)/shard_map/ppermute | solution.py:32
  27.7 11.5 %collective-permute-start.2 = (bf16[528,128]{1,0:T(8,128)(2,1)}, bf16[528,128]{1,0:T(8,128)(2,1)S(1)}, u32[]{:S(2)}, u32[]{:S(2)}) collective-permute-start(bf16[528,128]{1,0:T(8,128)(2,1)} %get-tuple-element.23), channel_id=1, source_target_pairs={{0,2},{1,3},{2,4},{3,5},{4,6},{5,7},{6,8},{7,9},{8,10},{9,11},{10,... | collective-permute-start | bytes 405512 | tf_op jit(solution)/shard_map/ppermute | solution.py:32
  29.6 11.0 %collective-permute-start.3 = (bf16[528,128]{1,0:T(8,128)(2,1)}, bf16[528,128]{1,0:T(8,128)(2,1)S(1)}, u32[]{:S(2)}, u32[]{:S(2)}) collective-permute-start(bf16[528,128]{1,0:T(8,128)(2,1)} %get-tuple-element.24), channel_id=1, source_target_pairs={{2,0},{3,1},{4,2},{5,3},{6,4},{7,5},{8,6},{9,7},{10,8},{11,9},{12,... | collective-permute-start | bytes 405512 | tf_op jit(solution)/shard_map/ppermute | solution.py:32
  39.1 1.5 copy-start.4
  39.1 1.5 copy-start.5
  39.1 1.5 copy-start.6
  40.6 0.7 copy-start.7
  52.2 19.9 %collective-permute-start.4 = (bf16[528,512]{1,0:T(8,128)(2,1)}, bf16[528,512]{1,0:T(8,128)(2,1)S(1)}, u32[]{:S(2)}, u32[]{:S(2)}) collective-permute-start(bf16[528,512]{1,0:T(8,128)(2,1)} %get-tuple-element.28), channel_id=1, source_target_pairs={{0,1},{1,2},{2,3},{3,4},{4,5},{5,6},{6,7},{7,8},{8,9},{9,10},{10,1... | collective-permute-start | bytes 1622024 | tf_op jit(solution)/shard_map/ppermute | solution.py:32
  54.1 18.0 %collective-permute-start.5 = (bf16[528,512]{1,0:T(8,128)(2,1)}, bf16[528,512]{1,0:T(8,128)(2,1)S(1)}, u32[]{:S(2)}, u32[]{:S(2)}) collective-permute-start(bf16[528,512]{1,0:T(8,128)(2,1)} %get-tuple-element.29), channel_id=1, source_target_pairs={{1,0},{2,1},{3,2},{4,3},{5,4},{6,5},{7,6},{8,7},{9,8},{10,9},{11,1... | collective-permute-start | bytes 1622024 | tf_op jit(solution)/shard_map/ppermute | solution.py:32
  62.0 16.9 %collective-permute-start.6 = (bf16[528,512]{1,0:T(8,128)(2,1)}, bf16[528,512]{1,0:T(8,128)(2,1)S(1)}, u32[]{:S(2)}, u32[]{:S(2)}) collective-permute-start(bf16[528,512]{1,0:T(8,128)(2,1)} %get-tuple-element.30), channel_id=1, source_target_pairs={{0,2},{1,3},{2,4},{3,5},{4,6},{5,7},{6,8},{7,9},{8,10},{9,11},{10,... | collective-permute-start | bytes 1622024 | tf_op jit(solution)/shard_map/ppermute | solution.py:32
  63.9 16.8 %collective-permute-start.7 = (bf16[528,512]{1,0:T(8,128)(2,1)}, bf16[528,512]{1,0:T(8,128)(2,1)S(1)}, u32[]{:S(2)}, u32[]{:S(2)}) collective-permute-start(bf16[528,512]{1,0:T(8,128)(2,1)} %get-tuple-element.31), channel_id=1, source_target_pairs={{2,0},{3,1},{4,2},{5,3},{6,4},{7,5},{8,6},{9,7},{10,8},{11,9},{12,... | collective-permute-start | bytes 1622024 | tf_op jit(solution)/shard_map/ppermute | solution.py:32
  72.0 8.7 %copy-start = (bf16[528,512]{1,0:T(8,128)(2,1)}, bf16[528,512]{1,0:T(8,128)(2,1)S(1)}, u32[]{:S(2)}) copy-start(bf16[528,512]{1,0:T(8,128)(2,1)S(1)} %collective-permute-done.4.g0) | copy-start | bytes 1622020
  72.1 8.7 %copy-start.1 = (bf16[528,512]{1,0:T(8,128)(2,1)}, bf16[528,512]{1,0:T(8,128)(2,1)S(1)}, u32[]{:S(2)}) copy-start(bf16[528,512]{1,0:T(8,128)(2,1)S(1)} %collective-permute-done.5.g1) | copy-start | bytes 1622020
  78.8 1.9 %copy-start.2 = (bf16[528,512]{1,0:T(8,128)(2,1)}, bf16[528,512]{1,0:T(8,128)(2,1)S(1)}, u32[]{:S(2)}) copy-start(bf16[528,512]{1,0:T(8,128)(2,1)S(1)} %collective-permute-done.6.g2) | copy-start | bytes 1622020
  80.7 0.8 copy-start.3
  109.2 24.2 %collective-permute-start.8 = (bf16[2,128,2304]{2,1,0:T(8,128)(2,1)}, bf16[2,128,2304]{2,1,0:T(8,128)(2,1)S(1)}, u32[]{:S(2)}, u32[]{:S(2)}) collective-permute-start(bf16[2,128,2304]{2,1,0:T(8,128)(2,1)} %get-tuple-element.33), channel_id=1, source_target_pairs={{0,1},{1,2},{2,3},{3,4},{4,5},{5,6},{6,7},{7,8},{8,9},{9,10},{10,1... | collective-permute-start | bytes 3538952 | tf_op jit(solution)/shard_map/ppermute | solution.py:32
  111.2 30.3 %collective-permute-start.9 = (bf16[2,128,2304]{2,1,0:T(8,128)(2,1)}, bf16[2,128,2304]{2,1,0:T(8,128)(2,1)S(1)}, u32[]{:S(2)}, u32[]{:S(2)}) collective-permute-start(bf16[2,128,2304]{2,1,0:T(8,128)(2,1)} %get-tuple-element.34), channel_id=1, source_target_pairs={{1,0},{2,1},{3,2},{4,3},{5,4},{6,5},{7,6},{8,7},{9,8},{10,9},{11,1... | collective-permute-start | bytes 3538952 | tf_op jit(solution)/shard_map/ppermute | solution.py:32
  119.0 35.2 %collective-permute-start.10 = (bf16[2,128,2304]{2,1,0:T(8,128)(2,1)}, bf16[2,128,2304]{2,1,0:T(8,128)(2,1)S(1)}, u32[]{:S(2)}, u32[]{:S(2)}) collective-permute-start(bf16[2,128,2304]{2,1,0:T(8,128)(2,1)} %get-tuple-element.35), channel_id=1, source_target_pairs={{0,2},{1,3},{2,4},{3,5},{4,6},{5,7},{6,8},{7,9},{8,10},{9,11},{10,... | collective-permute-start | bytes 3538952 | tf_op jit(solution)/shard_map/ppermute | solution.py:32
  121.0 37.4 %collective-permute-start.11 = (bf16[2,128,2304]{2,1,0:T(8,128)(2,1)}, bf16[2,128,2304]{2,1,0:T(8,128)(2,1)S(1)}, u32[]{:S(2)}, u32[]{:S(2)}) collective-permute-start(bf16[2,128,2304]{2,1,0:T(8,128)(2,1)} %get-tuple-element.36), channel_id=1, source_target_pairs={{2,0},{3,1},{4,2},{5,3},{6,4},{7,5},{8,6},{9,7},{10,8},{11,9},{12,... | collective-permute-start | bytes 3538952 | tf_op jit(solution)/shard_map/ppermute | solution.py:32

commit v2 on v1

v2 whole, which is shorter than its diff:
```python
import jax
import jax.numpy as jnp
from jax import lax
from jax.experimental import pallas as pl
from jax.experimental.pallas import tpu as pltpu
from jax.sharding import PartitionSpec as P

AXES = ("bulk", "coarse")
OFFSETS = (1, -1, 2, -2)
START_ORDER = (2, 3, 0, 1)
BS = 128
NB = 16
NG = 4
NT = NB + 4 * NG
FRAME = 18
WIDE = FRAME * BS
SLOTW = 4 * BS
CHIPWIDE = 20 * BS
BANDWIDE = 26 * BS
TILES = [slice(t * 2 * BS, (t + 1) * 2 * BS) for t in range(FRAME // 2)]
GROUP = 4
CHUNK = 4
EXTRA = 16
BF = jnp.bfloat16
F32 = jnp.float32
SMEM = pltpu.SMEM
ANY = pl.ANY
VMEM_LIMIT = 56 * 1024 * 1024


def spec(space):
    return pl.BlockSpec(memory_space=space)


def shift(value, steps):
    count = lax.axis_size(AXES)
    first, last = max(0, -steps), min(count, count - steps)
    return lax.ppermute(value, AXES, [(s, s + steps) for s in range(first, last)])


def label_rows(values, width):
    lane = lax.broadcasted_iota(jnp.int32, (EXTRA, width), 1)
    total = jnp.zeros((EXTRA, width), jnp.int32)
    for at, value in enumerate(values):
        total = jnp.where(lane == at, value, total)
    return total.astype(F32).astype(BF)


def pack_kernel(send_rows, aggregate, tent, *refs):
    outs, labels, sem = refs[:4], refs[4], refs[5]
    copies = []
    for n in START_ORDER:
        for g in range(NG):
            copies.append(
                pltpu.make_async_copy(
                    tent.at[send_rows[n, g]], outs[n].at[pl.ds(g * BS, BS)], sem.at[n, g]
                )
            )
    for copy in copies:
        copy.start()
    for n in START_ORDER:
        labels[n] = label_rows([aggregate[send_rows[n, g]] for g in range(NG)], BS)
        copy = pltpu.make_async_copy(labels.at[n], outs[n].at[pl.ds(NG * BS, EXTRA)], sem.at[n, NG])
        copy.start()
        copies.append(copy)
    for copy in copies:
        copy.wait()


def pack(send_rows, aggregate, tent):
    shape = jax.ShapeDtypeStruct((NG * BS + EXTRA, BS), BF)
    return pl.pallas_call(
        pack_kernel,
        out_shape=[shape] * 4,
        in_specs=[spec(SMEM), spec(SMEM), spec(pltpu.VMEM)],
        out_specs=[spec(ANY)] * 4,
        scratch_shapes=[pltpu.VMEM((4, EXTRA, BS), BF), pltpu.SemaphoreType.DMA((4, NG + 1))],
        name="pack",
    )(send_rows, aggregate, tent)


def local_slots_kernel(off_columns, aggregate, diag, off, tent, labels, ghost_list, ghost_count, slots, scales):
    eye = lax.broadcasted_iota(jnp.int32, (BS, BS), 0) == lax.broadcasted_iota(jnp.int32, (BS, BS), 1)
    ghost_count[0] = 0

    def row(i, carry):
        block = diag[i]
        inv = 1.0 / jnp.sum(jnp.where(eye, block.astype(F32), 0.0), axis=1, keepdims=True)
        scale = 0.6 * inv
        scales[i] = jnp.broadcast_to(scale, (BS, BS))
        own = tent[i]
        first = own.astype(F32) - scale * jnp.dot(block, own, preferred_element_type=F32)
        slots[i, :, :BS] = first.astype(BF)
        labels[i, 0] = aggregate[i] + 8
        for k in range(1, 4):
            c = off_columns[i, k - 1]
            near = tent[jnp.minimum(c, NB - 1)]
            part = -scale * jnp.dot(off[i, k - 1], near, preferred_element_type=F32)
            slots[i, :, k * BS : (k + 1) * BS] = part.astype(BF)
            labels[i, k] = aggregate[jnp.minimum(c, NB - 1)] + 8
            at = ghost_count[0]
            ghost_list[at] = i * 4 + k
            ghost_count[0] = at + jnp.where(c < NB, 0, 1)
        return carry

    lax.fori_loop(0, NB, row, 0, unroll=4)
    at = ghost_count[0]
    for d in range(GROUP):
        ghost_list[at + d] = NB * 4 + 1


def local_slots(off_columns, aggregate, diag, off, tent):
    return pl.pallas_call(
        local_slots_kernel,
        out_shape=[
            jax.ShapeDtypeStruct((NB, 4), jnp.int32),
            jax.ShapeDtypeStruct((3 * NB + GROUP,), jnp.int32),
            jax.ShapeDtypeStruct((1,), jnp.int32),
            jax.ShapeDtypeStruct((NB, BS, SLOTW), BF),
            jax.ShapeDtypeStruct((NB, BS, BS), F32),
        ],
        in_specs=[spec(SMEM)] * 2 + [spec(pltpu.VMEM)] * 3,
        out_specs=[spec(SMEM)] * 3 + [spec(pltpu.VMEM)] * 2,
        compiler_params=pltpu.CompilerParams(vmem_limit_bytes=VMEM_LIMIT),
        cost_estimate=pl.CostEstimate(flops=10**9, bytes_accessed=6 * 10**6, transcendentals=0),
        name="local_slots",
    )(off_columns, aggregate, diag, off, tent)


def ghost_slots_kernel(
    send_rows, off_columns, local_labels, ghost_list, ghost_count, off, slots_in, scales, g2, g3, g0, g1,
    labels, slots, s2, s3, s0, s1,
    table, labels_in, labels_out, label_smem, slot_buf, off_buf, scale_buf, sem_in, sem_lab, sem_out, sem_big,
):
    ghosts, sends = (g0, g1, g2, g3), (s0, s1, s2, s3)
    big = [
        pltpu.make_async_copy(scales, scale_buf, sem_big.at[0]),
        pltpu.make_async_copy(off, off_buf, sem_big.at[1]),
        pltpu.make_async_copy(slots_in, slot_buf.at[pl.ds(0, NB)], sem_big.at[2]),
    ]
    copies = []
    for n in range(4):
        for g in range(NG):
            copies.append(
                pltpu.make_async_copy(
                    ghosts[n].at[pl.ds(g * BS, BS)], table.at[n * NG + g], sem_in.at[n * NG + g]
                )
            )
    lab = [
        pltpu.make_async_copy(ghosts[n].at[pl.ds(NG * BS, EXTRA)], labels_out.at[n, :, pl.ds(0, BS)], sem_lab.at[n])
        for n in range(4)
    ]
    for copy in lab + copies + big:
        copy.start()
    for i in range(NB):
        for k in range(4):
            labels[i, k] = local_labels[i, k]
    for copy in lab:
        copy.wait()
    for n in range(4):
        base = 8 - 2 * OFFSETS[n]
        labels_in[n] = labels_out[n, :, pl.ds(0, BS)].astype(F32).astype(jnp.int32)[:8] + base
    to_smem = pltpu.make_async_copy(labels_in, label_smem, sem_lab.at[0])
    to_smem.start()
    for copy in copies + big:
        copy.wait()
    to_smem.wait()

    def group(q, carry):
        for u in range(GROUP):
            entry = ghost_list[q * GROUP + u]
            i, k = lax.div(entry, 4), lax.rem(entry, 4)
            row = jnp.minimum(i, NB - 1)
            ghost = jnp.clip(off_columns[row, k - 1] - NB, 0, 4 * NG - 1)
            part = jnp.dot(off_buf[row, k - 1], table[ghost], preferred_element_type=F32)
            part = -scale_buf[row] * part
            slot_buf[i, :, pl.ds(pl.multiple_of(k * BS, BS), BS)] = part.astype(BF)
            labels[i, k] = label_smem[lax.div(ghost, NG), 0, lax.rem(ghost, NG)]
        return carry

    lax.fori_loop(0, lax.div(ghost_count[0] + GROUP - 1, GROUP), group, 0)

    outs = []
    for n in START_ORDER:
        for g in range(NG):
            outs.append(
                pltpu.make_async_copy(
                    slot_buf.at[send_rows[n, g]], sends[n].at[pl.ds(g * BS, BS)], sem_out.at[n * NG + g]
                )
            )
    outs.append(pltpu.make_async_copy(slot_buf.at[pl.ds(0, NB)], slots, sem_big.at[0]))
    for copy in outs:
        copy.start()
    for n in START_ORDER:
        values = [labels[send_rows[n, g], k] for g in range(NG) for k in range(4)]
        labels_out[n] = label_rows(values, SLOTW)
        copy = pltpu.make_async_copy(labels_out.at[n], sends[n].at[pl.ds(NG * BS, EXTRA)], sem_lab.at[n])
        copy.start()
        outs.append(copy)
    for copy in outs:
        copy.wait()


def ghost_slots(send_rows, off_columns, local_labels, ghost_list, ghost_count, off, slots_in, scales, ghosts):
    send = jax.ShapeDtypeStruct((NG * BS + EXTRA, SLOTW), BF)
    labels, slots, *sends = pl.pallas_call(
        ghost_slots_kernel,
        out_shape=[
            jax.ShapeDtypeStruct((NB + 1, 4), jnp.int32),
            jax.ShapeDtypeStruct((NB, BS, SLOTW), BF),
        ]
        + [send] * 4,
        in_specs=[spec(SMEM)] * 5 + [spec(ANY)] * 7,
        out_specs=[spec(SMEM)] + [spec(ANY)] * 5,
        scratch_shapes=[
            pltpu.VMEM((4 * NG, BS, BS), BF),
            pltpu.VMEM((4, 8, BS), jnp.int32),
            pltpu.VMEM((4, EXTRA, SLOTW), BF),
            pltpu.SMEM((4, 8, BS), jnp.int32),
            pltpu.VMEM((NB + 1, BS, SLOTW), BF),
            pltpu.VMEM((NB, 3, BS, BS), BF),
            pltpu.VMEM((NB, BS, BS), F32),
            pltpu.SemaphoreType.DMA((4 * NG,)),
            pltpu.SemaphoreType.DMA((4,)),
            pltpu.SemaphoreType.DMA((4 * NG,)),
            pltpu.SemaphoreType.DMA((3,)),
        ],
        compiler_params=pltpu.CompilerParams(vmem_limit_bytes=VMEM_LIMIT),
        name="ghost_slots",
    )(send_rows, off_columns, local_labels, ghost_list, ghost_count, off, slots_in, scales,
      *[ghosts[n] for n in START_ORDER])
    return labels, slots, [sends[START_ORDER.index(n)] for n in range(4)]


def lists_kernel(labels, slots, lists, counts, blocks):
    for t in range(10):
        counts[t] = 0

    def row(i, carry):
        for k in range(4):
            blocks[i * 4 + k] = slots[i, :, k * BS : (k + 1) * BS].T
            t = jnp.clip(labels[i, k] - 4, 0, 9)
            at = counts[t]
            lists[t, at] = i * 4 + k
            counts[t] = at + 1
        return carry

    lax.fori_loop(0, NB, row, 0, unroll=2)
    blocks[4 * NB] = jnp.zeros((BS, BS), BF)
    for t in range(10):
        at = counts[t]
        for d in range(CHUNK - 1):
            lists[t, at + d] = 4 * NB
        counts[t] = lax.div(at + CHUNK - 1, CHUNK)


def make_lists(labels, slots):
    return pl.pallas_call(
        lists_kernel,
        out_shape=[
            jax.ShapeDtypeStruct((10, 4 * NB + CHUNK), jnp.int32),
            jax.ShapeDtypeStruct((10,), jnp.int32),
            jax.ShapeDtypeStruct((4 * NB + 1, BS, BS), BF),
        ],
        in_specs=[spec(SMEM), spec(pltpu.VMEM)],
        out_specs=[spec(SMEM)] * 2 + [spec(pltpu.VMEM)],
        compiler_params=pltpu.CompilerParams(vmem_limit_bytes=VMEM_LIMIT),
        cost_estimate=pl.CostEstimate(flops=10**8, bytes_accessed=6 * 10**6, transcendentals=0),
        name="lists",
    )(labels, slots)


def coarse_rows(t, at, lists, counts, blocks, applied, coarse):
    def chunk(q, carry):
        entries = [lists[t, q * CHUNK + u] for u in range(CHUNK)]
        left = jnp.concatenate([blocks[e] for e in entries], axis=1)
        rows = [jnp.minimum(lax.div(e, 4), NB - 1) for e in entries]
        for cols in TILES:
            right = jnp.concatenate([applied[r, :, cols] for r in rows], axis=0)
            res = jnp.dot(left, right, preferred_element_type=F32)
            coarse[at, :, cols] = coarse[at, :, cols] + res
        return carry

    coarse[at] = jnp.zeros((BS, WIDE), F32)
    lax.fori_loop(0, counts[t], chunk, 0)


def far_kernel(
    parity, off_columns, labels, lists, counts, diag, off, slots, blocks, g2, g3, g0, g1,
    applied_out, relay_out, relayed_out, direct_out,
    table, labels_in, labels_vmem, label_smem, total, applied, coarse, relay, relayed, direct,
    sem_in, sem_lab, sem_out, sem_piece,
):
    ghosts = (g0, g1, g2, g3)
    copies = [pltpu.make_async_copy(slots, table.at[pl.ds(0, NB)], sem_in.at[0])]
    for n in range(4):
        for g in range(NG):
            copies.append(
                pltpu.make_async_copy(
                    ghosts[n].at[pl.ds(g * BS, BS)], table.at[NB + n * NG + g], sem_in.at[1 + n * NG + g]
                )
            )
    lab = [
        pltpu.make_async_copy(ghosts[n].at[pl.ds(NG * BS, EXTRA), pl.ds(0, BS)], labels_in.at[n], sem_lab.at[n])
        for n in range(4)
    ]
    for copy in lab + copies:
        copy.start()
    odd = parity[0] == 1
    relay_level = jnp.where(odd, 3, 1)
    relayed_level = jnp.where(odd, 0, 4)
    rest = pl.ds(pl.multiple_of((1 - parity[0]) * WIDE, BS), 2 * BS)
    relay[:, :, rest] = jnp.zeros((2, BS, 2 * BS), BF)
    relayed[:, :, rest] = jnp.zeros((2, BS, 2 * BS), F32)
    for copy in lab:
        copy.wait()
    for n in range(4):
        labels_vmem[n] = labels_in[n].astype(F32).astype(jnp.int32)[:8] - 2 * OFFSETS[n]
    to_smem = pltpu.make_async_copy(labels_vmem, label_smem, sem_lab.at[0])
    to_smem.start()
    for copy in copies:
        copy.wait()
    to_smem.wait()

    def label_of(j, m):
        ghost = jnp.maximum(j - NB, 0)
        remote = label_smem[lax.div(ghost, NG), 0, lax.rem(ghost, NG) * 4 + m]
        local = labels[jnp.minimum(j, NB - 1), m]
        return jnp.clip(jnp.where(j < NB, local, remote), 0, FRAME - 1)

    def row(i, carry):
        total[...] = jnp.zeros_like(total)
        for k in range(4):
            j = i if k == 0 else off_columns[i, k - 1]
            block = diag[i] if k == 0 else off[i, k - 1]
            prod = jnp.dot(block, table[j], preferred_element_type=F32)
            for m in range(4):
                at = label_of(j, m)
                total[at] = total[at] + prod[:, m * BS : (m + 1) * BS]
        for at in range(FRAME):
            applied[i, :, at * BS : (at + 1) * BS] = total[at].astype(BF)
        pltpu.make_async_copy(applied.at[i], applied_out.at[i], sem_out.at[i]).start()
        return carry

    lax.fori_loop(0, NB, row, 0)
    into = pl.ds(pl.multiple_of(parity[0] * (2 * BS), BS), WIDE)

    def rows_of(level):
        def one(b, carry):
            coarse_rows(2 * level + b, b, lists, counts, blocks, applied, coarse)
            return carry

        lax.fori_loop(0, 2, one, 0)

    rows_of(4 - relayed_level)
    direct[...] = coarse[...].astype(BF)
    pieces = [pltpu.make_async_copy(direct, direct_out, sem_piece.at[0])]
    pieces[-1].start()
    rows_of(relay_level)
    relay[:, :, into] = coarse[...].astype(BF)
    pieces.append(pltpu.make_async_copy(relay, relay_out, sem_piece.at[1]))
    pieces[-1].start()
    rows_of(relayed_level)
    relayed[:, :, into] = coarse[...]
    pieces.append(pltpu.make_async_copy(relayed, relayed_out, sem_piece.at[2]))
    pieces[-1].start()

    def wait(i, carry):
        pltpu.make_async_copy(applied.at[i], applied_out.at[i], sem_out.at[i]).wait()
        return carry

    lax.fori_loop(0, NB, wait, 0)
    for copy in pieces:
        copy.wait()


def make_far(parity, off_columns, labels, lists, counts, diag, off, slots, blocks, ghosts):
    return pl.pallas_call(
        far_kernel,
        out_shape=[
            jax.ShapeDtypeStruct((NB, BS, WIDE), BF),
            jax.ShapeDtypeStruct((2, BS, CHIPWIDE), BF),
            jax.ShapeDtypeStruct((2, BS, CHIPWIDE), F32),
            jax.ShapeDtypeStruct((2, BS, WIDE), BF),
        ],
        in_specs=[spec(SMEM)] * 5 + [spec(pltpu.VMEM)] * 2 + [spec(ANY), spec(pltpu.VMEM)] + [spec(ANY)] * 4,
        out_specs=[spec(ANY)] * 4,
        scratch_shapes=[
            pltpu.VMEM((NT, BS, SLOTW), BF),
            pltpu.VMEM((4, EXTRA, BS), BF),
            pltpu.VMEM((4, 8, BS), jnp.int32),
            pltpu.SMEM((4, 8, BS), jnp.int32),
            pltpu.VMEM((FRAME, BS, BS), F32),
            pltpu.VMEM((NB, BS, WIDE), BF),
            pltpu.VMEM((2, BS, WIDE), F32),
            pltpu.VMEM((2, BS, CHIPWIDE), BF),
            pltpu.VMEM((2, BS, CHIPWIDE), F32),
            pltpu.VMEM((2, BS, WIDE), BF),
            pltpu.SemaphoreType.DMA((1 + 4 * NG,)),
            pltpu.SemaphoreType.DMA((4,)),
            pltpu.SemaphoreType.DMA((NB,)),
            pltpu.SemaphoreType.DMA((3,)),
        ],
        compiler_params=pltpu.CompilerParams(vmem_limit_bytes=VMEM_LIMIT),
        cost_estimate=pl.CostEstimate(flops=4 * 10**9, bytes_accessed=20 * 10**6, transcendentals=0),
        name="far_rows",
    )(parity, off_columns, labels, lists, counts, diag, off, slots, blocks,
      *[ghosts[n] for n in START_ORDER])


def near_kernel(parity, lists, counts, blocks, applied, own, mate, coarse):
    mate_level = jnp.where(parity[0] == 1, 1, 3)

    def one(b, carry):
        t = jnp.where(b < 2, 2 * mate_level + b, b + 2)
        coarse_rows(t, b, lists, counts, blocks, applied, coarse)
        return carry

    lax.fori_loop(0, 4, one, 0)
    own[...] = coarse[2:4]
    mate[...] = coarse[0:2].astype(BF)


def make_near(parity, lists, counts, blocks, applied):
    return pl.pallas_call(
        near_kernel,
        out_shape=[
            jax.ShapeDtypeStruct((2, BS, WIDE), F32),
            jax.ShapeDtypeStruct((2, BS, WIDE), BF),
        ],
        in_specs=[spec(SMEM)] * 3 + [spec(pltpu.VMEM)] * 2,
        out_specs=[spec(pltpu.VMEM)] * 2,
        scratch_shapes=[pltpu.VMEM((4, BS, WIDE), F32)],
        compiler_params=pltpu.CompilerParams(vmem_limit_bytes=VMEM_LIMIT),
        cost_estimate=pl.CostEstimate(flops=4 * 10**9, bytes_accessed=20 * 10**6, transcendentals=0),
        name="near_rows",
    )(parity, lists, counts, blocks, applied)


def add_kernel(starts, *refs):
    pieces, out = refs[:-1], refs[-1]
    out[...] = jnp.zeros_like(out)
    for at, piece in enumerate(pieces):
        cols = pl.ds(pl.multiple_of(starts[at] * (2 * BS), BS), piece.shape[2])
        out[:, :, cols] = out[:, :, cols] + piece[...].astype(F32)


def add_pieces(starts, pieces):
    rows = 16

    def block(width):
        return pl.BlockSpec((2, rows, width), lambda r: (0, r, 0))

    return pl.pallas_call(
        add_kernel,
        grid=(BS // rows,),
        out_shape=jax.ShapeDtypeStruct((2, BS, BANDWIDE), F32),
        in_specs=[spec(SMEM)] + [block(p.shape[2]) for p in pieces],
        out_specs=block(BANDWIDE),
        compiler_params=pltpu.CompilerParams(vmem_limit_bytes=VMEM_LIMIT),
        cost_estimate=pl.CostEstimate(flops=10**6, bytes_accessed=9 * 10**6, transcendentals=0),
        name="add_pieces",
    )(starts, *pieces)


def permute_by(value, even_step, odd_step):
    count = lax.axis_size(AXES)
    pairs = [(s, s + (odd_step if s % 2 else even_step)) for s in range(count)]
    return lax.ppermute(value, AXES, [(s, t) for s, t in pairs if 0 <= t < count])


def exchange(sends):
    arrived = [None] * 4
    for n in START_ORDER:
        arrived[n] = shift(sends[n], OFFSETS[n])
    return arrived


def local(diag_blocks, off_blocks, off_columns, tentative, aggregate, send_rows):
    odd = lax.rem(lax.axis_index(AXES), 2)
    parity = odd.reshape(1)
    ghosts = exchange(pack(send_rows, aggregate, tentative))
    labels, ghost_list, ghost_count, slots, scales = local_slots(
        off_columns, aggregate, diag_blocks, off_blocks, tentative
    )
    labels, slots, sends = ghost_slots(
        send_rows, off_columns, labels, ghost_list, ghost_count, off_blocks, slots, scales, ghosts
    )
    ghosts = exchange(sends)
    lists, counts, blocks = make_lists(labels, slots)
    applied, relay, relayed, direct = make_far(
        parity, off_columns, labels, lists, counts, diag_blocks, off_blocks, slots, blocks, ghosts
    )
    direct_in = permute_by(direct, -2, 2)
    relay_in = permute_by(relay, 1, -1)
    pair_sum = (relayed + relay_in.astype(F32)).astype(BF)
    pair_in = permute_by(pair_sum, 2, -2)
    applied, pair_sum = lax.optimization_barrier((applied, pair_sum))
    own, mate = make_near(parity, lists, counts, blocks, applied)
    mate_in = permute_by(mate, 1, -1)
    starts = jnp.stack([jnp.int32(2), jnp.where(odd == 1, 1, 3), jnp.where(odd == 1, 0, 4), 3 * odd])
    return add_pieces(starts, [own, mate_in, direct_in, pair_in])


def solution(mesh):
    in_specs = (
        P(AXES, None, None),
        P(AXES, None, None, None),
        P(AXES, None),
        P(AXES, None, None),
        P(AXES),
        P(AXES, None),
    )
    return jax.shard_map(
        local, mesh=mesh, in_specs=in_specs, out_specs=P(AXES, None, None), check_vma=False
    )
```

time: 164 us -> 129 us (0.79)
  waiting for transfers between devices: 39.3 us -> 12.7 us
  starting transfers between devices: 59.5 us -> 50.7 us
    ppermute x12 -> x8, waiting for transfers between devices: 39.3 us -> 3.15 us  [shift(): lax.ppermute(value, AXES, [(s, s + steps) for s in range(first, last)])]
    ppermute x12 -> x8, starting transfers between devices: 59.5 us -> 39.9 us  [shift(): lax.ppermute(value, AXES, [(s, s + steps) for s in range(first, last)])]
    pallas_call x2 -> x6, Pallas kernels: 38.6 us -> 54.7 us  [the longest x1 17.5 us: make_far(): pl.pallas_call(far_kernel, out_shape=[jax.ShapeDtypeStruct((NB, BS, WIDE)...]
    pallas_call x1, Pallas kernels: 17.9 us -> 2.06 us  [pack(): pl.pallas_call(pack_kernel, out_shape=[shape] * 4, in_specs=[spec(SMEM),...]
    ppermute x0 -> x4, starting transfers between devices: none -> 10.9 us  [permute_by(): lax.ppermute(value, AXES, [(s, t) for s, t in pairs if 0 <= t < count])]
    ppermute x0 -> x4, waiting for transfers between devices: none -> 9.6 us  [permute_by(): lax.ppermute(value, AXES, [(s, t) for s, t in pairs if 0 <= t < count])]
    add x1 -> x0, other arithmetic: 4.17 us -> none  [local(): summed = summed + band(shift(value, by), 2 - by)]
    convert_element_type x0 -> x1, other arithmetic: none -> 2.11 us  [local(): pair_sum = (relayed + relay_in.astype(F32)).astype(BF)]
  transfers between devices with their start and end apart: 12 -> 12, of which waited for: 7 -> 4; matrix products, arithmetic and copies ran while one was open for 1% -> 3% of each run, Pallas kernels for 0% -> 17%
where the time goes in v2:
time: 129 us; the launch traced here: 127 us
  Pallas kernels  56.7 us (44%)
  starting transfers between devices  50.7 us (39%)
  waiting for transfers between devices  12.7 us (10%)
  local copies, waits for them, and re-layouts  3.96 us (3%)
  other arithmetic  2.7 us (2%)
    ppermute x8, starting transfers between devices, shift(): lax.ppermute(value, AXES, [(s, s + steps) for s in range(first, last)])  39.9 us
    pallas_call x1, Pallas kernels, make_far(): pl.pallas_call(far_kernel, out_shape=[jax.ShapeDtypeStruct((NB, BS, WIDE)...  17.5 us
    pallas_call x1, Pallas kernels, make_near(): pl.pallas_call(near_kernel, out_shape=[jax.ShapeDtypeStruct((2, BS, WIDE)...  13 us
    ppermute x4, starting transfers between devices, permute_by(): lax.ppermute(value, AXES, [(s, t) for s, t in pairs if 0 <= t < count])  10.9 us
    ppermute x4, waiting for transfers between devices, permute_by(): lax.ppermute(value, AXES, [(s, t) for s, t in pairs if 0 <= t < count])  9.6 us
    pallas_call x1, Pallas kernels, ghost_slots(): pl.pallas_call(ghost_slots_kernel, out_shape=[jax.ShapeDtypeStruct((NB +...  8.57 us
    pallas_call x1, Pallas kernels, add_pieces(): pl.pallas_call(add_kernel, grid=(BS // rows,), out_shape=jax.ShapeDtypeSt...  7.19 us
    pallas_call x1, Pallas kernels, local_slots(): pl.pallas_call(local_slots_kernel, out_shape=[jax.ShapeDtypeStruct((NB, 4...  4.49 us
  transfers between devices with their start and end apart: 12, of which 4 were waited for; matrix products, arithmetic and copies ran while one was open for 3% of the time, Pallas kernels for 17%

profile of v2, /device:TPU:24, one launch (start us, length us, event | category | flops | bytes accessed | tf_op | source)
XLA Modules:
  0.0 127.1 jit_solution(3157207672630774336)
XLA Ops:
  0.0 2.1 %pack.1 = (bf16[528,128]{1,0:T(8,128)(2,1)}, bf16[528,128]{1,0:T(8,128)(2,1)}, bf16[528,128]{1,0:T(8,128)(2,1)}, bf16[528,128]{1,0:T(8,128)(2,1)}) custom-call(s32[4,4]{1,0:T(4,128)} %send_rows.3, s32[16]{0:T(128)} %aggregate.3, bf16[16,128,128]{2,1,0:T(8,128)(2,1)} %tent.3), custom_call_target="tpu_custom_call" | custom-call | tf_op jit(solution)/shard_map/pack/pallas_call | solution.py:72
  2.1 3.8 %collective-permute-start = (bf16[528,128]{1,0:T(8,128)(2,1)}, bf16[528,128]{1,0:T(8,128)(2,1)S(1)}, u32[]{:S(2)}, u32[]{:S(2)}) collective-permute-start(bf16[528,128]{1,0:T(8,128)(2,1)} %get-tuple-element.35), channel_id=1, source_target_pairs={{0,2},{1,3},{2,4},{3,5},{4,6},{5,7},{6,8},{7,9},{8,10},{9,11},{10,... | collective-permute-start | bytes 405512 | tf_op jit(solution)/shard_map/ppermute | solution.py:38
  5.9 6.4 %collective-permute-start.1 = (bf16[528,128]{1,0:T(8,128)(2,1)}, bf16[528,128]{1,0:T(8,128)(2,1)S(1)}, u32[]{:S(2)}, u32[]{:S(2)}) collective-permute-start(bf16[528,128]{1,0:T(8,128)(2,1)} %get-tuple-element.36), channel_id=1, source_target_pairs={{2,0},{3,1},{4,2},{5,3},{6,4},{7,5},{8,6},{9,7},{10,8},{11,9},{12,... | collective-permute-start | bytes 405512 | tf_op jit(solution)/shard_map/ppermute | solution.py:38
  12.3 1.9 %collective-permute-start.2 = (bf16[528,128]{1,0:T(8,128)(2,1)}, bf16[528,128]{1,0:T(8,128)(2,1)S(1)}, u32[]{:S(2)}, u32[]{:S(2)}) collective-permute-start(bf16[528,128]{1,0:T(8,128)(2,1)} %get-tuple-element.37), channel_id=1, source_target_pairs={{0,1},{1,2},{2,3},{3,4},{4,5},{5,6},{6,7},{7,8},{8,9},{9,10},{10,1... | collective-permute-start | bytes 405512 | tf_op jit(solution)/shard_map/ppermute | solution.py:38
  14.3 7.9 %collective-permute-start.3 = (bf16[528,128]{1,0:T(8,128)(2,1)}, bf16[528,128]{1,0:T(8,128)(2,1)S(1)}, u32[]{:S(2)}, u32[]{:S(2)}) collective-permute-start(bf16[528,128]{1,0:T(8,128)(2,1)} %get-tuple-element.38), channel_id=1, source_target_pairs={{1,0},{2,1},{3,2},{4,3},{5,4},{6,5},{7,6},{8,7},{9,8},{10,9},{11,1... | collective-permute-start | bytes 405512 | tf_op jit(solution)/shard_map/ppermute | solution.py:38
  22.1 1.4 %copy.8.off_columns = s32[16,3]{1,0:T(8,128)} copy(s32[16,3]{0,1:T(4,128)} %param.8) | data formatting | bytes 384 | tf_op args[2]
  23.5 4.5 %local_slots.1 = (s32[16,4]{1,0:T(8,128)}, s32[52]{0:T(128)}, s32[1]{0:T(128)}, bf16[16,128,512]{2,1,0:T(8,128)(2,1)}, f32[16,128,128]{2,1,0:T(8,128)}) custom-call(s32[16,3]{1,0:T(8,128)} %copy.8.off_columns, s32[16]{0:T(128)} %aggregate.3, bf16[16,128,128]{2,1,0:T(8,128)(2,1)} %diag.3, bf16[16,3,128,128]{3,2,1,0:T(8,128)(2,1)} %off.5, ...), custom_call_target="tpu_custom_call" | custom-call | flops 1000000000 | bytes 6000000 | tf_op jit(solution)/shard_map/local_slots/pallas_call | solution.py:113
  28.0 0.0 collective-permute-done.g2
  28.0 0.0 copy-start.1
  28.0 0.0 collective-permute-done.1.g3
  28.0 0.0 copy-start.2
  28.0 0.0 collective-permute-done.2.g0
  28.0 0.0 copy-start.3
  28.0 0.0 collective-permute-done.3.g1
  28.0 0.0 copy-start.4
  28.1 0.6 copy-done.1
  28.6 0.1 copy-done.2
  28.7 0.0 copy-done.3
  28.7 0.1 copy-done.4
  28.8 8.6 %ghost_slots.1 = (s32[17,4]{1,0:T(8,128)}, bf16[16,128,512]{2,1,0:T(8,128)(2,1)}, bf16[528,512]{1,0:T(8,128)(2,1)}, bf16[528,512]{1,0:T(8,128)(2,1)}, bf16[528,5...) custom-call(s32[4,4]{1,0:T(4,128)} %send_rows.3, s32[16,3]{1,0:T(8,128)} %copy.8.off_columns, ...), custom_call_target="tpu_custom_call" | custom-call | tf_op jit(solution)/shard_map/ghost_slots/pallas_call | solution.py:206
  37.4 1.9 %collective-permute-start.4 = (bf16[528,512]{1,0:T(8,128)(2,1)}, bf16[528,512]{1,0:T(8,128)(2,1)S(1)}, u32[]{:S(2)}, u32[]{:S(2)}) collective-permute-start(bf16[528,512]{1,0:T(8,128)(2,1)} %get-tuple-element.44), channel_id=1, source_target_pairs={{0,2},{1,3},{2,4},{3,5},{4,6},{5,7},{6,8},{7,9},{8,10},{9,11},{10,... | collective-permute-start | bytes 1622024 | tf_op jit(solution)/shard_map/ppermute | solution.py:38
  39.3 8.1 %collective-permute-start.5 = (bf16[528,512]{1,0:T(8,128)(2,1)}, bf16[528,512]{1,0:T(8,128)(2,1)S(1)}, u32[]{:S(2)}, u32[]{:S(2)}) collective-permute-start(bf16[528,512]{1,0:T(8,128)(2,1)} %get-tuple-element.45), channel_id=1, source_target_pairs={{2,0},{3,1},{4,2},{5,3},{6,4},{7,5},{8,6},{9,7},{10,8},{11,9},{12,... | collective-permute-start | bytes 1622024 | tf_op jit(solution)/shard_map/ppermute | solution.py:38
  47.5 1.9 %collective-permute-start.6 = (bf16[528,512]{1,0:T(8,128)(2,1)}, bf16[528,512]{1,0:T(8,128)(2,1)S(1)}, u32[]{:S(2)}, u32[]{:S(2)}) collective-permute-start(bf16[528,512]{1,0:T(8,128)(2,1)} %get-tuple-element.46), channel_id=1, source_target_pairs={{0,1},{1,2},{2,3},{3,4},{4,5},{5,6},{6,7},{7,8},{8,9},{9,10},{10,1... | collective-permute-start | bytes 1622024 | tf_op jit(solution)/shard_map/ppermute | solution.py:38
  49.4 7.9 %collective-permute-start.7 = (bf16[528,512]{1,0:T(8,128)(2,1)}, bf16[528,512]{1,0:T(8,128)(2,1)S(1)}, u32[]{:S(2)}, u32[]{:S(2)}) collective-permute-start(bf16[528,512]{1,0:T(8,128)(2,1)} %get-tuple-element.47), channel_id=1, source_target_pairs={{1,0},{2,1},{3,2},{4,3},{5,4},{6,5},{7,6},{8,7},{9,8},{10,9},{11,1... | collective-permute-start | bytes 1622024 | tf_op jit(solution)/shard_map/ppermute | solution.py:38
  57.3 4.0 %lists.1 = (s32[10,68]{1,0:T(8,128)}, s32[10]{0:T(128)}, bf16[65,128,128]{2,1,0:T(8,128)(2,1)}) custom-call(s32[17,4]{1,0:T(8,128)} %get-tuple-element.39.labels, bf16[16,128,512]{2,1,0:T(8,128)(2,1)} %get-tuple-element.40.slots), custom_call_target="tpu_custom_call" | custom-call | flops 100000000 | bytes 6000000 | tf_op jit(solution)/shard_map/lists/pallas_call | solution.py:258
  61.2 0.0 collective-permute-done.4.g2
  61.3 0.0 copy-start.5
  61.3 0.0 collective-permute-done.5.g3
  61.3 0.0 copy-start.6
  61.3 1.3 %collective-permute-done.6.g0 = bf16[528,512]{1,0:T(8,128)(2,1)S(1)} collective-permute-done((bf16[528,512]{1,0:T(8,128)(2,1)}, bf16[528,512]{1,0:T(8,128)(2,1)S(1)}, u32[]{:S(2)}, u32[]{:S(2)}) %collective-permute-start.6) | collective-permute-done | bytes 540704 | tf_op jit(solution)/shard_map/ppermute | solution.py:38
  62.6 1.9 %collective-permute-done.7.g1 = bf16[528,512]{1,0:T(8,128)(2,1)S(1)} collective-permute-done((bf16[528,512]{1,0:T(8,128)(2,1)}, bf16[528,512]{1,0:T(8,128)(2,1)S(1)}, u32[]{:S(2)}, u32[]{:S(2)}) %collective-permute-start.7) | collective-permute-done | bytes 540704 | tf_op jit(solution)/shard_map/ppermute | solution.py:38
  64.4 0.0 copy-done.5
  64.4 0.0 copy-done.6
  64.4 0.8 copy-done.8
  65.2 17.5 %far_rows.1 = (bf16[16,128,2304]{2,1,0:T(8,128)(2,1)}, bf16[2,128,2560]{2,1,0:T(8,128)(2,1)}, f32[2,128,2560]{2,1,0:T(8,128)}, bf16[2,128,2304]{2,1,0:T(8,128)(2,1)}) custom-call(s32[1]{0:T(128)} %bitcast.3.parity, s32[16,3]{1,0:T(8,128)} %copy.8.off_columns, s32[17,4]{1,0:T(8,128)} %get-tuple-element.39.labels, s32[10,68]{1,0:T(8,128)} %get-tuple-element.41.lists, ...), custom_call_target="tpu_custom_call" | custom-call | flops 4000000000 | bytes 20000000 | tf_op jit(solution)/shard_map/far_rows/pallas_call | solution.py:378
  82.7 0.1 collective-permute-start.8
  82.8 8.3 %collective-permute-start.10 = (bf16[2,128,2304]{2,1,0:T(8,128)(2,1)}, bf16[2,128,2304]{2,1,0:T(8,128)(2,1)}, u32[]{:S(2)}, u32[]{:S(2)}) collective-permute-start(bf16[2,128,2304]{2,1,0:T(8,128)(2,1)} %get-tuple-element.54), channel_id=1, source_target_pairs={{1,3},{2,0},{3,5},{4,2},{5,7},{6,4},{7,9},{8,6},{9,11},{10,8},{11,... | collective-permute-start | bytes 3538952 | tf_op jit(solution)/shard_map/ppermute | solution.py:469
  91.1 0.0 collective-permute-done.8
  91.1 2.1 %add_convert_fusion = bf16[2,128,2560]{2,1,0:T(8,128)(2,1)S(1)} fusion(f32[2,128,2560]{2,1,0:T(8,128)} %get-tuple-element.49, bf16[2,128,2560]{2,1,0:T(8,128)(2,1)S(1)} %collective-permute-done.8), kind=kLoop, calls=%fused_computation | loop fusion | flops 1966080 | bytes 5242880 | tf_op jit(solution)/shard_map/convert_element_type | solution.py:496
  93.2 1.9 %collective-permute-start.11 = (bf16[2,128,2560]{2,1,0:T(8,128)(2,1)S(1)}, bf16[2,128,2560]{2,1,0:T(8,128)(2,1)S(1)}, u32[]{:S(2)}, u32[]{:S(2)}) collective-permute-start(bf16[2,128,2560]{2,1,0:T(8,128)(2,1)S(1)} %add_convert_fusion), channel_id=1, source_target_pairs={{0,2},{2,4},{3,1},{4,6},{5,3},{6,8},{7,5},{8,10},{9,7},{10,12},{11... | collective-permute-start | bytes 3932168 | tf_op jit(solution)/shard_map/ppermute | solution.py:469
  95.1 13.0 %near_rows.1 = (f32[2,128,2304]{2,1,0:T(8,128)}, bf16[2,128,2304]{2,1,0:T(8,128)(2,1)}) custom-call(s32[1]{0:T(128)} %bitcast.3.parity, s32[10,68]{1,0:T(8,128)} %get-tuple-element.41.lists, s32[10]{0:T(128)} %get-tuple-element.42.counts, bf16[65,128,128]{2,1,0:T(8,128)(2,1)} %get-tuple-element.43.blocks, bf16[16,128,2304]{2,1,0:T(8,128)(2,1)} %get-tuple-element.51.applied), custom_call_target="tpu_custom_call" | custom-call | flops 4000000000 | bytes 20000000 | tf_op jit(solution)/shard_map/near_rows/pallas_call | solution.py:425
  108.1 0.6 collective-permute-start.9
  108.7 0.6 pad_add_fusion.starts
  109.3 4.2 %collective-permute-done.10.refs_2_ = bf16[2,128,2304]{2,1,0:T(8,128)(2,1)} collective-permute-done((bf16[2,128,2304]{2,1,0:T(8,128)(2,1)}, bf16[2,128,2304]{2,1,0:T(8,128)(2,1)}, u32[]{:S(2)}, u32[]{:S(2)}) %collective-permute-start.10) | collective-permute-done | bytes 1179680 | tf_op jit(solution)/shard_map/ppermute | solution.py:469
  113.5 0.0 collective-permute-done.9.refs_1_
  113.5 5.4 %collective-permute-done.11.refs_3_ = bf16[2,128,2560]{2,1,0:T(8,128)(2,1)S(1)} collective-permute-done((bf16[2,128,2560]{2,1,0:T(8,128)(2,1)S(1)}, bf16[2,128,2560]{2,1,0:T(8,128)(2,1)S(1)}, u32[]{:S(2)}, u32[]{:S(2)}) %collective-permute-start.11) | collective-permute-done | bytes 1310752 | tf_op jit(solution)/shard_map/ppermute | solution.py:469
  118.9 1.1 copy-done
  119.9 7.2 %add_pieces.1 = f32[2,128,3328]{2,1,0:T(8,128)} custom-call(s32[4]{0:T(128)} %pad_add_fusion.starts, f32[2,128,2304]{2,1,0:T(8,128)} %get-tuple-element.52.refs_0_, bf16[2,128,2304]{2,1,0:T(8,128)(2,1)} %collective-permute-done.9.refs_1_, bf16[2,128,2304]{2,1,0:T(8,128)(2,1)} %collective-permute-done.10.refs_2_, bf16[2,128,2560]{2,1,0:T(8,128)(2,1)} %copy-done), custom_call_target="tpu_custom_call" | custom-call | flops 1000000 | bytes 9000000 | tf_op jit(solution)/shard_map/add_pieces/pallas_call | solution.py:454
  (4 shorter events, 0.0 us)
Async XLA Ops:
  2.1 25.9 %collective-permute-start = (bf16[528,128]{1,0:T(8,128)(2,1)}, bf16[528,128]{1,0:T(8,128)(2,1)S(1)}, u32[]{:S(2)}, u32[]{:S(2)}) collective-permute-start(bf16[528,128]{1,0:T(8,128)(2,1)} %get-tuple-element.35), channel_id=1, source_target_pairs={{0,2},{1,3},{2,4},{3,5},{4,6},{5,7},{6,8},{7,9},{8,10},{9,11},{10,... | collective-permute-start | bytes 405512 | tf_op jit(solution)/shard_map/ppermute | solution.py:38
  5.9 22.1 %collective-permute-start.1 = (bf16[528,128]{1,0:T(8,128)(2,1)}, bf16[528,128]{1,0:T(8,128)(2,1)S(1)}, u32[]{:S(2)}, u32[]{:S(2)}) collective-permute-start(bf16[528,128]{1,0:T(8,128)(2,1)} %get-tuple-element.36), channel_id=1, source_target_pairs={{2,0},{3,1},{4,2},{5,3},{6,4},{7,5},{8,6},{9,7},{10,8},{11,9},{12,... | collective-permute-start | bytes 405512 | tf_op jit(solution)/shard_map/ppermute | solution.py:38
  12.3 15.7 %collective-permute-start.2 = (bf16[528,128]{1,0:T(8,128)(2,1)}, bf16[528,128]{1,0:T(8,128)(2,1)S(1)}, u32[]{:S(2)}, u32[]{:S(2)}) collective-permute-start(bf16[528,128]{1,0:T(8,128)(2,1)} %get-tuple-element.37), channel_id=1, source_target_pairs={{0,1},{1,2},{2,3},{3,4},{4,5},{5,6},{6,7},{7,8},{8,9},{9,10},{10,1... | collective-permute-start | bytes 405512 | tf_op jit(solution)/shard_map/ppermute | solution.py:38
  14.3 13.8 %collective-permute-start.3 = (bf16[528,128]{1,0:T(8,128)(2,1)}, bf16[528,128]{1,0:T(8,128)(2,1)S(1)}, u32[]{:S(2)}, u32[]{:S(2)}) collective-permute-start(bf16[528,128]{1,0:T(8,128)(2,1)} %get-tuple-element.38), channel_id=1, source_target_pairs={{1,0},{2,1},{3,2},{4,3},{5,4},{6,5},{7,6},{8,7},{9,8},{10,9},{11,1... | collective-permute-start | bytes 405512 | tf_op jit(solution)/shard_map/ppermute | solution.py:38
  28.0 0.6 copy-start.1
  28.0 0.7 copy-start.2
  28.0 0.7 copy-start.3
  28.0 0.8 copy-start.4
  37.4 23.9 %collective-permute-start.4 = (bf16[528,512]{1,0:T(8,128)(2,1)}, bf16[528,512]{1,0:T(8,128)(2,1)S(1)}, u32[]{:S(2)}, u32[]{:S(2)}) collective-permute-start(bf16[528,512]{1,0:T(8,128)(2,1)} %get-tuple-element.44), channel_id=1, source_target_pairs={{0,2},{1,3},{2,4},{3,5},{4,6},{5,7},{6,8},{7,9},{8,10},{9,11},{10,... | collective-permute-start | bytes 1622024 | tf_op jit(solution)/shard_map/ppermute | solution.py:38
  39.3 22.0 %collective-permute-start.5 = (bf16[528,512]{1,0:T(8,128)(2,1)}, bf16[528,512]{1,0:T(8,128)(2,1)S(1)}, u32[]{:S(2)}, u32[]{:S(2)}) collective-permute-start(bf16[528,512]{1,0:T(8,128)(2,1)} %get-tuple-element.45), channel_id=1, source_target_pairs={{2,0},{3,1},{4,2},{5,3},{6,4},{7,5},{8,6},{9,7},{10,8},{11,9},{12,... | collective-permute-start | bytes 1622024 | tf_op jit(solution)/shard_map/ppermute | solution.py:38
  47.5 15.1 %collective-permute-start.6 = (bf16[528,512]{1,0:T(8,128)(2,1)}, bf16[528,512]{1,0:T(8,128)(2,1)S(1)}, u32[]{:S(2)}, u32[]{:S(2)}) collective-permute-start(bf16[528,512]{1,0:T(8,128)(2,1)} %get-tuple-element.46), channel_id=1, source_target_pairs={{0,1},{1,2},{2,3},{3,4},{4,5},{5,6},{6,7},{7,8},{8,9},{9,10},{10,1... | collective-permute-start | bytes 1622024 | tf_op jit(solution)/shard_map/ppermute | solution.py:38
  49.4 15.0 %collective-permute-start.7 = (bf16[528,512]{1,0:T(8,128)(2,1)}, bf16[528,512]{1,0:T(8,128)(2,1)S(1)}, u32[]{:S(2)}, u32[]{:S(2)}) collective-permute-start(bf16[528,512]{1,0:T(8,128)(2,1)} %get-tuple-element.47), channel_id=1, source_target_pairs={{1,0},{2,1},{3,2},{4,3},{5,4},{6,5},{7,6},{8,7},{9,8},{10,9},{11,1... | collective-permute-start | bytes 1622024 | tf_op jit(solution)/shard_map/ppermute | solution.py:38
  61.3 3.2 %copy-start.5 = (bf16[528,512]{1,0:T(8,128)(2,1)}, bf16[528,512]{1,0:T(8,128)(2,1)S(1)}, u32[]{:S(2)}) copy-start(bf16[528,512]{1,0:T(8,128)(2,1)S(1)} %collective-permute-done.4.g2) | copy-start | bytes 1622020
  61.3 3.1 %copy-start.6 = (bf16[528,512]{1,0:T(8,128)(2,1)}, bf16[528,512]{1,0:T(8,128)(2,1)S(1)}, u32[]{:S(2)}) copy-start(bf16[528,512]{1,0:T(8,128)(2,1)S(1)} %collective-permute-done.5.g3) | copy-start | bytes 1622020
  62.6 1.9 %copy-start.7 = (bf16[528,512]{1,0:T(8,128)(2,1)}, bf16[528,512]{1,0:T(8,128)(2,1)S(1)}, u32[]{:S(2)}) copy-start(bf16[528,512]{1,0:T(8,128)(2,1)S(1)} %collective-permute-done.6.g0) | copy-start | bytes 1622020
  64.4 0.8 copy-start.8
  82.7 8.4 %collective-permute-start.8 = (bf16[2,128,2560]{2,1,0:T(8,128)(2,1)}, bf16[2,128,2560]{2,1,0:T(8,128)(2,1)S(1)}, u32[]{:S(2)}, u32[]{:S(2)}) collective-permute-start(bf16[2,128,2560]{2,1,0:T(8,128)(2,1)} %get-tuple-element.50), channel_id=1, source_target_pairs={{0,1},{1,0},{2,3},{3,2},{4,5},{5,4},{6,7},{7,6},{8,9},{9,8},{10,11... | collective-permute-start | bytes 3932168 | tf_op jit(solution)/shard_map/ppermute | solution.py:469
  82.8 30.7 %collective-permute-start.10 = (bf16[2,128,2304]{2,1,0:T(8,128)(2,1)}, bf16[2,128,2304]{2,1,0:T(8,128)(2,1)}, u32[]{:S(2)}, u32[]{:S(2)}) collective-permute-start(bf16[2,128,2304]{2,1,0:T(8,128)(2,1)} %get-tuple-element.54), channel_id=1, source_target_pairs={{1,3},{2,0},{3,5},{4,2},{5,7},{6,4},{7,9},{8,6},{9,11},{10,8},{11,... | collective-permute-start | bytes 3538952 | tf_op jit(solution)/shard_map/ppermute | solution.py:469
  93.2 25.7 %collective-permute-start.11 = (bf16[2,128,2560]{2,1,0:T(8,128)(2,1)S(1)}, bf16[2,128,2560]{2,1,0:T(8,128)(2,1)S(1)}, u32[]{:S(2)}, u32[]{:S(2)}) collective-permute-start(bf16[2,128,2560]{2,1,0:T(8,128)(2,1)S(1)} %add_convert_fusion), channel_id=1, source_target_pairs={{0,2},{2,4},{3,1},{4,6},{5,3},{6,8},{7,5},{8,10},{9,7},{10,12},{11... | collective-permute-start | bytes 3932168 | tf_op jit(solution)/shard_map/ppermute | solution.py:469
  108.1 5.4 %collective-permute-start.9 = (bf16[2,128,2304]{2,1,0:T(8,128)(2,1)}, bf16[2,128,2304]{2,1,0:T(8,128)(2,1)}, u32[]{:S(2)}, u32[]{:S(2)}) collective-permute-start(bf16[2,128,2304]{2,1,0:T(8,128)(2,1)} %get-tuple-element.53), channel_id=1, source_target_pairs={{0,1},{1,0},{2,3},{3,2},{4,5},{5,4},{6,7},{7,6},{8,9},{9,8},{10,11... | collective-permute-start | bytes 3538952 | tf_op jit(solution)/shard_map/ppermute | solution.py:469
  118.9 1.1 copy-start

commit v3 on v2

--- a/solution.py
+++ b/solution.py
@@ -15,6 +15,7 @@
 FRAME = 18
 WIDE = FRAME * BS
 SLOTW = 4 * BS
+SENDW = 3 * BS
 CHIPWIDE = 20 * BS
 BANDWIDE = 26 * BS
 TILES = [slice(t * 2 * BS, (t + 1) * 2 * BS) for t in range(FRAME // 2)]
@@ -46,7 +47,7 @@
     return total.astype(F32).astype(BF)
 
 
-def pack_kernel(send_rows, aggregate, tent, *refs):
+def pack_kernel(send_rows, aggregate, tent, diag, *refs):
     outs, labels, sem = refs[:4], refs[4], refs[5]
     copies = []
     for n in START_ORDER:
@@ -56,27 +57,39 @@
                     tent.at[send_rows[n, g]], outs[n].at[pl.ds(g * BS, BS)], sem.at[n, g]
                 )
             )
+            copies.append(
+                pltpu.make_async_copy(
+                    diag.at[send_rows[n, g]], outs[n].at[pl.ds((NG + g) * BS, BS)], sem.at[n, NG + g]
+                )
+            )
     for copy in copies:
         copy.start()
     for n in START_ORDER:
         labels[n] = label_rows([aggregate[send_rows[n, g]] for g in range(NG)], BS)
-        copy = pltpu.make_async_copy(labels.at[n], outs[n].at[pl.ds(NG * BS, EXTRA)], sem.at[n, NG])
+        copy = pltpu.make_async_copy(labels.at[n], outs[n].at[pl.ds(2 * NG * BS, EXTRA)], sem.at[n, 2 * NG])
         copy.start()
         copies.append(copy)
     for copy in copies:
         copy.wait()
 
 
-def pack(send_rows, aggregate, tent):
-    shape = jax.ShapeDtypeStruct((NG * BS + EXTRA, BS), BF)
+def pack(send_rows, aggregate, tent, diag):
+    shape = jax.ShapeDtypeStruct((2 * NG * BS + EXTRA, BS), BF)
     return pl.pallas_call(
         pack_kernel,
         out_shape=[shape] * 4,
-        in_specs=[spec(SMEM), spec(SMEM), spec(pltpu.VMEM)],
+        in_specs=[spec(SMEM), spec(SMEM), spec(pltpu.VMEM), spec(pltpu.VMEM)],
         out_specs=[spec(ANY)] * 4,
-        scratch_shapes=[pltpu.VMEM((4, EXTRA, BS), BF), pltpu.SemaphoreType.DMA((4, NG + 1))],
+        scratch_shapes=[pltpu.VMEM((4, EXTRA, BS), BF), pltpu.SemaphoreType.DMA((4, 2 * NG + 1))],
         name="pack",
-    )(send_rows, aggregate, tent)
+    )(send_rows, aggregate, tent, diag)
+
+
+def first_slot(eye, block, own):
+    diagonal = jnp.sum(jnp.where(eye, block.astype(F32), 0.0), axis=1, keepdims=True)
+    scale = 0.6 * (1.0 / jnp.where(diagonal == 0.0, 1.0, diagonal))
+    first = own.astype(F32) - scale * jnp.dot(block, own, preferred_element_type=F32)
+    return first.astype(BF), scale
 
 
 def local_slots_kernel(off_columns, aggregate, diag, off, tent, labels, ghost_list, ghost_count, slots, scales):
@@ -84,16 +97,11 @@
     ghost_count[0] = 0
 
     def row(i, carry):
-        block = diag[i]
-        inv = 1.0 / jnp.sum(jnp.where(eye, block.astype(F32), 0.0), axis=1, keepdims=True)
-        scale = 0.6 * inv
+        slots[i, :, :BS], scale = first_slot(eye, diag[i], tent[i])
         scales[i] = jnp.broadcast_to(scale, (BS, BS))
-        own = tent[i]
-        first = own.astype(F32) - scale * jnp.dot(block, own, preferred_element_type=F32)
-        slots[i, :, :BS] = first.astype(BF)
         labels[i, 0] = aggregate[i] + 8
         for k in range(1, 4):
-            c = off_columns[i, k - 1]
+            c = off_columns[k - 1, i]
             near = tent[jnp.minimum(c, NB - 1)]
             part = -scale * jnp.dot(off[i, k - 1], near, preferred_element_type=F32)
             slots[i, :, k * BS : (k + 1) * BS] = part.astype(BF)
@@ -121,7 +129,7 @@
         ],
         in_specs=[spec(SMEM)] * 2 + [spec(pltpu.VMEM)] * 3,
         out_specs=[spec(SMEM)] * 3 + [spec(pltpu.VMEM)] * 2,
-        compiler_params=pltpu.CompilerParams(vmem_limit_bytes=VMEM_LIMIT),
+        compiler_params=pltpu.CompilerParams(vmem_limit_bytes=10 * 1024 * 1024),
         cost_estimate=pl.CostEstimate(flops=10**9, bytes_accessed=6 * 10**6, transcendentals=0),
         name="local_slots",
     )(off_columns, aggregate, diag, off, tent)
@@ -147,7 +155,7 @@
                 )
             )
     lab = [
-        pltpu.make_async_copy(ghosts[n].at[pl.ds(NG * BS, EXTRA)], labels_out.at[n, :, pl.ds(0, BS)], sem_lab.at[n])
+        pltpu.make_async_copy(ghosts[n].at[pl.ds(2 * NG * BS, EXTRA)], labels_out.at[n, :, pl.ds(0, BS)], sem_lab.at[n])
         for n in range(4)
     ]
     for copy in lab + copies + big:
@@ -171,7 +179,7 @@
             entry = ghost_list[q * GROUP + u]
             i, k = lax.div(entry, 4), lax.rem(entry, 4)
             row = jnp.minimum(i, NB - 1)
-            ghost = jnp.clip(off_columns[row, k - 1] - NB, 0, 4 * NG - 1)
+            ghost = jnp.clip(off_columns[k - 1, row] - NB, 0, 4 * NG - 1)
             part = jnp.dot(off_buf[row, k - 1], table[ghost], preferred_element_type=F32)
             part = -scale_buf[row] * part
             slot_buf[i, :, pl.ds(pl.multiple_of(k * BS, BS), BS)] = part.astype(BF)
@@ -185,7 +193,7 @@
         for g in range(NG):
             outs.append(
                 pltpu.make_async_copy(
-                    slot_buf.at[send_rows[n, g]], sends[n].at[pl.ds(g * BS, BS)], sem_out.at[n * NG + g]
+                    slot_buf.at[send_rows[n, g], :, pl.ds(BS, SENDW)], sends[n].at[pl.ds(g * BS, BS)], sem_out.at[n * NG + g]
                 )
             )
     outs.append(pltpu.make_async_copy(slot_buf.at[pl.ds(0, NB)], slots, sem_big.at[0]))
@@ -193,7 +201,7 @@
         copy.start()
     for n in START_ORDER:
         values = [labels[send_rows[n, g], k] for g in range(NG) for k in range(4)]
-        labels_out[n] = label_rows(values, SLOTW)
+        labels_out[n] = label_rows(values, SENDW)
         copy = pltpu.make_async_copy(labels_out.at[n], sends[n].at[pl.ds(NG * BS, EXTRA)], sem_lab.at[n])
         copy.start()
         outs.append(copy)
@@ -202,7 +210,7 @@
 
 
 def ghost_slots(send_rows, off_columns, local_labels, ghost_list, ghost_count, off, slots_in, scales, ghosts):
-    send = jax.ShapeDtypeStruct((NG * BS + EXTRA, SLOTW), BF)
+    send = jax.ShapeDtypeStruct((NG * BS + EXTRA, SENDW), BF)
     labels, slots, *sends = pl.pallas_call(
         ghost_slots_kernel,
         out_shape=[
@@ -215,7 +223,7 @@
         scratch_shapes=[
             pltpu.VMEM((4 * NG, BS, BS), BF),
             pltpu.VMEM((4, 8, BS), jnp.int32),
-            pltpu.VMEM((4, EXTRA, SLOTW), BF),
+            pltpu.VMEM((4, EXTRA, SENDW), BF),
             pltpu.SMEM((4, 8, BS), jnp.int32),
             pltpu.VMEM((NB + 1, BS, SLOTW), BF),
             pltpu.VMEM((NB, 3, BS, BS), BF),
@@ -225,14 +233,21 @@
             pltpu.SemaphoreType.DMA((4 * NG,)),
             pltpu.SemaphoreType.DMA((3,)),
         ],
-        compiler_params=pltpu.CompilerParams(vmem_limit_bytes=VMEM_LIMIT),
+        compiler_params=pltpu.CompilerParams(vmem_limit_bytes=12 * 1024 * 1024),
         name="ghost_slots",
     )(send_rows, off_columns, local_labels, ghost_list, ghost_count, off, slots_in, scales,
       *[ghosts[n] for n in START_ORDER])
     return labels, slots, [sends[START_ORDER.index(n)] for n in range(4)]
 
 
-def lists_kernel(labels, slots, lists, counts, blocks):
+def lists_kernel(labels, slots, g2, g3, g0, g1, lists, counts, blocks, first_slots, ghost_buf, sem):
+    ghosts = (g0, g1, g2, g3)
+    copies = [
+        pltpu.make_async_copy(ghosts[n].at[pl.ds(0, 2 * NG * BS)], ghost_buf.at[n], sem.at[n])
+        for n in range(4)
+    ]
+    for copy in copies:
+        copy.start()
     for t in range(10):
         counts[t] = 0
 
@@ -252,22 +267,36 @@
         for d in range(CHUNK - 1):
             lists[t, at + d] = 4 * NB
         counts[t] = lax.div(at + CHUNK - 1, CHUNK)
-
-
-def make_lists(labels, slots):
+    for copy in copies:
+        copy.wait()
+    eye = lax.broadcasted_iota(jnp.int32, (BS, BS), 0) == lax.broadcasted_iota(jnp.int32, (BS, BS), 1)
+
+    def ghost(n, carry):
+        for g in range(NG):
+            first_slots[n * NG + g] = first_slot(
+                eye, ghost_buf[n, (NG + g) * BS : (NG + g + 1) * BS], ghost_buf[n, g * BS : (g + 1) * BS]
+            )[0]
+        return carry
+
+    lax.fori_loop(0, 4, ghost, 0)
+
+
+def make_lists(labels, slots, ghosts):
     return pl.pallas_call(
         lists_kernel,
         out_shape=[
             jax.ShapeDtypeStruct((10, 4 * NB + CHUNK), jnp.int32),
             jax.ShapeDtypeStruct((10,), jnp.int32),
             jax.ShapeDtypeStruct((4 * NB + 1, BS, BS), BF),
+            jax.ShapeDtypeStruct((4 * NG, BS, BS), BF),
         ],
-        in_specs=[spec(SMEM), spec(pltpu.VMEM)],
-        out_specs=[spec(SMEM)] * 2 + [spec(pltpu.VMEM)],
-        compiler_params=pltpu.CompilerParams(vmem_limit_bytes=VMEM_LIMIT),
+        in_specs=[spec(SMEM), spec(pltpu.VMEM)] + [spec(ANY)] * 4,
+        out_specs=[spec(SMEM)] * 2 + [spec(pltpu.VMEM)] * 2,
+        scratch_shapes=[pltpu.VMEM((4, 2 * NG * BS, BS), BF), pltpu.SemaphoreType.DMA((4,))],
+        compiler_params=pltpu.CompilerParams(vmem_limit_bytes=12 * 1024 * 1024),
         cost_estimate=pl.CostEstimate(flops=10**8, bytes_accessed=6 * 10**6, transcendentals=0),
         name="lists",
-    )(labels, slots)
+    )(labels, slots, *[ghosts[n] for n in START_ORDER])
 
 
 def coarse_rows(t, at, lists, counts, blocks, applied, coarse):
@@ -286,18 +315,23 @@
 
 
 def far_kernel(
-    parity, off_columns, labels, lists, counts, diag, off, slots, blocks, g2, g3, g0, g1,
+    parity, off_columns, labels, lists, counts, diag, off, slots, blocks, first_slots, g2, g3, g0, g1,
     applied_out, relay_out, relayed_out, direct_out,
-    table, labels_in, labels_vmem, label_smem, total, applied, coarse, relay, relayed, direct,
+    table, labels_in, labels_vmem, label_smem, total_a, total_b, applied, coarse, relay, relayed, direct,
     sem_in, sem_lab, sem_out, sem_piece,
 ):
     ghosts = (g0, g1, g2, g3)
-    copies = [pltpu.make_async_copy(slots, table.at[pl.ds(0, NB)], sem_in.at[0])]
+    copies = [
+        pltpu.make_async_copy(slots, table.at[pl.ds(0, NB)], sem_in.at[0]),
+        pltpu.make_async_copy(first_slots, table.at[pl.ds(NB, 4 * NG), :, pl.ds(0, BS)], sem_in.at[1]),
+    ]
     for n in range(4):
         for g in range(NG):
             copies.append(
                 pltpu.make_async_copy(
-                    ghosts[n].at[pl.ds(g * BS, BS)], table.at[NB + n * NG + g], sem_in.at[1 + n * NG + g]
+                    ghosts[n].at[pl.ds(g * BS, BS)],
+                    table.at[NB + n * NG + g, :, pl.ds(BS, SENDW)],
+                    sem_in.at[2 + n * NG + g],
                 )
             )
     lab = [
@@ -328,10 +362,10 @@
         local = labels[jnp.minimum(j, NB - 1), m]
         return jnp.clip(jnp.where(j < NB, local, remote), 0, FRAME - 1)
 
-    def row(i, carry):
+    def row(i, total):
         total[...] = jnp.zeros_like(total)
         for k in range(4):
-            j = i if k == 0 else off_columns[i, k - 1]
+            j = i if k == 0 else off_columns[k - 1, i]
             block = diag[i] if k == 0 else off[i, k - 1]
             prod = jnp.dot(block, table[j], preferred_element_type=F32)
             for m in range(4):
@@ -340,9 +374,13 @@
         for at in range(FRAME):
             applied[i, :, at * BS : (at + 1) * BS] = total[at].astype(BF)
         pltpu.make_async_copy(applied.at[i], applied_out.at[i], sem_out.at[i]).start()
-        return carry
-
-    lax.fori_loop(0, NB, row, 0)
+
+    def row_pair(q, carry):
+        row(2 * q, total_a)
+        row(2 * q + 1, total_b)
+        return carry
+
+    lax.fori_loop(0, NB // 2, row_pair, 0)
     into = pl.ds(pl.multiple_of(parity[0] * (2 * BS), BS), WIDE)
 
     def rows_of(level):
@@ -374,7 +412,7 @@
         copy.wait()
 
 
-def make_far(parity, off_columns, labels, lists, counts, diag, off, slots, blocks, ghosts):
+def make_far(parity, off_columns, labels, lists, counts, diag, off, slots, blocks, first_slots, ghosts):
     return pl.pallas_call(
         far_kernel,
         out_shape=[
@@ -383,7 +421,7 @@
             jax.ShapeDtypeStruct((2, BS, CHIPWIDE), F32),
             jax.ShapeDtypeStruct((2, BS, WIDE), BF),
         ],
-        in_specs=[spec(SMEM)] * 5 + [spec(pltpu.VMEM)] * 2 + [spec(ANY), spec(pltpu.VMEM)] + [spec(ANY)] * 4,
+        in_specs=[spec(SMEM)] * 5 + [spec(pltpu.VMEM)] * 2 + [spec(ANY), spec(pltpu.VMEM)] + [spec(ANY)] * 5,
         out_specs=[spec(ANY)] * 4,
         scratch_shapes=[
             pltpu.VMEM((NT, BS, SLOTW), BF),
@@ -391,20 +429,21 @@
             pltpu.VMEM((4, 8, BS), jnp.int32),
             pltpu.SMEM((4, 8, BS), jnp.int32),
             pltpu.VMEM((FRAME, BS, BS), F32),
+            pltpu.VMEM((FRAME, BS, BS), F32),
             pltpu.VMEM((NB, BS, WIDE), BF),
             pltpu.VMEM((2, BS, WIDE), F32),
             pltpu.VMEM((2, BS, CHIPWIDE), BF),
             pltpu.VMEM((2, BS, CHIPWIDE), F32),
             pltpu.VMEM((2, BS, WIDE), BF),
-            pltpu.SemaphoreType.DMA((1 + 4 * NG,)),
+            pltpu.SemaphoreType.DMA((2 + 4 * NG,)),
             pltpu.SemaphoreType.DMA((4,)),
             pltpu.SemaphoreType.DMA((NB,)),
             pltpu.SemaphoreType.DMA((3,)),
         ],
-        compiler_params=pltpu.CompilerParams(vmem_limit_bytes=VMEM_LIMIT),
+        compiler_params=pltpu.CompilerParams(vmem_limit_bytes=34 * 1024 * 1024),
         cost_estimate=pl.CostEstimate(flops=4 * 10**9, bytes_accessed=20 * 10**6, transcendentals=0),
         name="far_rows",
-    )(parity, off_columns, labels, lists, counts, diag, off, slots, blocks,
+    )(parity, off_columns, labels, lists, counts, diag, off, slots, blocks, first_slots,
       *[ghosts[n] for n in START_ORDER])
 
 
@@ -431,36 +470,80 @@
         in_specs=[spec(SMEM)] * 3 + [spec(pltpu.VMEM)] * 2,
         out_specs=[spec(pltpu.VMEM)] * 2,
         scratch_shapes=[pltpu.VMEM((4, BS, WIDE), F32)],
-        compiler_params=pltpu.CompilerParams(vmem_limit_bytes=VMEM_LIMIT),
+        compiler_params=pltpu.CompilerParams(vmem_limit_bytes=26 * 1024 * 1024),
         cost_estimate=pl.CostEstimate(flops=4 * 10**9, bytes_accessed=20 * 10**6, transcendentals=0),
         name="near_rows",
     )(parity, lists, counts, blocks, applied)
 
 
-def add_kernel(starts, *refs):
-    pieces, out = refs[:-1], refs[-1]
-    out[...] = jnp.zeros_like(out)
-    for at, piece in enumerate(pieces):
-        cols = pl.ds(pl.multiple_of(starts[at] * (2 * BS), BS), piece.shape[2])
+def add_near_kernel(parity, own, mate, direct, out):
+    edge = 4 * BS
+    out[:, :, :edge] = jnp.zeros((2, own.shape[1], edge), F32)
+    out[:, :, edge + WIDE :] = jnp.zeros((2, own.shape[1], edge), F32)
+    out[:, :, edge : edge + WIDE] = own[...]
+    for start, piece in ((3 - 2 * parity[0], mate), (4 - 4 * parity[0], direct)):
+        cols = pl.ds(pl.multiple_of(start * (2 * BS), BS), WIDE)
         out[:, :, cols] = out[:, :, cols] + piece[...].astype(F32)
 
 
-def add_pieces(starts, pieces):
-    rows = 16
+def add_near(parity, own, mate, direct):
+    rows = 32
 
     def block(width):
         return pl.BlockSpec((2, rows, width), lambda r: (0, r, 0))
 
     return pl.pallas_call(
-        add_kernel,
+        add_near_kernel,
         grid=(BS // rows,),
         out_shape=jax.ShapeDtypeStruct((2, BS, BANDWIDE), F32),
-        in_specs=[spec(SMEM)] + [block(p.shape[2]) for p in pieces],
+        in_specs=[spec(SMEM)] + [block(WIDE)] * 3,
         out_specs=block(BANDWIDE),
-        compiler_params=pltpu.CompilerParams(vmem_limit_bytes=VMEM_LIMIT),
+        compiler_params=pltpu.CompilerParams(vmem_limit_bytes=16 * 1024 * 1024),
         cost_estimate=pl.CostEstimate(flops=10**6, bytes_accessed=9 * 10**6, transcendentals=0),
-        name="add_pieces",
-    )(starts, *pieces)
+        name="add_near",
+    )(parity, own, mate, direct)
+
+
+def add_pair_kernel(parity, band, pair, out, band_buf, pair_buf, sem):
+    rows = BS // 4
+    cols = pl.ds(pl.multiple_of(parity[0] * (6 * BS), BS), CHIPWIDE)
+    parts = [(b, pl.ds(r * rows, rows)) for b in range(2) for r in range(4)]
+    loads, stores = [], []
+    for at, (b, r) in enumerate(parts):
+        loads.append(
+            (
+                pltpu.make_async_copy(pair.at[b, r], pair_buf.at[b, r], sem.at[0, at]),
+                pltpu.make_async_copy(band.at[b, r, cols], band_buf.at[b, r], sem.at[1, at]),
+            )
+        )
+        stores.append(pltpu.make_async_copy(band_buf.at[b, r], out.at[b, r, cols], sem.at[2, at]))
+    for pair_of in loads:
+        for copy in pair_of:
+            copy.start()
+    for at, (b, r) in enumerate(parts):
+        for copy in loads[at]:
+            copy.wait()
+        band_buf[b, r] = band_buf[b, r] + pair_buf[b, r].astype(F32)
+        stores[at].start()
+    for copy in stores:
+        copy.wait()
+
+
+def add_pair(parity, band, pair):
+    return pl.pallas_call(
+        add_pair_kernel,
+        out_shape=jax.ShapeDtypeStruct((2, BS, BANDWIDE), F32),
+        in_specs=[spec(SMEM), spec(ANY), spec(ANY)],
+        out_specs=spec(ANY),
+        input_output_aliases={1: 0},
+        scratch_shapes=[
+            pltpu.VMEM((2, BS, CHIPWIDE), F32),
+            pltpu.VMEM((2, BS, CHIPWIDE), BF),
+            pltpu.SemaphoreType.DMA((3, 8)),
+        ],
+        compiler_params=pltpu.CompilerParams(vmem_limit_bytes=8 * 1024 * 1024),
+        name="add_pair",
+    )(parity, band, pair)
 
 
 def permute_by(value, even_step, odd_step):
@@ -477,19 +560,20 @@
 
 
 def local(diag_blocks, off_blocks, off_columns, tentative, aggregate, send_rows):
+    off_columns = off_columns.T
     odd = lax.rem(lax.axis_index(AXES), 2)
     parity = odd.reshape(1)
-    ghosts = exchange(pack(send_rows, aggregate, tentative))
+    ghosts = exchange(pack(send_rows, aggregate, tentative, diag_blocks))
     labels, ghost_list, ghost_count, slots, scales = local_slots(
         off_columns, aggregate, diag_blocks, off_blocks, tentative
     )
     labels, slots, sends = ghost_slots(
         send_rows, off_columns, labels, ghost_list, ghost_count, off_blocks, slots, scales, ghosts
     )
+    lists, counts, blocks, first_slots = make_lists(labels, slots, ghosts)
     ghosts = exchange(sends)
-    lists, counts, blocks = make_lists(labels, slots)
     applied, relay, relayed, direct = make_far(
-        parity, off_columns, labels, lists, counts, diag_blocks, off_blocks, slots, blocks, ghosts
+        parity, off_columns, labels, lists, counts, diag_blocks, off_blocks, slots, blocks, first_slots, ghosts
     )
     direct_in = permute_by(direct, -2, 2)
     relay_in = permute_by(relay, 1, -1)
@@ -498,8 +582,8 @@
     applied, pair_sum = lax.optimization_barrier((applied, pair_sum))
     own, mate = make_near(parity, lists, counts, blocks, applied)
     mate_in = permute_by(mate, 1, -1)
-    starts = jnp.stack([jnp.int32(2), jnp.where(odd == 1, 1, 3), jnp.where(odd == 1, 0, 4), 3 * odd])
-    return add_pieces(starts, [own, mate_in, direct_in, pair_in])
+    band = add_near(parity, own, mate_in, direct_in)
+    return add_pair(parity, band, pair_in)
 
 
 def solution(mesh):

time: 129 us -> 117 us (0.907)
  Pallas kernels: 56.7 us -> 41.4 us
  local copies, waits for them, and re-layouts: 3.96 us -> 8.52 us
  other arithmetic: 2.7 us -> 0.36 us
  starting transfers between devices: 50.7 us -> 52.1 us
    pallas_call x1, Pallas kernels: 13 us -> 7.11 us  [make_near(): pl.pallas_call(near_kernel, out_shape=[jax.ShapeDtypeStruct((2, BS, WIDE)...]
    pallas_call x1, Pallas kernels: 17.5 us -> 12.7 us  [make_far(): pl.pallas_call(far_kernel, out_shape=[jax.ShapeDtypeStruct((NB, BS, WIDE)...]
    unnamed x19 -> x22, local copies, waits for them, and re-layouts: 3.96 us -> 8.52 us
    pallas_call x1, Pallas kernels: 4.49 us -> 2.4 us  [local_slots(): pl.pallas_call(local_slots_kernel, out_shape=[jax.ShapeDtypeStruct((NB, 4...]
    convert_element_type x1, other arithmetic: 2.11 us -> 0.36 us  [local(): pair_sum = (relayed + relay_in.astype(F32)).astype(BF)]
    pallas_call x1, Pallas kernels: 8.57 us -> 6.97 us  [ghost_slots(): pl.pallas_call(ghost_slots_kernel, out_shape=[jax.ShapeDtypeStruct((NB +...]
    ppermute x4, starting transfers between devices: 10.9 us -> 12.3 us  [permute_by(): lax.ppermute(value, AXES, [(s, t) for s, t in pairs if 0 <= t < count])]
    pallas_call x1 -> x2, Pallas kernels: 7.19 us -> 6.52 us  [the longest x1 3.82 us: add_pair(): pl.pallas_call(add_pair_kernel, out_shape=jax.ShapeDtypeStruct((2, BS, BA...]
  transfers between devices with their start and end apart: 12 -> 12, of which waited for: 4 -> 4; matrix products, arithmetic and copies ran while one was open for 3% -> 0% of each run, Pallas kernels for 17% -> 13%
where the time goes in v3:
time: 117 us; the launch traced here: 115 us
  starting transfers between devices  52.1 us (45%)
  Pallas kernels  41.4 us (35%)
  waiting for transfers between devices  12.3 us (11%)
  local copies, waits for them, and re-layouts  8.52 us (7%)
    ppermute x8, starting transfers between devices, shift(): lax.ppermute(value, AXES, [(s, s + steps) for s in range(first, last)])  39.9 us
    pallas_call x1, Pallas kernels, make_far(): pl.pallas_call(far_kernel, out_shape=[jax.ShapeDtypeStruct((NB, BS, WIDE)...  12.7 us
    ppermute x4, starting transfers between devices, permute_by(): lax.ppermute(value, AXES, [(s, t) for s, t in pairs if 0 <= t < count])  12.3 us
    ppermute x4, waiting for transfers between devices, permute_by(): lax.ppermute(value, AXES, [(s, t) for s, t in pairs if 0 <= t < count])  9.87 us
    unnamed x22, local copies, waits for them, and re-layouts  8.52 us
    pallas_call x1, Pallas kernels, make_near(): pl.pallas_call(near_kernel, out_shape=[jax.ShapeDtypeStruct((2, BS, WIDE)...  7.11 us
    pallas_call x1, Pallas kernels, ghost_slots(): pl.pallas_call(ghost_slots_kernel, out_shape=[jax.ShapeDtypeStruct((NB +...  6.97 us
    pallas_call x1, Pallas kernels, add_pair(): pl.pallas_call(add_pair_kernel, out_shape=jax.ShapeDtypeStruct((2, BS, BA...  3.82 us
  transfers between devices with their start and end apart: 12, of which 4 were waited for; matrix products, arithmetic and copies ran while one was open for 0% of the time, Pallas kernels for 13%

profile of v3, /device:TPU:24, one launch (start us, length us, event | category | flops | bytes accessed | tf_op | source)
XLA Modules:
  0.0 115.0 jit_solution(8488561349221916037)
XLA Ops:
  0.0 2.5 %pack.1 = (bf16[1040,128]{1,0:T(8,128)(2,1)}, bf16[1040,128]{1,0:T(8,128)(2,1)}, bf16[1040,128]{1,0:T(8,128)(2,1)}, bf16[1040,128]{1,0:T(8,128)(2,1)}) custom-call(s32[4,4]{1,0:T(4,128)} %send_rows.3, s32[16]{0:T(128)} %aggregate.3, bf16[16,128,128]{2,1,0:T(8,128)(2,1)} %tent.3, bf16[16,128,128]{2,1,0:T(8,128)(2,1)} %diag.5), custom_call_target="tpu_custom_call" | custom-call | tf_op jit(solution)/shard_map/pack/pallas_call | solution.py:78
  2.5 0.0 copy-start.6
  2.5 0.0 copy-start.8
  2.5 3.8 %collective-permute-start = (bf16[1040,128]{1,0:T(8,128)(2,1)}, bf16[1040,128]{1,0:T(8,128)(2,1)S(1)}, u32[]{:S(2)}, u32[]{:S(2)}) collective-permute-start(bf16[1040,128]{1,0:T(8,128)(2,1)} %get-tuple-element.36), channel_id=1, source_target_pairs={{0,2},{1,3},{2,4},{3,5},{4,6},{5,7},{6,8},{7,9},{8,10},{9,11},{10,... | collective-permute-start | bytes 798728 | tf_op jit(solution)/shard_map/ppermute | solution.py:39
  6.3 6.4 %collective-permute-start.1 = (bf16[1040,128]{1,0:T(8,128)(2,1)}, bf16[1040,128]{1,0:T(8,128)(2,1)S(1)}, u32[]{:S(2)}, u32[]{:S(2)}) collective-permute-start(bf16[1040,128]{1,0:T(8,128)(2,1)} %get-tuple-element.37), channel_id=1, source_target_pairs={{2,0},{3,1},{4,2},{5,3},{6,4},{7,5},{8,6},{9,7},{10,8},{11,9},{12,... | collective-permute-start | bytes 798728 | tf_op jit(solution)/shard_map/ppermute | solution.py:39
  12.8 1.9 %collective-permute-start.2 = (bf16[1040,128]{1,0:T(8,128)(2,1)}, bf16[1040,128]{1,0:T(8,128)(2,1)S(1)}, u32[]{:S(2)}, u32[]{:S(2)}) collective-permute-start(bf16[1040,128]{1,0:T(8,128)(2,1)} %get-tuple-element.38), channel_id=1, source_target_pairs={{0,1},{1,2},{2,3},{3,4},{4,5},{5,6},{6,7},{7,8},{8,9},{9,10},{10,1... | collective-permute-start | bytes 798728 | tf_op jit(solution)/shard_map/ppermute | solution.py:39
  14.7 7.9 %collective-permute-start.3 = (bf16[1040,128]{1,0:T(8,128)(2,1)}, bf16[1040,128]{1,0:T(8,128)(2,1)S(1)}, u32[]{:S(2)}, u32[]{:S(2)}) collective-permute-start(bf16[1040,128]{1,0:T(8,128)(2,1)} %get-tuple-element.39), channel_id=1, source_target_pairs={{1,0},{2,1},{3,2},{4,3},{5,4},{6,5},{7,6},{8,7},{9,8},{10,9},{11,1... | collective-permute-start | bytes 798728 | tf_op jit(solution)/shard_map/ppermute | solution.py:39
  22.6 0.0 copy-start
  22.6 1.4 %copy-done = bf16[16,3,128,128]{3,2,1,0:T(8,128)(2,1)S(1)} copy-done((bf16[16,3,128,128]{3,2,1,0:T(8,128)(2,1)S(1)}, bf16[16,3,128,128]{3,2,1,0:T(8,128)(2,1)}, u32[]{:S(2)}) %copy-start) | copy-done | bytes 1572888
  24.0 1.0 copy-done.3
  25.0 1.0 copy-done.4
  26.1 0.7 copy-done.7
  26.7 0.7 copy-done.9
  27.4 2.4 %local_slots.1 = (s32[16,4]{1,0:T(8,128)S(1)}, s32[52]{0:T(128)S(1)}, s32[1]{0:T(128)}, bf16[16,128,512]{2,1,0:T(8,128)(2,1)S(1)}, f32[16,128,128]{2,1,0:T(8,128)S(1)}) custom-call(s32[3,16]{1,0:T(4,128)S(1)} %bitcast.2, s32[16]{0:T(128)S(1)} %copy-done.9, bf16[16,128,128]{2,1,0:T(8,128)(2,1)S(1)} %copy-done.4, bf16[16,3,128,128]{3,2,1,0:T(8,128)(2,1)S(1)} %copy-done, ...), custom_call_target="tpu_custom_call" | custom-call | flops 1000000000 | bytes 6000000 | tf_op jit(solution)/shard_map/local_slots/pallas_call | solution.py:121
  29.8 0.0 collective-permute-done.g2
  29.8 0.0 collective-permute-done.1.g3
  29.8 0.0 collective-permute-done.2.g0
  29.8 0.0 collective-permute-done.3.g1
  29.8 0.0 copy-done.6
  29.9 0.0 copy-done.8
  29.9 0.0 copy-done.1
  29.9 7.0 %ghost_slots.1 = (s32[17,4]{1,0:T(8,128)S(1)}, bf16[16,128,512]{2,1,0:T(8,128)(2,1)S(1)}, bf16[528,384]{1,0:T(8,128)(2,1)}, bf16[528,384]{1,0:T(8,128)(2,1)}, bf...) custom-call(s32[4,4]{1,0:T(4,128)S(1)} %copy-done.6, s32[3,16]{1,0:T(4,128)S(1)} %bitcast.3, ...), custom_call_target="tpu_custom_call" | custom-call | tf_op jit(solution)/shard_map/ghost_slots/pallas_call | solution.py:214
  36.9 1.9 %collective-permute-start.4 = (bf16[528,384]{1,0:T(8,128)(2,1)}, bf16[528,384]{1,0:T(8,128)(2,1)}, u32[]{:S(2)}, u32[]{:S(2)}) collective-permute-start(bf16[528,384]{1,0:T(8,128)(2,1)} %get-tuple-element.46), channel_id=1, source_target_pairs={{0,2},{1,3},{2,4},{3,5},{4,6},{5,7},{6,8},{7,9},{8,10},{9,11},{10,... | collective-permute-start | bytes 1216520 | tf_op jit(solution)/shard_map/ppermute | solution.py:39
  38.8 8.1 %collective-permute-start.5 = (bf16[528,384]{1,0:T(8,128)(2,1)}, bf16[528,384]{1,0:T(8,128)(2,1)}, u32[]{:S(2)}, u32[]{:S(2)}) collective-permute-start(bf16[528,384]{1,0:T(8,128)(2,1)} %get-tuple-element.47), channel_id=1, source_target_pairs={{2,0},{3,1},{4,2},{5,3},{6,4},{7,5},{8,6},{9,7},{10,8},{11,9},{12,... | collective-permute-start | bytes 1216520 | tf_op jit(solution)/shard_map/ppermute | solution.py:39
  46.9 1.9 %collective-permute-start.6 = (bf16[528,384]{1,0:T(8,128)(2,1)}, bf16[528,384]{1,0:T(8,128)(2,1)}, u32[]{:S(2)}, u32[]{:S(2)}) collective-permute-start(bf16[528,384]{1,0:T(8,128)(2,1)} %get-tuple-element.48), channel_id=1, source_target_pairs={{0,1},{1,2},{2,3},{3,4},{4,5},{5,6},{6,7},{7,8},{8,9},{9,10},{10,1... | collective-permute-start | bytes 1216520 | tf_op jit(solution)/shard_map/ppermute | solution.py:39
  48.9 7.9 %collective-permute-start.7 = (bf16[528,384]{1,0:T(8,128)(2,1)}, bf16[528,384]{1,0:T(8,128)(2,1)}, u32[]{:S(2)}, u32[]{:S(2)}) collective-permute-start(bf16[528,384]{1,0:T(8,128)(2,1)} %get-tuple-element.49), channel_id=1, source_target_pairs={{1,0},{2,1},{3,2},{4,3},{5,4},{6,5},{7,6},{8,7},{9,8},{10,9},{11,1... | collective-permute-start | bytes 1216520 | tf_op jit(solution)/shard_map/ppermute | solution.py:39
  56.7 0.0 copy-start.2
  56.8 0.0 copy-start.5
  56.8 3.2 %lists.1 = (s32[10,68]{1,0:T(8,128)S(1)}, s32[10]{0:T(128)S(1)}, bf16[65,128,128]{2,1,0:T(8,128)(2,1)S(1)}, bf16[16,128,128]{2,1,0:T(8,128)(2,1)S(1)}) custom-call(s32[17,4]{1,0:T(8,128)S(1)} %get-tuple-element.40.labels, bf16[16,128,512]{2,1,0:T(8,128)(2,1)S(1)} %get-tuple-element.41.slots, bf16[1040,128]{1,0:T(8,128)(2,1)S(1)} %collective-permute-done.g2, ...), custom_call_target="tpu_custom_call" | custom-call | flops 100000000 | bytes 6000000 | tf_op jit(solution)/shard_map/lists/pallas_call | solution.py:285
  60.0 0.0 collective-permute-done.4.g2
  60.0 0.0 collective-permute-done.5.g3
  60.0 0.7 collective-permute-done.6.g0
  60.7 1.8 %collective-permute-done.7.g1 = bf16[528,384]{1,0:T(8,128)(2,1)} collective-permute-done((bf16[528,384]{1,0:T(8,128)(2,1)}, bf16[528,384]{1,0:T(8,128)(2,1)}, u32[]{:S(2)}, u32[]{:S(2)}) %collective-permute-start.7) | collective-permute-done | bytes 405536 | tf_op jit(solution)/shard_map/ppermute | solution.py:39
  62.5 0.0 copy-done.2
  62.5 12.7 %far_rows.1 = (bf16[16,128,2304]{2,1,0:T(8,128)(2,1)}, bf16[2,128,2560]{2,1,0:T(8,128)(2,1)S(1)}, f32[2,128,2560]{2,1,0:T(8,128)S(1)}, bf16[2,128,2304]{2,1,0:T(8,128)(2,1)S(1)}) custom-call(s32[1]{0:T(128)} %bitcast.parity, s32[3,16]{1,0:T(4,128)S(1)} %bitcast.4, s32[17,4]{1,0:T(8,128)S(1)} %get-tuple-element.40.labels, ...), custom_call_target="tpu_custom_call" | custom-call | flops 4000000000 | bytes 20000000 | tf_op jit(solution)/shard_map/far_rows/pallas_call | solution.py:416
  75.2 0.1 collective-permute-start.8
  75.3 8.4 %collective-permute-start.10 = (bf16[2,128,2304]{2,1,0:T(8,128)(2,1)S(1)}, bf16[2,128,2304]{2,1,0:T(8,128)(2,1)S(1)}, u32[]{:S(2)}, u32[]{:S(2)}) collective-permute-start(bf16[2,128,2304]{2,1,0:T(8,128)(2,1)S(1)} %get-tuple-element.56), channel_id=1, source_target_pairs={{1,3},{2,0},{3,5},{4,2},{5,7},{6,4},{7,9},{8,6},{9,11},{10,8},{11,... | collective-permute-start | bytes 3538952 | tf_op jit(solution)/shard_map/ppermute | solution.py:552
  83.7 0.0 collective-permute-done.8
  83.7 0.4 add_convert_fusion
  84.0 1.9 %collective-permute-start.11 = (bf16[2,128,2560]{2,1,0:T(8,128)(2,1)S(1)}, bf16[2,128,2560]{2,1,0:T(8,128)(2,1)S(1)}, u32[]{:S(2)}, u32[]{:S(2)}) collective-permute-start(bf16[2,128,2560]{2,1,0:T(8,128)(2,1)S(1)} %add_convert_fusion), channel_id=1, source_target_pairs={{0,2},{2,4},{3,1},{4,6},{5,3},{6,8},{7,5},{8,10},{9,7},{10,12},{11... | collective-permute-start | bytes 3932168 | tf_op jit(solution)/shard_map/ppermute | solution.py:552
  86.0 3.7 %copy-done.10 = bf16[16,128,2304]{2,1,0:T(8,128)(2,1)S(1)} copy-done((bf16[16,128,2304]{2,1,0:T(8,128)(2,1)S(1)}, bf16[16,128,2304]{2,1,0:T(8,128)(2,1)}, u32[]{:S(2)}) %copy-start.10) | copy-done | bytes 9437208
  89.7 7.1 %near_rows.1 = (f32[2,128,2304]{2,1,0:T(8,128)S(1)}, bf16[2,128,2304]{2,1,0:T(8,128)(2,1)S(1)}) custom-call(s32[1]{0:T(128)} %bitcast.parity, s32[10,68]{1,0:T(8,128)S(1)} %get-tuple-element.42.lists, s32[10]{0:T(128)S(1)} %get-tuple-element.43.counts, bf16[65,128,128]{2,1,0:T(8,128)(2,1)S(1)} %get-tuple-element.44.blocks, bf16[16,128,2304]{2,1,0:T(8,128)(2,1)S(1)} %copy-done.10), custom_call_target="tpu_custom_call" | custom-call | flops 4000000000 | bytes 20000000 | tf_op jit(solution)/shard_map/near_rows/pallas_call | solution.py:464
  96.8 1.9 %collective-permute-start.9 = (bf16[2,128,2304]{2,1,0:T(8,128)(2,1)S(1)}, bf16[2,128,2304]{2,1,0:T(8,128)(2,1)S(1)}, u32[]{:S(2)}, u32[]{:S(2)}) collective-permute-start(bf16[2,128,2304]{2,1,0:T(8,128)(2,1)S(1)} %get-tuple-element.55), channel_id=1, source_target_pairs={{0,1},{1,0},{2,3},{3,2},{4,5},{5,4},{6,7},{7,6},{8,9},{9,8},{10,11... | collective-permute-start | bytes 3538952 | tf_op jit(solution)/shard_map/ppermute | solution.py:552
  98.6 8.8 %collective-permute-done.10.direct = bf16[2,128,2304]{2,1,0:T(8,128)(2,1)S(1)} collective-permute-done((bf16[2,128,2304]{2,1,0:T(8,128)(2,1)S(1)}, bf16[2,128,2304]{2,1,0:T(8,128)(2,1)S(1)}, u32[]{:S(2)}, u32[]{:S(2)}) %collective-permute-start.10) | collective-permute-done | bytes 1179680 | tf_op jit(solution)/shard_map/ppermute | solution.py:552
  107.5 0.0 collective-permute-done.9.mate
  107.5 2.7 %add_near.1.band = f32[2,128,3328]{2,1,0:T(8,128)} custom-call(s32[1]{0:T(128)} %bitcast.parity, f32[2,128,2304]{2,1,0:T(8,128)S(1)} %get-tuple-element.54.own, bf16[2,128,2304]{2,1,0:T(8,128)(2,1)S(1)} %collective-permute-done.9.mate, bf16[2,128,2304]{2,1,0:T(8,128)(2,1)S(1)} %collective-permute-done.10.direct), custom_call_target="tpu_custom_call" | custom-call | flops 1000000 | bytes 9000000 | tf_op jit(solution)/shard_map/add_near/pallas_call | solution.py:495
  110.2 1.0 collective-permute-done.11.pair
  111.2 3.8 %add_pair.1 = f32[2,128,3328]{2,1,0:T(8,128)} custom-call(s32[1]{0:T(128)} %bitcast.parity, f32[2,128,3328]{2,1,0:T(8,128)} %add_near.1.band, bf16[2,128,2560]{2,1,0:T(8,128)(2,1)S(1)} %collective-permute-done.11.pair), custom_call_target="tpu_custom_call", output_to_operand_aliasing={{}: (1, {})} | custom-call | tf_op jit(solution)/shard_map/add_pair/pallas_call | solution.py:533
  (7 shorter events, 0.0 us)
Async XLA Ops:
  2.5 27.4 %copy-start.6 = (s32[4,4]{1,0:T(4,128)S(1)}, s32[4,4]{1,0:T(4,128)}, u32[]{:S(2)}) copy-start(s32[4,4]{1,0:T(4,128)} %send_rows.3) | copy-start | bytes 196
  2.5 27.4 %copy-start.8 = (s32[16,3]{0,1:T(4,128)S(1)}, s32[16,3]{0,1:T(4,128)}, u32[]{:S(2)}) copy-start(s32[16,3]{0,1:T(4,128)} %param.8) | copy-start | bytes 580
  2.5 27.3 %collective-permute-start = (bf16[1040,128]{1,0:T(8,128)(2,1)}, bf16[1040,128]{1,0:T(8,128)(2,1)S(1)}, u32[]{:S(2)}, u32[]{:S(2)}) collective-permute-start(bf16[1040,128]{1,0:T(8,128)(2,1)} %get-tuple-element.36), channel_id=1, source_target_pairs={{0,2},{1,3},{2,4},{3,5},{4,6},{5,7},{6,8},{7,9},{8,10},{9,11},{10,... | collective-permute-start | bytes 798728 | tf_op jit(solution)/shard_map/ppermute | solution.py:39
  6.3 23.5 %collective-permute-start.1 = (bf16[1040,128]{1,0:T(8,128)(2,1)}, bf16[1040,128]{1,0:T(8,128)(2,1)S(1)}, u32[]{:S(2)}, u32[]{:S(2)}) collective-permute-start(bf16[1040,128]{1,0:T(8,128)(2,1)} %get-tuple-element.37), channel_id=1, source_target_pairs={{2,0},{3,1},{4,2},{5,3},{6,4},{7,5},{8,6},{9,7},{10,8},{11,9},{12,... | collective-permute-start | bytes 798728 | tf_op jit(solution)/shard_map/ppermute | solution.py:39
  12.8 17.1 %collective-permute-start.2 = (bf16[1040,128]{1,0:T(8,128)(2,1)}, bf16[1040,128]{1,0:T(8,128)(2,1)S(1)}, u32[]{:S(2)}, u32[]{:S(2)}) collective-permute-start(bf16[1040,128]{1,0:T(8,128)(2,1)} %get-tuple-element.38), channel_id=1, source_target_pairs={{0,1},{1,2},{2,3},{3,4},{4,5},{5,6},{6,7},{7,8},{8,9},{9,10},{10,1... | collective-permute-start | bytes 798728 | tf_op jit(solution)/shard_map/ppermute | solution.py:39
  14.7 15.1 %collective-permute-start.3 = (bf16[1040,128]{1,0:T(8,128)(2,1)}, bf16[1040,128]{1,0:T(8,128)(2,1)S(1)}, u32[]{:S(2)}, u32[]{:S(2)}) collective-permute-start(bf16[1040,128]{1,0:T(8,128)(2,1)} %get-tuple-element.39), channel_id=1, source_target_pairs={{1,0},{2,1},{3,2},{4,3},{5,4},{6,5},{7,6},{8,7},{9,8},{10,9},{11,1... | collective-permute-start | bytes 798728 | tf_op jit(solution)/shard_map/ppermute | solution.py:39
  22.6 1.4 %copy-start = (bf16[16,3,128,128]{3,2,1,0:T(8,128)(2,1)S(1)}, bf16[16,3,128,128]{3,2,1,0:T(8,128)(2,1)}, u32[]{:S(2)}) copy-start(bf16[16,3,128,128]{3,2,1,0:T(8,128)(2,1)} %off.5) | copy-start | bytes 4718596
  24.0 1.0 copy-start.3
  25.0 1.0 copy-start.4
  26.1 0.7 copy-start.7
  26.7 0.7 copy-start.9
  27.4 2.5 %copy-start.1 = (bf16[16,3,128,128]{3,2,1,0:T(8,128)(2,1)S(1)}, bf16[16,3,128,128]{3,2,1,0:T(8,128)(2,1)}, u32[]{:S(2)}) copy-start(bf16[16,3,128,128]{3,2,1,0:T(8,128)(2,1)} %off.5) | copy-start | bytes 4718596
  36.9 23.2 %collective-permute-start.4 = (bf16[528,384]{1,0:T(8,128)(2,1)}, bf16[528,384]{1,0:T(8,128)(2,1)}, u32[]{:S(2)}, u32[]{:S(2)}) collective-permute-start(bf16[528,384]{1,0:T(8,128)(2,1)} %get-tuple-element.46), channel_id=1, source_target_pairs={{0,2},{1,3},{2,4},{3,5},{4,6},{5,7},{6,8},{7,9},{8,10},{9,11},{10,... | collective-permute-start | bytes 1216520 | tf_op jit(solution)/shard_map/ppermute | solution.py:39
  38.8 21.2 %collective-permute-start.5 = (bf16[528,384]{1,0:T(8,128)(2,1)}, bf16[528,384]{1,0:T(8,128)(2,1)}, u32[]{:S(2)}, u32[]{:S(2)}) collective-permute-start(bf16[528,384]{1,0:T(8,128)(2,1)} %get-tuple-element.47), channel_id=1, source_target_pairs={{2,0},{3,1},{4,2},{5,3},{6,4},{7,5},{8,6},{9,7},{10,8},{11,9},{12,... | collective-permute-start | bytes 1216520 | tf_op jit(solution)/shard_map/ppermute | solution.py:39
  46.9 13.8 %collective-permute-start.6 = (bf16[528,384]{1,0:T(8,128)(2,1)}, bf16[528,384]{1,0:T(8,128)(2,1)}, u32[]{:S(2)}, u32[]{:S(2)}) collective-permute-start(bf16[528,384]{1,0:T(8,128)(2,1)} %get-tuple-element.48), channel_id=1, source_target_pairs={{0,1},{1,2},{2,3},{3,4},{4,5},{5,6},{6,7},{7,8},{8,9},{9,10},{10,1... | collective-permute-start | bytes 1216520 | tf_op jit(solution)/shard_map/ppermute | solution.py:39
  48.9 13.6 %collective-permute-start.7 = (bf16[528,384]{1,0:T(8,128)(2,1)}, bf16[528,384]{1,0:T(8,128)(2,1)}, u32[]{:S(2)}, u32[]{:S(2)}) collective-permute-start(bf16[528,384]{1,0:T(8,128)(2,1)} %get-tuple-element.49), channel_id=1, source_target_pairs={{1,0},{2,1},{3,2},{4,3},{5,4},{6,5},{7,6},{8,7},{9,8},{10,9},{11,1... | collective-permute-start | bytes 1216520 | tf_op jit(solution)/shard_map/ppermute | solution.py:39
  56.7 5.7 %copy-start.2 = (bf16[16,3,128,128]{3,2,1,0:T(8,128)(2,1)S(1)}, bf16[16,3,128,128]{3,2,1,0:T(8,128)(2,1)}, u32[]{:S(2)}) copy-start(bf16[16,3,128,128]{3,2,1,0:T(8,128)(2,1)} %off.5) | copy-start | bytes 4718596
  56.8 5.7 %copy-start.5 = (bf16[16,128,128]{2,1,0:T(8,128)(2,1)S(1)}, bf16[16,128,128]{2,1,0:T(8,128)(2,1)}, u32[]{:S(2)}) copy-start(bf16[16,128,128]{2,1,0:T(8,128)(2,1)} %diag.5) | copy-start | bytes 1572868
  75.2 8.5 %collective-permute-start.8 = (bf16[2,128,2560]{2,1,0:T(8,128)(2,1)S(1)}, bf16[2,128,2560]{2,1,0:T(8,128)(2,1)S(1)}, u32[]{:S(2)}, u32[]{:S(2)}) collective-permute-start(bf16[2,128,2560]{2,1,0:T(8,128)(2,1)S(1)} %get-tuple-element.52), channel_id=1, source_target_pairs={{0,1},{1,0},{2,3},{3,2},{4,5},{5,4},{6,7},{7,6},{8,9},{9,8},{10,11... | collective-permute-start | bytes 3932168 | tf_op jit(solution)/shard_map/ppermute | solution.py:552
  75.3 32.2 %collective-permute-start.10 = (bf16[2,128,2304]{2,1,0:T(8,128)(2,1)S(1)}, bf16[2,128,2304]{2,1,0:T(8,128)(2,1)S(1)}, u32[]{:S(2)}, u32[]{:S(2)}) collective-permute-start(bf16[2,128,2304]{2,1,0:T(8,128)(2,1)S(1)} %get-tuple-element.56), channel_id=1, source_target_pairs={{1,3},{2,0},{3,5},{4,2},{5,7},{6,4},{7,9},{8,6},{9,11},{10,8},{11,... | collective-permute-start | bytes 3538952 | tf_op jit(solution)/shard_map/ppermute | solution.py:552
  84.0 27.2 %collective-permute-start.11 = (bf16[2,128,2560]{2,1,0:T(8,128)(2,1)S(1)}, bf16[2,128,2560]{2,1,0:T(8,128)(2,1)S(1)}, u32[]{:S(2)}, u32[]{:S(2)}) collective-permute-start(bf16[2,128,2560]{2,1,0:T(8,128)(2,1)S(1)} %add_convert_fusion), channel_id=1, source_target_pairs={{0,2},{2,4},{3,1},{4,6},{5,3},{6,8},{7,5},{8,10},{9,7},{10,12},{11... | collective-permute-start | bytes 3932168 | tf_op jit(solution)/shard_map/ppermute | solution.py:552
  86.0 3.7 %copy-start.10 = (bf16[16,128,2304]{2,1,0:T(8,128)(2,1)S(1)}, bf16[16,128,2304]{2,1,0:T(8,128)(2,1)}, u32[]{:S(2)}) copy-start(bf16[16,128,2304]{2,1,0:T(8,128)(2,1)} %get-tuple-element.53.applied) | copy-start | bytes 28311556
  96.8 10.7 %collective-permute-start.9 = (bf16[2,128,2304]{2,1,0:T(8,128)(2,1)S(1)}, bf16[2,128,2304]{2,1,0:T(8,128)(2,1)S(1)}, u32[]{:S(2)}, u32[]{:S(2)}) collective-permute-start(bf16[2,128,2304]{2,1,0:T(8,128)(2,1)S(1)} %get-tuple-element.55), channel_id=1, source_target_pairs={{0,1},{1,0},{2,3},{3,2},{4,5},{5,4},{6,7},{7,6},{8,9},{9,8},{10,11... | collective-permute-start | bytes 3538952 | tf_op jit(solution)/shard_map/ppermute | solution.py:552

commit v4 on v3

--- a/solution.py
+++ b/solution.py
@@ -6,8 +6,7 @@
 from jax.sharding import PartitionSpec as P
 
 AXES = ("bulk", "coarse")
-OFFSETS = (1, -1, 2, -2)
-START_ORDER = (2, 3, 0, 1)
+STEPS = ((-2, 2), (2, -2), (-1, 1), (1, -1))
 BS = 128
 NB = 16
 NG = 4
@@ -33,10 +32,17 @@
     return pl.BlockSpec(memory_space=space)
 
 
-def shift(value, steps):
-    count = lax.axis_size(AXES)
-    first, last = max(0, -steps), min(count, count - steps)
-    return lax.ppermute(value, AXES, [(s, s + steps) for s in range(first, last)])
+def sent_to(odd):
+    return (3 - odd, 2 + odd, 1 - odd, odd)
+
+
+def came_from(odd):
+    return (
+        (3 - odd, 4 * odd - 2),
+        (2 + odd, 2 - 4 * odd),
+        (odd, 1 - 2 * odd),
+        (1 - odd, 2 * odd - 1),
+    )
 
 
 def label_rows(values, width):
@@ -47,42 +53,44 @@
     return total.astype(F32).astype(BF)
 
 
-def pack_kernel(send_rows, aggregate, tent, diag, *refs):
+def pack_kernel(parity, send_rows, aggregate, tent, diag, *refs):
     outs, labels, sem = refs[:4], refs[4], refs[5]
+    targets = sent_to(parity[0])
     copies = []
-    for n in START_ORDER:
+    for at, n in enumerate(targets):
         for g in range(NG):
+            row = send_rows[n, g]
             copies.append(
-                pltpu.make_async_copy(
-                    tent.at[send_rows[n, g]], outs[n].at[pl.ds(g * BS, BS)], sem.at[n, g]
-                )
+                pltpu.make_async_copy(tent.at[row], outs[at].at[pl.ds(g * BS, BS)], sem.at[at, g])
             )
             copies.append(
                 pltpu.make_async_copy(
-                    diag.at[send_rows[n, g]], outs[n].at[pl.ds((NG + g) * BS, BS)], sem.at[n, NG + g]
+                    diag.at[row], outs[at].at[pl.ds((NG + g) * BS, BS)], sem.at[at, NG + g]
                 )
             )
     for copy in copies:
         copy.start()
-    for n in START_ORDER:
-        labels[n] = label_rows([aggregate[send_rows[n, g]] for g in range(NG)], BS)
-        copy = pltpu.make_async_copy(labels.at[n], outs[n].at[pl.ds(2 * NG * BS, EXTRA)], sem.at[n, 2 * NG])
+    for at, n in enumerate(targets):
+        labels[at] = label_rows([aggregate[send_rows[n, g]] for g in range(NG)], BS)
+        copy = pltpu.make_async_copy(
+            labels.at[at], outs[at].at[pl.ds(2 * NG * BS, EXTRA)], sem.at[at, 2 * NG]
+        )
         copy.start()
         copies.append(copy)
     for copy in copies:
         copy.wait()
 
 
-def pack(send_rows, aggregate, tent, diag):
+def pack(parity, send_rows, aggregate, tent, diag):
     shape = jax.ShapeDtypeStruct((2 * NG * BS + EXTRA, BS), BF)
     return pl.pallas_call(
         pack_kernel,
         out_shape=[shape] * 4,
-        in_specs=[spec(SMEM), spec(SMEM), spec(pltpu.VMEM), spec(pltpu.VMEM)],
+        in_specs=[spec(SMEM)] * 3 + [spec(pltpu.VMEM)] * 2,
         out_specs=[spec(ANY)] * 4,
         scratch_shapes=[pltpu.VMEM((4, EXTRA, BS), BF), pltpu.SemaphoreType.DMA((4, 2 * NG + 1))],
         name="pack",
-    )(send_rows, aggregate, tent, diag)
+    )(parity, send_rows, aggregate, tent, diag)
 
 
 def first_slot(eye, block, own):
@@ -136,43 +144,28 @@
 
 
 def ghost_slots_kernel(
-    send_rows, off_columns, local_labels, ghost_list, ghost_count, off, slots_in, scales, g2, g3, g0, g1,
-    labels, slots, s2, s3, s0, s1,
-    table, labels_in, labels_out, label_smem, slot_buf, off_buf, scale_buf, sem_in, sem_lab, sem_out, sem_big,
+    parity, send_rows, off_columns, local_labels, ghost_list, ghost_count, off, slots_in, scales,
+    g0, g1, g2, g3,
+    labels, slots, s0, s1, s2, s3,
+    table, labels_in, label_smem, sem,
 ):
     ghosts, sends = (g0, g1, g2, g3), (s0, s1, s2, s3)
-    big = [
-        pltpu.make_async_copy(scales, scale_buf, sem_big.at[0]),
-        pltpu.make_async_copy(off, off_buf, sem_big.at[1]),
-        pltpu.make_async_copy(slots_in, slot_buf.at[pl.ds(0, NB)], sem_big.at[2]),
-    ]
-    copies = []
-    for n in range(4):
+    copy = pltpu.make_async_copy(slots_in, slots.at[pl.ds(0, NB)], sem.at[0])
+    copy.start()
+    arrivals = came_from(parity[0])
+    for at, (n, offset) in enumerate(arrivals):
+        row = ghosts[at][2 * NG * BS :, :].astype(F32).astype(jnp.int32)[:8]
+        labels_in[n] = row + (8 - 2 * offset)
+    to_smem = pltpu.make_async_copy(labels_in, label_smem, sem.at[1])
+    to_smem.start()
+    for at, (n, _) in enumerate(arrivals):
         for g in range(NG):
-            copies.append(
-                pltpu.make_async_copy(
-                    ghosts[n].at[pl.ds(g * BS, BS)], table.at[n * NG + g], sem_in.at[n * NG + g]
-                )
-            )
-    lab = [
-        pltpu.make_async_copy(ghosts[n].at[pl.ds(2 * NG * BS, EXTRA)], labels_out.at[n, :, pl.ds(0, BS)], sem_lab.at[n])
-        for n in range(4)
-    ]
-    for copy in lab + copies + big:
-        copy.start()
+            table[n * NG + g] = ghosts[at][g * BS : (g + 1) * BS, :]
     for i in range(NB):
         for k in range(4):
             labels[i, k] = local_labels[i, k]
-    for copy in lab:
-        copy.wait()
-    for n in range(4):
-        base = 8 - 2 * OFFSETS[n]
-        labels_in[n] = labels_out[n, :, pl.ds(0, BS)].astype(F32).astype(jnp.int32)[:8] + base
-    to_smem = pltpu.make_async_copy(labels_in, label_smem, sem_lab.at[0])
-    to_smem.start()
-    for copy in copies + big:
-        copy.wait()
     to_smem.wait()
+    copy.wait()
 
     def group(q, carry):
         for u in range(GROUP):
@@ -180,67 +173,44 @@
             i, k = lax.div(entry, 4), lax.rem(entry, 4)
             row = jnp.minimum(i, NB - 1)
             ghost = jnp.clip(off_columns[k - 1, row] - NB, 0, 4 * NG - 1)
-            part = jnp.dot(off_buf[row, k - 1], table[ghost], preferred_element_type=F32)
-            part = -scale_buf[row] * part
-            slot_buf[i, :, pl.ds(pl.multiple_of(k * BS, BS), BS)] = part.astype(BF)
+            part = jnp.dot(off[row, k - 1], table[ghost], preferred_element_type=F32)
+            part = -scales[row] * part
+            slots[i, :, pl.ds(pl.multiple_of(k * BS, BS), BS)] = part.astype(BF)
             labels[i, k] = label_smem[lax.div(ghost, NG), 0, lax.rem(ghost, NG)]
         return carry
 
     lax.fori_loop(0, lax.div(ghost_count[0] + GROUP - 1, GROUP), group, 0)
 
-    outs = []
-    for n in START_ORDER:
+    for at, n in enumerate(sent_to(parity[0])):
         for g in range(NG):
-            outs.append(
-                pltpu.make_async_copy(
-                    slot_buf.at[send_rows[n, g], :, pl.ds(BS, SENDW)], sends[n].at[pl.ds(g * BS, BS)], sem_out.at[n * NG + g]
-                )
-            )
-    outs.append(pltpu.make_async_copy(slot_buf.at[pl.ds(0, NB)], slots, sem_big.at[0]))
-    for copy in outs:
-        copy.start()
-    for n in START_ORDER:
+            sends[at][g * BS : (g + 1) * BS, :] = slots[send_rows[n, g], :, BS:]
         values = [labels[send_rows[n, g], k] for g in range(NG) for k in range(4)]
-        labels_out[n] = label_rows(values, SENDW)
-        copy = pltpu.make_async_copy(labels_out.at[n], sends[n].at[pl.ds(NG * BS, EXTRA)], sem_lab.at[n])
-        copy.start()
-        outs.append(copy)
-    for copy in outs:
-        copy.wait()
-
-
-def ghost_slots(send_rows, off_columns, local_labels, ghost_list, ghost_count, off, slots_in, scales, ghosts):
+        sends[at][NG * BS :, :] = label_rows(values, SENDW)
+
+
+def ghost_slots(parity, send_rows, off_columns, local_labels, ghost_list, ghost_count, off, slots_in, scales, ghosts):
     send = jax.ShapeDtypeStruct((NG * BS + EXTRA, SENDW), BF)
-    labels, slots, *sends = pl.pallas_call(
+    return pl.pallas_call(
         ghost_slots_kernel,
         out_shape=[
             jax.ShapeDtypeStruct((NB + 1, 4), jnp.int32),
-            jax.ShapeDtypeStruct((NB, BS, SLOTW), BF),
+            jax.ShapeDtypeStruct((NB + 1, BS, SLOTW), BF),
         ]
         + [send] * 4,
-        in_specs=[spec(SMEM)] * 5 + [spec(ANY)] * 7,
-        out_specs=[spec(SMEM)] + [spec(ANY)] * 5,
+        in_specs=[spec(SMEM)] * 6 + [spec(pltpu.VMEM)] * 7,
+        out_specs=[spec(SMEM)] + [spec(pltpu.VMEM)] * 5,
         scratch_shapes=[
             pltpu.VMEM((4 * NG, BS, BS), BF),
             pltpu.VMEM((4, 8, BS), jnp.int32),
-            pltpu.VMEM((4, EXTRA, SENDW), BF),
             pltpu.SMEM((4, 8, BS), jnp.int32),
-            pltpu.VMEM((NB + 1, BS, SLOTW), BF),
-            pltpu.VMEM((NB, 3, BS, BS), BF),
-            pltpu.VMEM((NB, BS, BS), F32),
-            pltpu.SemaphoreType.DMA((4 * NG,)),
-            pltpu.SemaphoreType.DMA((4,)),
-            pltpu.SemaphoreType.DMA((4 * NG,)),
-            pltpu.SemaphoreType.DMA((3,)),
+            pltpu.SemaphoreType.DMA((2,)),
         ],
-        compiler_params=pltpu.CompilerParams(vmem_limit_bytes=12 * 1024 * 1024),
+        compiler_params=pltpu.CompilerParams(vmem_limit_bytes=16 * 1024 * 1024),
         name="ghost_slots",
-    )(send_rows, off_columns, local_labels, ghost_list, ghost_count, off, slots_in, scales,
-      *[ghosts[n] for n in START_ORDER])
-    return labels, slots, [sends[START_ORDER.index(n)] for n in range(4)]
-
-
-def lists_kernel(labels, slots, g2, g3, g0, g1, lists, counts, blocks, first_slots, ghost_buf, sem):
+    )(parity, send_rows, off_columns, local_labels, ghost_list, ghost_count, off, slots_in, scales, *ghosts)
+
+
+def lists_kernel(parity, labels, slots, g0, g1, g2, g3, lists, counts, blocks, first_slots, ghost_buf, sem):
     ghosts = (g0, g1, g2, g3)
     copies = [
         pltpu.make_async_copy(ghosts[n].at[pl.ds(0, 2 * NG * BS)], ghost_buf.at[n], sem.at[n])
@@ -271,17 +241,14 @@
         copy.wait()
     eye = lax.broadcasted_iota(jnp.int32, (BS, BS), 0) == lax.broadcasted_iota(jnp.int32, (BS, BS), 1)
 
-    def ghost(n, carry):
+    for at, (n, _) in enumerate(came_from(parity[0])):
         for g in range(NG):
             first_slots[n * NG + g] = first_slot(
-                eye, ghost_buf[n, (NG + g) * BS : (NG + g + 1) * BS], ghost_buf[n, g * BS : (g + 1) * BS]
+                eye, ghost_buf[at, (NG + g) * BS : (NG + g + 1) * BS], ghost_buf[at, g * BS : (g + 1) * BS]
             )[0]
-        return carry
-
-    lax.fori_loop(0, 4, ghost, 0)
-
-
-def make_lists(labels, slots, ghosts):
+
+
+def make_lists(parity, labels, slots, ghosts):
     return pl.pallas_call(
         lists_kernel,
         out_shape=[
@@ -290,13 +257,13 @@
             jax.ShapeDtypeStruct((4 * NB + 1, BS, BS), BF),
             jax.ShapeDtypeStruct((4 * NG, BS, BS), BF),
         ],
-        in_specs=[spec(SMEM), spec(pltpu.VMEM)] + [spec(ANY)] * 4,
+        in_specs=[spec(SMEM)] * 2 + [spec(pltpu.VMEM)] + [spec(ANY)] * 4,
         out_specs=[spec(SMEM)] * 2 + [spec(pltpu.VMEM)] * 2,
         scratch_shapes=[pltpu.VMEM((4, 2 * NG * BS, BS), BF), pltpu.SemaphoreType.DMA((4,))],
         compiler_params=pltpu.CompilerParams(vmem_limit_bytes=12 * 1024 * 1024),
         cost_estimate=pl.CostEstimate(flops=10**8, bytes_accessed=6 * 10**6, transcendentals=0),
         name="lists",
-    )(labels, slots, *[ghosts[n] for n in START_ORDER])
+    )(parity, labels, slots, *ghosts)
 
 
 def coarse_rows(t, at, lists, counts, blocks, applied, coarse):
@@ -315,23 +282,24 @@
 
 
 def far_kernel(
-    parity, off_columns, labels, lists, counts, diag, off, slots, blocks, first_slots, g2, g3, g0, g1,
+    parity, off_columns, labels, lists, counts, diag, off, slots, blocks, first_slots, g0, g1, g2, g3,
     applied_out, relay_out, relayed_out, direct_out,
     table, labels_in, labels_vmem, label_smem, total_a, total_b, applied, coarse, relay, relayed, direct,
     sem_in, sem_lab, sem_out, sem_piece,
 ):
     ghosts = (g0, g1, g2, g3)
     copies = [
-        pltpu.make_async_copy(slots, table.at[pl.ds(0, NB)], sem_in.at[0]),
+        pltpu.make_async_copy(slots.at[pl.ds(0, NB)], table.at[pl.ds(0, NB)], sem_in.at[0]),
         pltpu.make_async_copy(first_slots, table.at[pl.ds(NB, 4 * NG), :, pl.ds(0, BS)], sem_in.at[1]),
     ]
-    for n in range(4):
+    arrivals = came_from(parity[0])
+    for at, (n, _) in enumerate(arrivals):
         for g in range(NG):
             copies.append(
                 pltpu.make_async_copy(
-                    ghosts[n].at[pl.ds(g * BS, BS)],
+                    ghosts[at].at[pl.ds(g * BS, BS)],
                     table.at[NB + n * NG + g, :, pl.ds(BS, SENDW)],
-                    sem_in.at[2 + n * NG + g],
+                    sem_in.at[2 + at * NG + g],
                 )
             )
     lab = [
@@ -348,8 +316,8 @@
     relayed[:, :, rest] = jnp.zeros((2, BS, 2 * BS), F32)
     for copy in lab:
         copy.wait()
-    for n in range(4):
-        labels_vmem[n] = labels_in[n].astype(F32).astype(jnp.int32)[:8] - 2 * OFFSETS[n]
+    for at, (n, offset) in enumerate(arrivals):
+        labels_vmem[n] = labels_in[at].astype(F32).astype(jnp.int32)[:8] - 2 * offset
     to_smem = pltpu.make_async_copy(labels_vmem, label_smem, sem_lab.at[0])
     to_smem.start()
     for copy in copies:
@@ -443,8 +411,7 @@
         compiler_params=pltpu.CompilerParams(vmem_limit_bytes=34 * 1024 * 1024),
         cost_estimate=pl.CostEstimate(flops=4 * 10**9, bytes_accessed=20 * 10**6, transcendentals=0),
         name="far_rows",
-    )(parity, off_columns, labels, lists, counts, diag, off, slots, blocks, first_slots,
-      *[ghosts[n] for n in START_ORDER])
+    )(parity, off_columns, labels, lists, counts, diag, off, slots, blocks, first_slots, *ghosts)
 
 
 def near_kernel(parity, lists, counts, blocks, applied, own, mate, coarse):
@@ -504,27 +471,17 @@
     )(parity, own, mate, direct)
 
 
-def add_pair_kernel(parity, band, pair, out, band_buf, pair_buf, sem):
+def add_pair_kernel(parity, band, pair, out, buf, sem):
     rows = BS // 4
     cols = pl.ds(pl.multiple_of(parity[0] * (6 * BS), BS), CHIPWIDE)
-    parts = [(b, pl.ds(r * rows, rows)) for b in range(2) for r in range(4)]
-    loads, stores = [], []
-    for at, (b, r) in enumerate(parts):
-        loads.append(
-            (
-                pltpu.make_async_copy(pair.at[b, r], pair_buf.at[b, r], sem.at[0, at]),
-                pltpu.make_async_copy(band.at[b, r, cols], band_buf.at[b, r], sem.at[1, at]),
-            )
-        )
-        stores.append(pltpu.make_async_copy(band_buf.at[b, r], out.at[b, r, cols], sem.at[2, at]))
-    for pair_of in loads:
-        for copy in pair_of:
-            copy.start()
-    for at, (b, r) in enumerate(parts):
-        for copy in loads[at]:
-            copy.wait()
-        band_buf[b, r] = band_buf[b, r] + pair_buf[b, r].astype(F32)
-        stores[at].start()
+    stores = []
+    for b in range(2):
+        for r in range(4):
+            part = pl.ds(r * rows, rows)
+            buf[b, part] = band[b, part]
+            buf[b, part, cols] = band[b, part, cols] + pair[b, part].astype(F32)
+            stores.append(pltpu.make_async_copy(buf.at[b, part], out.at[b, part], sem.at[b, r]))
+            stores[-1].start()
     for copy in stores:
         copy.wait()
 
@@ -533,15 +490,10 @@
     return pl.pallas_call(
         add_pair_kernel,
         out_shape=jax.ShapeDtypeStruct((2, BS, BANDWIDE), F32),
-        in_specs=[spec(SMEM), spec(ANY), spec(ANY)],
+        in_specs=[spec(SMEM)] + [spec(pltpu.VMEM)] * 2,
         out_specs=spec(ANY),
-        input_output_aliases={1: 0},
-        scratch_shapes=[
-            pltpu.VMEM((2, BS, CHIPWIDE), F32),
-            pltpu.VMEM((2, BS, CHIPWIDE), BF),
-            pltpu.SemaphoreType.DMA((3, 8)),
-        ],
-        compiler_params=pltpu.CompilerParams(vmem_limit_bytes=8 * 1024 * 1024),
+        scratch_shapes=[pltpu.VMEM((2, BS, BANDWIDE), F32), pltpu.SemaphoreType.DMA((2, 4))],
+        compiler_params=pltpu.CompilerParams(vmem_limit_bytes=12 * 1024 * 1024),
         name="add_pair",
     )(parity, band, pair)
 
@@ -553,24 +505,21 @@
 
 
 def exchange(sends):
-    arrived = [None] * 4
-    for n in START_ORDER:
-        arrived[n] = shift(sends[n], OFFSETS[n])
-    return arrived
+    return [permute_by(value, *steps) for value, steps in zip(sends, STEPS)]
 
 
 def local(diag_blocks, off_blocks, off_columns, tentative, aggregate, send_rows):
     off_columns = off_columns.T
     odd = lax.rem(lax.axis_index(AXES), 2)
     parity = odd.reshape(1)
-    ghosts = exchange(pack(send_rows, aggregate, tentative, diag_blocks))
+    ghosts = exchange(pack(parity, send_rows, aggregate, tentative, diag_blocks))
     labels, ghost_list, ghost_count, slots, scales = local_slots(
         off_columns, aggregate, diag_blocks, off_blocks, tentative
     )
-    labels, slots, sends = ghost_slots(
-        send_rows, off_columns, labels, ghost_list, ghost_count, off_blocks, slots, scales, ghosts
+    labels, slots, *sends = ghost_slots(
+        parity, send_rows, off_columns, labels, ghost_list, ghost_count, off_blocks, slots, scales, ghosts
     )
-    lists, counts, blocks, first_slots = make_lists(labels, slots, ghosts)
+    lists, counts, blocks, first_slots = make_lists(parity, labels, slots, ghosts)
     ghosts = exchange(sends)
     applied, relay, relayed, direct = make_far(
         parity, off_columns, labels, lists, counts, diag_blocks, off_blocks, slots, blocks, first_slots, ghosts

time: 117 us -> 105 us (0.90)
  starting transfers between devices: 52.1 us -> 32.9 us
  waiting for transfers between devices: 12.3 us -> 26.2 us
  Pallas kernels: 41.4 us -> 35.5 us
    ppermute x8 -> x0, starting transfers between devices: 39.9 us -> none  [shift(): lax.ppermute(value, AXES, [(s, s + steps) for s in range(first, last)])]
    ppermute x4 -> x12, starting transfers between devices: 12.3 us -> 32.9 us  [permute_by(): lax.ppermute(value, AXES, [(s, t) for s, t in pairs if 0 <= t < count])]
    ppermute x4 -> x12, waiting for transfers between devices: 9.87 us -> 26.2 us  [permute_by(): lax.ppermute(value, AXES, [(s, t) for s, t in pairs if 0 <= t < count])]
    pallas_call x1, Pallas kernels: 6.97 us -> 4.44 us  [ghost_slots(): pl.pallas_call(ghost_slots_kernel, out_shape=[jax.ShapeDtypeStruct((NB +...]
    ppermute x8 -> x0, waiting for transfers between devices: 2.44 us -> none  [shift(): lax.ppermute(value, AXES, [(s, s + steps) for s in range(first, last)])]
    pallas_call x1, Pallas kernels: 3.82 us -> 1.87 us  [add_pair(): pl.pallas_call(add_pair_kernel, out_shape=jax.ShapeDtypeStruct((2, BS, BA...]
    pallas_call x1, Pallas kernels: 2.7 us -> 1.33 us  [add_near(): pl.pallas_call(add_near_kernel, grid=(BS // rows,), out_shape=jax.ShapeDt...]
    unnamed x22 -> x20, local copies, waits for them, and re-layouts: 8.52 us -> 8.52 us
  transfers between devices with their start and end apart: 12 -> 12, of which waited for: 4 -> 7; matrix products, arithmetic and copies ran while one was open for 0% -> 0% of each run, Pallas kernels for 13% -> 14%
where the time goes in v4:
time: 105 us; the launch traced here: 104 us
  Pallas kernels  35.5 us (34%)
  starting transfers between devices  32.9 us (31%)
  waiting for transfers between devices  26.2 us (25%)
  local copies, waits for them, and re-layouts  8.52 us (8%)
    ppermute x12, starting transfers between devices, permute_by(): lax.ppermute(value, AXES, [(s, t) for s, t in pairs if 0 <= t < count])  32.9 us
    ppermute x12, waiting for transfers between devices, permute_by(): lax.ppermute(value, AXES, [(s, t) for s, t in pairs if 0 <= t < count])  26.2 us
    pallas_call x1, Pallas kernels, make_far(): pl.pallas_call(far_kernel, out_shape=[jax.ShapeDtypeStruct((NB, BS, WIDE)...  12.3 us
    unnamed x20, local copies, waits for them, and re-layouts  8.52 us
    pallas_call x1, Pallas kernels, make_near(): pl.pallas_call(near_kernel, out_shape=[jax.ShapeDtypeStruct((2, BS, WIDE)...  8.08 us
    pallas_call x1, Pallas kernels, ghost_slots(): pl.pallas_call(ghost_slots_kernel, out_shape=[jax.ShapeDtypeStruct((NB +...  4.44 us
    pallas_call x1, Pallas kernels, make_lists(): pl.pallas_call(lists_kernel, out_shape=[jax.ShapeDtypeStruct((10, 4 * NB...  2.65 us
    pallas_call x1, Pallas kernels, pack(): pl.pallas_call(pack_kernel, out_shape=[shape] * 4, in_specs=[spec(SMEM)]...  2.47 us
  transfers between devices with their start and end apart: 12, of which 7 were waited for; matrix products, arithmetic and copies ran while one was open for 0% of the time, Pallas kernels for 14%

profile of v4, /device:TPU:24, one launch (start us, length us, event | category | flops | bytes accessed | tf_op | source)
XLA Modules:
  0.0 103.6 jit_solution(18001757041209788551)
XLA Ops:
  0.0 2.5 %pack.1 = (bf16[1040,128]{1,0:T(8,128)(2,1)}, bf16[1040,128]{1,0:T(8,128)(2,1)}, bf16[1040,128]{1,0:T(8,128)(2,1)}, bf16[1040,128]{1,0:T(8,128)(2,1)}) custom-call(s32[1]{0:T(128)} %bitcast.parity, s32[4,4]{1,0:T(4,128)} %send_rows.3, s32[16]{0:T(128)} %aggregate.3, bf16[16,128,128]{2,1,0:T(8,128)(2,1)} %tent.3, bf16[16,128,128]{2,1,0:T(8,128)(2,1)} %diag.5), custom_call_target="tpu_custom_call" | custom-call | tf_op jit(solution)/shard_map/pack/pallas_call | solution.py:86
  2.5 0.0 copy-start.5
  2.5 0.0 copy-start.7
  2.5 8.3 %collective-permute-start = (bf16[1040,128]{1,0:T(8,128)(2,1)}, bf16[1040,128]{1,0:T(8,128)(2,1)S(1)}, u32[]{:S(2)}, u32[]{:S(2)}) collective-permute-start(bf16[1040,128]{1,0:T(8,128)(2,1)} %get-tuple-element.36), channel_id=1, source_target_pairs={{1,3},{2,0},{3,5},{4,2},{5,7},{6,4},{7,9},{8,6},{9,11},{10,8},{11,... | collective-permute-start | bytes 798728 | tf_op jit(solution)/shard_map/ppermute | solution.py:504
  10.8 1.9 %collective-permute-start.1 = (bf16[1040,128]{1,0:T(8,128)(2,1)}, bf16[1040,128]{1,0:T(8,128)(2,1)S(1)}, u32[]{:S(2)}, u32[]{:S(2)}) collective-permute-start(bf16[1040,128]{1,0:T(8,128)(2,1)} %get-tuple-element.37), channel_id=1, source_target_pairs={{0,2},{2,4},{3,1},{4,6},{5,3},{6,8},{7,5},{8,10},{9,7},{10,12},{11... | collective-permute-start | bytes 798728 | tf_op jit(solution)/shard_map/ppermute | solution.py:504
  12.8 2.8 %collective-permute-start.2 = (bf16[1040,128]{1,0:T(8,128)(2,1)}, bf16[1040,128]{1,0:T(8,128)(2,1)S(1)}, u32[]{:S(2)}, u32[]{:S(2)}) collective-permute-start(bf16[1040,128]{1,0:T(8,128)(2,1)} %get-tuple-element.38), channel_id=1, source_target_pairs={{1,2},{2,1},{3,4},{4,3},{5,6},{6,5},{7,8},{8,7},{9,10},{10,9},{11,... | collective-permute-start | bytes 798728 | tf_op jit(solution)/shard_map/ppermute | solution.py:504
  15.6 0.1 collective-permute-start.3
  15.7 0.0 copy-start
  15.7 1.4 %copy-done = bf16[16,3,128,128]{3,2,1,0:T(8,128)(2,1)S(1)} copy-done((bf16[16,3,128,128]{3,2,1,0:T(8,128)(2,1)S(1)}, bf16[16,3,128,128]{3,2,1,0:T(8,128)(2,1)}, u32[]{:S(2)}) %copy-start) | copy-done | bytes 1572888
  17.1 1.0 %copy-done.2 = bf16[16,128,128]{2,1,0:T(8,128)(2,1)S(1)} copy-done((bf16[16,128,128]{2,1,0:T(8,128)(2,1)S(1)}, bf16[16,128,128]{2,1,0:T(8,128)(2,1)}, u32[]{:S(2)}) %copy-start.2) | copy-done | bytes 524312
  18.1 1.0 %copy-done.3 = bf16[16,128,128]{2,1,0:T(8,128)(2,1)S(1)} copy-done((bf16[16,128,128]{2,1,0:T(8,128)(2,1)S(1)}, bf16[16,128,128]{2,1,0:T(8,128)(2,1)}, u32[]{:S(2)}) %copy-start.3) | copy-done | bytes 524312
  19.2 0.7 copy-done.6
  19.8 0.7 copy-done.8
  20.5 2.4 %local_slots.1 = (s32[16,4]{1,0:T(8,128)S(1)}, s32[52]{0:T(128)S(1)}, s32[1]{0:T(128)}, bf16[16,128,512]{2,1,0:T(8,128)(2,1)S(1)}, f32[16,128,128]{2,1,0:T(8,128)S(1)}) custom-call(s32[3,16]{1,0:T(4,128)S(1)} %bitcast.2, s32[16]{0:T(128)S(1)} %copy-done.8, bf16[16,128,128]{2,1,0:T(8,128)(2,1)S(1)} %copy-done.3, bf16[16,3,128,128]{3,2,1,0:T(8,128)(2,1)S(1)} %copy-done, ...), custom_call_target="tpu_custom_call" | custom-call | flops 1000000000 | bytes 6000000 | tf_op jit(solution)/shard_map/local_slots/pallas_call | solution.py:129
  22.9 0.0 collective-permute-done.g0
  22.9 2.1 %collective-permute-done.1.g1 = bf16[1040,128]{1,0:T(8,128)(2,1)S(1)} collective-permute-done((bf16[1040,128]{1,0:T(8,128)(2,1)}, bf16[1040,128]{1,0:T(8,128)(2,1)S(1)}, u32[]{:S(2)}, u32[]{:S(2)}) %collective-permute-start.1) | collective-permute-done | bytes 266272 | tf_op jit(solution)/shard_map/ppermute | solution.py:504
  25.0 1.4 %collective-permute-done.2.g2 = bf16[1040,128]{1,0:T(8,128)(2,1)S(1)} collective-permute-done((bf16[1040,128]{1,0:T(8,128)(2,1)}, bf16[1040,128]{1,0:T(8,128)(2,1)S(1)}, u32[]{:S(2)}, u32[]{:S(2)}) %collective-permute-start.2) | collective-permute-done | bytes 266272 | tf_op jit(solution)/shard_map/ppermute | solution.py:504
  26.4 0.0 collective-permute-done.3.g3
  26.4 0.0 copy-done.5
  26.4 0.0 copy-done.7
  26.4 0.0 copy-done.1
  26.4 4.4 %ghost_slots.1 = (s32[17,4]{1,0:T(8,128)S(1)}, bf16[17,128,512]{2,1,0:T(8,128)(2,1)S(1)}, bf16[528,384]{1,0:T(8,128)(2,1)S(1)}, bf16[528,384]{1,0:T(8,128)(2,1)S...) custom-call(s32[1]{0:T(128)} %bitcast.parity, s32[4,4]{1,0:T(4,128)S(1)} %copy-done.5, ...), custom_call_target="tpu_custom_call" | custom-call | tf_op jit(solution)/shard_map/ghost_slots/pallas_call | solution.py:193
  30.9 0.0 copy-start.4
  30.9 4.2 %collective-permute-start.4 = (bf16[528,384]{1,0:T(8,128)(2,1)S(1)}, bf16[528,384]{1,0:T(8,128)(2,1)S(1)}, u32[]{:S(2)}, u32[]{:S(2)}) collective-permute-start(bf16[528,384]{1,0:T(8,128)(2,1)S(1)} %get-tuple-element.46), channel_id=1, source_target_pairs={{1,3},{2,0},{3,5},{4,2},{5,7},{6,4},{7,9},{8,6},{9,11},{10,8},{11,... | collective-permute-start | bytes 1216520 | tf_op jit(solution)/shard_map/ppermute | solution.py:504
  35.1 1.9 %collective-permute-start.5 = (bf16[528,384]{1,0:T(8,128)(2,1)S(1)}, bf16[528,384]{1,0:T(8,128)(2,1)S(1)}, u32[]{:S(2)}, u32[]{:S(2)}) collective-permute-start(bf16[528,384]{1,0:T(8,128)(2,1)S(1)} %get-tuple-element.47), channel_id=1, source_target_pairs={{0,2},{2,4},{3,1},{4,6},{5,3},{6,8},{7,5},{8,10},{9,7},{10,12},{11... | collective-permute-start | bytes 1216520 | tf_op jit(solution)/shard_map/ppermute | solution.py:504
  37.1 3.4 %collective-permute-start.6 = (bf16[528,384]{1,0:T(8,128)(2,1)S(1)}, bf16[528,384]{1,0:T(8,128)(2,1)S(1)}, u32[]{:S(2)}, u32[]{:S(2)}) collective-permute-start(bf16[528,384]{1,0:T(8,128)(2,1)S(1)} %get-tuple-element.48), channel_id=1, source_target_pairs={{1,2},{2,1},{3,4},{4,3},{5,6},{6,5},{7,8},{8,7},{9,10},{10,9},{11,... | collective-permute-start | bytes 1216520 | tf_op jit(solution)/shard_map/ppermute | solution.py:504
  40.4 0.1 collective-permute-start.7
  40.5 2.6 %lists.1 = (s32[10,68]{1,0:T(8,128)S(1)}, s32[10]{0:T(128)S(1)}, bf16[65,128,128]{2,1,0:T(8,128)(2,1)S(1)}, bf16[16,128,128]{2,1,0:T(8,128)(2,1)S(1)}) custom-call(s32[1]{0:T(128)} %bitcast.parity, s32[17,4]{1,0:T(8,128)S(1)} %get-tuple-element.40.labels, bf16[17,128,512]{2,1,0:T(8,128)(2,1)S(1)} %get-tuple-element.41.slots, ...), custom_call_target="tpu_custom_call" | custom-call | flops 100000000 | bytes 6000000 | tf_op jit(solution)/shard_map/lists/pallas_call | solution.py:252
  43.2 0.6 collective-permute-done.4.g0
  43.8 8.3 %collective-permute-done.5.g1 = bf16[528,384]{1,0:T(8,128)(2,1)S(1)} collective-permute-done((bf16[528,384]{1,0:T(8,128)(2,1)S(1)}, bf16[528,384]{1,0:T(8,128)(2,1)S(1)}, u32[]{:S(2)}, u32[]{:S(2)}) %collective-permute-start.5) | collective-permute-done | bytes 405536 | tf_op jit(solution)/shard_map/ppermute | solution.py:504
  52.1 1.4 %collective-permute-done.6.g2 = bf16[528,384]{1,0:T(8,128)(2,1)S(1)} collective-permute-done((bf16[528,384]{1,0:T(8,128)(2,1)S(1)}, bf16[528,384]{1,0:T(8,128)(2,1)S(1)}, u32[]{:S(2)}, u32[]{:S(2)}) %collective-permute-start.6) | collective-permute-done | bytes 405536 | tf_op jit(solution)/shard_map/ppermute | solution.py:504
  53.5 0.0 collective-permute-done.7.g3
  53.5 0.0 copy-done.4
  53.5 12.3 %far_rows.1 = (bf16[16,128,2304]{2,1,0:T(8,128)(2,1)}, bf16[2,128,2560]{2,1,0:T(8,128)(2,1)S(1)}, f32[2,128,2560]{2,1,0:T(8,128)S(1)}, bf16[2,128,2304]{2,1,0:T(8,128)(2,1)S(1)}) custom-call(s32[1]{0:T(128)} %bitcast.parity, s32[3,16]{1,0:T(4,128)S(1)} %bitcast.4, s32[17,4]{1,0:T(8,128)S(1)} %get-tuple-element.40.labels, ...), custom_call_target="tpu_custom_call" | custom-call | flops 4000000000 | bytes 20000000 | tf_op jit(solution)/shard_map/far_rows/pallas_call | solution.py:384
  65.8 0.1 collective-permute-start.8
  65.9 4.6 %collective-permute-start.10 = (bf16[2,128,2304]{2,1,0:T(8,128)(2,1)S(1)}, bf16[2,128,2304]{2,1,0:T(8,128)(2,1)S(1)}, u32[]{:S(2)}, u32[]{:S(2)}) collective-permute-start(bf16[2,128,2304]{2,1,0:T(8,128)(2,1)S(1)} %get-tuple-element.56), channel_id=1, source_target_pairs={{1,3},{2,0},{3,5},{4,2},{5,7},{6,4},{7,9},{8,6},{9,11},{10,8},{11,... | collective-permute-start | bytes 3538952 | tf_op jit(solution)/shard_map/ppermute | solution.py:504
  70.5 0.0 collective-permute-done.8
  70.5 0.3 add_convert_fusion
  70.8 1.9 %collective-permute-start.11 = (bf16[2,128,2560]{2,1,0:T(8,128)(2,1)S(1)}, bf16[2,128,2560]{2,1,0:T(8,128)(2,1)S(1)}, u32[]{:S(2)}, u32[]{:S(2)}) collective-permute-start(bf16[2,128,2560]{2,1,0:T(8,128)(2,1)S(1)} %add_convert_fusion), channel_id=1, source_target_pairs={{0,2},{2,4},{3,1},{4,6},{5,3},{6,8},{7,5},{8,10},{9,7},{10,12},{11... | collective-permute-start | bytes 3932168 | tf_op jit(solution)/shard_map/ppermute | solution.py:504
  72.8 0.0 copy-start.9
  72.8 3.7 %copy-done.9 = bf16[16,128,2304]{2,1,0:T(8,128)(2,1)S(1)} copy-done((bf16[16,128,2304]{2,1,0:T(8,128)(2,1)S(1)}, bf16[16,128,2304]{2,1,0:T(8,128)(2,1)}, u32[]{:S(2)}) %copy-start.9) | copy-done | bytes 9437208
  76.4 8.1 %near_rows.1 = (f32[2,128,2304]{2,1,0:T(8,128)S(1)}, bf16[2,128,2304]{2,1,0:T(8,128)(2,1)S(1)}) custom-call(s32[1]{0:T(128)} %bitcast.parity, s32[10,68]{1,0:T(8,128)S(1)} %get-tuple-element.42.lists, s32[10]{0:T(128)S(1)} %get-tuple-element.43.counts, bf16[65,128,128]{2,1,0:T(8,128)(2,1)S(1)} %get-tuple-element.44.blocks, bf16[16,128,2304]{2,1,0:T(8,128)(2,1)S(1)} %copy-done.9), custom_call_target="tpu_custom_call" | custom-call | flops 4000000000 | bytes 20000000 | tf_op jit(solution)/shard_map/near_rows/pallas_call | solution.py:431
  84.5 3.5 %collective-permute-start.9 = (bf16[2,128,2304]{2,1,0:T(8,128)(2,1)S(1)}, bf16[2,128,2304]{2,1,0:T(8,128)(2,1)S(1)}, u32[]{:S(2)}, u32[]{:S(2)}) collective-permute-start(bf16[2,128,2304]{2,1,0:T(8,128)(2,1)S(1)} %get-tuple-element.55), channel_id=1, source_target_pairs={{0,1},{1,0},{2,3},{3,2},{4,5},{5,4},{6,7},{7,6},{8,9},{9,8},{10,11... | collective-permute-start | bytes 3538952 | tf_op jit(solution)/shard_map/ppermute | solution.py:504
  88.0 6.0 %collective-permute-done.10.direct = bf16[2,128,2304]{2,1,0:T(8,128)(2,1)S(1)} collective-permute-done((bf16[2,128,2304]{2,1,0:T(8,128)(2,1)S(1)}, bf16[2,128,2304]{2,1,0:T(8,128)(2,1)S(1)}, u32[]{:S(2)}, u32[]{:S(2)}) %collective-permute-start.10) | collective-permute-done | bytes 1179680 | tf_op jit(solution)/shard_map/ppermute | solution.py:504
  94.1 0.0 collective-permute-done.9.mate
  94.1 1.3 %add_near.1.band = f32[2,128,3328]{2,1,0:T(8,128)S(1)} custom-call(s32[1]{0:T(128)} %bitcast.parity, f32[2,128,2304]{2,1,0:T(8,128)S(1)} %get-tuple-element.54.own, bf16[2,128,2304]{2,1,0:T(8,128)(2,1)S(1)} %collective-permute-done.9.mate, bf16[2,128,2304]{2,1,0:T(8,128)(2,1)S(1)} %collective-permute-done.10.direct), custom_call_target="tpu_custom_call" | custom-call | flops 1000000 | bytes 9000000 | tf_op jit(solution)/shard_map/add_near/pallas_call | solution.py:462
  95.4 6.4 %collective-permute-done.11.pair = bf16[2,128,2560]{2,1,0:T(8,128)(2,1)S(1)} collective-permute-done((bf16[2,128,2560]{2,1,0:T(8,128)(2,1)S(1)}, bf16[2,128,2560]{2,1,0:T(8,128)(2,1)S(1)}, u32[]{:S(2)}, u32[]{:S(2)}) %collective-permute-start.11) | collective-permute-done | bytes 1310752 | tf_op jit(solution)/shard_map/ppermute | solution.py:504
  101.7 1.9 %add_pair.1 = f32[2,128,3328]{2,1,0:T(8,128)} custom-call(s32[1]{0:T(128)} %bitcast.parity, f32[2,128,3328]{2,1,0:T(8,128)S(1)} %add_near.1.band, bf16[2,128,2560]{2,1,0:T(8,128)(2,1)S(1)} %collective-permute-done.11.pair), custom_call_target="tpu_custom_call" | custom-call | tf_op jit(solution)/shard_map/add_pair/pallas_call | solution.py:490
  (5 shorter events, 0.0 us)
Async XLA Ops:
  2.5 23.9 %copy-start.5 = (s32[4,4]{1,0:T(4,128)S(1)}, s32[4,4]{1,0:T(4,128)}, u32[]{:S(2)}) copy-start(s32[4,4]{1,0:T(4,128)} %send_rows.3) | copy-start | bytes 196
  2.5 23.9 %copy-start.7 = (s32[16,3]{0,1:T(4,128)S(1)}, s32[16,3]{0,1:T(4,128)}, u32[]{:S(2)}) copy-start(s32[16,3]{0,1:T(4,128)} %param.8) | copy-start | bytes 580
  2.5 20.4 %collective-permute-start = (bf16[1040,128]{1,0:T(8,128)(2,1)}, bf16[1040,128]{1,0:T(8,128)(2,1)S(1)}, u32[]{:S(2)}, u32[]{:S(2)}) collective-permute-start(bf16[1040,128]{1,0:T(8,128)(2,1)} %get-tuple-element.36), channel_id=1, source_target_pairs={{1,3},{2,0},{3,5},{4,2},{5,7},{6,4},{7,9},{8,6},{9,11},{10,8},{11,... | collective-permute-start | bytes 798728 | tf_op jit(solution)/shard_map/ppermute | solution.py:504
  10.8 14.2 %collective-permute-start.1 = (bf16[1040,128]{1,0:T(8,128)(2,1)}, bf16[1040,128]{1,0:T(8,128)(2,1)S(1)}, u32[]{:S(2)}, u32[]{:S(2)}) collective-permute-start(bf16[1040,128]{1,0:T(8,128)(2,1)} %get-tuple-element.37), channel_id=1, source_target_pairs={{0,2},{2,4},{3,1},{4,6},{5,3},{6,8},{7,5},{8,10},{9,7},{10,12},{11... | collective-permute-start | bytes 798728 | tf_op jit(solution)/shard_map/ppermute | solution.py:504
  12.8 13.7 %collective-permute-start.2 = (bf16[1040,128]{1,0:T(8,128)(2,1)}, bf16[1040,128]{1,0:T(8,128)(2,1)S(1)}, u32[]{:S(2)}, u32[]{:S(2)}) collective-permute-start(bf16[1040,128]{1,0:T(8,128)(2,1)} %get-tuple-element.38), channel_id=1, source_target_pairs={{1,2},{2,1},{3,4},{4,3},{5,6},{6,5},{7,8},{8,7},{9,10},{10,9},{11,... | collective-permute-start | bytes 798728 | tf_op jit(solution)/shard_map/ppermute | solution.py:504
  15.6 10.9 %collective-permute-start.3 = (bf16[1040,128]{1,0:T(8,128)(2,1)}, bf16[1040,128]{1,0:T(8,128)(2,1)S(1)}, u32[]{:S(2)}, u32[]{:S(2)}) collective-permute-start(bf16[1040,128]{1,0:T(8,128)(2,1)} %get-tuple-element.39), channel_id=1, source_target_pairs={{0,1},{1,0},{2,3},{3,2},{4,5},{5,4},{6,7},{7,6},{8,9},{9,8},{10,11... | collective-permute-start | bytes 798728 | tf_op jit(solution)/shard_map/ppermute | solution.py:504
  15.7 1.4 %copy-start = (bf16[16,3,128,128]{3,2,1,0:T(8,128)(2,1)S(1)}, bf16[16,3,128,128]{3,2,1,0:T(8,128)(2,1)}, u32[]{:S(2)}) copy-start(bf16[16,3,128,128]{3,2,1,0:T(8,128)(2,1)} %off.5) | copy-start | bytes 4718596
  17.1 1.0 %copy-start.2 = (bf16[16,128,128]{2,1,0:T(8,128)(2,1)S(1)}, bf16[16,128,128]{2,1,0:T(8,128)(2,1)}, u32[]{:S(2)}) copy-start(bf16[16,128,128]{2,1,0:T(8,128)(2,1)} %tent.3) | copy-start | bytes 1572868
  18.1 1.0 %copy-start.3 = (bf16[16,128,128]{2,1,0:T(8,128)(2,1)S(1)}, bf16[16,128,128]{2,1,0:T(8,128)(2,1)}, u32[]{:S(2)}) copy-start(bf16[16,128,128]{2,1,0:T(8,128)(2,1)} %diag.5) | copy-start | bytes 1572868
  19.2 0.7 copy-start.6
  19.8 0.7 copy-start.8
  20.5 5.9 %copy-start.1 = (bf16[16,3,128,128]{3,2,1,0:T(8,128)(2,1)S(1)}, bf16[16,3,128,128]{3,2,1,0:T(8,128)(2,1)}, u32[]{:S(2)}) copy-start(bf16[16,3,128,128]{3,2,1,0:T(8,128)(2,1)} %off.5) | copy-start | bytes 4718596
  30.9 22.6 %copy-start.4 = (bf16[16,128,128]{2,1,0:T(8,128)(2,1)S(1)}, bf16[16,128,128]{2,1,0:T(8,128)(2,1)}, u32[]{:S(2)}) copy-start(bf16[16,128,128]{2,1,0:T(8,128)(2,1)} %diag.5) | copy-start | bytes 1572868
  30.9 12.9 %collective-permute-start.4 = (bf16[528,384]{1,0:T(8,128)(2,1)S(1)}, bf16[528,384]{1,0:T(8,128)(2,1)S(1)}, u32[]{:S(2)}, u32[]{:S(2)}) collective-permute-start(bf16[528,384]{1,0:T(8,128)(2,1)S(1)} %get-tuple-element.46), channel_id=1, source_target_pairs={{1,3},{2,0},{3,5},{4,2},{5,7},{6,4},{7,9},{8,6},{9,11},{10,8},{11,... | collective-permute-start | bytes 1216520 | tf_op jit(solution)/shard_map/ppermute | solution.py:504
  35.1 17.0 %collective-permute-start.5 = (bf16[528,384]{1,0:T(8,128)(2,1)S(1)}, bf16[528,384]{1,0:T(8,128)(2,1)S(1)}, u32[]{:S(2)}, u32[]{:S(2)}) collective-permute-start(bf16[528,384]{1,0:T(8,128)(2,1)S(1)} %get-tuple-element.47), channel_id=1, source_target_pairs={{0,2},{2,4},{3,1},{4,6},{5,3},{6,8},{7,5},{8,10},{9,7},{10,12},{11... | collective-permute-start | bytes 1216520 | tf_op jit(solution)/shard_map/ppermute | solution.py:504
  37.1 16.4 %collective-permute-start.6 = (bf16[528,384]{1,0:T(8,128)(2,1)S(1)}, bf16[528,384]{1,0:T(8,128)(2,1)S(1)}, u32[]{:S(2)}, u32[]{:S(2)}) collective-permute-start(bf16[528,384]{1,0:T(8,128)(2,1)S(1)} %get-tuple-element.48), channel_id=1, source_target_pairs={{1,2},{2,1},{3,4},{4,3},{5,6},{6,5},{7,8},{8,7},{9,10},{10,9},{11,... | collective-permute-start | bytes 1216520 | tf_op jit(solution)/shard_map/ppermute | solution.py:504
  40.4 13.1 %collective-permute-start.7 = (bf16[528,384]{1,0:T(8,128)(2,1)S(1)}, bf16[528,384]{1,0:T(8,128)(2,1)S(1)}, u32[]{:S(2)}, u32[]{:S(2)}) collective-permute-start(bf16[528,384]{1,0:T(8,128)(2,1)S(1)} %get-tuple-element.49), channel_id=1, source_target_pairs={{0,1},{1,0},{2,3},{3,2},{4,5},{5,4},{6,7},{7,6},{8,9},{9,8},{10,11... | collective-permute-start | bytes 1216520 | tf_op jit(solution)/shard_map/ppermute | solution.py:504
  65.8 4.7 %collective-permute-start.8 = (bf16[2,128,2560]{2,1,0:T(8,128)(2,1)S(1)}, bf16[2,128,2560]{2,1,0:T(8,128)(2,1)S(1)}, u32[]{:S(2)}, u32[]{:S(2)}) collective-permute-start(bf16[2,128,2560]{2,1,0:T(8,128)(2,1)S(1)} %get-tuple-element.52), channel_id=1, source_target_pairs={{0,1},{1,0},{2,3},{3,2},{4,5},{5,4},{6,7},{7,6},{8,9},{9,8},{10,11... | collective-permute-start | bytes 3932168 | tf_op jit(solution)/shard_map/ppermute | solution.py:504
  65.9 28.2 %collective-permute-start.10 = (bf16[2,128,2304]{2,1,0:T(8,128)(2,1)S(1)}, bf16[2,128,2304]{2,1,0:T(8,128)(2,1)S(1)}, u32[]{:S(2)}, u32[]{:S(2)}) collective-permute-start(bf16[2,128,2304]{2,1,0:T(8,128)(2,1)S(1)} %get-tuple-element.56), channel_id=1, source_target_pairs={{1,3},{2,0},{3,5},{4,2},{5,7},{6,4},{7,9},{8,6},{9,11},{10,8},{11,... | collective-permute-start | bytes 3538952 | tf_op jit(solution)/shard_map/ppermute | solution.py:504
  70.8 30.9 %collective-permute-start.11 = (bf16[2,128,2560]{2,1,0:T(8,128)(2,1)S(1)}, bf16[2,128,2560]{2,1,0:T(8,128)(2,1)S(1)}, u32[]{:S(2)}, u32[]{:S(2)}) collective-permute-start(bf16[2,128,2560]{2,1,0:T(8,128)(2,1)S(1)} %add_convert_fusion), channel_id=1, source_target_pairs={{0,2},{2,4},{3,1},{4,6},{5,3},{6,8},{7,5},{8,10},{9,7},{10,12},{11... | collective-permute-start | bytes 3932168 | tf_op jit(solution)/shard_map/ppermute | solution.py:504
  72.8 3.7 %copy-start.9 = (bf16[16,128,2304]{2,1,0:T(8,128)(2,1)S(1)}, bf16[16,128,2304]{2,1,0:T(8,128)(2,1)}, u32[]{:S(2)}) copy-start(bf16[16,128,2304]{2,1,0:T(8,128)(2,1)} %get-tuple-element.53.applied) | copy-start | bytes 28311556
  84.5 9.5 %collective-permute-start.9 = (bf16[2,128,2304]{2,1,0:T(8,128)(2,1)S(1)}, bf16[2,128,2304]{2,1,0:T(8,128)(2,1)S(1)}, u32[]{:S(2)}, u32[]{:S(2)}) collective-permute-start(bf16[2,128,2304]{2,1,0:T(8,128)(2,1)S(1)} %get-tuple-element.55), channel_id=1, source_target_pairs={{0,1},{1,0},{2,3},{3,2},{4,5},{5,4},{6,7},{7,6},{8,9},{9,8},{10,11... | collective-permute-start | bytes 3538952 | tf_op jit(solution)/shard_map/ppermute | solution.py:504

commit v5 on v4

--- a/solution.py
+++ b/solution.py
@@ -18,6 +18,7 @@
 CHIPWIDE = 20 * BS
 BANDWIDE = 26 * BS
 TILES = [slice(t * 2 * BS, (t + 1) * 2 * BS) for t in range(FRAME // 2)]
+FAR_MB = 26
 GROUP = 4
 CHUNK = 4
 EXTRA = 16
@@ -281,11 +282,23 @@
     lax.fori_loop(0, counts[t], chunk, 0)
 
 
+def rows_of(level, lists, counts, blocks, applied, coarse):
+    def one(b, carry):
+        coarse_rows(2 * level + b, b, lists, counts, blocks, applied, coarse)
+        return carry
+
+    lax.fori_loop(0, 2, one, 0)
+
+
+def chip_frame(odd):
+    into = pl.ds(pl.multiple_of(odd * (2 * BS), BS), WIDE)
+    return into, pl.ds(pl.multiple_of((1 - odd) * WIDE, BS), 2 * BS)
+
+
 def far_kernel(
     parity, off_columns, labels, lists, counts, diag, off, slots, blocks, first_slots, g0, g1, g2, g3,
-    applied_out, relay_out, relayed_out, direct_out,
-    table, labels_in, labels_vmem, label_smem, total_a, total_b, applied, coarse, relay, relayed, direct,
-    sem_in, sem_lab, sem_out, sem_piece,
+    applied, direct, relay,
+    table, labels_in, labels_vmem, label_smem, total_a, total_b, coarse, sem_in, sem_lab,
 ):
     ghosts = (g0, g1, g2, g3)
     copies = [
@@ -308,12 +321,6 @@
     ]
     for copy in lab + copies:
         copy.start()
-    odd = parity[0] == 1
-    relay_level = jnp.where(odd, 3, 1)
-    relayed_level = jnp.where(odd, 0, 4)
-    rest = pl.ds(pl.multiple_of((1 - parity[0]) * WIDE, BS), 2 * BS)
-    relay[:, :, rest] = jnp.zeros((2, BS, 2 * BS), BF)
-    relayed[:, :, rest] = jnp.zeros((2, BS, 2 * BS), F32)
     for copy in lab:
         copy.wait()
     for at, (n, offset) in enumerate(arrivals):
@@ -341,7 +348,6 @@
                 total[at] = total[at] + prod[:, m * BS : (m + 1) * BS]
         for at in range(FRAME):
             applied[i, :, at * BS : (at + 1) * BS] = total[at].astype(BF)
-        pltpu.make_async_copy(applied.at[i], applied_out.at[i], sem_out.at[i]).start()
 
     def row_pair(q, carry):
         row(2 * q, total_a)
@@ -349,35 +355,12 @@
         return carry
 
     lax.fori_loop(0, NB // 2, row_pair, 0)
-    into = pl.ds(pl.multiple_of(parity[0] * (2 * BS), BS), WIDE)
-
-    def rows_of(level):
-        def one(b, carry):
-            coarse_rows(2 * level + b, b, lists, counts, blocks, applied, coarse)
-            return carry
-
-        lax.fori_loop(0, 2, one, 0)
-
-    rows_of(4 - relayed_level)
+    rows_of(4 * parity[0], lists, counts, blocks, applied, coarse)
     direct[...] = coarse[...].astype(BF)
-    pieces = [pltpu.make_async_copy(direct, direct_out, sem_piece.at[0])]
-    pieces[-1].start()
-    rows_of(relay_level)
+    rows_of(1 + 2 * parity[0], lists, counts, blocks, applied, coarse)
+    into, rest = chip_frame(parity[0])
+    relay[:, :, rest] = jnp.zeros((2, BS, 2 * BS), BF)
     relay[:, :, into] = coarse[...].astype(BF)
-    pieces.append(pltpu.make_async_copy(relay, relay_out, sem_piece.at[1]))
-    pieces[-1].start()
-    rows_of(relayed_level)
-    relayed[:, :, into] = coarse[...]
-    pieces.append(pltpu.make_async_copy(relayed, relayed_out, sem_piece.at[2]))
-    pieces[-1].start()
-
-    def wait(i, carry):
-        pltpu.make_async_copy(applied.at[i], applied_out.at[i], sem_out.at[i]).wait()
-        return carry
-
-    lax.fori_loop(0, NB, wait, 0)
-    for copy in pieces:
-        copy.wait()
 
 
 def make_far(parity, off_columns, labels, lists, counts, diag, off, slots, blocks, first_slots, ghosts):
@@ -385,12 +368,11 @@
         far_kernel,
         out_shape=[
             jax.ShapeDtypeStruct((NB, BS, WIDE), BF),
+            jax.ShapeDtypeStruct((2, BS, WIDE), BF),
             jax.ShapeDtypeStruct((2, BS, CHIPWIDE), BF),
-            jax.ShapeDtypeStruct((2, BS, CHIPWIDE), F32),
-            jax.ShapeDtypeStruct((2, BS, WIDE), BF),
         ],
         in_specs=[spec(SMEM)] * 5 + [spec(pltpu.VMEM)] * 2 + [spec(ANY), spec(pltpu.VMEM)] + [spec(ANY)] * 5,
-        out_specs=[spec(ANY)] * 4,
+        out_specs=[spec(pltpu.VMEM)] * 3,
         scratch_shapes=[
             pltpu.VMEM((NT, BS, SLOTW), BF),
             pltpu.VMEM((4, EXTRA, BS), BF),
@@ -398,20 +380,34 @@
             pltpu.SMEM((4, 8, BS), jnp.int32),
             pltpu.VMEM((FRAME, BS, BS), F32),
             pltpu.VMEM((FRAME, BS, BS), F32),
-            pltpu.VMEM((NB, BS, WIDE), BF),
             pltpu.VMEM((2, BS, WIDE), F32),
-            pltpu.VMEM((2, BS, CHIPWIDE), BF),
-            pltpu.VMEM((2, BS, CHIPWIDE), F32),
-            pltpu.VMEM((2, BS, WIDE), BF),
             pltpu.SemaphoreType.DMA((2 + 4 * NG,)),
             pltpu.SemaphoreType.DMA((4,)),
-            pltpu.SemaphoreType.DMA((NB,)),
-            pltpu.SemaphoreType.DMA((3,)),
         ],
-        compiler_params=pltpu.CompilerParams(vmem_limit_bytes=34 * 1024 * 1024),
+        compiler_params=pltpu.CompilerParams(vmem_limit_bytes=FAR_MB * 1024 * 1024),
         cost_estimate=pl.CostEstimate(flops=4 * 10**9, bytes_accessed=20 * 10**6, transcendentals=0),
         name="far_rows",
     )(parity, off_columns, labels, lists, counts, diag, off, slots, blocks, first_slots, *ghosts)
+
+
+def pair_kernel(parity, lists, counts, blocks, applied, relay, pair, coarse):
+    rows_of(4 - 4 * parity[0], lists, counts, blocks, applied, coarse)
+    into, rest = chip_frame(parity[0])
+    pair[:, :, rest] = relay[:, :, rest]
+    pair[:, :, into] = (coarse[...] + relay[:, :, into].astype(F32)).astype(BF)
+
+
+def make_pair(parity, lists, counts, blocks, applied, relay):
+    return pl.pallas_call(
+        pair_kernel,
+        out_shape=jax.ShapeDtypeStruct((2, BS, CHIPWIDE), BF),
+        in_specs=[spec(SMEM)] * 3 + [spec(pltpu.VMEM)] * 3,
+        out_specs=spec(pltpu.VMEM),
+        scratch_shapes=[pltpu.VMEM((2, BS, WIDE), F32)],
+        compiler_params=pltpu.CompilerParams(vmem_limit_bytes=22 * 1024 * 1024),
+        cost_estimate=pl.CostEstimate(flops=2 * 10**9, bytes_accessed=10 * 10**6, transcendentals=0),
+        name="pair_rows",
+    )(parity, lists, counts, blocks, applied, relay)
 
 
 def near_kernel(parity, lists, counts, blocks, applied, own, mate, coarse):
@@ -521,12 +517,12 @@
     )
     lists, counts, blocks, first_slots = make_lists(parity, labels, slots, ghosts)
     ghosts = exchange(sends)
-    applied, relay, relayed, direct = make_far(
+    applied, direct, relay = make_far(
         parity, off_columns, labels, lists, counts, diag_blocks, off_blocks, slots, blocks, first_slots, ghosts
     )
     direct_in = permute_by(direct, -2, 2)
     relay_in = permute_by(relay, 1, -1)
-    pair_sum = (relayed + relay_in.astype(F32)).astype(BF)
+    pair_sum = make_pair(parity, lists, counts, blocks, applied, relay_in)
     pair_in = permute_by(pair_sum, 2, -2)
     applied, pair_sum = lax.optimization_barrier((applied, pair_sum))
     own, mate = make_near(parity, lists, counts, blocks, applied)

time: 105 us -> 102 us (0.971)
  local copies, waits for them, and re-layouts: 8.52 us -> 4.84 us
  waiting for transfers between devices: 26.2 us -> 27.5 us
    unnamed x20 -> x18, local copies, waits for them, and re-layouts: 8.52 us -> 4.84 us
    pallas_call x0 -> x1, Pallas kernels: none -> 2.02 us  [make_pair(): pl.pallas_call(pair_kernel, out_shape=jax.ShapeDtypeStruct((2, BS, CHIPWI...]
    pallas_call x1, Pallas kernels: 12.3 us -> 10.4 us  [make_far(): pl.pallas_call(far_kernel, out_shape=[jax.ShapeDtypeStruct((NB, BS, WIDE)...]
    ppermute x12, waiting for transfers between devices: 26.2 us -> 27.5 us  [permute_by(): lax.ppermute(value, AXES, [(s, t) for s, t in pairs if 0 <= t < count])]
  transfers between devices with their start and end apart: 12 -> 12, of which waited for: 7 -> 6; matrix products, arithmetic and copies ran while one was open for 0% -> 0% of each run, Pallas kernels for 14% -> 16%
where the time goes in v5:
time: 102 us
  Pallas kernels  35.6 us (35%)
  starting transfers between devices  33.5 us (33%)
  waiting for transfers between devices  27.5 us (27%)
  local copies, waits for them, and re-layouts  4.84 us (5%)
    ppermute x12, starting transfers between devices, permute_by(): lax.ppermute(value, AXES, [(s, t) for s, t in pairs if 0 <= t < count])  33.5 us
    ppermute x12, waiting for transfers between devices, permute_by(): lax.ppermute(value, AXES, [(s, t) for s, t in pairs if 0 <= t < count])  27.5 us
    pallas_call x1, Pallas kernels, make_far(): pl.pallas_call(far_kernel, out_shape=[jax.ShapeDtypeStruct((NB, BS, WIDE)...  10.4 us
    pallas_call x1, Pallas kernels, make_near(): pl.pallas_call(near_kernel, out_shape=[jax.ShapeDtypeStruct((2, BS, WIDE)...  7.6 us
    pallas_call x1, Pallas kernels, ghost_slots(): pl.pallas_call(ghost_slots_kernel, out_shape=[jax.ShapeDtypeStruct((NB +...  4.86 us
    unnamed x18, local copies, waits for them, and re-layouts  4.84 us
    pallas_call x1, Pallas kernels, make_lists(): pl.pallas_call(lists_kernel, out_shape=[jax.ShapeDtypeStruct((10, 4 * NB...  2.65 us
    pallas_call x1, Pallas kernels, pack(): pl.pallas_call(pack_kernel, out_shape=[shape] * 4, in_specs=[spec(SMEM)]...  2.48 us
  transfers between devices with their start and end apart: 12, of which 6 were waited for; matrix products, arithmetic and copies ran while one was open for 0% of the time, Pallas kernels for 16%

profile of v5, /device:TPU:24, one launch (start us, length us, event | category | flops | bytes accessed | tf_op | source)
XLA Modules:
  0.0 101.6 jit_solution(17757325814975866531)
XLA Ops:
  0.0 2.5 %pack.1 = (bf16[1040,128]{1,0:T(8,128)(2,1)}, bf16[1040,128]{1,0:T(8,128)(2,1)}, bf16[1040,128]{1,0:T(8,128)(2,1)}, bf16[1040,128]{1,0:T(8,128)(2,1)}) custom-call(s32[1]{0:T(128)} %bitcast.parity, s32[4,4]{1,0:T(4,128)} %send_rows.3, s32[16]{0:T(128)} %aggregate.3, bf16[16,128,128]{2,1,0:T(8,128)(2,1)} %tent.3, bf16[16,128,128]{2,1,0:T(8,128)(2,1)} %diag.5), custom_call_target="tpu_custom_call" | custom-call | tf_op jit(solution)/shard_map/pack/pallas_call | solution.py:87
  2.5 8.3 %collective-permute-start = (bf16[1040,128]{1,0:T(8,128)(2,1)}, bf16[1040,128]{1,0:T(8,128)(2,1)S(1)}, u32[]{:S(2)}, u32[]{:S(2)}) collective-permute-start(bf16[1040,128]{1,0:T(8,128)(2,1)} %get-tuple-element.35), channel_id=1, source_target_pairs={{1,3},{2,0},{3,5},{4,2},{5,7},{6,4},{7,9},{8,6},{9,11},{10,8},{11,... | collective-permute-start | bytes 798728 | tf_op jit(solution)/shard_map/ppermute | solution.py:500
  10.8 1.9 %collective-permute-start.1 = (bf16[1040,128]{1,0:T(8,128)(2,1)}, bf16[1040,128]{1,0:T(8,128)(2,1)S(1)}, u32[]{:S(2)}, u32[]{:S(2)}) collective-permute-start(bf16[1040,128]{1,0:T(8,128)(2,1)} %get-tuple-element.36), channel_id=1, source_target_pairs={{0,2},{2,4},{3,1},{4,6},{5,3},{6,8},{7,5},{8,10},{9,7},{10,12},{11... | collective-permute-start | bytes 798728 | tf_op jit(solution)/shard_map/ppermute | solution.py:500
  12.7 2.8 %collective-permute-start.2 = (bf16[1040,128]{1,0:T(8,128)(2,1)}, bf16[1040,128]{1,0:T(8,128)(2,1)S(1)}, u32[]{:S(2)}, u32[]{:S(2)}) collective-permute-start(bf16[1040,128]{1,0:T(8,128)(2,1)} %get-tuple-element.37), channel_id=1, source_target_pairs={{1,2},{2,1},{3,4},{4,3},{5,6},{6,5},{7,8},{8,7},{9,10},{10,9},{11,... | collective-permute-start | bytes 798728 | tf_op jit(solution)/shard_map/ppermute | solution.py:500
  15.6 0.1 collective-permute-start.3
  15.6 0.0 copy-start
  15.7 1.4 %copy-done = bf16[16,3,128,128]{3,2,1,0:T(8,128)(2,1)S(1)} copy-done((bf16[16,3,128,128]{3,2,1,0:T(8,128)(2,1)S(1)}, bf16[16,3,128,128]{3,2,1,0:T(8,128)(2,1)}, u32[]{:S(2)}) %copy-start) | copy-done | bytes 1572888
  17.1 0.0 copy-start.2
  17.1 1.0 %copy-done.2 = bf16[16,128,128]{2,1,0:T(8,128)(2,1)S(1)} copy-done((bf16[16,128,128]{2,1,0:T(8,128)(2,1)S(1)}, bf16[16,128,128]{2,1,0:T(8,128)(2,1)}, u32[]{:S(2)}) %copy-start.2) | copy-done | bytes 524312
  18.1 0.0 copy-start.3
  18.1 1.0 %copy-done.3 = bf16[16,128,128]{2,1,0:T(8,128)(2,1)S(1)} copy-done((bf16[16,128,128]{2,1,0:T(8,128)(2,1)S(1)}, bf16[16,128,128]{2,1,0:T(8,128)(2,1)}, u32[]{:S(2)}) %copy-start.3) | copy-done | bytes 524312
  19.1 0.0 copy-start.6
  19.1 0.7 copy-done.6
  19.8 0.0 copy-start.8
  19.8 0.7 copy-done.8
  20.5 2.4 %local_slots.1 = (s32[16,4]{1,0:T(8,128)S(1)}, s32[52]{0:T(128)S(1)}, s32[1]{0:T(128)}, bf16[16,128,512]{2,1,0:T(8,128)(2,1)S(1)}, f32[16,128,128]{2,1,0:T(8,128)S(1)}) custom-call(s32[3,16]{1,0:T(4,128)S(1)} %bitcast.2, s32[16]{0:T(128)S(1)} %copy-done.8, bf16[16,128,128]{2,1,0:T(8,128)(2,1)S(1)} %copy-done.3, bf16[16,3,128,128]{3,2,1,0:T(8,128)(2,1)S(1)} %copy-done, ...), custom_call_target="tpu_custom_call" | custom-call | flops 1000000000 | bytes 6000000 | tf_op jit(solution)/shard_map/local_slots/pallas_call | solution.py:130
  22.9 0.0 collective-permute-done.g0
  22.9 2.1 %collective-permute-done.1.g1 = bf16[1040,128]{1,0:T(8,128)(2,1)S(1)} collective-permute-done((bf16[1040,128]{1,0:T(8,128)(2,1)}, bf16[1040,128]{1,0:T(8,128)(2,1)S(1)}, u32[]{:S(2)}, u32[]{:S(2)}) %collective-permute-start.1) | collective-permute-done | bytes 266272 | tf_op jit(solution)/shard_map/ppermute | solution.py:500
  25.0 1.4 %collective-permute-done.2.g2 = bf16[1040,128]{1,0:T(8,128)(2,1)S(1)} collective-permute-done((bf16[1040,128]{1,0:T(8,128)(2,1)}, bf16[1040,128]{1,0:T(8,128)(2,1)S(1)}, u32[]{:S(2)}, u32[]{:S(2)}) %collective-permute-start.2) | collective-permute-done | bytes 266272 | tf_op jit(solution)/shard_map/ppermute | solution.py:500
  26.4 0.0 collective-permute-done.3.g3
  26.4 0.0 copy-done.1
  26.4 0.0 copy-done.5
  26.4 0.0 copy-done.7
  26.4 4.9 %ghost_slots.1 = (s32[17,4]{1,0:T(8,128)S(1)}, bf16[17,128,512]{2,1,0:T(8,128)(2,1)S(1)}, bf16[528,384]{1,0:T(8,128)(2,1)S(1)}, bf16[528,384]{1,0:T(8,128)(2,1)S...) custom-call(s32[1]{0:T(128)} %bitcast.parity, s32[4,4]{1,0:T(4,128)S(1)} %copy-done.5, ...), custom_call_target="tpu_custom_call" | custom-call | tf_op jit(solution)/shard_map/ghost_slots/pallas_call | solution.py:194
  31.3 3.7 %collective-permute-start.4 = (bf16[528,384]{1,0:T(8,128)(2,1)S(1)}, bf16[528,384]{1,0:T(8,128)(2,1)S(1)}, u32[]{:S(2)}, u32[]{:S(2)}) collective-permute-start(bf16[528,384]{1,0:T(8,128)(2,1)S(1)} %get-tuple-element.45), channel_id=1, source_target_pairs={{1,3},{2,0},{3,5},{4,2},{5,7},{6,4},{7,9},{8,6},{9,11},{10,8},{11,... | collective-permute-start | bytes 1216520 | tf_op jit(solution)/shard_map/ppermute | solution.py:500
  35.0 2.2 %collective-permute-start.5 = (bf16[528,384]{1,0:T(8,128)(2,1)S(1)}, bf16[528,384]{1,0:T(8,128)(2,1)S(1)}, u32[]{:S(2)}, u32[]{:S(2)}) collective-permute-start(bf16[528,384]{1,0:T(8,128)(2,1)S(1)} %get-tuple-element.46), channel_id=1, source_target_pairs={{0,2},{2,4},{3,1},{4,6},{5,3},{6,8},{7,5},{8,10},{9,7},{10,12},{11... | collective-permute-start | bytes 1216520 | tf_op jit(solution)/shard_map/ppermute | solution.py:500
  37.2 3.7 %collective-permute-start.6 = (bf16[528,384]{1,0:T(8,128)(2,1)S(1)}, bf16[528,384]{1,0:T(8,128)(2,1)S(1)}, u32[]{:S(2)}, u32[]{:S(2)}) collective-permute-start(bf16[528,384]{1,0:T(8,128)(2,1)S(1)} %get-tuple-element.47), channel_id=1, source_target_pairs={{1,2},{2,1},{3,4},{4,3},{5,6},{6,5},{7,8},{8,7},{9,10},{10,9},{11,... | collective-permute-start | bytes 1216520 | tf_op jit(solution)/shard_map/ppermute | solution.py:500
  40.9 0.1 collective-permute-start.7
  41.0 0.0 copy-start.4
  41.0 2.6 %lists.1 = (s32[10,68]{1,0:T(8,128)S(1)}, s32[10]{0:T(128)S(1)}, bf16[65,128,128]{2,1,0:T(8,128)(2,1)S(1)}, bf16[16,128,128]{2,1,0:T(8,128)(2,1)S(1)}) custom-call(s32[1]{0:T(128)} %bitcast.parity, s32[17,4]{1,0:T(8,128)S(1)} %get-tuple-element.39.labels, bf16[17,128,512]{2,1,0:T(8,128)(2,1)S(1)} %get-tuple-element.40.slots, ...), custom_call_target="tpu_custom_call" | custom-call | flops 100000000 | bytes 6000000 | tf_op jit(solution)/shard_map/lists/pallas_call | solution.py:253
  43.7 0.0 collective-permute-done.4.g0
  43.7 8.0 %collective-permute-done.5.g1 = bf16[528,384]{1,0:T(8,128)(2,1)S(1)} collective-permute-done((bf16[528,384]{1,0:T(8,128)(2,1)S(1)}, bf16[528,384]{1,0:T(8,128)(2,1)S(1)}, u32[]{:S(2)}, u32[]{:S(2)}) %collective-permute-start.5) | collective-permute-done | bytes 405536 | tf_op jit(solution)/shard_map/ppermute | solution.py:500
  51.7 1.7 %collective-permute-done.6.g2 = bf16[528,384]{1,0:T(8,128)(2,1)S(1)} collective-permute-done((bf16[528,384]{1,0:T(8,128)(2,1)S(1)}, bf16[528,384]{1,0:T(8,128)(2,1)S(1)}, u32[]{:S(2)}, u32[]{:S(2)}) %collective-permute-start.6) | collective-permute-done | bytes 405536 | tf_op jit(solution)/shard_map/ppermute | solution.py:500
  53.3 0.0 collective-permute-done.7.g3
  53.3 0.0 copy-done.4
  53.3 10.4 %far_rows.1 = (bf16[16,128,2304]{2,1,0:T(8,128)(2,1)S(1)}, bf16[2,128,2304]{2,1,0:T(8,128)(2,1)S(1)}, bf16[2,128,2560]{2,1,0:T(8,128)(2,1)S(1)}) custom-call(s32[1]{0:T(128)} %bitcast.parity, s32[3,16]{1,0:T(4,128)S(1)} %bitcast.4, s32[17,4]{1,0:T(8,128)S(1)} %get-tuple-element.39.labels, s32[10,68]{1,0:T(8,128)S(1)} %get-tuple-element.41.lists, ...), custom_call_target="tpu_custom_call" | custom-call | flops 4000000000 | bytes 20000000 | tf_op jit(solution)/shard_map/far_rows/pallas_call | solution.py:367
  63.8 0.1 collective-permute-start.8
  63.8 5.1 %collective-permute-start.10 = (bf16[2,128,2304]{2,1,0:T(8,128)(2,1)S(1)}, bf16[2,128,2304]{2,1,0:T(8,128)(2,1)S(1)}, u32[]{:S(2)}, u32[]{:S(2)}) collective-permute-start(bf16[2,128,2304]{2,1,0:T(8,128)(2,1)S(1)} %get-tuple-element.54), channel_id=1, source_target_pairs={{1,3},{2,0},{3,5},{4,2},{5,7},{6,4},{7,9},{8,6},{9,11},{10,8},{11,... | collective-permute-start | bytes 3538952 | tf_op jit(solution)/shard_map/ppermute | solution.py:500
  69.0 0.0 collective-permute-done.8.relay
  69.0 2.0 %pair_rows.1 = bf16[2,128,2560]{2,1,0:T(8,128)(2,1)S(1)} custom-call(s32[1]{0:T(128)} %bitcast.parity, s32[10,68]{1,0:T(8,128)S(1)} %get-tuple-element.41.lists, s32[10]{0:T(128)S(1)} %get-tuple-element.42.counts, bf16[65,128,128]{2,1,0:T(8,128)(2,1)S(1)} %get-tuple-element.43.blocks, bf16[16,128,2304]{2,1,0:T(8,128)(2,1)S(1)} %get-tuple-element.51.applied, ...), custom_call_target="tpu_custom_call" | custom-call | flops 2000000000 | bytes 10000000 | tf_op jit(solution)/shard_map/pair_rows/pallas_call | solution.py:401
  71.0 1.9 %collective-permute-start.11 = (bf16[2,128,2560]{2,1,0:T(8,128)(2,1)S(1)}, bf16[2,128,2560]{2,1,0:T(8,128)(2,1)S(1)}, u32[]{:S(2)}, u32[]{:S(2)}) collective-permute-start(bf16[2,128,2560]{2,1,0:T(8,128)(2,1)S(1)} %pair_rows.1), channel_id=1, source_target_pairs={{0,2},{2,4},{3,1},{4,6},{5,3},{6,8},{7,5},{8,10},{9,7},{10,12},{11... | collective-permute-start | bytes 3932168 | tf_op jit(solution)/shard_map/ppermute | solution.py:500
  72.9 7.6 %near_rows.1 = (f32[2,128,2304]{2,1,0:T(8,128)S(1)}, bf16[2,128,2304]{2,1,0:T(8,128)(2,1)S(1)}) custom-call(s32[1]{0:T(128)} %bitcast.parity, s32[10,68]{1,0:T(8,128)S(1)} %get-tuple-element.41.lists, s32[10]{0:T(128)S(1)} %get-tuple-element.42.counts, bf16[65,128,128]{2,1,0:T(8,128)(2,1)S(1)} %get-tuple-element.43.blocks, ...), custom_call_target="tpu_custom_call" | custom-call | flops 4000000000 | bytes 20000000 | tf_op jit(solution)/shard_map/near_rows/pallas_call | solution.py:427
  80.5 3.6 %collective-permute-start.9 = (bf16[2,128,2304]{2,1,0:T(8,128)(2,1)S(1)}, bf16[2,128,2304]{2,1,0:T(8,128)(2,1)S(1)}, u32[]{:S(2)}, u32[]{:S(2)}) collective-permute-start(bf16[2,128,2304]{2,1,0:T(8,128)(2,1)S(1)} %get-tuple-element.53), channel_id=1, source_target_pairs={{0,1},{1,0},{2,3},{3,2},{4,5},{5,4},{6,7},{7,6},{8,9},{9,8},{10,11... | collective-permute-start | bytes 3538952 | tf_op jit(solution)/shard_map/ppermute | solution.py:500
  84.1 6.1 %collective-permute-done.10.direct = bf16[2,128,2304]{2,1,0:T(8,128)(2,1)S(1)} collective-permute-done((bf16[2,128,2304]{2,1,0:T(8,128)(2,1)S(1)}, bf16[2,128,2304]{2,1,0:T(8,128)(2,1)S(1)}, u32[]{:S(2)}, u32[]{:S(2)}) %collective-permute-start.10) | collective-permute-done | bytes 1179680 | tf_op jit(solution)/shard_map/ppermute | solution.py:500
  90.2 0.0 collective-permute-done.9.mate
  90.2 1.3 %add_near.1.band = f32[2,128,3328]{2,1,0:T(8,128)S(1)} custom-call(s32[1]{0:T(128)} %bitcast.parity, f32[2,128,2304]{2,1,0:T(8,128)S(1)} %get-tuple-element.52.own, bf16[2,128,2304]{2,1,0:T(8,128)(2,1)S(1)} %collective-permute-done.9.mate, bf16[2,128,2304]{2,1,0:T(8,128)(2,1)S(1)} %collective-permute-done.10.direct), custom_call_target="tpu_custom_call" | custom-call | flops 1000000 | bytes 9000000 | tf_op jit(solution)/shard_map/add_near/pallas_call | solution.py:458
  91.6 8.1 %collective-permute-done.11.pair = bf16[2,128,2560]{2,1,0:T(8,128)(2,1)S(1)} collective-permute-done((bf16[2,128,2560]{2,1,0:T(8,128)(2,1)S(1)}, bf16[2,128,2560]{2,1,0:T(8,128)(2,1)S(1)}, u32[]{:S(2)}, u32[]{:S(2)}) %collective-permute-start.11) | collective-permute-done | bytes 1310752 | tf_op jit(solution)/shard_map/ppermute | solution.py:500
  99.7 1.9 %add_pair.1 = f32[2,128,3328]{2,1,0:T(8,128)} custom-call(s32[1]{0:T(128)} %bitcast.parity, f32[2,128,3328]{2,1,0:T(8,128)S(1)} %add_near.1.band, bf16[2,128,2560]{2,1,0:T(8,128)(2,1)S(1)} %collective-permute-done.11.pair), custom_call_target="tpu_custom_call" | custom-call | tf_op jit(solution)/shard_map/add_pair/pallas_call | solution.py:486
  (3 shorter events, 0.0 us)
Async XLA Ops:
  2.5 20.4 %collective-permute-start = (bf16[1040,128]{1,0:T(8,128)(2,1)}, bf16[1040,128]{1,0:T(8,128)(2,1)S(1)}, u32[]{:S(2)}, u32[]{:S(2)}) collective-permute-start(bf16[1040,128]{1,0:T(8,128)(2,1)} %get-tuple-element.35), channel_id=1, source_target_pairs={{1,3},{2,0},{3,5},{4,2},{5,7},{6,4},{7,9},{8,6},{9,11},{10,8},{11,... | collective-permute-start | bytes 798728 | tf_op jit(solution)/shard_map/ppermute | solution.py:500
  10.8 14.2 %collective-permute-start.1 = (bf16[1040,128]{1,0:T(8,128)(2,1)}, bf16[1040,128]{1,0:T(8,128)(2,1)S(1)}, u32[]{:S(2)}, u32[]{:S(2)}) collective-permute-start(bf16[1040,128]{1,0:T(8,128)(2,1)} %get-tuple-element.36), channel_id=1, source_target_pairs={{0,2},{2,4},{3,1},{4,6},{5,3},{6,8},{7,5},{8,10},{9,7},{10,12},{11... | collective-permute-start | bytes 798728 | tf_op jit(solution)/shard_map/ppermute | solution.py:500
  12.7 13.7 %collective-permute-start.2 = (bf16[1040,128]{1,0:T(8,128)(2,1)}, bf16[1040,128]{1,0:T(8,128)(2,1)S(1)}, u32[]{:S(2)}, u32[]{:S(2)}) collective-permute-start(bf16[1040,128]{1,0:T(8,128)(2,1)} %get-tuple-element.37), channel_id=1, source_target_pairs={{1,2},{2,1},{3,4},{4,3},{5,6},{6,5},{7,8},{8,7},{9,10},{10,9},{11,... | collective-permute-start | bytes 798728 | tf_op jit(solution)/shard_map/ppermute | solution.py:500
  15.6 10.9 %collective-permute-start.3 = (bf16[1040,128]{1,0:T(8,128)(2,1)}, bf16[1040,128]{1,0:T(8,128)(2,1)S(1)}, u32[]{:S(2)}, u32[]{:S(2)}) collective-permute-start(bf16[1040,128]{1,0:T(8,128)(2,1)} %get-tuple-element.38), channel_id=1, source_target_pairs={{0,1},{1,0},{2,3},{3,2},{4,5},{5,4},{6,7},{7,6},{8,9},{9,8},{10,11... | collective-permute-start | bytes 798728 | tf_op jit(solution)/shard_map/ppermute | solution.py:500
  15.6 1.4 %copy-start = (bf16[16,3,128,128]{3,2,1,0:T(8,128)(2,1)S(1)}, bf16[16,3,128,128]{3,2,1,0:T(8,128)(2,1)}, u32[]{:S(2)}) copy-start(bf16[16,3,128,128]{3,2,1,0:T(8,128)(2,1)} %off.5) | copy-start | bytes 4718596
  17.1 1.0 %copy-start.2 = (bf16[16,128,128]{2,1,0:T(8,128)(2,1)S(1)}, bf16[16,128,128]{2,1,0:T(8,128)(2,1)}, u32[]{:S(2)}) copy-start(bf16[16,128,128]{2,1,0:T(8,128)(2,1)} %tent.3) | copy-start | bytes 1572868
  18.1 1.0 %copy-start.3 = (bf16[16,128,128]{2,1,0:T(8,128)(2,1)S(1)}, bf16[16,128,128]{2,1,0:T(8,128)(2,1)}, u32[]{:S(2)}) copy-start(bf16[16,128,128]{2,1,0:T(8,128)(2,1)} %diag.5) | copy-start | bytes 1572868
  19.1 0.7 copy-start.6
  19.8 0.7 copy-start.8
  20.5 5.9 %copy-start.1 = (bf16[16,3,128,128]{3,2,1,0:T(8,128)(2,1)S(1)}, bf16[16,3,128,128]{3,2,1,0:T(8,128)(2,1)}, u32[]{:S(2)}) copy-start(bf16[16,3,128,128]{3,2,1,0:T(8,128)(2,1)} %off.5) | copy-start | bytes 4718596
  20.5 5.9 %copy-start.5 = (s32[4,4]{1,0:T(4,128)S(1)}, s32[4,4]{1,0:T(4,128)}, u32[]{:S(2)}) copy-start(s32[4,4]{1,0:T(4,128)} %send_rows.3) | copy-start | bytes 196
  20.5 5.9 %copy-start.7 = (s32[16,3]{0,1:T(4,128)S(1)}, s32[16,3]{0,1:T(4,128)}, u32[]{:S(2)}) copy-start(s32[16,3]{0,1:T(4,128)} %param.8) | copy-start | bytes 580
  31.3 12.4 %collective-permute-start.4 = (bf16[528,384]{1,0:T(8,128)(2,1)S(1)}, bf16[528,384]{1,0:T(8,128)(2,1)S(1)}, u32[]{:S(2)}, u32[]{:S(2)}) collective-permute-start(bf16[528,384]{1,0:T(8,128)(2,1)S(1)} %get-tuple-element.45), channel_id=1, source_target_pairs={{1,3},{2,0},{3,5},{4,2},{5,7},{6,4},{7,9},{8,6},{9,11},{10,8},{11,... | collective-permute-start | bytes 1216520 | tf_op jit(solution)/shard_map/ppermute | solution.py:500
  35.0 16.7 %collective-permute-start.5 = (bf16[528,384]{1,0:T(8,128)(2,1)S(1)}, bf16[528,384]{1,0:T(8,128)(2,1)S(1)}, u32[]{:S(2)}, u32[]{:S(2)}) collective-permute-start(bf16[528,384]{1,0:T(8,128)(2,1)S(1)} %get-tuple-element.46), channel_id=1, source_target_pairs={{0,2},{2,4},{3,1},{4,6},{5,3},{6,8},{7,5},{8,10},{9,7},{10,12},{11... | collective-permute-start | bytes 1216520 | tf_op jit(solution)/shard_map/ppermute | solution.py:500
  37.2 16.2 %collective-permute-start.6 = (bf16[528,384]{1,0:T(8,128)(2,1)S(1)}, bf16[528,384]{1,0:T(8,128)(2,1)S(1)}, u32[]{:S(2)}, u32[]{:S(2)}) collective-permute-start(bf16[528,384]{1,0:T(8,128)(2,1)S(1)} %get-tuple-element.47), channel_id=1, source_target_pairs={{1,2},{2,1},{3,4},{4,3},{5,6},{6,5},{7,8},{8,7},{9,10},{10,9},{11,... | collective-permute-start | bytes 1216520 | tf_op jit(solution)/shard_map/ppermute | solution.py:500
  40.9 12.4 %collective-permute-start.7 = (bf16[528,384]{1,0:T(8,128)(2,1)S(1)}, bf16[528,384]{1,0:T(8,128)(2,1)S(1)}, u32[]{:S(2)}, u32[]{:S(2)}) collective-permute-start(bf16[528,384]{1,0:T(8,128)(2,1)S(1)} %get-tuple-element.48), channel_id=1, source_target_pairs={{0,1},{1,0},{2,3},{3,2},{4,5},{5,4},{6,7},{7,6},{8,9},{9,8},{10,11... | collective-permute-start | bytes 1216520 | tf_op jit(solution)/shard_map/ppermute | solution.py:500
  41.0 12.4 %copy-start.4 = (bf16[16,128,128]{2,1,0:T(8,128)(2,1)S(1)}, bf16[16,128,128]{2,1,0:T(8,128)(2,1)}, u32[]{:S(2)}) copy-start(bf16[16,128,128]{2,1,0:T(8,128)(2,1)} %diag.5) | copy-start | bytes 1572868
  63.8 5.2 %collective-permute-start.8 = (bf16[2,128,2560]{2,1,0:T(8,128)(2,1)S(1)}, bf16[2,128,2560]{2,1,0:T(8,128)(2,1)S(1)}, u32[]{:S(2)}, u32[]{:S(2)}) collective-permute-start(bf16[2,128,2560]{2,1,0:T(8,128)(2,1)S(1)} %get-tuple-element.50), channel_id=1, source_target_pairs={{0,1},{1,0},{2,3},{3,2},{4,5},{5,4},{6,7},{7,6},{8,9},{9,8},{10,11... | collective-permute-start | bytes 3932168 | tf_op jit(solution)/shard_map/ppermute | solution.py:500
  63.8 26.4 %collective-permute-start.10 = (bf16[2,128,2304]{2,1,0:T(8,128)(2,1)S(1)}, bf16[2,128,2304]{2,1,0:T(8,128)(2,1)S(1)}, u32[]{:S(2)}, u32[]{:S(2)}) collective-permute-start(bf16[2,128,2304]{2,1,0:T(8,128)(2,1)S(1)} %get-tuple-element.54), channel_id=1, source_target_pairs={{1,3},{2,0},{3,5},{4,2},{5,7},{6,4},{7,9},{8,6},{9,11},{10,8},{11,... | collective-permute-start | bytes 3538952 | tf_op jit(solution)/shard_map/ppermute | solution.py:500
  71.0 28.7 %collective-permute-start.11 = (bf16[2,128,2560]{2,1,0:T(8,128)(2,1)S(1)}, bf16[2,128,2560]{2,1,0:T(8,128)(2,1)S(1)}, u32[]{:S(2)}, u32[]{:S(2)}) collective-permute-start(bf16[2,128,2560]{2,1,0:T(8,128)(2,1)S(1)} %pair_rows.1), channel_id=1, source_target_pairs={{0,2},{2,4},{3,1},{4,6},{5,3},{6,8},{7,5},{8,10},{9,7},{10,12},{11... | collective-permute-start | bytes 3932168 | tf_op jit(solution)/shard_map/ppermute | solution.py:500
  80.5 9.7 %collective-permute-start.9 = (bf16[2,128,2304]{2,1,0:T(8,128)(2,1)S(1)}, bf16[2,128,2304]{2,1,0:T(8,128)(2,1)S(1)}, u32[]{:S(2)}, u32[]{:S(2)}) collective-permute-start(bf16[2,128,2304]{2,1,0:T(8,128)(2,1)S(1)} %get-tuple-element.53), channel_id=1, source_target_pairs={{0,1},{1,0},{2,3},{3,2},{4,5},{5,4},{6,7},{7,6},{8,9},{9,8},{10,11... | collective-permute-start | bytes 3538952 | tf_op jit(solution)/shard_map/ppermute | solution.py:500

commit v6 on v5

--- a/solution.py
+++ b/solution.py
@@ -19,7 +19,7 @@
 BANDWIDE = 26 * BS
 TILES = [slice(t * 2 * BS, (t + 1) * 2 * BS) for t in range(FRAME // 2)]
 FAR_MB = 26
-GROUP = 4
+GROUP = 8
 CHUNK = 4
 EXTRA = 16
 BF = jnp.bfloat16
@@ -151,22 +151,24 @@
     table, labels_in, label_smem, sem,
 ):
     ghosts, sends = (g0, g1, g2, g3), (s0, s1, s2, s3)
-    copy = pltpu.make_async_copy(slots_in, slots.at[pl.ds(0, NB)], sem.at[0])
-    copy.start()
     arrivals = came_from(parity[0])
     for at, (n, offset) in enumerate(arrivals):
         row = ghosts[at][2 * NG * BS :, :].astype(F32).astype(jnp.int32)[:8]
         labels_in[n] = row + (8 - 2 * offset)
-    to_smem = pltpu.make_async_copy(labels_in, label_smem, sem.at[1])
+    to_smem = pltpu.make_async_copy(labels_in, label_smem, sem.at[0])
     to_smem.start()
     for at, (n, _) in enumerate(arrivals):
         for g in range(NG):
             table[n * NG + g] = ghosts[at][g * BS : (g + 1) * BS, :]
-    for i in range(NB):
+
+    def keep(i, carry):
+        slots[i] = slots_in[i]
         for k in range(4):
             labels[i, k] = local_labels[i, k]
+        return carry
+
+    lax.fori_loop(0, NB, keep, 0)
     to_smem.wait()
-    copy.wait()
 
     def group(q, carry):
         for u in range(GROUP):
@@ -204,7 +206,7 @@
             pltpu.VMEM((4 * NG, BS, BS), BF),
             pltpu.VMEM((4, 8, BS), jnp.int32),
             pltpu.SMEM((4, 8, BS), jnp.int32),
-            pltpu.SemaphoreType.DMA((2,)),
+            pltpu.SemaphoreType.DMA((1,)),
         ],
         compiler_params=pltpu.CompilerParams(vmem_limit_bytes=16 * 1024 * 1024),
         name="ghost_slots",
@@ -298,37 +300,25 @@
 def far_kernel(
     parity, off_columns, labels, lists, counts, diag, off, slots, blocks, first_slots, g0, g1, g2, g3,
     applied, direct, relay,
-    table, labels_in, labels_vmem, label_smem, total_a, total_b, coarse, sem_in, sem_lab,
+    table, labels_vmem, label_smem, total_a, total_b, coarse, sem,
 ):
     ghosts = (g0, g1, g2, g3)
-    copies = [
-        pltpu.make_async_copy(slots.at[pl.ds(0, NB)], table.at[pl.ds(0, NB)], sem_in.at[0]),
-        pltpu.make_async_copy(first_slots, table.at[pl.ds(NB, 4 * NG), :, pl.ds(0, BS)], sem_in.at[1]),
-    ]
     arrivals = came_from(parity[0])
+    for at, (n, offset) in enumerate(arrivals):
+        row = ghosts[at][NG * BS :, :BS].astype(F32).astype(jnp.int32)[:8]
+        labels_vmem[n] = row - 2 * offset
+    to_smem = pltpu.make_async_copy(labels_vmem, label_smem, sem.at[0])
+    to_smem.start()
+
+    def keep(i, carry):
+        table[i] = slots[i]
+        table[NB + i, :, :BS] = first_slots[i]
+        return carry
+
+    lax.fori_loop(0, NB, keep, 0)
     for at, (n, _) in enumerate(arrivals):
         for g in range(NG):
-            copies.append(
-                pltpu.make_async_copy(
-                    ghosts[at].at[pl.ds(g * BS, BS)],
-                    table.at[NB + n * NG + g, :, pl.ds(BS, SENDW)],
-                    sem_in.at[2 + at * NG + g],
-                )
-            )
-    lab = [
-        pltpu.make_async_copy(ghosts[n].at[pl.ds(NG * BS, EXTRA), pl.ds(0, BS)], labels_in.at[n], sem_lab.at[n])
-        for n in range(4)
-    ]
-    for copy in lab + copies:
-        copy.start()
-    for copy in lab:
-        copy.wait()
-    for at, (n, offset) in enumerate(arrivals):
-        labels_vmem[n] = labels_in[at].astype(F32).astype(jnp.int32)[:8] - 2 * offset
-    to_smem = pltpu.make_async_copy(labels_vmem, label_smem, sem_lab.at[0])
-    to_smem.start()
-    for copy in copies:
-        copy.wait()
+            table[NB + n * NG + g, :, BS:] = ghosts[at][g * BS : (g + 1) * BS, :]
     to_smem.wait()
 
     def label_of(j, m):
@@ -371,18 +361,16 @@
             jax.ShapeDtypeStruct((2, BS, WIDE), BF),
             jax.ShapeDtypeStruct((2, BS, CHIPWIDE), BF),
         ],
-        in_specs=[spec(SMEM)] * 5 + [spec(pltpu.VMEM)] * 2 + [spec(ANY), spec(pltpu.VMEM)] + [spec(ANY)] * 5,
+        in_specs=[spec(SMEM)] * 5 + [spec(pltpu.VMEM)] * 9,
         out_specs=[spec(pltpu.VMEM)] * 3,
         scratch_shapes=[
             pltpu.VMEM((NT, BS, SLOTW), BF),
-            pltpu.VMEM((4, EXTRA, BS), BF),
             pltpu.VMEM((4, 8, BS), jnp.int32),
             pltpu.SMEM((4, 8, BS), jnp.int32),
             pltpu.VMEM((FRAME, BS, BS), F32),
             pltpu.VMEM((FRAME, BS, BS), F32),
             pltpu.VMEM((2, BS, WIDE), F32),
-            pltpu.SemaphoreType.DMA((2 + 4 * NG,)),
-            pltpu.SemaphoreType.DMA((4,)),
+            pltpu.SemaphoreType.DMA((1,)),
         ],
         compiler_params=pltpu.CompilerParams(vmem_limit_bytes=FAR_MB * 1024 * 1024),
         cost_estimate=pl.CostEstimate(flops=4 * 10**9, bytes_accessed=20 * 10**6, transcendentals=0),

time: 102 us -> 101 us (level)
  Pallas kernels: 35.6 us -> 34.2 us
  transfers between devices with their start and end apart: 12 -> 12, of which waited for: 6 -> 7; matrix products, arithmetic and copies ran while one was open for 0% -> 0% of each run, Pallas kernels for 16% -> 16%
where the time goes in v6:
time: 101 us; the launch traced here: 100 us
  Pallas kernels  34.2 us (34%)
  starting transfers between devices  33.1 us (33%)
  waiting for transfers between devices  28.1 us (28%)
  local copies, waits for them, and re-layouts  4.84 us (5%)
    ppermute x12, starting transfers between devices, permute_by(): lax.ppermute(value, AXES, [(s, t) for s, t in pairs if 0 <= t < count])  33.1 us
    ppermute x12, waiting for transfers between devices, permute_by(): lax.ppermute(value, AXES, [(s, t) for s, t in pairs if 0 <= t < count])  28.1 us
    pallas_call x1, Pallas kernels, make_far(): pl.pallas_call(far_kernel, out_shape=[jax.ShapeDtypeStruct((NB, BS, WIDE)...  9.79 us
    pallas_call x1, Pallas kernels, make_near(): pl.pallas_call(near_kernel, out_shape=[jax.ShapeDtypeStruct((2, BS, WIDE)...  7.6 us
    unnamed x18, local copies, waits for them, and re-layouts  4.84 us
    pallas_call x1, Pallas kernels, ghost_slots(): pl.pallas_call(ghost_slots_kernel, out_shape=[jax.ShapeDtypeStruct((NB +...  4.06 us
    pallas_call x1, Pallas kernels, make_lists(): pl.pallas_call(lists_kernel, out_shape=[jax.ShapeDtypeStruct((10, 4 * NB...  2.65 us
    pallas_call x1, Pallas kernels, pack(): pl.pallas_call(pack_kernel, out_shape=[shape] * 4, in_specs=[spec(SMEM)]...  2.48 us
  transfers between devices with their start and end apart: 12, of which 7 were waited for; matrix products, arithmetic and copies ran while one was open for 0% of the time, Pallas kernels for 16%

profile of v6, /device:TPU:24, one launch (start us, length us, event | category | flops | bytes accessed | tf_op | source)
XLA Modules:
  0.0 100.4 jit_solution(3208758052950922782)
XLA Ops:
  0.0 2.5 %pack.1 = (bf16[1040,128]{1,0:T(8,128)(2,1)}, bf16[1040,128]{1,0:T(8,128)(2,1)}, bf16[1040,128]{1,0:T(8,128)(2,1)}, bf16[1040,128]{1,0:T(8,128)(2,1)}) custom-call(s32[1]{0:T(128)} %bitcast.parity, s32[4,4]{1,0:T(4,128)} %send_rows.3, s32[16]{0:T(128)} %aggregate.3, bf16[16,128,128]{2,1,0:T(8,128)(2,1)} %tent.3, bf16[16,128,128]{2,1,0:T(8,128)(2,1)} %diag.5), custom_call_target="tpu_custom_call" | custom-call | tf_op jit(solution)/shard_map/pack/pallas_call | solution.py:87
  2.5 8.3 %collective-permute-start = (bf16[1040,128]{1,0:T(8,128)(2,1)}, bf16[1040,128]{1,0:T(8,128)(2,1)S(1)}, u32[]{:S(2)}, u32[]{:S(2)}) collective-permute-start(bf16[1040,128]{1,0:T(8,128)(2,1)} %get-tuple-element.35), channel_id=1, source_target_pairs={{1,3},{2,0},{3,5},{4,2},{5,7},{6,4},{7,9},{8,6},{9,11},{10,8},{11,... | collective-permute-start | bytes 798728 | tf_op jit(solution)/shard_map/ppermute | solution.py:488
  10.8 1.9 %collective-permute-start.1 = (bf16[1040,128]{1,0:T(8,128)(2,1)}, bf16[1040,128]{1,0:T(8,128)(2,1)S(1)}, u32[]{:S(2)}, u32[]{:S(2)}) collective-permute-start(bf16[1040,128]{1,0:T(8,128)(2,1)} %get-tuple-element.36), channel_id=1, source_target_pairs={{0,2},{2,4},{3,1},{4,6},{5,3},{6,8},{7,5},{8,10},{9,7},{10,12},{11... | collective-permute-start | bytes 798728 | tf_op jit(solution)/shard_map/ppermute | solution.py:488
  12.7 2.8 %collective-permute-start.2 = (bf16[1040,128]{1,0:T(8,128)(2,1)}, bf16[1040,128]{1,0:T(8,128)(2,1)S(1)}, u32[]{:S(2)}, u32[]{:S(2)}) collective-permute-start(bf16[1040,128]{1,0:T(8,128)(2,1)} %get-tuple-element.37), channel_id=1, source_target_pairs={{1,2},{2,1},{3,4},{4,3},{5,6},{6,5},{7,8},{8,7},{9,10},{10,9},{11,... | collective-permute-start | bytes 798728 | tf_op jit(solution)/shard_map/ppermute | solution.py:488
  15.6 0.1 collective-permute-start.3
  15.6 0.0 copy-start
  15.7 1.4 %copy-done = bf16[16,3,128,128]{3,2,1,0:T(8,128)(2,1)S(1)} copy-done((bf16[16,3,128,128]{3,2,1,0:T(8,128)(2,1)S(1)}, bf16[16,3,128,128]{3,2,1,0:T(8,128)(2,1)}, u32[]{:S(2)}) %copy-start) | copy-done | bytes 1572888
  17.1 1.0 %copy-done.2 = bf16[16,128,128]{2,1,0:T(8,128)(2,1)S(1)} copy-done((bf16[16,128,128]{2,1,0:T(8,128)(2,1)S(1)}, bf16[16,128,128]{2,1,0:T(8,128)(2,1)}, u32[]{:S(2)}) %copy-start.2) | copy-done | bytes 524312
  18.1 0.0 copy-start.3
  18.1 1.0 %copy-done.3 = bf16[16,128,128]{2,1,0:T(8,128)(2,1)S(1)} copy-done((bf16[16,128,128]{2,1,0:T(8,128)(2,1)S(1)}, bf16[16,128,128]{2,1,0:T(8,128)(2,1)}, u32[]{:S(2)}) %copy-start.3) | copy-done | bytes 524312
  19.1 0.0 copy-start.6
  19.1 0.7 copy-done.6
  19.8 0.0 copy-start.8
  19.8 0.7 copy-done.8
  20.5 0.0 copy-start.1
  20.5 2.4 %local_slots.1 = (s32[16,4]{1,0:T(8,128)S(1)}, s32[56]{0:T(128)S(1)}, s32[1]{0:T(128)}, bf16[16,128,512]{2,1,0:T(8,128)(2,1)S(1)}, f32[16,128,128]{2,1,0:T(8,128)S(1)}) custom-call(s32[3,16]{1,0:T(4,128)S(1)} %bitcast.2, s32[16]{0:T(128)S(1)} %copy-done.8, bf16[16,128,128]{2,1,0:T(8,128)(2,1)S(1)} %copy-done.3, bf16[16,3,128,128]{3,2,1,0:T(8,128)(2,1)S(1)} %copy-done, ...), custom_call_target="tpu_custom_call" | custom-call | flops 1000000000 | bytes 6000000 | tf_op jit(solution)/shard_map/local_slots/pallas_call | solution.py:130
  22.9 0.0 collective-permute-done.g0
  22.9 2.1 %collective-permute-done.1.g1 = bf16[1040,128]{1,0:T(8,128)(2,1)S(1)} collective-permute-done((bf16[1040,128]{1,0:T(8,128)(2,1)}, bf16[1040,128]{1,0:T(8,128)(2,1)S(1)}, u32[]{:S(2)}, u32[]{:S(2)}) %collective-permute-start.1) | collective-permute-done | bytes 266272 | tf_op jit(solution)/shard_map/ppermute | solution.py:488
  25.0 1.4 %collective-permute-done.2.g2 = bf16[1040,128]{1,0:T(8,128)(2,1)S(1)} collective-permute-done((bf16[1040,128]{1,0:T(8,128)(2,1)}, bf16[1040,128]{1,0:T(8,128)(2,1)S(1)}, u32[]{:S(2)}, u32[]{:S(2)}) %collective-permute-start.2) | collective-permute-done | bytes 266272 | tf_op jit(solution)/shard_map/ppermute | solution.py:488
  26.4 0.0 collective-permute-done.3.g3
  26.4 0.0 copy-done.1
  26.4 0.0 copy-done.5
  26.4 0.0 copy-done.7
  26.4 4.1 %ghost_slots.1 = (s32[17,4]{1,0:T(8,128)S(1)}, bf16[17,128,512]{2,1,0:T(8,128)(2,1)S(1)}, bf16[528,384]{1,0:T(8,128)(2,1)S(1)}, bf16[528,384]{1,0:T(8,128)(2,1)S...) custom-call(s32[1]{0:T(128)} %bitcast.parity, s32[4,4]{1,0:T(4,128)S(1)} %copy-done.5, ...), custom_call_target="tpu_custom_call" | custom-call | tf_op jit(solution)/shard_map/ghost_slots/pallas_call | solution.py:196
  30.5 3.9 %collective-permute-start.4 = (bf16[528,384]{1,0:T(8,128)(2,1)S(1)}, bf16[528,384]{1,0:T(8,128)(2,1)S(1)}, u32[]{:S(2)}, u32[]{:S(2)}) collective-permute-start(bf16[528,384]{1,0:T(8,128)(2,1)S(1)} %get-tuple-element.45), channel_id=1, source_target_pairs={{1,3},{2,0},{3,5},{4,2},{5,7},{6,4},{7,9},{8,6},{9,11},{10,8},{11,... | collective-permute-start | bytes 1216520 | tf_op jit(solution)/shard_map/ppermute | solution.py:488
  34.4 2.0 %collective-permute-start.5 = (bf16[528,384]{1,0:T(8,128)(2,1)S(1)}, bf16[528,384]{1,0:T(8,128)(2,1)S(1)}, u32[]{:S(2)}, u32[]{:S(2)}) collective-permute-start(bf16[528,384]{1,0:T(8,128)(2,1)S(1)} %get-tuple-element.46), channel_id=1, source_target_pairs={{0,2},{2,4},{3,1},{4,6},{5,3},{6,8},{7,5},{8,10},{9,7},{10,12},{11... | collective-permute-start | bytes 1216520 | tf_op jit(solution)/shard_map/ppermute | solution.py:488
  36.4 3.3 %collective-permute-start.6 = (bf16[528,384]{1,0:T(8,128)(2,1)S(1)}, bf16[528,384]{1,0:T(8,128)(2,1)S(1)}, u32[]{:S(2)}, u32[]{:S(2)}) collective-permute-start(bf16[528,384]{1,0:T(8,128)(2,1)S(1)} %get-tuple-element.47), channel_id=1, source_target_pairs={{1,2},{2,1},{3,4},{4,3},{5,6},{6,5},{7,8},{8,7},{9,10},{10,9},{11,... | collective-permute-start | bytes 1216520 | tf_op jit(solution)/shard_map/ppermute | solution.py:488
  39.7 0.1 collective-permute-start.7
  39.8 0.0 copy-start.4
  39.8 2.6 %lists.1 = (s32[10,68]{1,0:T(8,128)S(1)}, s32[10]{0:T(128)S(1)}, bf16[65,128,128]{2,1,0:T(8,128)(2,1)S(1)}, bf16[16,128,128]{2,1,0:T(8,128)(2,1)S(1)}) custom-call(s32[1]{0:T(128)} %bitcast.parity, s32[17,4]{1,0:T(8,128)S(1)} %get-tuple-element.39.labels, bf16[17,128,512]{2,1,0:T(8,128)(2,1)S(1)} %get-tuple-element.40.slots, ...), custom_call_target="tpu_custom_call" | custom-call | flops 100000000 | bytes 6000000 | tf_op jit(solution)/shard_map/lists/pallas_call | solution.py:255
  42.4 0.3 collective-permute-done.4.g0
  42.8 8.5 %collective-permute-done.5.g1 = bf16[528,384]{1,0:T(8,128)(2,1)S(1)} collective-permute-done((bf16[528,384]{1,0:T(8,128)(2,1)S(1)}, bf16[528,384]{1,0:T(8,128)(2,1)S(1)}, u32[]{:S(2)}, u32[]{:S(2)}) %collective-permute-start.5) | collective-permute-done | bytes 405536 | tf_op jit(solution)/shard_map/ppermute | solution.py:488
  51.3 1.5 %collective-permute-done.6.g2 = bf16[528,384]{1,0:T(8,128)(2,1)S(1)} collective-permute-done((bf16[528,384]{1,0:T(8,128)(2,1)S(1)}, bf16[528,384]{1,0:T(8,128)(2,1)S(1)}, u32[]{:S(2)}, u32[]{:S(2)}) %collective-permute-start.6) | collective-permute-done | bytes 405536 | tf_op jit(solution)/shard_map/ppermute | solution.py:488
  52.8 0.0 collective-permute-done.7.g3
  52.8 0.0 copy-done.4
  52.8 9.8 %far_rows.1 = (bf16[16,128,2304]{2,1,0:T(8,128)(2,1)S(1)}, bf16[2,128,2304]{2,1,0:T(8,128)(2,1)S(1)}, bf16[2,128,2560]{2,1,0:T(8,128)(2,1)S(1)}) custom-call(s32[1]{0:T(128)} %bitcast.parity, s32[3,16]{1,0:T(4,128)S(1)} %bitcast.4, s32[17,4]{1,0:T(8,128)S(1)} %get-tuple-element.39.labels, s32[10,68]{1,0:T(8,128)S(1)} %get-tuple-element.41.lists, ...), custom_call_target="tpu_custom_call" | custom-call | flops 4000000000 | bytes 20000000 | tf_op jit(solution)/shard_map/far_rows/pallas_call | solution.py:357
  62.6 0.1 collective-permute-start.8
  62.6 3.2 %collective-permute-start.10 = (bf16[2,128,2304]{2,1,0:T(8,128)(2,1)S(1)}, bf16[2,128,2304]{2,1,0:T(8,128)(2,1)S(1)}, u32[]{:S(2)}, u32[]{:S(2)}) collective-permute-start(bf16[2,128,2304]{2,1,0:T(8,128)(2,1)S(1)} %get-tuple-element.54), channel_id=1, source_target_pairs={{1,3},{2,0},{3,5},{4,2},{5,7},{6,4},{7,9},{8,6},{9,11},{10,8},{11,... | collective-permute-start | bytes 3538952 | tf_op jit(solution)/shard_map/ppermute | solution.py:488
  65.8 0.0 collective-permute-done.8.relay
  65.8 2.0 %pair_rows.1 = bf16[2,128,2560]{2,1,0:T(8,128)(2,1)S(1)} custom-call(s32[1]{0:T(128)} %bitcast.parity, s32[10,68]{1,0:T(8,128)S(1)} %get-tuple-element.41.lists, s32[10]{0:T(128)S(1)} %get-tuple-element.42.counts, bf16[65,128,128]{2,1,0:T(8,128)(2,1)S(1)} %get-tuple-element.43.blocks, bf16[16,128,2304]{2,1,0:T(8,128)(2,1)S(1)} %get-tuple-element.51.applied, ...), custom_call_target="tpu_custom_call" | custom-call | flops 2000000000 | bytes 10000000 | tf_op jit(solution)/shard_map/pair_rows/pallas_call | solution.py:389
  67.9 2.7 %collective-permute-start.11 = (bf16[2,128,2560]{2,1,0:T(8,128)(2,1)S(1)}, bf16[2,128,2560]{2,1,0:T(8,128)(2,1)S(1)}, u32[]{:S(2)}, u32[]{:S(2)}) collective-permute-start(bf16[2,128,2560]{2,1,0:T(8,128)(2,1)S(1)} %pair_rows.1), channel_id=1, source_target_pairs={{0,2},{2,4},{3,1},{4,6},{5,3},{6,8},{7,5},{8,10},{9,7},{10,12},{11... | collective-permute-start | bytes 3932168 | tf_op jit(solution)/shard_map/ppermute | solution.py:488
  70.5 7.6 %near_rows.1 = (f32[2,128,2304]{2,1,0:T(8,128)S(1)}, bf16[2,128,2304]{2,1,0:T(8,128)(2,1)S(1)}) custom-call(s32[1]{0:T(128)} %bitcast.parity, s32[10,68]{1,0:T(8,128)S(1)} %get-tuple-element.41.lists, s32[10]{0:T(128)S(1)} %get-tuple-element.42.counts, bf16[65,128,128]{2,1,0:T(8,128)(2,1)S(1)} %get-tuple-element.43.blocks, ...), custom_call_target="tpu_custom_call" | custom-call | flops 4000000000 | bytes 20000000 | tf_op jit(solution)/shard_map/near_rows/pallas_call | solution.py:415
  78.1 4.8 %collective-permute-start.9 = (bf16[2,128,2304]{2,1,0:T(8,128)(2,1)S(1)}, bf16[2,128,2304]{2,1,0:T(8,128)(2,1)S(1)}, u32[]{:S(2)}, u32[]{:S(2)}) collective-permute-start(bf16[2,128,2304]{2,1,0:T(8,128)(2,1)S(1)} %get-tuple-element.53), channel_id=1, source_target_pairs={{0,1},{1,0},{2,3},{3,2},{4,5},{5,4},{6,7},{7,6},{8,9},{9,8},{10,11... | collective-permute-start | bytes 3538952 | tf_op jit(solution)/shard_map/ppermute | solution.py:488
  82.9 5.6 %collective-permute-done.10.direct = bf16[2,128,2304]{2,1,0:T(8,128)(2,1)S(1)} collective-permute-done((bf16[2,128,2304]{2,1,0:T(8,128)(2,1)S(1)}, bf16[2,128,2304]{2,1,0:T(8,128)(2,1)S(1)}, u32[]{:S(2)}, u32[]{:S(2)}) %collective-permute-start.10) | collective-permute-done | bytes 1179680 | tf_op jit(solution)/shard_map/ppermute | solution.py:488
  88.6 0.0 collective-permute-done.9.mate
  88.6 1.3 %add_near.1.band = f32[2,128,3328]{2,1,0:T(8,128)S(1)} custom-call(s32[1]{0:T(128)} %bitcast.parity, f32[2,128,2304]{2,1,0:T(8,128)S(1)} %get-tuple-element.52.own, bf16[2,128,2304]{2,1,0:T(8,128)(2,1)S(1)} %collective-permute-done.9.mate, bf16[2,128,2304]{2,1,0:T(8,128)(2,1)S(1)} %collective-permute-done.10.direct), custom_call_target="tpu_custom_call" | custom-call | flops 1000000 | bytes 9000000 | tf_op jit(solution)/shard_map/add_near/pallas_call | solution.py:446
  89.9 8.6 %collective-permute-done.11.pair = bf16[2,128,2560]{2,1,0:T(8,128)(2,1)S(1)} collective-permute-done((bf16[2,128,2560]{2,1,0:T(8,128)(2,1)S(1)}, bf16[2,128,2560]{2,1,0:T(8,128)(2,1)S(1)}, u32[]{:S(2)}, u32[]{:S(2)}) %collective-permute-start.11) | collective-permute-done | bytes 1310752 | tf_op jit(solution)/shard_map/ppermute | solution.py:488
  98.5 1.9 %add_pair.1 = f32[2,128,3328]{2,1,0:T(8,128)} custom-call(s32[1]{0:T(128)} %bitcast.parity, f32[2,128,3328]{2,1,0:T(8,128)S(1)} %add_near.1.band, bf16[2,128,2560]{2,1,0:T(8,128)(2,1)S(1)} %collective-permute-done.11.pair), custom_call_target="tpu_custom_call" | custom-call | tf_op jit(solution)/shard_map/add_pair/pallas_call | solution.py:474
  (3 shorter events, 0.0 us)
Async XLA Ops:
  2.5 20.4 %collective-permute-start = (bf16[1040,128]{1,0:T(8,128)(2,1)}, bf16[1040,128]{1,0:T(8,128)(2,1)S(1)}, u32[]{:S(2)}, u32[]{:S(2)}) collective-permute-start(bf16[1040,128]{1,0:T(8,128)(2,1)} %get-tuple-element.35), channel_id=1, source_target_pairs={{1,3},{2,0},{3,5},{4,2},{5,7},{6,4},{7,9},{8,6},{9,11},{10,8},{11,... | collective-permute-start | bytes 798728 | tf_op jit(solution)/shard_map/ppermute | solution.py:488
  10.8 14.2 %collective-permute-start.1 = (bf16[1040,128]{1,0:T(8,128)(2,1)}, bf16[1040,128]{1,0:T(8,128)(2,1)S(1)}, u32[]{:S(2)}, u32[]{:S(2)}) collective-permute-start(bf16[1040,128]{1,0:T(8,128)(2,1)} %get-tuple-element.36), channel_id=1, source_target_pairs={{0,2},{2,4},{3,1},{4,6},{5,3},{6,8},{7,5},{8,10},{9,7},{10,12},{11... | collective-permute-start | bytes 798728 | tf_op jit(solution)/shard_map/ppermute | solution.py:488
  12.7 13.7 %collective-permute-start.2 = (bf16[1040,128]{1,0:T(8,128)(2,1)}, bf16[1040,128]{1,0:T(8,128)(2,1)S(1)}, u32[]{:S(2)}, u32[]{:S(2)}) collective-permute-start(bf16[1040,128]{1,0:T(8,128)(2,1)} %get-tuple-element.37), channel_id=1, source_target_pairs={{1,2},{2,1},{3,4},{4,3},{5,6},{6,5},{7,8},{8,7},{9,10},{10,9},{11,... | collective-permute-start | bytes 798728 | tf_op jit(solution)/shard_map/ppermute | solution.py:488
  15.6 10.9 %collective-permute-start.3 = (bf16[1040,128]{1,0:T(8,128)(2,1)}, bf16[1040,128]{1,0:T(8,128)(2,1)S(1)}, u32[]{:S(2)}, u32[]{:S(2)}) collective-permute-start(bf16[1040,128]{1,0:T(8,128)(2,1)} %get-tuple-element.38), channel_id=1, source_target_pairs={{0,1},{1,0},{2,3},{3,2},{4,5},{5,4},{6,7},{7,6},{8,9},{9,8},{10,11... | collective-permute-start | bytes 798728 | tf_op jit(solution)/shard_map/ppermute | solution.py:488
  15.6 1.4 %copy-start = (bf16[16,3,128,128]{3,2,1,0:T(8,128)(2,1)S(1)}, bf16[16,3,128,128]{3,2,1,0:T(8,128)(2,1)}, u32[]{:S(2)}) copy-start(bf16[16,3,128,128]{3,2,1,0:T(8,128)(2,1)} %off.5) | copy-start | bytes 4718596
  17.1 1.0 %copy-start.2 = (bf16[16,128,128]{2,1,0:T(8,128)(2,1)S(1)}, bf16[16,128,128]{2,1,0:T(8,128)(2,1)}, u32[]{:S(2)}) copy-start(bf16[16,128,128]{2,1,0:T(8,128)(2,1)} %tent.3) | copy-start | bytes 1572868
  18.1 1.0 %copy-start.3 = (bf16[16,128,128]{2,1,0:T(8,128)(2,1)S(1)}, bf16[16,128,128]{2,1,0:T(8,128)(2,1)}, u32[]{:S(2)}) copy-start(bf16[16,128,128]{2,1,0:T(8,128)(2,1)} %diag.5) | copy-start | bytes 1572868
  19.1 0.7 copy-start.6
  19.8 0.7 copy-start.8
  20.5 5.9 %copy-start.1 = (bf16[16,3,128,128]{3,2,1,0:T(8,128)(2,1)S(1)}, bf16[16,3,128,128]{3,2,1,0:T(8,128)(2,1)}, u32[]{:S(2)}) copy-start(bf16[16,3,128,128]{3,2,1,0:T(8,128)(2,1)} %off.5) | copy-start | bytes 4718596
  20.5 5.9 %copy-start.5 = (s32[4,4]{1,0:T(4,128)S(1)}, s32[4,4]{1,0:T(4,128)}, u32[]{:S(2)}) copy-start(s32[4,4]{1,0:T(4,128)} %send_rows.3) | copy-start | bytes 196
  20.5 5.9 %copy-start.7 = (s32[16,3]{0,1:T(4,128)S(1)}, s32[16,3]{0,1:T(4,128)}, u32[]{:S(2)}) copy-start(s32[16,3]{0,1:T(4,128)} %param.8) | copy-start | bytes 580
  30.5 12.3 %collective-permute-start.4 = (bf16[528,384]{1,0:T(8,128)(2,1)S(1)}, bf16[528,384]{1,0:T(8,128)(2,1)S(1)}, u32[]{:S(2)}, u32[]{:S(2)}) collective-permute-start(bf16[528,384]{1,0:T(8,128)(2,1)S(1)} %get-tuple-element.45), channel_id=1, source_target_pairs={{1,3},{2,0},{3,5},{4,2},{5,7},{6,4},{7,9},{8,6},{9,11},{10,8},{11,... | collective-permute-start | bytes 1216520 | tf_op jit(solution)/shard_map/ppermute | solution.py:488
  34.4 16.9 %collective-permute-start.5 = (bf16[528,384]{1,0:T(8,128)(2,1)S(1)}, bf16[528,384]{1,0:T(8,128)(2,1)S(1)}, u32[]{:S(2)}, u32[]{:S(2)}) collective-permute-start(bf16[528,384]{1,0:T(8,128)(2,1)S(1)} %get-tuple-element.46), channel_id=1, source_target_pairs={{0,2},{2,4},{3,1},{4,6},{5,3},{6,8},{7,5},{8,10},{9,7},{10,12},{11... | collective-permute-start | bytes 1216520 | tf_op jit(solution)/shard_map/ppermute | solution.py:488
  36.4 16.4 %collective-permute-start.6 = (bf16[528,384]{1,0:T(8,128)(2,1)S(1)}, bf16[528,384]{1,0:T(8,128)(2,1)S(1)}, u32[]{:S(2)}, u32[]{:S(2)}) collective-permute-start(bf16[528,384]{1,0:T(8,128)(2,1)S(1)} %get-tuple-element.47), channel_id=1, source_target_pairs={{1,2},{2,1},{3,4},{4,3},{5,6},{6,5},{7,8},{8,7},{9,10},{10,9},{11,... | collective-permute-start | bytes 1216520 | tf_op jit(solution)/shard_map/ppermute | solution.py:488
  39.7 13.1 %collective-permute-start.7 = (bf16[528,384]{1,0:T(8,128)(2,1)S(1)}, bf16[528,384]{1,0:T(8,128)(2,1)S(1)}, u32[]{:S(2)}, u32[]{:S(2)}) collective-permute-start(bf16[528,384]{1,0:T(8,128)(2,1)S(1)} %get-tuple-element.48), channel_id=1, source_target_pairs={{0,1},{1,0},{2,3},{3,2},{4,5},{5,4},{6,7},{7,6},{8,9},{9,8},{10,11... | collective-permute-start | bytes 1216520 | tf_op jit(solution)/shard_map/ppermute | solution.py:488
  39.8 13.0 %copy-start.4 = (bf16[16,128,128]{2,1,0:T(8,128)(2,1)S(1)}, bf16[16,128,128]{2,1,0:T(8,128)(2,1)}, u32[]{:S(2)}) copy-start(bf16[16,128,128]{2,1,0:T(8,128)(2,1)} %diag.5) | copy-start | bytes 1572868
  62.6 3.3 %collective-permute-start.8 = (bf16[2,128,2560]{2,1,0:T(8,128)(2,1)S(1)}, bf16[2,128,2560]{2,1,0:T(8,128)(2,1)S(1)}, u32[]{:S(2)}, u32[]{:S(2)}) collective-permute-start(bf16[2,128,2560]{2,1,0:T(8,128)(2,1)S(1)} %get-tuple-element.50), channel_id=1, source_target_pairs={{0,1},{1,0},{2,3},{3,2},{4,5},{5,4},{6,7},{7,6},{8,9},{9,8},{10,11... | collective-permute-start | bytes 3932168 | tf_op jit(solution)/shard_map/ppermute | solution.py:488
  62.6 25.9 %collective-permute-start.10 = (bf16[2,128,2304]{2,1,0:T(8,128)(2,1)S(1)}, bf16[2,128,2304]{2,1,0:T(8,128)(2,1)S(1)}, u32[]{:S(2)}, u32[]{:S(2)}) collective-permute-start(bf16[2,128,2304]{2,1,0:T(8,128)(2,1)S(1)} %get-tuple-element.54), channel_id=1, source_target_pairs={{1,3},{2,0},{3,5},{4,2},{5,7},{6,4},{7,9},{8,6},{9,11},{10,8},{11,... | collective-permute-start | bytes 3538952 | tf_op jit(solution)/shard_map/ppermute | solution.py:488
  67.9 30.7 %collective-permute-start.11 = (bf16[2,128,2560]{2,1,0:T(8,128)(2,1)S(1)}, bf16[2,128,2560]{2,1,0:T(8,128)(2,1)S(1)}, u32[]{:S(2)}, u32[]{:S(2)}) collective-permute-start(bf16[2,128,2560]{2,1,0:T(8,128)(2,1)S(1)} %pair_rows.1), channel_id=1, source_target_pairs={{0,2},{2,4},{3,1},{4,6},{5,3},{6,8},{7,5},{8,10},{9,7},{10,12},{11... | collective-permute-start | bytes 3932168 | tf_op jit(solution)/shard_map/ppermute | solution.py:488
  78.1 10.4 %collective-permute-start.9 = (bf16[2,128,2304]{2,1,0:T(8,128)(2,1)S(1)}, bf16[2,128,2304]{2,1,0:T(8,128)(2,1)S(1)}, u32[]{:S(2)}, u32[]{:S(2)}) collective-permute-start(bf16[2,128,2304]{2,1,0:T(8,128)(2,1)S(1)} %get-tuple-element.53), channel_id=1, source_target_pairs={{0,1},{1,0},{2,3},{3,2},{4,5},{5,4},{6,7},{7,6},{8,9},{9,8},{10,11... | collective-permute-start | bytes 3538952 | tf_op jit(solution)/shard_map/ppermute | solution.py:488

commit v7 on v6

--- a/solution.py
+++ b/solution.py
@@ -7,6 +7,8 @@
 
 AXES = ("bulk", "coarse")
 STEPS = ((-2, 2), (2, -2), (-1, 1), (1, -1))
+TENT_ORDER = (0, 1, 2, 3)
+SLOT_ORDER = (0, 2, 1, 3)
 BS = 128
 NB = 16
 NG = 4
@@ -33,17 +35,19 @@
     return pl.BlockSpec(memory_space=space)
 
 
-def sent_to(odd):
-    return (3 - odd, 2 + odd, 1 - odd, odd)
-
-
-def came_from(odd):
-    return (
+def sent_to(odd, order):
+    all_four = (3 - odd, 2 + odd, 1 - odd, odd)
+    return [all_four[at] for at in order]
+
+
+def came_from(odd, order):
+    all_four = (
         (3 - odd, 4 * odd - 2),
         (2 + odd, 2 - 4 * odd),
         (odd, 1 - 2 * odd),
         (1 - odd, 2 * odd - 1),
     )
+    return [all_four[at] for at in order]
 
 
 def label_rows(values, width):
@@ -56,7 +60,7 @@
 
 def pack_kernel(parity, send_rows, aggregate, tent, diag, *refs):
     outs, labels, sem = refs[:4], refs[4], refs[5]
-    targets = sent_to(parity[0])
+    targets = sent_to(parity[0], TENT_ORDER)
     copies = []
     for at, n in enumerate(targets):
         for g in range(NG):
@@ -151,7 +155,7 @@
     table, labels_in, label_smem, sem,
 ):
     ghosts, sends = (g0, g1, g2, g3), (s0, s1, s2, s3)
-    arrivals = came_from(parity[0])
+    arrivals = came_from(parity[0], TENT_ORDER)
     for at, (n, offset) in enumerate(arrivals):
         row = ghosts[at][2 * NG * BS :, :].astype(F32).astype(jnp.int32)[:8]
         labels_in[n] = row + (8 - 2 * offset)
@@ -184,7 +188,7 @@
 
     lax.fori_loop(0, lax.div(ghost_count[0] + GROUP - 1, GROUP), group, 0)
 
-    for at, n in enumerate(sent_to(parity[0])):
+    for at, n in enumerate(sent_to(parity[0], SLOT_ORDER)):
         for g in range(NG):
             sends[at][g * BS : (g + 1) * BS, :] = slots[send_rows[n, g], :, BS:]
         values = [labels[send_rows[n, g], k] for g in range(NG) for k in range(4)]
@@ -244,7 +248,7 @@
         copy.wait()
     eye = lax.broadcasted_iota(jnp.int32, (BS, BS), 0) == lax.broadcasted_iota(jnp.int32, (BS, BS), 1)
 
-    for at, (n, _) in enumerate(came_from(parity[0])):
+    for at, (n, _) in enumerate(came_from(parity[0], TENT_ORDER)):
         for g in range(NG):
             first_slots[n * NG + g] = first_slot(
                 eye, ghost_buf[at, (NG + g) * BS : (NG + g + 1) * BS], ghost_buf[at, g * BS : (g + 1) * BS]
@@ -303,7 +307,7 @@
     table, labels_vmem, label_smem, total_a, total_b, coarse, sem,
 ):
     ghosts = (g0, g1, g2, g3)
-    arrivals = came_from(parity[0])
+    arrivals = came_from(parity[0], SLOT_ORDER)
     for at, (n, offset) in enumerate(arrivals):
         row = ghosts[at][NG * BS :, :BS].astype(F32).astype(jnp.int32)[:8]
         labels_vmem[n] = row - 2 * offset
@@ -488,15 +492,15 @@
     return lax.ppermute(value, AXES, [(s, t) for s, t in pairs if 0 <= t < count])
 
 
-def exchange(sends):
-    return [permute_by(value, *steps) for value, steps in zip(sends, STEPS)]
+def exchange(sends, order):
+    return [permute_by(value, *STEPS[at]) for value, at in zip(sends, order)]
 
 
 def local(diag_blocks, off_blocks, off_columns, tentative, aggregate, send_rows):
     off_columns = off_columns.T
     odd = lax.rem(lax.axis_index(AXES), 2)
     parity = odd.reshape(1)
-    ghosts = exchange(pack(parity, send_rows, aggregate, tentative, diag_blocks))
+    ghosts = exchange(pack(parity, send_rows, aggregate, tentative, diag_blocks), TENT_ORDER)
     labels, ghost_list, ghost_count, slots, scales = local_slots(
         off_columns, aggregate, diag_blocks, off_blocks, tentative
     )
@@ -504,7 +508,7 @@
         parity, send_rows, off_columns, labels, ghost_list, ghost_count, off_blocks, slots, scales, ghosts
     )
     lists, counts, blocks, first_slots = make_lists(parity, labels, slots, ghosts)
-    ghosts = exchange(sends)
+    ghosts = exchange(sends, SLOT_ORDER)
     applied, direct, relay = make_far(
         parity, off_columns, labels, lists, counts, diag_blocks, off_blocks, slots, blocks, first_slots, ghosts
     )

time: 101 us -> 101 us (level)
  waiting for transfers between devices: 28.1 us -> 22.9 us
  starting transfers between devices: 33.1 us -> 37.2 us
    ppermute x12, waiting for transfers between devices: 28.1 us -> 22.9 us  [permute_by(): lax.ppermute(value, AXES, [(s, t) for s, t in pairs if 0 <= t < count])]
    ppermute x12, starting transfers between devices: 33.1 us -> 37.2 us  [permute_by(): lax.ppermute(value, AXES, [(s, t) for s, t in pairs if 0 <= t < count])]
  transfers between devices with their start and end apart: 12 -> 12, of which waited for: 7 -> 6; matrix products, arithmetic and copies ran while one was open for 0% -> 0% of each run, Pallas kernels for 16% -> 16%
where the time goes in v7:
time: 101 us; the launch traced here: 99.8 us
  starting transfers between devices  37.2 us (37%)
  Pallas kernels  34.6 us (34%)
  waiting for transfers between devices  22.9 us (23%)
  local copies, waits for them, and re-layouts  4.84 us (5%)
    ppermute x12, starting transfers between devices, permute_by(): lax.ppermute(value, AXES, [(s, t) for s, t in pairs if 0 <= t < count])  37.2 us
    ppermute x12, waiting for transfers between devices, permute_by(): lax.ppermute(value, AXES, [(s, t) for s, t in pairs if 0 <= t < count])  22.9 us
    pallas_call x1, Pallas kernels, make_far(): pl.pallas_call(far_kernel, out_shape=[jax.ShapeDtypeStruct((NB, BS, WIDE)...  9.78 us
    pallas_call x1, Pallas kernels, make_near(): pl.pallas_call(near_kernel, out_shape=[jax.ShapeDtypeStruct((2, BS, WIDE)...  8.08 us
    unnamed x18, local copies, waits for them, and re-layouts  4.84 us
    pallas_call x1, Pallas kernels, ghost_slots(): pl.pallas_call(ghost_slots_kernel, out_shape=[jax.ShapeDtypeStruct((NB +...  4.06 us
    pallas_call x1, Pallas kernels, make_lists(): pl.pallas_call(lists_kernel, out_shape=[jax.ShapeDtypeStruct((10, 4 * NB...  2.64 us
    pallas_call x1, Pallas kernels, pack(): pl.pallas_call(pack_kernel, out_shape=[shape] * 4, in_specs=[spec(SMEM)]...  2.48 us
  transfers between devices with their start and end apart: 12, of which 6 were waited for; matrix products, arithmetic and copies ran while one was open for 0% of the time, Pallas kernels for 16%

profile of v7, /device:TPU:24, one launch (start us, length us, event | category | flops | bytes accessed | tf_op | source)
XLA Modules:
  0.0 99.8 jit_solution(601920790847318756)
XLA Ops:
  0.0 2.5 %pack.1 = (bf16[1040,128]{1,0:T(8,128)(2,1)}, bf16[1040,128]{1,0:T(8,128)(2,1)}, bf16[1040,128]{1,0:T(8,128)(2,1)}, bf16[1040,128]{1,0:T(8,128)(2,1)}) custom-call(s32[1]{0:T(128)} %bitcast.parity, s32[4,4]{1,0:T(4,128)} %send_rows.3, s32[16]{0:T(128)} %aggregate.3, bf16[16,128,128]{2,1,0:T(8,128)(2,1)} %tent.3, bf16[16,128,128]{2,1,0:T(8,128)(2,1)} %diag.5), custom_call_target="tpu_custom_call" | custom-call | tf_op jit(solution)/shard_map/pack/pallas_call | solution.py:91
  2.5 8.3 %collective-permute-start = (bf16[1040,128]{1,0:T(8,128)(2,1)}, bf16[1040,128]{1,0:T(8,128)(2,1)S(1)}, u32[]{:S(2)}, u32[]{:S(2)}) collective-permute-start(bf16[1040,128]{1,0:T(8,128)(2,1)} %get-tuple-element.35), channel_id=1, source_target_pairs={{1,3},{2,0},{3,5},{4,2},{5,7},{6,4},{7,9},{8,6},{9,11},{10,8},{11,... | collective-permute-start | bytes 798728 | tf_op jit(solution)/shard_map/ppermute | solution.py:492
  10.8 1.9 %collective-permute-start.1 = (bf16[1040,128]{1,0:T(8,128)(2,1)}, bf16[1040,128]{1,0:T(8,128)(2,1)S(1)}, u32[]{:S(2)}, u32[]{:S(2)}) collective-permute-start(bf16[1040,128]{1,0:T(8,128)(2,1)} %get-tuple-element.36), channel_id=1, source_target_pairs={{0,2},{2,4},{3,1},{4,6},{5,3},{6,8},{7,5},{8,10},{9,7},{10,12},{11... | collective-permute-start | bytes 798728 | tf_op jit(solution)/shard_map/ppermute | solution.py:492
  12.7 2.8 %collective-permute-start.2 = (bf16[1040,128]{1,0:T(8,128)(2,1)}, bf16[1040,128]{1,0:T(8,128)(2,1)S(1)}, u32[]{:S(2)}, u32[]{:S(2)}) collective-permute-start(bf16[1040,128]{1,0:T(8,128)(2,1)} %get-tuple-element.37), channel_id=1, source_target_pairs={{1,2},{2,1},{3,4},{4,3},{5,6},{6,5},{7,8},{8,7},{9,10},{10,9},{11,... | collective-permute-start | bytes 798728 | tf_op jit(solution)/shard_map/ppermute | solution.py:492
  15.6 0.1 collective-permute-start.3
  15.6 0.0 copy-start
  15.7 1.4 %copy-done = bf16[16,3,128,128]{3,2,1,0:T(8,128)(2,1)S(1)} copy-done((bf16[16,3,128,128]{3,2,1,0:T(8,128)(2,1)S(1)}, bf16[16,3,128,128]{3,2,1,0:T(8,128)(2,1)}, u32[]{:S(2)}) %copy-start) | copy-done | bytes 1572888
  17.1 0.0 copy-start.2
  17.1 1.0 %copy-done.2 = bf16[16,128,128]{2,1,0:T(8,128)(2,1)S(1)} copy-done((bf16[16,128,128]{2,1,0:T(8,128)(2,1)S(1)}, bf16[16,128,128]{2,1,0:T(8,128)(2,1)}, u32[]{:S(2)}) %copy-start.2) | copy-done | bytes 524312
  18.1 0.0 copy-start.3
  18.1 1.0 %copy-done.3 = bf16[16,128,128]{2,1,0:T(8,128)(2,1)S(1)} copy-done((bf16[16,128,128]{2,1,0:T(8,128)(2,1)S(1)}, bf16[16,128,128]{2,1,0:T(8,128)(2,1)}, u32[]{:S(2)}) %copy-start.3) | copy-done | bytes 524312
  19.1 0.0 copy-start.6
  19.1 0.7 copy-done.6
  19.8 0.0 copy-start.8
  19.8 0.7 copy-done.8
  20.5 0.0 copy-start.1
  20.5 2.4 %local_slots.1 = (s32[16,4]{1,0:T(8,128)S(1)}, s32[56]{0:T(128)S(1)}, s32[1]{0:T(128)}, bf16[16,128,512]{2,1,0:T(8,128)(2,1)S(1)}, f32[16,128,128]{2,1,0:T(8,128)S(1)}) custom-call(s32[3,16]{1,0:T(4,128)S(1)} %bitcast.2, s32[16]{0:T(128)S(1)} %copy-done.8, bf16[16,128,128]{2,1,0:T(8,128)(2,1)S(1)} %copy-done.3, bf16[16,3,128,128]{3,2,1,0:T(8,128)(2,1)S(1)} %copy-done, ...), custom_call_target="tpu_custom_call" | custom-call | flops 1000000000 | bytes 6000000 | tf_op jit(solution)/shard_map/local_slots/pallas_call | solution.py:134
  22.9 0.0 collective-permute-done.g0
  22.9 2.1 %collective-permute-done.1.g1 = bf16[1040,128]{1,0:T(8,128)(2,1)S(1)} collective-permute-done((bf16[1040,128]{1,0:T(8,128)(2,1)}, bf16[1040,128]{1,0:T(8,128)(2,1)S(1)}, u32[]{:S(2)}, u32[]{:S(2)}) %collective-permute-start.1) | collective-permute-done | bytes 266272 | tf_op jit(solution)/shard_map/ppermute | solution.py:492
  25.0 1.4 %collective-permute-done.2.g2 = bf16[1040,128]{1,0:T(8,128)(2,1)S(1)} collective-permute-done((bf16[1040,128]{1,0:T(8,128)(2,1)}, bf16[1040,128]{1,0:T(8,128)(2,1)S(1)}, u32[]{:S(2)}, u32[]{:S(2)}) %collective-permute-start.2) | collective-permute-done | bytes 266272 | tf_op jit(solution)/shard_map/ppermute | solution.py:492
  26.4 0.0 collective-permute-done.3.g3
  26.4 0.0 copy-done.1
  26.4 0.0 copy-done.5
  26.4 0.0 copy-done.7
  26.4 4.1 %ghost_slots.1 = (s32[17,4]{1,0:T(8,128)S(1)}, bf16[17,128,512]{2,1,0:T(8,128)(2,1)S(1)}, bf16[528,384]{1,0:T(8,128)(2,1)S(1)}, bf16[528,384]{1,0:T(8,128)(2,1)S...) custom-call(s32[1]{0:T(128)} %bitcast.parity, s32[4,4]{1,0:T(4,128)S(1)} %copy-done.5, ...), custom_call_target="tpu_custom_call" | custom-call | tf_op jit(solution)/shard_map/ghost_slots/pallas_call | solution.py:200
  30.5 3.9 %collective-permute-start.4 = (bf16[528,384]{1,0:T(8,128)(2,1)S(1)}, bf16[528,384]{1,0:T(8,128)(2,1)S(1)}, u32[]{:S(2)}, u32[]{:S(2)}) collective-permute-start(bf16[528,384]{1,0:T(8,128)(2,1)S(1)} %get-tuple-element.45), channel_id=1, source_target_pairs={{1,3},{2,0},{3,5},{4,2},{5,7},{6,4},{7,9},{8,6},{9,11},{10,8},{11,... | collective-permute-start | bytes 1216520 | tf_op jit(solution)/shard_map/ppermute | solution.py:492
  34.4 2.5 %collective-permute-start.5 = (bf16[528,384]{1,0:T(8,128)(2,1)S(1)}, bf16[528,384]{1,0:T(8,128)(2,1)S(1)}, u32[]{:S(2)}, u32[]{:S(2)}) collective-permute-start(bf16[528,384]{1,0:T(8,128)(2,1)S(1)} %get-tuple-element.46), channel_id=1, source_target_pairs={{1,2},{2,1},{3,4},{4,3},{5,6},{6,5},{7,8},{8,7},{9,10},{10,9},{11,... | collective-permute-start | bytes 1216520 | tf_op jit(solution)/shard_map/ppermute | solution.py:492
  36.9 1.9 %collective-permute-start.6 = (bf16[528,384]{1,0:T(8,128)(2,1)S(1)}, bf16[528,384]{1,0:T(8,128)(2,1)S(1)}, u32[]{:S(2)}, u32[]{:S(2)}) collective-permute-start(bf16[528,384]{1,0:T(8,128)(2,1)S(1)} %get-tuple-element.47), channel_id=1, source_target_pairs={{0,2},{2,4},{3,1},{4,6},{5,3},{6,8},{7,5},{8,10},{9,7},{10,12},{11... | collective-permute-start | bytes 1216520 | tf_op jit(solution)/shard_map/ppermute | solution.py:492
  38.8 5.5 %collective-permute-start.7 = (bf16[528,384]{1,0:T(8,128)(2,1)S(1)}, bf16[528,384]{1,0:T(8,128)(2,1)S(1)}, u32[]{:S(2)}, u32[]{:S(2)}) collective-permute-start(bf16[528,384]{1,0:T(8,128)(2,1)S(1)} %get-tuple-element.48), channel_id=1, source_target_pairs={{0,1},{1,0},{2,3},{3,2},{4,5},{5,4},{6,7},{7,6},{8,9},{9,8},{10,11... | collective-permute-start | bytes 1216520 | tf_op jit(solution)/shard_map/ppermute | solution.py:492
  44.4 2.6 %lists.1 = (s32[10,68]{1,0:T(8,128)S(1)}, s32[10]{0:T(128)S(1)}, bf16[65,128,128]{2,1,0:T(8,128)(2,1)S(1)}, bf16[16,128,128]{2,1,0:T(8,128)(2,1)S(1)}) custom-call(s32[1]{0:T(128)} %bitcast.parity, s32[17,4]{1,0:T(8,128)S(1)} %get-tuple-element.39.labels, bf16[17,128,512]{2,1,0:T(8,128)(2,1)S(1)} %get-tuple-element.40.slots, ...), custom_call_target="tpu_custom_call" | custom-call | flops 100000000 | bytes 6000000 | tf_op jit(solution)/shard_map/lists/pallas_call | solution.py:259
  47.0 0.0 collective-permute-done.4.g0
  47.0 2.0 %collective-permute-done.5.g1 = bf16[528,384]{1,0:T(8,128)(2,1)S(1)} collective-permute-done((bf16[528,384]{1,0:T(8,128)(2,1)S(1)}, bf16[528,384]{1,0:T(8,128)(2,1)S(1)}, u32[]{:S(2)}, u32[]{:S(2)}) %collective-permute-start.5) | collective-permute-done | bytes 405536 | tf_op jit(solution)/shard_map/ppermute | solution.py:492
  49.0 3.2 %collective-permute-done.6.g2 = bf16[528,384]{1,0:T(8,128)(2,1)S(1)} collective-permute-done((bf16[528,384]{1,0:T(8,128)(2,1)S(1)}, bf16[528,384]{1,0:T(8,128)(2,1)S(1)}, u32[]{:S(2)}, u32[]{:S(2)}) %collective-permute-start.6) | collective-permute-done | bytes 405536 | tf_op jit(solution)/shard_map/ppermute | solution.py:492
  52.2 0.0 collective-permute-done.7.g3
  52.2 0.0 copy-done.4
  52.2 9.8 %far_rows.1 = (bf16[16,128,2304]{2,1,0:T(8,128)(2,1)S(1)}, bf16[2,128,2304]{2,1,0:T(8,128)(2,1)S(1)}, bf16[2,128,2560]{2,1,0:T(8,128)(2,1)S(1)}) custom-call(s32[1]{0:T(128)} %bitcast.parity, s32[3,16]{1,0:T(4,128)S(1)} %bitcast.4, s32[17,4]{1,0:T(8,128)S(1)} %get-tuple-element.39.labels, s32[10,68]{1,0:T(8,128)S(1)} %get-tuple-element.41.lists, ...), custom_call_target="tpu_custom_call" | custom-call | flops 4000000000 | bytes 20000000 | tf_op jit(solution)/shard_map/far_rows/pallas_call | solution.py:361
  62.0 0.1 collective-permute-start.8
  62.1 6.2 %collective-permute-start.10 = (bf16[2,128,2304]{2,1,0:T(8,128)(2,1)S(1)}, bf16[2,128,2304]{2,1,0:T(8,128)(2,1)S(1)}, u32[]{:S(2)}, u32[]{:S(2)}) collective-permute-start(bf16[2,128,2304]{2,1,0:T(8,128)(2,1)S(1)} %get-tuple-element.54), channel_id=1, source_target_pairs={{1,3},{2,0},{3,5},{4,2},{5,7},{6,4},{7,9},{8,6},{9,11},{10,8},{11,... | collective-permute-start | bytes 3538952 | tf_op jit(solution)/shard_map/ppermute | solution.py:492
  68.3 0.0 collective-permute-done.8.relay
  68.3 2.0 %pair_rows.1 = bf16[2,128,2560]{2,1,0:T(8,128)(2,1)S(1)} custom-call(s32[1]{0:T(128)} %bitcast.parity, s32[10,68]{1,0:T(8,128)S(1)} %get-tuple-element.41.lists, s32[10]{0:T(128)S(1)} %get-tuple-element.42.counts, bf16[65,128,128]{2,1,0:T(8,128)(2,1)S(1)} %get-tuple-element.43.blocks, bf16[16,128,2304]{2,1,0:T(8,128)(2,1)S(1)} %get-tuple-element.51.applied, ...), custom_call_target="tpu_custom_call" | custom-call | flops 2000000000 | bytes 10000000 | tf_op jit(solution)/shard_map/pair_rows/pallas_call | solution.py:393
  70.3 1.9 %collective-permute-start.11 = (bf16[2,128,2560]{2,1,0:T(8,128)(2,1)S(1)}, bf16[2,128,2560]{2,1,0:T(8,128)(2,1)S(1)}, u32[]{:S(2)}, u32[]{:S(2)}) collective-permute-start(bf16[2,128,2560]{2,1,0:T(8,128)(2,1)S(1)} %pair_rows.1), channel_id=1, source_target_pairs={{0,2},{2,4},{3,1},{4,6},{5,3},{6,8},{7,5},{8,10},{9,7},{10,12},{11... | collective-permute-start | bytes 3932168 | tf_op jit(solution)/shard_map/ppermute | solution.py:492
  72.2 8.1 %near_rows.1 = (f32[2,128,2304]{2,1,0:T(8,128)S(1)}, bf16[2,128,2304]{2,1,0:T(8,128)(2,1)S(1)}) custom-call(s32[1]{0:T(128)} %bitcast.parity, s32[10,68]{1,0:T(8,128)S(1)} %get-tuple-element.41.lists, s32[10]{0:T(128)S(1)} %get-tuple-element.42.counts, bf16[65,128,128]{2,1,0:T(8,128)(2,1)S(1)} %get-tuple-element.43.blocks, ...), custom_call_target="tpu_custom_call" | custom-call | flops 4000000000 | bytes 20000000 | tf_op jit(solution)/shard_map/near_rows/pallas_call | solution.py:419
  80.3 2.0 %collective-permute-start.9 = (bf16[2,128,2304]{2,1,0:T(8,128)(2,1)S(1)}, bf16[2,128,2304]{2,1,0:T(8,128)(2,1)S(1)}, u32[]{:S(2)}, u32[]{:S(2)}) collective-permute-start(bf16[2,128,2304]{2,1,0:T(8,128)(2,1)S(1)} %get-tuple-element.53), channel_id=1, source_target_pairs={{0,1},{1,0},{2,3},{3,2},{4,5},{5,4},{6,7},{7,6},{8,9},{9,8},{10,11... | collective-permute-start | bytes 3538952 | tf_op jit(solution)/shard_map/ppermute | solution.py:492
  82.3 6.6 %collective-permute-done.10.direct = bf16[2,128,2304]{2,1,0:T(8,128)(2,1)S(1)} collective-permute-done((bf16[2,128,2304]{2,1,0:T(8,128)(2,1)S(1)}, bf16[2,128,2304]{2,1,0:T(8,128)(2,1)S(1)}, u32[]{:S(2)}, u32[]{:S(2)}) %collective-permute-start.10) | collective-permute-done | bytes 1179680 | tf_op jit(solution)/shard_map/ppermute | solution.py:492
  88.9 0.0 collective-permute-done.9.mate
  88.9 1.3 %add_near.1.band = f32[2,128,3328]{2,1,0:T(8,128)S(1)} custom-call(s32[1]{0:T(128)} %bitcast.parity, f32[2,128,2304]{2,1,0:T(8,128)S(1)} %get-tuple-element.52.own, bf16[2,128,2304]{2,1,0:T(8,128)(2,1)S(1)} %collective-permute-done.9.mate, bf16[2,128,2304]{2,1,0:T(8,128)(2,1)S(1)} %collective-permute-done.10.direct), custom_call_target="tpu_custom_call" | custom-call | flops 1000000 | bytes 9000000 | tf_op jit(solution)/shard_map/add_near/pallas_call | solution.py:450
  90.3 7.7 %collective-permute-done.11.pair = bf16[2,128,2560]{2,1,0:T(8,128)(2,1)S(1)} collective-permute-done((bf16[2,128,2560]{2,1,0:T(8,128)(2,1)S(1)}, bf16[2,128,2560]{2,1,0:T(8,128)(2,1)S(1)}, u32[]{:S(2)}, u32[]{:S(2)}) %collective-permute-start.11) | collective-permute-done | bytes 1310752 | tf_op jit(solution)/shard_map/ppermute | solution.py:492
  97.9 1.9 %add_pair.1 = f32[2,128,3328]{2,1,0:T(8,128)} custom-call(s32[1]{0:T(128)} %bitcast.parity, f32[2,128,3328]{2,1,0:T(8,128)S(1)} %add_near.1.band, bf16[2,128,2560]{2,1,0:T(8,128)(2,1)S(1)} %collective-permute-done.11.pair), custom_call_target="tpu_custom_call" | custom-call | tf_op jit(solution)/shard_map/add_pair/pallas_call | solution.py:478
  (3 shorter events, 0.0 us)
Async XLA Ops:
  2.5 20.4 %collective-permute-start = (bf16[1040,128]{1,0:T(8,128)(2,1)}, bf16[1040,128]{1,0:T(8,128)(2,1)S(1)}, u32[]{:S(2)}, u32[]{:S(2)}) collective-permute-start(bf16[1040,128]{1,0:T(8,128)(2,1)} %get-tuple-element.35), channel_id=1, source_target_pairs={{1,3},{2,0},{3,5},{4,2},{5,7},{6,4},{7,9},{8,6},{9,11},{10,8},{11,... | collective-permute-start | bytes 798728 | tf_op jit(solution)/shard_map/ppermute | solution.py:492
  10.8 14.2 %collective-permute-start.1 = (bf16[1040,128]{1,0:T(8,128)(2,1)}, bf16[1040,128]{1,0:T(8,128)(2,1)S(1)}, u32[]{:S(2)}, u32[]{:S(2)}) collective-permute-start(bf16[1040,128]{1,0:T(8,128)(2,1)} %get-tuple-element.36), channel_id=1, source_target_pairs={{0,2},{2,4},{3,1},{4,6},{5,3},{6,8},{7,5},{8,10},{9,7},{10,12},{11... | collective-permute-start | bytes 798728 | tf_op jit(solution)/shard_map/ppermute | solution.py:492
  12.7 13.7 %collective-permute-start.2 = (bf16[1040,128]{1,0:T(8,128)(2,1)}, bf16[1040,128]{1,0:T(8,128)(2,1)S(1)}, u32[]{:S(2)}, u32[]{:S(2)}) collective-permute-start(bf16[1040,128]{1,0:T(8,128)(2,1)} %get-tuple-element.37), channel_id=1, source_target_pairs={{1,2},{2,1},{3,4},{4,3},{5,6},{6,5},{7,8},{8,7},{9,10},{10,9},{11,... | collective-permute-start | bytes 798728 | tf_op jit(solution)/shard_map/ppermute | solution.py:492
  15.6 10.9 %collective-permute-start.3 = (bf16[1040,128]{1,0:T(8,128)(2,1)}, bf16[1040,128]{1,0:T(8,128)(2,1)S(1)}, u32[]{:S(2)}, u32[]{:S(2)}) collective-permute-start(bf16[1040,128]{1,0:T(8,128)(2,1)} %get-tuple-element.38), channel_id=1, source_target_pairs={{0,1},{1,0},{2,3},{3,2},{4,5},{5,4},{6,7},{7,6},{8,9},{9,8},{10,11... | collective-permute-start | bytes 798728 | tf_op jit(solution)/shard_map/ppermute | solution.py:492
  15.6 1.4 %copy-start = (bf16[16,3,128,128]{3,2,1,0:T(8,128)(2,1)S(1)}, bf16[16,3,128,128]{3,2,1,0:T(8,128)(2,1)}, u32[]{:S(2)}) copy-start(bf16[16,3,128,128]{3,2,1,0:T(8,128)(2,1)} %off.5) | copy-start | bytes 4718596
  17.1 1.0 %copy-start.2 = (bf16[16,128,128]{2,1,0:T(8,128)(2,1)S(1)}, bf16[16,128,128]{2,1,0:T(8,128)(2,1)}, u32[]{:S(2)}) copy-start(bf16[16,128,128]{2,1,0:T(8,128)(2,1)} %tent.3) | copy-start | bytes 1572868
  18.1 1.0 %copy-start.3 = (bf16[16,128,128]{2,1,0:T(8,128)(2,1)S(1)}, bf16[16,128,128]{2,1,0:T(8,128)(2,1)}, u32[]{:S(2)}) copy-start(bf16[16,128,128]{2,1,0:T(8,128)(2,1)} %diag.5) | copy-start | bytes 1572868
  19.1 0.7 copy-start.6
  19.8 0.7 copy-start.8
  20.5 5.9 %copy-start.1 = (bf16[16,3,128,128]{3,2,1,0:T(8,128)(2,1)S(1)}, bf16[16,3,128,128]{3,2,1,0:T(8,128)(2,1)}, u32[]{:S(2)}) copy-start(bf16[16,3,128,128]{3,2,1,0:T(8,128)(2,1)} %off.5) | copy-start | bytes 4718596
  20.5 5.9 %copy-start.5 = (s32[4,4]{1,0:T(4,128)S(1)}, s32[4,4]{1,0:T(4,128)}, u32[]{:S(2)}) copy-start(s32[4,4]{1,0:T(4,128)} %send_rows.3) | copy-start | bytes 196
  20.5 5.9 %copy-start.7 = (s32[16,3]{0,1:T(4,128)S(1)}, s32[16,3]{0,1:T(4,128)}, u32[]{:S(2)}) copy-start(s32[16,3]{0,1:T(4,128)} %param.8) | copy-start | bytes 580
  30.5 16.5 %collective-permute-start.4 = (bf16[528,384]{1,0:T(8,128)(2,1)S(1)}, bf16[528,384]{1,0:T(8,128)(2,1)S(1)}, u32[]{:S(2)}, u32[]{:S(2)}) collective-permute-start(bf16[528,384]{1,0:T(8,128)(2,1)S(1)} %get-tuple-element.45), channel_id=1, source_target_pairs={{1,3},{2,0},{3,5},{4,2},{5,7},{6,4},{7,9},{8,6},{9,11},{10,8},{11,... | collective-permute-start | bytes 1216520 | tf_op jit(solution)/shard_map/ppermute | solution.py:492
  34.4 14.6 %collective-permute-start.5 = (bf16[528,384]{1,0:T(8,128)(2,1)S(1)}, bf16[528,384]{1,0:T(8,128)(2,1)S(1)}, u32[]{:S(2)}, u32[]{:S(2)}) collective-permute-start(bf16[528,384]{1,0:T(8,128)(2,1)S(1)} %get-tuple-element.46), channel_id=1, source_target_pairs={{1,2},{2,1},{3,4},{4,3},{5,6},{6,5},{7,8},{8,7},{9,10},{10,9},{11,... | collective-permute-start | bytes 1216520 | tf_op jit(solution)/shard_map/ppermute | solution.py:492
  36.9 15.3 %collective-permute-start.6 = (bf16[528,384]{1,0:T(8,128)(2,1)S(1)}, bf16[528,384]{1,0:T(8,128)(2,1)S(1)}, u32[]{:S(2)}, u32[]{:S(2)}) collective-permute-start(bf16[528,384]{1,0:T(8,128)(2,1)S(1)} %get-tuple-element.47), channel_id=1, source_target_pairs={{0,2},{2,4},{3,1},{4,6},{5,3},{6,8},{7,5},{8,10},{9,7},{10,12},{11... | collective-permute-start | bytes 1216520 | tf_op jit(solution)/shard_map/ppermute | solution.py:492
  38.8 13.3 %collective-permute-start.7 = (bf16[528,384]{1,0:T(8,128)(2,1)S(1)}, bf16[528,384]{1,0:T(8,128)(2,1)S(1)}, u32[]{:S(2)}, u32[]{:S(2)}) collective-permute-start(bf16[528,384]{1,0:T(8,128)(2,1)S(1)} %get-tuple-element.48), channel_id=1, source_target_pairs={{0,1},{1,0},{2,3},{3,2},{4,5},{5,4},{6,7},{7,6},{8,9},{9,8},{10,11... | collective-permute-start | bytes 1216520 | tf_op jit(solution)/shard_map/ppermute | solution.py:492
  44.4 7.8 %copy-start.4 = (bf16[16,128,128]{2,1,0:T(8,128)(2,1)S(1)}, bf16[16,128,128]{2,1,0:T(8,128)(2,1)}, u32[]{:S(2)}) copy-start(bf16[16,128,128]{2,1,0:T(8,128)(2,1)} %diag.5) | copy-start | bytes 1572868
  62.0 6.3 %collective-permute-start.8 = (bf16[2,128,2560]{2,1,0:T(8,128)(2,1)S(1)}, bf16[2,128,2560]{2,1,0:T(8,128)(2,1)S(1)}, u32[]{:S(2)}, u32[]{:S(2)}) collective-permute-start(bf16[2,128,2560]{2,1,0:T(8,128)(2,1)S(1)} %get-tuple-element.50), channel_id=1, source_target_pairs={{0,1},{1,0},{2,3},{3,2},{4,5},{5,4},{6,7},{7,6},{8,9},{9,8},{10,11... | collective-permute-start | bytes 3932168 | tf_op jit(solution)/shard_map/ppermute | solution.py:492
  62.1 26.9 %collective-permute-start.10 = (bf16[2,128,2304]{2,1,0:T(8,128)(2,1)S(1)}, bf16[2,128,2304]{2,1,0:T(8,128)(2,1)S(1)}, u32[]{:S(2)}, u32[]{:S(2)}) collective-permute-start(bf16[2,128,2304]{2,1,0:T(8,128)(2,1)S(1)} %get-tuple-element.54), channel_id=1, source_target_pairs={{1,3},{2,0},{3,5},{4,2},{5,7},{6,4},{7,9},{8,6},{9,11},{10,8},{11,... | collective-permute-start | bytes 3538952 | tf_op jit(solution)/shard_map/ppermute | solution.py:492
  70.3 27.6 %collective-permute-start.11 = (bf16[2,128,2560]{2,1,0:T(8,128)(2,1)S(1)}, bf16[2,128,2560]{2,1,0:T(8,128)(2,1)S(1)}, u32[]{:S(2)}, u32[]{:S(2)}) collective-permute-start(bf16[2,128,2560]{2,1,0:T(8,128)(2,1)S(1)} %pair_rows.1), channel_id=1, source_target_pairs={{0,2},{2,4},{3,1},{4,6},{5,3},{6,8},{7,5},{8,10},{9,7},{10,12},{11... | collective-permute-start | bytes 3932168 | tf_op jit(solution)/shard_map/ppermute | solution.py:492
  80.3 8.6 %collective-permute-start.9 = (bf16[2,128,2304]{2,1,0:T(8,128)(2,1)S(1)}, bf16[2,128,2304]{2,1,0:T(8,128)(2,1)S(1)}, u32[]{:S(2)}, u32[]{:S(2)}) collective-permute-start(bf16[2,128,2304]{2,1,0:T(8,128)(2,1)S(1)} %get-tuple-element.53), channel_id=1, source_target_pairs={{0,1},{1,0},{2,3},{3,2},{4,5},{5,4},{6,7},{7,6},{8,9},{9,8},{10,11... | collective-permute-start | bytes 3538952 | tf_op jit(solution)/shard_map/ppermute | solution.py:492

commit v8 on v7

--- a/solution.py
+++ b/solution.py
@@ -21,7 +21,7 @@
 BANDWIDE = 26 * BS
 TILES = [slice(t * 2 * BS, (t + 1) * 2 * BS) for t in range(FRAME // 2)]
 FAR_MB = 26
-GROUP = 8
+GROUP = 12
 CHUNK = 4
 EXTRA = 16
 BF = jnp.bfloat16
@@ -331,21 +331,24 @@
         local = labels[jnp.minimum(j, NB - 1), m]
         return jnp.clip(jnp.where(j < NB, local, remote), 0, FRAME - 1)
 
-    def row(i, total):
-        total[...] = jnp.zeros_like(total)
+    def row_pair(q, carry):
+        pair = ((2 * q, total_a), (2 * q + 1, total_b))
+        for _, total in pair:
+            total[...] = jnp.zeros_like(total)
         for k in range(4):
-            j = i if k == 0 else off_columns[k - 1, i]
-            block = diag[i] if k == 0 else off[i, k - 1]
-            prod = jnp.dot(block, table[j], preferred_element_type=F32)
-            for m in range(4):
-                at = label_of(j, m)
-                total[at] = total[at] + prod[:, m * BS : (m + 1) * BS]
-        for at in range(FRAME):
-            applied[i, :, at * BS : (at + 1) * BS] = total[at].astype(BF)
-
-    def row_pair(q, carry):
-        row(2 * q, total_a)
-        row(2 * q + 1, total_b)
+            prods = []
+            for i, _ in pair:
+                j = i if k == 0 else off_columns[k - 1, i]
+                block = diag[i] if k == 0 else off[i, k - 1]
+                prods.append(jnp.dot(block, table[j], preferred_element_type=F32))
+            for (i, total), prod in zip(pair, prods):
+                j = i if k == 0 else off_columns[k - 1, i]
+                for m in range(4):
+                    at = label_of(j, m)
+                    total[at] = total[at] + prod[:, m * BS : (m + 1) * BS]
+        for i, total in pair:
+            for at in range(FRAME):
+                applied[i, :, at * BS : (at + 1) * BS] = total[at].astype(BF)
         return carry
 
     lax.fori_loop(0, NB // 2, row_pair, 0)

time: 101 us -> 101 us (level)
  transfers between devices with their start and end apart: 12 -> 12, of which waited for: 6 -> 6; matrix products, arithmetic and copies ran while one was open for 0% -> 0% of each run, Pallas kernels for 16% -> 15%
where the time goes in v8:
time: 101 us; the launch traced here: 100 us
  starting transfers between devices  37.7 us (37%)
  Pallas kernels  34 us (34%)
  waiting for transfers between devices  23.4 us (23%)
  local copies, waits for them, and re-layouts  4.84 us (5%)
    ppermute x12, starting transfers between devices, permute_by(): lax.ppermute(value, AXES, [(s, t) for s, t in pairs if 0 <= t < count])  37.7 us
    ppermute x12, waiting for transfers between devices, permute_by(): lax.ppermute(value, AXES, [(s, t) for s, t in pairs if 0 <= t < count])  23.4 us
    pallas_call x1, Pallas kernels, make_far(): pl.pallas_call(far_kernel, out_shape=[jax.ShapeDtypeStruct((NB, BS, WIDE)...  10.2 us
    pallas_call x1, Pallas kernels, make_near(): pl.pallas_call(near_kernel, out_shape=[jax.ShapeDtypeStruct((2, BS, WIDE)...  8.08 us
    unnamed x18, local copies, waits for them, and re-layouts  4.84 us
    pallas_call x1, Pallas kernels, ghost_slots(): pl.pallas_call(ghost_slots_kernel, out_shape=[jax.ShapeDtypeStruct((NB +...  3.94 us
    pallas_call x1, Pallas kernels, make_lists(): pl.pallas_call(lists_kernel, out_shape=[jax.ShapeDtypeStruct((10, 4 * NB...  2.64 us
    pallas_call x1, Pallas kernels, pack(): pl.pallas_call(pack_kernel, out_shape=[shape] * 4, in_specs=[spec(SMEM)]...  2.48 us
  transfers between devices with their start and end apart: 12, of which 6 were waited for; matrix products, arithmetic and copies ran while one was open for 0% of the time, Pallas kernels for 15%

profile of v8, /device:TPU:24, one launch (start us, length us, event | category | flops | bytes accessed | tf_op | source)
XLA Modules:
  0.0 100.1 jit_solution(16773290750069389092)
XLA Ops:
  0.0 2.5 %pack.1 = (bf16[1040,128]{1,0:T(8,128)(2,1)}, bf16[1040,128]{1,0:T(8,128)(2,1)}, bf16[1040,128]{1,0:T(8,128)(2,1)}, bf16[1040,128]{1,0:T(8,128)(2,1)}) custom-call(s32[1]{0:T(128)} %bitcast.parity, s32[4,4]{1,0:T(4,128)} %send_rows.3, s32[16]{0:T(128)} %aggregate.3, bf16[16,128,128]{2,1,0:T(8,128)(2,1)} %tent.3, bf16[16,128,128]{2,1,0:T(8,128)(2,1)} %diag.5), custom_call_target="tpu_custom_call" | custom-call | tf_op jit(solution)/shard_map/pack/pallas_call | solution.py:91
  2.5 8.3 %collective-permute-start = (bf16[1040,128]{1,0:T(8,128)(2,1)}, bf16[1040,128]{1,0:T(8,128)(2,1)S(1)}, u32[]{:S(2)}, u32[]{:S(2)}) collective-permute-start(bf16[1040,128]{1,0:T(8,128)(2,1)} %get-tuple-element.35), channel_id=1, source_target_pairs={{1,3},{2,0},{3,5},{4,2},{5,7},{6,4},{7,9},{8,6},{9,11},{10,8},{11,... | collective-permute-start | bytes 798728 | tf_op jit(solution)/shard_map/ppermute | solution.py:495
  10.8 1.9 %collective-permute-start.1 = (bf16[1040,128]{1,0:T(8,128)(2,1)}, bf16[1040,128]{1,0:T(8,128)(2,1)S(1)}, u32[]{:S(2)}, u32[]{:S(2)}) collective-permute-start(bf16[1040,128]{1,0:T(8,128)(2,1)} %get-tuple-element.36), channel_id=1, source_target_pairs={{0,2},{2,4},{3,1},{4,6},{5,3},{6,8},{7,5},{8,10},{9,7},{10,12},{11... | collective-permute-start | bytes 798728 | tf_op jit(solution)/shard_map/ppermute | solution.py:495
  12.7 2.8 %collective-permute-start.2 = (bf16[1040,128]{1,0:T(8,128)(2,1)}, bf16[1040,128]{1,0:T(8,128)(2,1)S(1)}, u32[]{:S(2)}, u32[]{:S(2)}) collective-permute-start(bf16[1040,128]{1,0:T(8,128)(2,1)} %get-tuple-element.37), channel_id=1, source_target_pairs={{1,2},{2,1},{3,4},{4,3},{5,6},{6,5},{7,8},{8,7},{9,10},{10,9},{11,... | collective-permute-start | bytes 798728 | tf_op jit(solution)/shard_map/ppermute | solution.py:495
  15.6 0.1 collective-permute-start.3
  15.6 0.0 copy-start
  15.7 1.4 %copy-done = bf16[16,3,128,128]{3,2,1,0:T(8,128)(2,1)S(1)} copy-done((bf16[16,3,128,128]{3,2,1,0:T(8,128)(2,1)S(1)}, bf16[16,3,128,128]{3,2,1,0:T(8,128)(2,1)}, u32[]{:S(2)}) %copy-start) | copy-done | bytes 1572888
  17.1 1.0 %copy-done.2 = bf16[16,128,128]{2,1,0:T(8,128)(2,1)S(1)} copy-done((bf16[16,128,128]{2,1,0:T(8,128)(2,1)S(1)}, bf16[16,128,128]{2,1,0:T(8,128)(2,1)}, u32[]{:S(2)}) %copy-start.2) | copy-done | bytes 524312
  18.1 0.0 copy-start.3
  18.1 1.0 %copy-done.3 = bf16[16,128,128]{2,1,0:T(8,128)(2,1)S(1)} copy-done((bf16[16,128,128]{2,1,0:T(8,128)(2,1)S(1)}, bf16[16,128,128]{2,1,0:T(8,128)(2,1)}, u32[]{:S(2)}) %copy-start.3) | copy-done | bytes 524312
  19.1 0.0 copy-start.6
  19.1 0.7 copy-done.6
  19.8 0.0 copy-start.8
  19.8 0.7 copy-done.8
  20.5 0.0 copy-start.1
  20.5 0.0 copy-start.5
  20.5 2.4 %local_slots.1 = (s32[16,4]{1,0:T(8,128)S(1)}, s32[60]{0:T(128)S(1)}, s32[1]{0:T(128)}, bf16[16,128,512]{2,1,0:T(8,128)(2,1)S(1)}, f32[16,128,128]{2,1,0:T(8,128)S(1)}) custom-call(s32[3,16]{1,0:T(4,128)S(1)} %bitcast.2, s32[16]{0:T(128)S(1)} %copy-done.8, bf16[16,128,128]{2,1,0:T(8,128)(2,1)S(1)} %copy-done.3, bf16[16,3,128,128]{3,2,1,0:T(8,128)(2,1)S(1)} %copy-done, ...), custom_call_target="tpu_custom_call" | custom-call | flops 1000000000 | bytes 6000000 | tf_op jit(solution)/shard_map/local_slots/pallas_call | solution.py:134
  22.9 0.0 collective-permute-done.g0
  22.9 2.1 %collective-permute-done.1.g1 = bf16[1040,128]{1,0:T(8,128)(2,1)S(1)} collective-permute-done((bf16[1040,128]{1,0:T(8,128)(2,1)}, bf16[1040,128]{1,0:T(8,128)(2,1)S(1)}, u32[]{:S(2)}, u32[]{:S(2)}) %collective-permute-start.1) | collective-permute-done | bytes 266272 | tf_op jit(solution)/shard_map/ppermute | solution.py:495
  25.0 1.4 %collective-permute-done.2.g2 = bf16[1040,128]{1,0:T(8,128)(2,1)S(1)} collective-permute-done((bf16[1040,128]{1,0:T(8,128)(2,1)}, bf16[1040,128]{1,0:T(8,128)(2,1)S(1)}, u32[]{:S(2)}, u32[]{:S(2)}) %collective-permute-start.2) | collective-permute-done | bytes 266272 | tf_op jit(solution)/shard_map/ppermute | solution.py:495
  26.4 0.0 collective-permute-done.3.g3
  26.4 0.0 copy-done.1
  26.4 0.0 copy-done.5
  26.4 0.0 copy-done.7
  26.4 3.9 %ghost_slots.1 = (s32[17,4]{1,0:T(8,128)S(1)}, bf16[17,128,512]{2,1,0:T(8,128)(2,1)S(1)}, bf16[528,384]{1,0:T(8,128)(2,1)S(1)}, bf16[528,384]{1,0:T(8,128)(2,1)S...) custom-call(s32[1]{0:T(128)} %bitcast.parity, s32[4,4]{1,0:T(4,128)S(1)} %copy-done.5, ...), custom_call_target="tpu_custom_call" | custom-call | tf_op jit(solution)/shard_map/ghost_slots/pallas_call | solution.py:200
  30.4 3.9 %collective-permute-start.4 = (bf16[528,384]{1,0:T(8,128)(2,1)S(1)}, bf16[528,384]{1,0:T(8,128)(2,1)S(1)}, u32[]{:S(2)}, u32[]{:S(2)}) collective-permute-start(bf16[528,384]{1,0:T(8,128)(2,1)S(1)} %get-tuple-element.45), channel_id=1, source_target_pairs={{1,3},{2,0},{3,5},{4,2},{5,7},{6,4},{7,9},{8,6},{9,11},{10,8},{11,... | collective-permute-start | bytes 1216520 | tf_op jit(solution)/shard_map/ppermute | solution.py:495
  34.3 2.5 %collective-permute-start.5 = (bf16[528,384]{1,0:T(8,128)(2,1)S(1)}, bf16[528,384]{1,0:T(8,128)(2,1)S(1)}, u32[]{:S(2)}, u32[]{:S(2)}) collective-permute-start(bf16[528,384]{1,0:T(8,128)(2,1)S(1)} %get-tuple-element.46), channel_id=1, source_target_pairs={{1,2},{2,1},{3,4},{4,3},{5,6},{6,5},{7,8},{8,7},{9,10},{10,9},{11,... | collective-permute-start | bytes 1216520 | tf_op jit(solution)/shard_map/ppermute | solution.py:495
  36.8 1.9 %collective-permute-start.6 = (bf16[528,384]{1,0:T(8,128)(2,1)S(1)}, bf16[528,384]{1,0:T(8,128)(2,1)S(1)}, u32[]{:S(2)}, u32[]{:S(2)}) collective-permute-start(bf16[528,384]{1,0:T(8,128)(2,1)S(1)} %get-tuple-element.47), channel_id=1, source_target_pairs={{0,2},{2,4},{3,1},{4,6},{5,3},{6,8},{7,5},{8,10},{9,7},{10,12},{11... | collective-permute-start | bytes 1216520 | tf_op jit(solution)/shard_map/ppermute | solution.py:495
  38.7 5.5 %collective-permute-start.7 = (bf16[528,384]{1,0:T(8,128)(2,1)S(1)}, bf16[528,384]{1,0:T(8,128)(2,1)S(1)}, u32[]{:S(2)}, u32[]{:S(2)}) collective-permute-start(bf16[528,384]{1,0:T(8,128)(2,1)S(1)} %get-tuple-element.48), channel_id=1, source_target_pairs={{0,1},{1,0},{2,3},{3,2},{4,5},{5,4},{6,7},{7,6},{8,9},{9,8},{10,11... | collective-permute-start | bytes 1216520 | tf_op jit(solution)/shard_map/ppermute | solution.py:495
  44.3 2.6 %lists.1 = (s32[10,68]{1,0:T(8,128)S(1)}, s32[10]{0:T(128)S(1)}, bf16[65,128,128]{2,1,0:T(8,128)(2,1)S(1)}, bf16[16,128,128]{2,1,0:T(8,128)(2,1)S(1)}) custom-call(s32[1]{0:T(128)} %bitcast.parity, s32[17,4]{1,0:T(8,128)S(1)} %get-tuple-element.39.labels, bf16[17,128,512]{2,1,0:T(8,128)(2,1)S(1)} %get-tuple-element.40.slots, ...), custom_call_target="tpu_custom_call" | custom-call | flops 100000000 | bytes 6000000 | tf_op jit(solution)/shard_map/lists/pallas_call | solution.py:259
  46.9 0.0 collective-permute-done.4.g0
  46.9 2.0 %collective-permute-done.5.g1 = bf16[528,384]{1,0:T(8,128)(2,1)S(1)} collective-permute-done((bf16[528,384]{1,0:T(8,128)(2,1)S(1)}, bf16[528,384]{1,0:T(8,128)(2,1)S(1)}, u32[]{:S(2)}, u32[]{:S(2)}) %collective-permute-start.5) | collective-permute-done | bytes 405536 | tf_op jit(solution)/shard_map/ppermute | solution.py:495
  48.9 3.2 %collective-permute-done.6.g2 = bf16[528,384]{1,0:T(8,128)(2,1)S(1)} collective-permute-done((bf16[528,384]{1,0:T(8,128)(2,1)S(1)}, bf16[528,384]{1,0:T(8,128)(2,1)S(1)}, u32[]{:S(2)}, u32[]{:S(2)}) %collective-permute-start.6) | collective-permute-done | bytes 405536 | tf_op jit(solution)/shard_map/ppermute | solution.py:495
  52.1 0.0 collective-permute-done.7.g3
  52.1 0.0 copy-done.4
  52.1 10.2 %far_rows.1 = (bf16[16,128,2304]{2,1,0:T(8,128)(2,1)S(1)}, bf16[2,128,2304]{2,1,0:T(8,128)(2,1)S(1)}, bf16[2,128,2560]{2,1,0:T(8,128)(2,1)S(1)}) custom-call(s32[1]{0:T(128)} %bitcast.parity, s32[3,16]{1,0:T(4,128)S(1)} %bitcast.4, s32[17,4]{1,0:T(8,128)S(1)} %get-tuple-element.39.labels, s32[10,68]{1,0:T(8,128)S(1)} %get-tuple-element.41.lists, ...), custom_call_target="tpu_custom_call" | custom-call | flops 4000000000 | bytes 20000000 | tf_op jit(solution)/shard_map/far_rows/pallas_call | solution.py:364
  62.3 0.1 collective-permute-start.8
  62.4 5.3 %collective-permute-start.10 = (bf16[2,128,2304]{2,1,0:T(8,128)(2,1)S(1)}, bf16[2,128,2304]{2,1,0:T(8,128)(2,1)S(1)}, u32[]{:S(2)}, u32[]{:S(2)}) collective-permute-start(bf16[2,128,2304]{2,1,0:T(8,128)(2,1)S(1)} %get-tuple-element.54), channel_id=1, source_target_pairs={{1,3},{2,0},{3,5},{4,2},{5,7},{6,4},{7,9},{8,6},{9,11},{10,8},{11,... | collective-permute-start | bytes 3538952 | tf_op jit(solution)/shard_map/ppermute | solution.py:495
  67.6 0.0 collective-permute-done.8.relay
  67.7 1.0 %pair_rows.1 = bf16[2,128,2560]{2,1,0:T(8,128)(2,1)S(1)} custom-call(s32[1]{0:T(128)} %bitcast.parity, s32[10,68]{1,0:T(8,128)S(1)} %get-tuple-element.41.lists, s32[10]{0:T(128)S(1)} %get-tuple-element.42.counts, bf16[65,128,128]{2,1,0:T(8,128)(2,1)S(1)} %get-tuple-element.43.blocks, bf16[16,128,2304]{2,1,0:T(8,128)(2,1)S(1)} %get-tuple-element.51.applied, ...), custom_call_target="tpu_custom_call" | custom-call | flops 2000000000 | bytes 10000000 | tf_op jit(solution)/shard_map/pair_rows/pallas_call | solution.py:396
  68.7 1.9 %collective-permute-start.11 = (bf16[2,128,2560]{2,1,0:T(8,128)(2,1)S(1)}, bf16[2,128,2560]{2,1,0:T(8,128)(2,1)S(1)}, u32[]{:S(2)}, u32[]{:S(2)}) collective-permute-start(bf16[2,128,2560]{2,1,0:T(8,128)(2,1)S(1)} %pair_rows.1), channel_id=1, source_target_pairs={{0,2},{2,4},{3,1},{4,6},{5,3},{6,8},{7,5},{8,10},{9,7},{10,12},{11... | collective-permute-start | bytes 3932168 | tf_op jit(solution)/shard_map/ppermute | solution.py:495
  70.6 8.1 %near_rows.1 = (f32[2,128,2304]{2,1,0:T(8,128)S(1)}, bf16[2,128,2304]{2,1,0:T(8,128)(2,1)S(1)}) custom-call(s32[1]{0:T(128)} %bitcast.parity, s32[10,68]{1,0:T(8,128)S(1)} %get-tuple-element.41.lists, s32[10]{0:T(128)S(1)} %get-tuple-element.42.counts, bf16[65,128,128]{2,1,0:T(8,128)(2,1)S(1)} %get-tuple-element.43.blocks, ...), custom_call_target="tpu_custom_call" | custom-call | flops 4000000000 | bytes 20000000 | tf_op jit(solution)/shard_map/near_rows/pallas_call | solution.py:422
  78.7 3.4 %collective-permute-start.9 = (bf16[2,128,2304]{2,1,0:T(8,128)(2,1)S(1)}, bf16[2,128,2304]{2,1,0:T(8,128)(2,1)S(1)}, u32[]{:S(2)}, u32[]{:S(2)}) collective-permute-start(bf16[2,128,2304]{2,1,0:T(8,128)(2,1)S(1)} %get-tuple-element.53), channel_id=1, source_target_pairs={{0,1},{1,0},{2,3},{3,2},{4,5},{5,4},{6,7},{7,6},{8,9},{9,8},{10,11... | collective-permute-start | bytes 3538952 | tf_op jit(solution)/shard_map/ppermute | solution.py:495
  82.2 6.6 %collective-permute-done.10.direct = bf16[2,128,2304]{2,1,0:T(8,128)(2,1)S(1)} collective-permute-done((bf16[2,128,2304]{2,1,0:T(8,128)(2,1)S(1)}, bf16[2,128,2304]{2,1,0:T(8,128)(2,1)S(1)}, u32[]{:S(2)}, u32[]{:S(2)}) %collective-permute-start.10) | collective-permute-done | bytes 1179680 | tf_op jit(solution)/shard_map/ppermute | solution.py:495
  88.8 0.0 collective-permute-done.9.mate
  88.8 1.3 %add_near.1.band = f32[2,128,3328]{2,1,0:T(8,128)S(1)} custom-call(s32[1]{0:T(128)} %bitcast.parity, f32[2,128,2304]{2,1,0:T(8,128)S(1)} %get-tuple-element.52.own, bf16[2,128,2304]{2,1,0:T(8,128)(2,1)S(1)} %collective-permute-done.9.mate, bf16[2,128,2304]{2,1,0:T(8,128)(2,1)S(1)} %collective-permute-done.10.direct), custom_call_target="tpu_custom_call" | custom-call | flops 1000000 | bytes 9000000 | tf_op jit(solution)/shard_map/add_near/pallas_call | solution.py:453
  90.1 8.1 %collective-permute-done.11.pair = bf16[2,128,2560]{2,1,0:T(8,128)(2,1)S(1)} collective-permute-done((bf16[2,128,2560]{2,1,0:T(8,128)(2,1)S(1)}, bf16[2,128,2560]{2,1,0:T(8,128)(2,1)S(1)}, u32[]{:S(2)}, u32[]{:S(2)}) %collective-permute-start.11) | collective-permute-done | bytes 1310752 | tf_op jit(solution)/shard_map/ppermute | solution.py:495
  98.3 1.9 %add_pair.1 = f32[2,128,3328]{2,1,0:T(8,128)} custom-call(s32[1]{0:T(128)} %bitcast.parity, f32[2,128,3328]{2,1,0:T(8,128)S(1)} %add_near.1.band, bf16[2,128,2560]{2,1,0:T(8,128)(2,1)S(1)} %collective-permute-done.11.pair), custom_call_target="tpu_custom_call" | custom-call | tf_op jit(solution)/shard_map/add_pair/pallas_call | solution.py:481
  (3 shorter events, 0.0 us)
Async XLA Ops:
  2.5 20.4 %collective-permute-start = (bf16[1040,128]{1,0:T(8,128)(2,1)}, bf16[1040,128]{1,0:T(8,128)(2,1)S(1)}, u32[]{:S(2)}, u32[]{:S(2)}) collective-permute-start(bf16[1040,128]{1,0:T(8,128)(2,1)} %get-tuple-element.35), channel_id=1, source_target_pairs={{1,3},{2,0},{3,5},{4,2},{5,7},{6,4},{7,9},{8,6},{9,11},{10,8},{11,... | collective-permute-start | bytes 798728 | tf_op jit(solution)/shard_map/ppermute | solution.py:495
  10.8 14.2 %collective-permute-start.1 = (bf16[1040,128]{1,0:T(8,128)(2,1)}, bf16[1040,128]{1,0:T(8,128)(2,1)S(1)}, u32[]{:S(2)}, u32[]{:S(2)}) collective-permute-start(bf16[1040,128]{1,0:T(8,128)(2,1)} %get-tuple-element.36), channel_id=1, source_target_pairs={{0,2},{2,4},{3,1},{4,6},{5,3},{6,8},{7,5},{8,10},{9,7},{10,12},{11... | collective-permute-start | bytes 798728 | tf_op jit(solution)/shard_map/ppermute | solution.py:495
  12.7 13.7 %collective-permute-start.2 = (bf16[1040,128]{1,0:T(8,128)(2,1)}, bf16[1040,128]{1,0:T(8,128)(2,1)S(1)}, u32[]{:S(2)}, u32[]{:S(2)}) collective-permute-start(bf16[1040,128]{1,0:T(8,128)(2,1)} %get-tuple-element.37), channel_id=1, source_target_pairs={{1,2},{2,1},{3,4},{4,3},{5,6},{6,5},{7,8},{8,7},{9,10},{10,9},{11,... | collective-permute-start | bytes 798728 | tf_op jit(solution)/shard_map/ppermute | solution.py:495
  15.6 10.9 %collective-permute-start.3 = (bf16[1040,128]{1,0:T(8,128)(2,1)}, bf16[1040,128]{1,0:T(8,128)(2,1)S(1)}, u32[]{:S(2)}, u32[]{:S(2)}) collective-permute-start(bf16[1040,128]{1,0:T(8,128)(2,1)} %get-tuple-element.38), channel_id=1, source_target_pairs={{0,1},{1,0},{2,3},{3,2},{4,5},{5,4},{6,7},{7,6},{8,9},{9,8},{10,11... | collective-permute-start | bytes 798728 | tf_op jit(solution)/shard_map/ppermute | solution.py:495
  15.6 1.4 %copy-start = (bf16[16,3,128,128]{3,2,1,0:T(8,128)(2,1)S(1)}, bf16[16,3,128,128]{3,2,1,0:T(8,128)(2,1)}, u32[]{:S(2)}) copy-start(bf16[16,3,128,128]{3,2,1,0:T(8,128)(2,1)} %off.5) | copy-start | bytes 4718596
  17.1 1.0 %copy-start.2 = (bf16[16,128,128]{2,1,0:T(8,128)(2,1)S(1)}, bf16[16,128,128]{2,1,0:T(8,128)(2,1)}, u32[]{:S(2)}) copy-start(bf16[16,128,128]{2,1,0:T(8,128)(2,1)} %tent.3) | copy-start | bytes 1572868
  18.1 1.0 %copy-start.3 = (bf16[16,128,128]{2,1,0:T(8,128)(2,1)S(1)}, bf16[16,128,128]{2,1,0:T(8,128)(2,1)}, u32[]{:S(2)}) copy-start(bf16[16,128,128]{2,1,0:T(8,128)(2,1)} %diag.5) | copy-start | bytes 1572868
  19.1 0.7 copy-start.6
  19.8 0.7 copy-start.8
  20.5 5.9 %copy-start.1 = (bf16[16,3,128,128]{3,2,1,0:T(8,128)(2,1)S(1)}, bf16[16,3,128,128]{3,2,1,0:T(8,128)(2,1)}, u32[]{:S(2)}) copy-start(bf16[16,3,128,128]{3,2,1,0:T(8,128)(2,1)} %off.5) | copy-start | bytes 4718596
  20.5 5.9 %copy-start.5 = (s32[4,4]{1,0:T(4,128)S(1)}, s32[4,4]{1,0:T(4,128)}, u32[]{:S(2)}) copy-start(s32[4,4]{1,0:T(4,128)} %send_rows.3) | copy-start | bytes 196
  20.5 5.9 %copy-start.7 = (s32[16,3]{0,1:T(4,128)S(1)}, s32[16,3]{0,1:T(4,128)}, u32[]{:S(2)}) copy-start(s32[16,3]{0,1:T(4,128)} %param.8) | copy-start | bytes 580
  30.4 16.5 %collective-permute-start.4 = (bf16[528,384]{1,0:T(8,128)(2,1)S(1)}, bf16[528,384]{1,0:T(8,128)(2,1)S(1)}, u32[]{:S(2)}, u32[]{:S(2)}) collective-permute-start(bf16[528,384]{1,0:T(8,128)(2,1)S(1)} %get-tuple-element.45), channel_id=1, source_target_pairs={{1,3},{2,0},{3,5},{4,2},{5,7},{6,4},{7,9},{8,6},{9,11},{10,8},{11,... | collective-permute-start | bytes 1216520 | tf_op jit(solution)/shard_map/ppermute | solution.py:495
  34.3 14.6 %collective-permute-start.5 = (bf16[528,384]{1,0:T(8,128)(2,1)S(1)}, bf16[528,384]{1,0:T(8,128)(2,1)S(1)}, u32[]{:S(2)}, u32[]{:S(2)}) collective-permute-start(bf16[528,384]{1,0:T(8,128)(2,1)S(1)} %get-tuple-element.46), channel_id=1, source_target_pairs={{1,2},{2,1},{3,4},{4,3},{5,6},{6,5},{7,8},{8,7},{9,10},{10,9},{11,... | collective-permute-start | bytes 1216520 | tf_op jit(solution)/shard_map/ppermute | solution.py:495
  36.8 15.3 %collective-permute-start.6 = (bf16[528,384]{1,0:T(8,128)(2,1)S(1)}, bf16[528,384]{1,0:T(8,128)(2,1)S(1)}, u32[]{:S(2)}, u32[]{:S(2)}) collective-permute-start(bf16[528,384]{1,0:T(8,128)(2,1)S(1)} %get-tuple-element.47), channel_id=1, source_target_pairs={{0,2},{2,4},{3,1},{4,6},{5,3},{6,8},{7,5},{8,10},{9,7},{10,12},{11... | collective-permute-start | bytes 1216520 | tf_op jit(solution)/shard_map/ppermute | solution.py:495
  38.7 13.3 %collective-permute-start.7 = (bf16[528,384]{1,0:T(8,128)(2,1)S(1)}, bf16[528,384]{1,0:T(8,128)(2,1)S(1)}, u32[]{:S(2)}, u32[]{:S(2)}) collective-permute-start(bf16[528,384]{1,0:T(8,128)(2,1)S(1)} %get-tuple-element.48), channel_id=1, source_target_pairs={{0,1},{1,0},{2,3},{3,2},{4,5},{5,4},{6,7},{7,6},{8,9},{9,8},{10,11... | collective-permute-start | bytes 1216520 | tf_op jit(solution)/shard_map/ppermute | solution.py:495
  44.3 7.8 %copy-start.4 = (bf16[16,128,128]{2,1,0:T(8,128)(2,1)S(1)}, bf16[16,128,128]{2,1,0:T(8,128)(2,1)}, u32[]{:S(2)}) copy-start(bf16[16,128,128]{2,1,0:T(8,128)(2,1)} %diag.5) | copy-start | bytes 1572868
  62.3 5.4 %collective-permute-start.8 = (bf16[2,128,2560]{2,1,0:T(8,128)(2,1)S(1)}, bf16[2,128,2560]{2,1,0:T(8,128)(2,1)S(1)}, u32[]{:S(2)}, u32[]{:S(2)}) collective-permute-start(bf16[2,128,2560]{2,1,0:T(8,128)(2,1)S(1)} %get-tuple-element.50), channel_id=1, source_target_pairs={{0,1},{1,0},{2,3},{3,2},{4,5},{5,4},{6,7},{7,6},{8,9},{9,8},{10,11... | collective-permute-start | bytes 3932168 | tf_op jit(solution)/shard_map/ppermute | solution.py:495
  62.4 26.4 %collective-permute-start.10 = (bf16[2,128,2304]{2,1,0:T(8,128)(2,1)S(1)}, bf16[2,128,2304]{2,1,0:T(8,128)(2,1)S(1)}, u32[]{:S(2)}, u32[]{:S(2)}) collective-permute-start(bf16[2,128,2304]{2,1,0:T(8,128)(2,1)S(1)} %get-tuple-element.54), channel_id=1, source_target_pairs={{1,3},{2,0},{3,5},{4,2},{5,7},{6,4},{7,9},{8,6},{9,11},{10,8},{11,... | collective-permute-start | bytes 3538952 | tf_op jit(solution)/shard_map/ppermute | solution.py:495
  68.7 29.6 %collective-permute-start.11 = (bf16[2,128,2560]{2,1,0:T(8,128)(2,1)S(1)}, bf16[2,128,2560]{2,1,0:T(8,128)(2,1)S(1)}, u32[]{:S(2)}, u32[]{:S(2)}) collective-permute-start(bf16[2,128,2560]{2,1,0:T(8,128)(2,1)S(1)} %pair_rows.1), channel_id=1, source_target_pairs={{0,2},{2,4},{3,1},{4,6},{5,3},{6,8},{7,5},{8,10},{9,7},{10,12},{11... | collective-permute-start | bytes 3932168 | tf_op jit(solution)/shard_map/ppermute | solution.py:495
  78.7 10.1 %collective-permute-start.9 = (bf16[2,128,2304]{2,1,0:T(8,128)(2,1)S(1)}, bf16[2,128,2304]{2,1,0:T(8,128)(2,1)S(1)}, u32[]{:S(2)}, u32[]{:S(2)}) collective-permute-start(bf16[2,128,2304]{2,1,0:T(8,128)(2,1)S(1)} %get-tuple-element.53), channel_id=1, source_target_pairs={{0,1},{1,0},{2,3},{3,2},{4,5},{5,4},{6,7},{7,6},{8,9},{9,8},{10,11... | collective-permute-start | bytes 3538952 | tf_op jit(solution)/shard_map/ppermute | solution.py:495

commit v9 on v8

--- a/solution.py
+++ b/solution.py
@@ -22,7 +22,7 @@
 TILES = [slice(t * 2 * BS, (t + 1) * 2 * BS) for t in range(FRAME // 2)]
 FAR_MB = 26
 GROUP = 12
-CHUNK = 4
+CHUNK = 6
 EXTRA = 16
 BF = jnp.bfloat16
 F32 = jnp.float32

time: 101 us -> 101 us (level)
  starting transfers between devices: 37.7 us -> 38.9 us
  waiting for transfers between devices: 23.4 us -> 22.3 us
    pallas_call x1, Pallas kernels: 1.05 us -> 2.33 us  [make_pair(): pl.pallas_call(pair_kernel, out_shape=jax.ShapeDtypeStruct((2, BS, CHIPWI...]
    ppermute x12, starting transfers between devices: 37.7 us -> 38.9 us  [permute_by(): lax.ppermute(value, AXES, [(s, t) for s, t in pairs if 0 <= t < count])]
    ppermute x12, waiting for transfers between devices: 23.4 us -> 22.3 us  [permute_by(): lax.ppermute(value, AXES, [(s, t) for s, t in pairs if 0 <= t < count])]
  transfers between devices with their start and end apart: 12 -> 12, of which waited for: 6 -> 6; matrix products, arithmetic and copies ran while one was open for 0% -> 0% of each run, Pallas kernels for 15% -> 16%
where the time goes in v9:
time: 101 us
  starting transfers between devices  38.9 us (39%)
  Pallas kernels  34.5 us (34%)
  waiting for transfers between devices  22.3 us (22%)
  local copies, waits for them, and re-layouts  4.84 us (5%)
    ppermute x12, starting transfers between devices, permute_by(): lax.ppermute(value, AXES, [(s, t) for s, t in pairs if 0 <= t < count])  38.9 us
    ppermute x12, waiting for transfers between devices, permute_by(): lax.ppermute(value, AXES, [(s, t) for s, t in pairs if 0 <= t < count])  22.3 us
    pallas_call x1, Pallas kernels, make_far(): pl.pallas_call(far_kernel, out_shape=[jax.ShapeDtypeStruct((NB, BS, WIDE)...  10.4 us
    pallas_call x1, Pallas kernels, make_near(): pl.pallas_call(near_kernel, out_shape=[jax.ShapeDtypeStruct((2, BS, WIDE)...  7.1 us
    unnamed x18, local copies, waits for them, and re-layouts  4.84 us
    pallas_call x1, Pallas kernels, ghost_slots(): pl.pallas_call(ghost_slots_kernel, out_shape=[jax.ShapeDtypeStruct((NB +...  3.94 us
    pallas_call x1, Pallas kernels, make_lists(): pl.pallas_call(lists_kernel, out_shape=[jax.ShapeDtypeStruct((10, 4 * NB...  2.68 us
    pallas_call x1, Pallas kernels, pack(): pl.pallas_call(pack_kernel, out_shape=[shape] * 4, in_specs=[spec(SMEM)]...  2.48 us
  transfers between devices with their start and end apart: 12, of which 6 were waited for; matrix products, arithmetic and copies ran while one was open for 0% of the time, Pallas kernels for 16%

profile of v9, /device:TPU:24, one launch (start us, length us, event | category | flops | bytes accessed | tf_op | source)
XLA Modules:
  0.0 100.6 jit_solution(9084739522105049623)
XLA Ops:
  0.0 2.5 %pack.1 = (bf16[1040,128]{1,0:T(8,128)(2,1)}, bf16[1040,128]{1,0:T(8,128)(2,1)}, bf16[1040,128]{1,0:T(8,128)(2,1)}, bf16[1040,128]{1,0:T(8,128)(2,1)}) custom-call(s32[1]{0:T(128)} %bitcast.parity, s32[4,4]{1,0:T(4,128)} %send_rows.3, s32[16]{0:T(128)} %aggregate.3, bf16[16,128,128]{2,1,0:T(8,128)(2,1)} %tent.3, bf16[16,128,128]{2,1,0:T(8,128)(2,1)} %diag.5), custom_call_target="tpu_custom_call" | custom-call | tf_op jit(solution)/shard_map/pack/pallas_call | solution.py:91
  2.5 8.3 %collective-permute-start = (bf16[1040,128]{1,0:T(8,128)(2,1)}, bf16[1040,128]{1,0:T(8,128)(2,1)S(1)}, u32[]{:S(2)}, u32[]{:S(2)}) collective-permute-start(bf16[1040,128]{1,0:T(8,128)(2,1)} %get-tuple-element.35), channel_id=1, source_target_pairs={{1,3},{2,0},{3,5},{4,2},{5,7},{6,4},{7,9},{8,6},{9,11},{10,8},{11,... | collective-permute-start | bytes 798728 | tf_op jit(solution)/shard_map/ppermute | solution.py:495
  10.8 1.9 %collective-permute-start.1 = (bf16[1040,128]{1,0:T(8,128)(2,1)}, bf16[1040,128]{1,0:T(8,128)(2,1)S(1)}, u32[]{:S(2)}, u32[]{:S(2)}) collective-permute-start(bf16[1040,128]{1,0:T(8,128)(2,1)} %get-tuple-element.36), channel_id=1, source_target_pairs={{0,2},{2,4},{3,1},{4,6},{5,3},{6,8},{7,5},{8,10},{9,7},{10,12},{11... | collective-permute-start | bytes 798728 | tf_op jit(solution)/shard_map/ppermute | solution.py:495
  12.7 2.8 %collective-permute-start.2 = (bf16[1040,128]{1,0:T(8,128)(2,1)}, bf16[1040,128]{1,0:T(8,128)(2,1)S(1)}, u32[]{:S(2)}, u32[]{:S(2)}) collective-permute-start(bf16[1040,128]{1,0:T(8,128)(2,1)} %get-tuple-element.37), channel_id=1, source_target_pairs={{1,2},{2,1},{3,4},{4,3},{5,6},{6,5},{7,8},{8,7},{9,10},{10,9},{11,... | collective-permute-start | bytes 798728 | tf_op jit(solution)/shard_map/ppermute | solution.py:495
  15.6 0.1 collective-permute-start.3
  15.6 0.0 copy-start
  15.7 1.4 %copy-done = bf16[16,3,128,128]{3,2,1,0:T(8,128)(2,1)S(1)} copy-done((bf16[16,3,128,128]{3,2,1,0:T(8,128)(2,1)S(1)}, bf16[16,3,128,128]{3,2,1,0:T(8,128)(2,1)}, u32[]{:S(2)}) %copy-start) | copy-done | bytes 1572888
  17.1 0.0 copy-start.2
  17.1 1.0 %copy-done.2 = bf16[16,128,128]{2,1,0:T(8,128)(2,1)S(1)} copy-done((bf16[16,128,128]{2,1,0:T(8,128)(2,1)S(1)}, bf16[16,128,128]{2,1,0:T(8,128)(2,1)}, u32[]{:S(2)}) %copy-start.2) | copy-done | bytes 524312
  18.1 0.0 copy-start.3
  18.1 1.0 %copy-done.3 = bf16[16,128,128]{2,1,0:T(8,128)(2,1)S(1)} copy-done((bf16[16,128,128]{2,1,0:T(8,128)(2,1)S(1)}, bf16[16,128,128]{2,1,0:T(8,128)(2,1)}, u32[]{:S(2)}) %copy-start.3) | copy-done | bytes 524312
  19.1 0.0 copy-start.6
  19.1 0.7 copy-done.6
  19.8 0.0 copy-start.8
  19.8 0.7 copy-done.8
  20.5 0.0 copy-start.1
  20.5 2.4 %local_slots.1 = (s32[16,4]{1,0:T(8,128)S(1)}, s32[60]{0:T(128)S(1)}, s32[1]{0:T(128)}, bf16[16,128,512]{2,1,0:T(8,128)(2,1)S(1)}, f32[16,128,128]{2,1,0:T(8,128)S(1)}) custom-call(s32[3,16]{1,0:T(4,128)S(1)} %bitcast.2, s32[16]{0:T(128)S(1)} %copy-done.8, bf16[16,128,128]{2,1,0:T(8,128)(2,1)S(1)} %copy-done.3, bf16[16,3,128,128]{3,2,1,0:T(8,128)(2,1)S(1)} %copy-done, ...), custom_call_target="tpu_custom_call" | custom-call | flops 1000000000 | bytes 6000000 | tf_op jit(solution)/shard_map/local_slots/pallas_call | solution.py:134
  22.9 0.0 collective-permute-done.g0
  22.9 2.1 %collective-permute-done.1.g1 = bf16[1040,128]{1,0:T(8,128)(2,1)S(1)} collective-permute-done((bf16[1040,128]{1,0:T(8,128)(2,1)}, bf16[1040,128]{1,0:T(8,128)(2,1)S(1)}, u32[]{:S(2)}, u32[]{:S(2)}) %collective-permute-start.1) | collective-permute-done | bytes 266272 | tf_op jit(solution)/shard_map/ppermute | solution.py:495
  25.0 1.4 %collective-permute-done.2.g2 = bf16[1040,128]{1,0:T(8,128)(2,1)S(1)} collective-permute-done((bf16[1040,128]{1,0:T(8,128)(2,1)}, bf16[1040,128]{1,0:T(8,128)(2,1)S(1)}, u32[]{:S(2)}, u32[]{:S(2)}) %collective-permute-start.2) | collective-permute-done | bytes 266272 | tf_op jit(solution)/shard_map/ppermute | solution.py:495
  26.4 0.0 collective-permute-done.3.g3
  26.4 0.0 copy-done.1
  26.4 0.0 copy-done.5
  26.4 0.0 copy-done.7
  26.4 3.9 %ghost_slots.1 = (s32[17,4]{1,0:T(8,128)S(1)}, bf16[17,128,512]{2,1,0:T(8,128)(2,1)S(1)}, bf16[528,384]{1,0:T(8,128)(2,1)S(1)}, bf16[528,384]{1,0:T(8,128)(2,1)S...) custom-call(s32[1]{0:T(128)} %bitcast.parity, s32[4,4]{1,0:T(4,128)S(1)} %copy-done.5, ...), custom_call_target="tpu_custom_call" | custom-call | tf_op jit(solution)/shard_map/ghost_slots/pallas_call | solution.py:200
  30.4 4.2 %collective-permute-start.4 = (bf16[528,384]{1,0:T(8,128)(2,1)S(1)}, bf16[528,384]{1,0:T(8,128)(2,1)S(1)}, u32[]{:S(2)}, u32[]{:S(2)}) collective-permute-start(bf16[528,384]{1,0:T(8,128)(2,1)S(1)} %get-tuple-element.45), channel_id=1, source_target_pairs={{1,3},{2,0},{3,5},{4,2},{5,7},{6,4},{7,9},{8,6},{9,11},{10,8},{11,... | collective-permute-start | bytes 1216520 | tf_op jit(solution)/shard_map/ppermute | solution.py:495
  34.6 2.2 %collective-permute-start.5 = (bf16[528,384]{1,0:T(8,128)(2,1)S(1)}, bf16[528,384]{1,0:T(8,128)(2,1)S(1)}, u32[]{:S(2)}, u32[]{:S(2)}) collective-permute-start(bf16[528,384]{1,0:T(8,128)(2,1)S(1)} %get-tuple-element.46), channel_id=1, source_target_pairs={{1,2},{2,1},{3,4},{4,3},{5,6},{6,5},{7,8},{8,7},{9,10},{10,9},{11,... | collective-permute-start | bytes 1216520 | tf_op jit(solution)/shard_map/ppermute | solution.py:495
  36.8 1.9 %collective-permute-start.6 = (bf16[528,384]{1,0:T(8,128)(2,1)S(1)}, bf16[528,384]{1,0:T(8,128)(2,1)S(1)}, u32[]{:S(2)}, u32[]{:S(2)}) collective-permute-start(bf16[528,384]{1,0:T(8,128)(2,1)S(1)} %get-tuple-element.47), channel_id=1, source_target_pairs={{0,2},{2,4},{3,1},{4,6},{5,3},{6,8},{7,5},{8,10},{9,7},{10,12},{11... | collective-permute-start | bytes 1216520 | tf_op jit(solution)/shard_map/ppermute | solution.py:495
  38.7 5.9 %collective-permute-start.7 = (bf16[528,384]{1,0:T(8,128)(2,1)S(1)}, bf16[528,384]{1,0:T(8,128)(2,1)S(1)}, u32[]{:S(2)}, u32[]{:S(2)}) collective-permute-start(bf16[528,384]{1,0:T(8,128)(2,1)S(1)} %get-tuple-element.48), channel_id=1, source_target_pairs={{0,1},{1,0},{2,3},{3,2},{4,5},{5,4},{6,7},{7,6},{8,9},{9,8},{10,11... | collective-permute-start | bytes 1216520 | tf_op jit(solution)/shard_map/ppermute | solution.py:495
  44.6 2.7 %lists.1 = (s32[10,70]{1,0:T(8,128)S(1)}, s32[10]{0:T(128)S(1)}, bf16[65,128,128]{2,1,0:T(8,128)(2,1)S(1)}, bf16[16,128,128]{2,1,0:T(8,128)(2,1)S(1)}) custom-call(s32[1]{0:T(128)} %bitcast.parity, s32[17,4]{1,0:T(8,128)S(1)} %get-tuple-element.39.labels, bf16[17,128,512]{2,1,0:T(8,128)(2,1)S(1)} %get-tuple-element.40.slots, ...), custom_call_target="tpu_custom_call" | custom-call | flops 100000000 | bytes 6000000 | tf_op jit(solution)/shard_map/lists/pallas_call | solution.py:259
  47.3 0.0 collective-permute-done.4.g0
  47.3 2.3 %collective-permute-done.5.g1 = bf16[528,384]{1,0:T(8,128)(2,1)S(1)} collective-permute-done((bf16[528,384]{1,0:T(8,128)(2,1)S(1)}, bf16[528,384]{1,0:T(8,128)(2,1)S(1)}, u32[]{:S(2)}, u32[]{:S(2)}) %collective-permute-start.5) | collective-permute-done | bytes 405536 | tf_op jit(solution)/shard_map/ppermute | solution.py:495
  49.6 2.8 %collective-permute-done.6.g2 = bf16[528,384]{1,0:T(8,128)(2,1)S(1)} collective-permute-done((bf16[528,384]{1,0:T(8,128)(2,1)S(1)}, bf16[528,384]{1,0:T(8,128)(2,1)S(1)}, u32[]{:S(2)}, u32[]{:S(2)}) %collective-permute-start.6) | collective-permute-done | bytes 405536 | tf_op jit(solution)/shard_map/ppermute | solution.py:495
  52.4 0.0 collective-permute-done.7.g3
  52.4 0.0 copy-done.4
  52.4 10.4 %far_rows.1 = (bf16[16,128,2304]{2,1,0:T(8,128)(2,1)S(1)}, bf16[2,128,2304]{2,1,0:T(8,128)(2,1)S(1)}, bf16[2,128,2560]{2,1,0:T(8,128)(2,1)S(1)}) custom-call(s32[1]{0:T(128)} %bitcast.parity, s32[3,16]{1,0:T(4,128)S(1)} %bitcast.4, s32[17,4]{1,0:T(8,128)S(1)} %get-tuple-element.39.labels, s32[10,70]{1,0:T(8,128)S(1)} %get-tuple-element.41.lists, ...), custom_call_target="tpu_custom_call" | custom-call | flops 4000000000 | bytes 20000000 | tf_op jit(solution)/shard_map/far_rows/pallas_call | solution.py:364
  62.8 0.1 collective-permute-start.8
  62.9 4.6 %collective-permute-start.10 = (bf16[2,128,2304]{2,1,0:T(8,128)(2,1)S(1)}, bf16[2,128,2304]{2,1,0:T(8,128)(2,1)S(1)}, u32[]{:S(2)}, u32[]{:S(2)}) collective-permute-start(bf16[2,128,2304]{2,1,0:T(8,128)(2,1)S(1)} %get-tuple-element.54), channel_id=1, source_target_pairs={{1,3},{2,0},{3,5},{4,2},{5,7},{6,4},{7,9},{8,6},{9,11},{10,8},{11,... | collective-permute-start | bytes 3538952 | tf_op jit(solution)/shard_map/ppermute | solution.py:495
  67.5 0.0 collective-permute-done.8.relay
  67.5 2.3 %pair_rows.1 = bf16[2,128,2560]{2,1,0:T(8,128)(2,1)S(1)} custom-call(s32[1]{0:T(128)} %bitcast.parity, s32[10,70]{1,0:T(8,128)S(1)} %get-tuple-element.41.lists, s32[10]{0:T(128)S(1)} %get-tuple-element.42.counts, bf16[65,128,128]{2,1,0:T(8,128)(2,1)S(1)} %get-tuple-element.43.blocks, bf16[16,128,2304]{2,1,0:T(8,128)(2,1)S(1)} %get-tuple-element.51.applied, ...), custom_call_target="tpu_custom_call" | custom-call | flops 2000000000 | bytes 10000000 | tf_op jit(solution)/shard_map/pair_rows/pallas_call | solution.py:396
  69.8 1.9 %collective-permute-start.11 = (bf16[2,128,2560]{2,1,0:T(8,128)(2,1)S(1)}, bf16[2,128,2560]{2,1,0:T(8,128)(2,1)S(1)}, u32[]{:S(2)}, u32[]{:S(2)}) collective-permute-start(bf16[2,128,2560]{2,1,0:T(8,128)(2,1)S(1)} %pair_rows.1), channel_id=1, source_target_pairs={{0,2},{2,4},{3,1},{4,6},{5,3},{6,8},{7,5},{8,10},{9,7},{10,12},{11... | collective-permute-start | bytes 3932168 | tf_op jit(solution)/shard_map/ppermute | solution.py:495
  71.8 7.1 %near_rows.1 = (f32[2,128,2304]{2,1,0:T(8,128)S(1)}, bf16[2,128,2304]{2,1,0:T(8,128)(2,1)S(1)}) custom-call(s32[1]{0:T(128)} %bitcast.parity, s32[10,70]{1,0:T(8,128)S(1)} %get-tuple-element.41.lists, s32[10]{0:T(128)S(1)} %get-tuple-element.42.counts, bf16[65,128,128]{2,1,0:T(8,128)(2,1)S(1)} %get-tuple-element.43.blocks, ...), custom_call_target="tpu_custom_call" | custom-call | flops 4000000000 | bytes 20000000 | tf_op jit(solution)/shard_map/near_rows/pallas_call | solution.py:422
  78.9 4.9 %collective-permute-start.9 = (bf16[2,128,2304]{2,1,0:T(8,128)(2,1)S(1)}, bf16[2,128,2304]{2,1,0:T(8,128)(2,1)S(1)}, u32[]{:S(2)}, u32[]{:S(2)}) collective-permute-start(bf16[2,128,2304]{2,1,0:T(8,128)(2,1)S(1)} %get-tuple-element.53), channel_id=1, source_target_pairs={{0,1},{1,0},{2,3},{3,2},{4,5},{5,4},{6,7},{7,6},{8,9},{9,8},{10,11... | collective-permute-start | bytes 3538952 | tf_op jit(solution)/shard_map/ppermute | solution.py:495
  83.8 5.8 %collective-permute-done.10.direct = bf16[2,128,2304]{2,1,0:T(8,128)(2,1)S(1)} collective-permute-done((bf16[2,128,2304]{2,1,0:T(8,128)(2,1)S(1)}, bf16[2,128,2304]{2,1,0:T(8,128)(2,1)S(1)}, u32[]{:S(2)}, u32[]{:S(2)}) %collective-permute-start.10) | collective-permute-done | bytes 1179680 | tf_op jit(solution)/shard_map/ppermute | solution.py:495
  89.6 0.0 collective-permute-done.9.mate
  89.6 1.3 %add_near.1.band = f32[2,128,3328]{2,1,0:T(8,128)S(1)} custom-call(s32[1]{0:T(128)} %bitcast.parity, f32[2,128,2304]{2,1,0:T(8,128)S(1)} %get-tuple-element.52.own, bf16[2,128,2304]{2,1,0:T(8,128)(2,1)S(1)} %collective-permute-done.9.mate, bf16[2,128,2304]{2,1,0:T(8,128)(2,1)S(1)} %collective-permute-done.10.direct), custom_call_target="tpu_custom_call" | custom-call | flops 1000000 | bytes 9000000 | tf_op jit(solution)/shard_map/add_near/pallas_call | solution.py:453
  90.9 7.8 %collective-permute-done.11.pair = bf16[2,128,2560]{2,1,0:T(8,128)(2,1)S(1)} collective-permute-done((bf16[2,128,2560]{2,1,0:T(8,128)(2,1)S(1)}, bf16[2,128,2560]{2,1,0:T(8,128)(2,1)S(1)}, u32[]{:S(2)}, u32[]{:S(2)}) %collective-permute-start.11) | collective-permute-done | bytes 1310752 | tf_op jit(solution)/shard_map/ppermute | solution.py:495
  98.8 1.9 %add_pair.1 = f32[2,128,3328]{2,1,0:T(8,128)} custom-call(s32[1]{0:T(128)} %bitcast.parity, f32[2,128,3328]{2,1,0:T(8,128)S(1)} %add_near.1.band, bf16[2,128,2560]{2,1,0:T(8,128)(2,1)S(1)} %collective-permute-done.11.pair), custom_call_target="tpu_custom_call" | custom-call | tf_op jit(solution)/shard_map/add_pair/pallas_call | solution.py:481
  (3 shorter events, 0.0 us)
Async XLA Ops:
  2.5 20.4 %collective-permute-start = (bf16[1040,128]{1,0:T(8,128)(2,1)}, bf16[1040,128]{1,0:T(8,128)(2,1)S(1)}, u32[]{:S(2)}, u32[]{:S(2)}) collective-permute-start(bf16[1040,128]{1,0:T(8,128)(2,1)} %get-tuple-element.35), channel_id=1, source_target_pairs={{1,3},{2,0},{3,5},{4,2},{5,7},{6,4},{7,9},{8,6},{9,11},{10,8},{11,... | collective-permute-start | bytes 798728 | tf_op jit(solution)/shard_map/ppermute | solution.py:495
  10.8 14.2 %collective-permute-start.1 = (bf16[1040,128]{1,0:T(8,128)(2,1)}, bf16[1040,128]{1,0:T(8,128)(2,1)S(1)}, u32[]{:S(2)}, u32[]{:S(2)}) collective-permute-start(bf16[1040,128]{1,0:T(8,128)(2,1)} %get-tuple-element.36), channel_id=1, source_target_pairs={{0,2},{2,4},{3,1},{4,6},{5,3},{6,8},{7,5},{8,10},{9,7},{10,12},{11... | collective-permute-start | bytes 798728 | tf_op jit(solution)/shard_map/ppermute | solution.py:495
  12.7 13.7 %collective-permute-start.2 = (bf16[1040,128]{1,0:T(8,128)(2,1)}, bf16[1040,128]{1,0:T(8,128)(2,1)S(1)}, u32[]{:S(2)}, u32[]{:S(2)}) collective-permute-start(bf16[1040,128]{1,0:T(8,128)(2,1)} %get-tuple-element.37), channel_id=1, source_target_pairs={{1,2},{2,1},{3,4},{4,3},{5,6},{6,5},{7,8},{8,7},{9,10},{10,9},{11,... | collective-permute-start | bytes 798728 | tf_op jit(solution)/shard_map/ppermute | solution.py:495
  15.6 10.9 %collective-permute-start.3 = (bf16[1040,128]{1,0:T(8,128)(2,1)}, bf16[1040,128]{1,0:T(8,128)(2,1)S(1)}, u32[]{:S(2)}, u32[]{:S(2)}) collective-permute-start(bf16[1040,128]{1,0:T(8,128)(2,1)} %get-tuple-element.38), channel_id=1, source_target_pairs={{0,1},{1,0},{2,3},{3,2},{4,5},{5,4},{6,7},{7,6},{8,9},{9,8},{10,11... | collective-permute-start | bytes 798728 | tf_op jit(solution)/shard_map/ppermute | solution.py:495
  15.6 1.4 %copy-start = (bf16[16,3,128,128]{3,2,1,0:T(8,128)(2,1)S(1)}, bf16[16,3,128,128]{3,2,1,0:T(8,128)(2,1)}, u32[]{:S(2)}) copy-start(bf16[16,3,128,128]{3,2,1,0:T(8,128)(2,1)} %off.5) | copy-start | bytes 4718596
  17.1 1.0 %copy-start.2 = (bf16[16,128,128]{2,1,0:T(8,128)(2,1)S(1)}, bf16[16,128,128]{2,1,0:T(8,128)(2,1)}, u32[]{:S(2)}) copy-start(bf16[16,128,128]{2,1,0:T(8,128)(2,1)} %tent.3) | copy-start | bytes 1572868
  18.1 1.0 %copy-start.3 = (bf16[16,128,128]{2,1,0:T(8,128)(2,1)S(1)}, bf16[16,128,128]{2,1,0:T(8,128)(2,1)}, u32[]{:S(2)}) copy-start(bf16[16,128,128]{2,1,0:T(8,128)(2,1)} %diag.5) | copy-start | bytes 1572868
  19.1 0.7 copy-start.6
  19.8 0.7 copy-start.8
  20.5 5.9 %copy-start.1 = (bf16[16,3,128,128]{3,2,1,0:T(8,128)(2,1)S(1)}, bf16[16,3,128,128]{3,2,1,0:T(8,128)(2,1)}, u32[]{:S(2)}) copy-start(bf16[16,3,128,128]{3,2,1,0:T(8,128)(2,1)} %off.5) | copy-start | bytes 4718596
  20.5 5.9 %copy-start.5 = (s32[4,4]{1,0:T(4,128)S(1)}, s32[4,4]{1,0:T(4,128)}, u32[]{:S(2)}) copy-start(s32[4,4]{1,0:T(4,128)} %send_rows.3) | copy-start | bytes 196
  20.5 5.9 %copy-start.7 = (s32[16,3]{0,1:T(4,128)S(1)}, s32[16,3]{0,1:T(4,128)}, u32[]{:S(2)}) copy-start(s32[16,3]{0,1:T(4,128)} %param.8) | copy-start | bytes 580
  30.4 16.9 %collective-permute-start.4 = (bf16[528,384]{1,0:T(8,128)(2,1)S(1)}, bf16[528,384]{1,0:T(8,128)(2,1)S(1)}, u32[]{:S(2)}, u32[]{:S(2)}) collective-permute-start(bf16[528,384]{1,0:T(8,128)(2,1)S(1)} %get-tuple-element.45), channel_id=1, source_target_pairs={{1,3},{2,0},{3,5},{4,2},{5,7},{6,4},{7,9},{8,6},{9,11},{10,8},{11,... | collective-permute-start | bytes 1216520 | tf_op jit(solution)/shard_map/ppermute | solution.py:495
  34.6 15.0 %collective-permute-start.5 = (bf16[528,384]{1,0:T(8,128)(2,1)S(1)}, bf16[528,384]{1,0:T(8,128)(2,1)S(1)}, u32[]{:S(2)}, u32[]{:S(2)}) collective-permute-start(bf16[528,384]{1,0:T(8,128)(2,1)S(1)} %get-tuple-element.46), channel_id=1, source_target_pairs={{1,2},{2,1},{3,4},{4,3},{5,6},{6,5},{7,8},{8,7},{9,10},{10,9},{11,... | collective-permute-start | bytes 1216520 | tf_op jit(solution)/shard_map/ppermute | solution.py:495
  36.8 15.6 %collective-permute-start.6 = (bf16[528,384]{1,0:T(8,128)(2,1)S(1)}, bf16[528,384]{1,0:T(8,128)(2,1)S(1)}, u32[]{:S(2)}, u32[]{:S(2)}) collective-permute-start(bf16[528,384]{1,0:T(8,128)(2,1)S(1)} %get-tuple-element.47), channel_id=1, source_target_pairs={{0,2},{2,4},{3,1},{4,6},{5,3},{6,8},{7,5},{8,10},{9,7},{10,12},{11... | collective-permute-start | bytes 1216520 | tf_op jit(solution)/shard_map/ppermute | solution.py:495
  38.7 13.7 %collective-permute-start.7 = (bf16[528,384]{1,0:T(8,128)(2,1)S(1)}, bf16[528,384]{1,0:T(8,128)(2,1)S(1)}, u32[]{:S(2)}, u32[]{:S(2)}) collective-permute-start(bf16[528,384]{1,0:T(8,128)(2,1)S(1)} %get-tuple-element.48), channel_id=1, source_target_pairs={{0,1},{1,0},{2,3},{3,2},{4,5},{5,4},{6,7},{7,6},{8,9},{9,8},{10,11... | collective-permute-start | bytes 1216520 | tf_op jit(solution)/shard_map/ppermute | solution.py:495
  44.6 7.8 %copy-start.4 = (bf16[16,128,128]{2,1,0:T(8,128)(2,1)S(1)}, bf16[16,128,128]{2,1,0:T(8,128)(2,1)}, u32[]{:S(2)}) copy-start(bf16[16,128,128]{2,1,0:T(8,128)(2,1)} %diag.5) | copy-start | bytes 1572868
  62.8 4.7 %collective-permute-start.8 = (bf16[2,128,2560]{2,1,0:T(8,128)(2,1)S(1)}, bf16[2,128,2560]{2,1,0:T(8,128)(2,1)S(1)}, u32[]{:S(2)}, u32[]{:S(2)}) collective-permute-start(bf16[2,128,2560]{2,1,0:T(8,128)(2,1)S(1)} %get-tuple-element.50), channel_id=1, source_target_pairs={{0,1},{1,0},{2,3},{3,2},{4,5},{5,4},{6,7},{7,6},{8,9},{9,8},{10,11... | collective-permute-start | bytes 3932168 | tf_op jit(solution)/shard_map/ppermute | solution.py:495
  62.9 26.7 %collective-permute-start.10 = (bf16[2,128,2304]{2,1,0:T(8,128)(2,1)S(1)}, bf16[2,128,2304]{2,1,0:T(8,128)(2,1)S(1)}, u32[]{:S(2)}, u32[]{:S(2)}) collective-permute-start(bf16[2,128,2304]{2,1,0:T(8,128)(2,1)S(1)} %get-tuple-element.54), channel_id=1, source_target_pairs={{1,3},{2,0},{3,5},{4,2},{5,7},{6,4},{7,9},{8,6},{9,11},{10,8},{11,... | collective-permute-start | bytes 3538952 | tf_op jit(solution)/shard_map/ppermute | solution.py:495
  69.8 28.9 %collective-permute-start.11 = (bf16[2,128,2560]{2,1,0:T(8,128)(2,1)S(1)}, bf16[2,128,2560]{2,1,0:T(8,128)(2,1)S(1)}, u32[]{:S(2)}, u32[]{:S(2)}) collective-permute-start(bf16[2,128,2560]{2,1,0:T(8,128)(2,1)S(1)} %pair_rows.1), channel_id=1, source_target_pairs={{0,2},{2,4},{3,1},{4,6},{5,3},{6,8},{7,5},{8,10},{9,7},{10,12},{11... | collective-permute-start | bytes 3932168 | tf_op jit(solution)/shard_map/ppermute | solution.py:495
  78.9 10.7 %collective-permute-start.9 = (bf16[2,128,2304]{2,1,0:T(8,128)(2,1)S(1)}, bf16[2,128,2304]{2,1,0:T(8,128)(2,1)S(1)}, u32[]{:S(2)}, u32[]{:S(2)}) collective-permute-start(bf16[2,128,2304]{2,1,0:T(8,128)(2,1)S(1)} %get-tuple-element.53), channel_id=1, source_target_pairs={{0,1},{1,0},{2,3},{3,2},{4,5},{5,4},{6,7},{7,6},{8,9},{9,8},{10,11... | collective-permute-start | bytes 3538952 | tf_op jit(solution)/shard_map/ppermute | solution.py:495

commit v10 on v8

--- a/solution.py
+++ b/solution.py
@@ -21,7 +21,7 @@
 BANDWIDE = 26 * BS
 TILES = [slice(t * 2 * BS, (t + 1) * 2 * BS) for t in range(FRAME // 2)]
 FAR_MB = 26
-GROUP = 12
+GROUP = 16
 CHUNK = 4
 EXTRA = 16
 BF = jnp.bfloat16

time: 101 us -> 101 us (level)
    pallas_call x1, Pallas kernels: 1.05 us -> 2.51 us  [make_pair(): pl.pallas_call(pair_kernel, out_shape=jax.ShapeDtypeStruct((2, BS, CHIPWI...]
  transfers between devices with their start and end apart: 12 -> 12, of which waited for: 6 -> 6; matrix products, arithmetic and copies ran while one was open for 0% -> 0% of each run, Pallas kernels for 15% -> 16%
where the time goes in v10:
time: 101 us; the launch traced here: 99.8 us
  starting transfers between devices  37.2 us (37%)
  Pallas kernels  34.1 us (34%)
  waiting for transfers between devices  23.4 us (23%)
  local copies, waits for them, and re-layouts  4.84 us (5%)
    ppermute x12, starting transfers between devices, permute_by(): lax.ppermute(value, AXES, [(s, t) for s, t in pairs if 0 <= t < count])  37.2 us
    ppermute x12, waiting for transfers between devices, permute_by(): lax.ppermute(value, AXES, [(s, t) for s, t in pairs if 0 <= t < count])  23.4 us
    pallas_call x1, Pallas kernels, make_far(): pl.pallas_call(far_kernel, out_shape=[jax.ShapeDtypeStruct((NB, BS, WIDE)...  9.73 us
    pallas_call x1, Pallas kernels, make_near(): pl.pallas_call(near_kernel, out_shape=[jax.ShapeDtypeStruct((2, BS, WIDE)...  7.11 us
    unnamed x18, local copies, waits for them, and re-layouts  4.84 us
    pallas_call x1, Pallas kernels, ghost_slots(): pl.pallas_call(ghost_slots_kernel, out_shape=[jax.ShapeDtypeStruct((NB +...  4.06 us
    pallas_call x1, Pallas kernels, make_lists(): pl.pallas_call(lists_kernel, out_shape=[jax.ShapeDtypeStruct((10, 4 * NB...  2.64 us
    pallas_call x1, Pallas kernels, make_pair(): pl.pallas_call(pair_kernel, out_shape=jax.ShapeDtypeStruct((2, BS, CHIPWI...  2.51 us
  transfers between devices with their start and end apart: 12, of which 6 were waited for; matrix products, arithmetic and copies ran while one was open for 0% of the time, Pallas kernels for 16%

profile of v10, /device:TPU:24, one launch (start us, length us, event | category | flops | bytes accessed | tf_op | source)
XLA Modules:
  0.0 99.8 jit_solution(4683998662654828872)
XLA Ops:
  0.0 2.5 %pack.1 = (bf16[1040,128]{1,0:T(8,128)(2,1)}, bf16[1040,128]{1,0:T(8,128)(2,1)}, bf16[1040,128]{1,0:T(8,128)(2,1)}, bf16[1040,128]{1,0:T(8,128)(2,1)}) custom-call(s32[1]{0:T(128)} %bitcast.parity, s32[4,4]{1,0:T(4,128)} %send_rows.3, s32[16]{0:T(128)} %aggregate.3, bf16[16,128,128]{2,1,0:T(8,128)(2,1)} %tent.3, bf16[16,128,128]{2,1,0:T(8,128)(2,1)} %diag.5), custom_call_target="tpu_custom_call" | custom-call | tf_op jit(solution)/shard_map/pack/pallas_call | solution.py:91
  2.5 8.3 %collective-permute-start = (bf16[1040,128]{1,0:T(8,128)(2,1)}, bf16[1040,128]{1,0:T(8,128)(2,1)S(1)}, u32[]{:S(2)}, u32[]{:S(2)}) collective-permute-start(bf16[1040,128]{1,0:T(8,128)(2,1)} %get-tuple-element.35), channel_id=1, source_target_pairs={{1,3},{2,0},{3,5},{4,2},{5,7},{6,4},{7,9},{8,6},{9,11},{10,8},{11,... | collective-permute-start | bytes 798728 | tf_op jit(solution)/shard_map/ppermute | solution.py:495
  10.8 1.9 %collective-permute-start.1 = (bf16[1040,128]{1,0:T(8,128)(2,1)}, bf16[1040,128]{1,0:T(8,128)(2,1)S(1)}, u32[]{:S(2)}, u32[]{:S(2)}) collective-permute-start(bf16[1040,128]{1,0:T(8,128)(2,1)} %get-tuple-element.36), channel_id=1, source_target_pairs={{0,2},{2,4},{3,1},{4,6},{5,3},{6,8},{7,5},{8,10},{9,7},{10,12},{11... | collective-permute-start | bytes 798728 | tf_op jit(solution)/shard_map/ppermute | solution.py:495
  12.7 2.8 %collective-permute-start.2 = (bf16[1040,128]{1,0:T(8,128)(2,1)}, bf16[1040,128]{1,0:T(8,128)(2,1)S(1)}, u32[]{:S(2)}, u32[]{:S(2)}) collective-permute-start(bf16[1040,128]{1,0:T(8,128)(2,1)} %get-tuple-element.37), channel_id=1, source_target_pairs={{1,2},{2,1},{3,4},{4,3},{5,6},{6,5},{7,8},{8,7},{9,10},{10,9},{11,... | collective-permute-start | bytes 798728 | tf_op jit(solution)/shard_map/ppermute | solution.py:495
  15.6 0.1 collective-permute-start.3
  15.6 0.0 copy-start
  15.7 1.4 %copy-done = bf16[16,3,128,128]{3,2,1,0:T(8,128)(2,1)S(1)} copy-done((bf16[16,3,128,128]{3,2,1,0:T(8,128)(2,1)S(1)}, bf16[16,3,128,128]{3,2,1,0:T(8,128)(2,1)}, u32[]{:S(2)}) %copy-start) | copy-done | bytes 1572888
  17.1 0.0 copy-start.2
  17.1 1.0 %copy-done.2 = bf16[16,128,128]{2,1,0:T(8,128)(2,1)S(1)} copy-done((bf16[16,128,128]{2,1,0:T(8,128)(2,1)S(1)}, bf16[16,128,128]{2,1,0:T(8,128)(2,1)}, u32[]{:S(2)}) %copy-start.2) | copy-done | bytes 524312
  18.1 0.0 copy-start.3
  18.1 1.0 %copy-done.3 = bf16[16,128,128]{2,1,0:T(8,128)(2,1)S(1)} copy-done((bf16[16,128,128]{2,1,0:T(8,128)(2,1)S(1)}, bf16[16,128,128]{2,1,0:T(8,128)(2,1)}, u32[]{:S(2)}) %copy-start.3) | copy-done | bytes 524312
  19.1 0.0 copy-start.6
  19.1 0.7 copy-done.6
  19.8 0.0 copy-start.8
  19.8 0.7 copy-done.8
  20.5 0.0 copy-start.1
  20.5 2.4 %local_slots.1 = (s32[16,4]{1,0:T(8,128)S(1)}, s32[64]{0:T(128)S(1)}, s32[1]{0:T(128)}, bf16[16,128,512]{2,1,0:T(8,128)(2,1)S(1)}, f32[16,128,128]{2,1,0:T(8,128)S(1)}) custom-call(s32[3,16]{1,0:T(4,128)S(1)} %bitcast.2, s32[16]{0:T(128)S(1)} %copy-done.8, bf16[16,128,128]{2,1,0:T(8,128)(2,1)S(1)} %copy-done.3, bf16[16,3,128,128]{3,2,1,0:T(8,128)(2,1)S(1)} %copy-done, ...), custom_call_target="tpu_custom_call" | custom-call | flops 1000000000 | bytes 6000000 | tf_op jit(solution)/shard_map/local_slots/pallas_call | solution.py:134
  22.9 0.0 collective-permute-done.g0
  22.9 2.1 %collective-permute-done.1.g1 = bf16[1040,128]{1,0:T(8,128)(2,1)S(1)} collective-permute-done((bf16[1040,128]{1,0:T(8,128)(2,1)}, bf16[1040,128]{1,0:T(8,128)(2,1)S(1)}, u32[]{:S(2)}, u32[]{:S(2)}) %collective-permute-start.1) | collective-permute-done | bytes 266272 | tf_op jit(solution)/shard_map/ppermute | solution.py:495
  25.0 1.4 %collective-permute-done.2.g2 = bf16[1040,128]{1,0:T(8,128)(2,1)S(1)} collective-permute-done((bf16[1040,128]{1,0:T(8,128)(2,1)}, bf16[1040,128]{1,0:T(8,128)(2,1)S(1)}, u32[]{:S(2)}, u32[]{:S(2)}) %collective-permute-start.2) | collective-permute-done | bytes 266272 | tf_op jit(solution)/shard_map/ppermute | solution.py:495
  26.4 0.0 collective-permute-done.3.g3
  26.4 0.0 copy-done.1
  26.4 0.0 copy-done.5
  26.4 0.0 copy-done.7
  26.4 4.1 %ghost_slots.1 = (s32[17,4]{1,0:T(8,128)S(1)}, bf16[17,128,512]{2,1,0:T(8,128)(2,1)S(1)}, bf16[528,384]{1,0:T(8,128)(2,1)S(1)}, bf16[528,384]{1,0:T(8,128)(2,1)S...) custom-call(s32[1]{0:T(128)} %bitcast.parity, s32[4,4]{1,0:T(4,128)S(1)} %copy-done.5, ...), custom_call_target="tpu_custom_call" | custom-call | tf_op jit(solution)/shard_map/ghost_slots/pallas_call | solution.py:200
  30.5 3.9 %collective-permute-start.4 = (bf16[528,384]{1,0:T(8,128)(2,1)S(1)}, bf16[528,384]{1,0:T(8,128)(2,1)S(1)}, u32[]{:S(2)}, u32[]{:S(2)}) collective-permute-start(bf16[528,384]{1,0:T(8,128)(2,1)S(1)} %get-tuple-element.45), channel_id=1, source_target_pairs={{1,3},{2,0},{3,5},{4,2},{5,7},{6,4},{7,9},{8,6},{9,11},{10,8},{11,... | collective-permute-start | bytes 1216520 | tf_op jit(solution)/shard_map/ppermute | solution.py:495
  34.4 2.5 %collective-permute-start.5 = (bf16[528,384]{1,0:T(8,128)(2,1)S(1)}, bf16[528,384]{1,0:T(8,128)(2,1)S(1)}, u32[]{:S(2)}, u32[]{:S(2)}) collective-permute-start(bf16[528,384]{1,0:T(8,128)(2,1)S(1)} %get-tuple-element.46), channel_id=1, source_target_pairs={{1,2},{2,1},{3,4},{4,3},{5,6},{6,5},{7,8},{8,7},{9,10},{10,9},{11,... | collective-permute-start | bytes 1216520 | tf_op jit(solution)/shard_map/ppermute | solution.py:495
  36.9 1.9 %collective-permute-start.6 = (bf16[528,384]{1,0:T(8,128)(2,1)S(1)}, bf16[528,384]{1,0:T(8,128)(2,1)S(1)}, u32[]{:S(2)}, u32[]{:S(2)}) collective-permute-start(bf16[528,384]{1,0:T(8,128)(2,1)S(1)} %get-tuple-element.47), channel_id=1, source_target_pairs={{0,2},{2,4},{3,1},{4,6},{5,3},{6,8},{7,5},{8,10},{9,7},{10,12},{11... | collective-permute-start | bytes 1216520 | tf_op jit(solution)/shard_map/ppermute | solution.py:495
  38.8 5.5 %collective-permute-start.7 = (bf16[528,384]{1,0:T(8,128)(2,1)S(1)}, bf16[528,384]{1,0:T(8,128)(2,1)S(1)}, u32[]{:S(2)}, u32[]{:S(2)}) collective-permute-start(bf16[528,384]{1,0:T(8,128)(2,1)S(1)} %get-tuple-element.48), channel_id=1, source_target_pairs={{0,1},{1,0},{2,3},{3,2},{4,5},{5,4},{6,7},{7,6},{8,9},{9,8},{10,11... | collective-permute-start | bytes 1216520 | tf_op jit(solution)/shard_map/ppermute | solution.py:495
  44.4 2.6 %lists.1 = (s32[10,68]{1,0:T(8,128)S(1)}, s32[10]{0:T(128)S(1)}, bf16[65,128,128]{2,1,0:T(8,128)(2,1)S(1)}, bf16[16,128,128]{2,1,0:T(8,128)(2,1)S(1)}) custom-call(s32[1]{0:T(128)} %bitcast.parity, s32[17,4]{1,0:T(8,128)S(1)} %get-tuple-element.39.labels, bf16[17,128,512]{2,1,0:T(8,128)(2,1)S(1)} %get-tuple-element.40.slots, ...), custom_call_target="tpu_custom_call" | custom-call | flops 100000000 | bytes 6000000 | tf_op jit(solution)/shard_map/lists/pallas_call | solution.py:259
  47.0 0.0 collective-permute-done.4.g0
  47.0 2.0 %collective-permute-done.5.g1 = bf16[528,384]{1,0:T(8,128)(2,1)S(1)} collective-permute-done((bf16[528,384]{1,0:T(8,128)(2,1)S(1)}, bf16[528,384]{1,0:T(8,128)(2,1)S(1)}, u32[]{:S(2)}, u32[]{:S(2)}) %collective-permute-start.5) | collective-permute-done | bytes 405536 | tf_op jit(solution)/shard_map/ppermute | solution.py:495
  49.0 3.2 %collective-permute-done.6.g2 = bf16[528,384]{1,0:T(8,128)(2,1)S(1)} collective-permute-done((bf16[528,384]{1,0:T(8,128)(2,1)S(1)}, bf16[528,384]{1,0:T(8,128)(2,1)S(1)}, u32[]{:S(2)}, u32[]{:S(2)}) %collective-permute-start.6) | collective-permute-done | bytes 405536 | tf_op jit(solution)/shard_map/ppermute | solution.py:495
  52.2 0.0 collective-permute-done.7.g3
  52.2 0.0 copy-done.4
  52.2 9.7 %far_rows.1 = (bf16[16,128,2304]{2,1,0:T(8,128)(2,1)S(1)}, bf16[2,128,2304]{2,1,0:T(8,128)(2,1)S(1)}, bf16[2,128,2560]{2,1,0:T(8,128)(2,1)S(1)}) custom-call(s32[1]{0:T(128)} %bitcast.parity, s32[3,16]{1,0:T(4,128)S(1)} %bitcast.4, s32[17,4]{1,0:T(8,128)S(1)} %get-tuple-element.39.labels, s32[10,68]{1,0:T(8,128)S(1)} %get-tuple-element.41.lists, ...), custom_call_target="tpu_custom_call" | custom-call | flops 4000000000 | bytes 20000000 | tf_op jit(solution)/shard_map/far_rows/pallas_call | solution.py:364
  61.9 0.1 collective-permute-start.8
  62.0 5.7 %collective-permute-start.10 = (bf16[2,128,2304]{2,1,0:T(8,128)(2,1)S(1)}, bf16[2,128,2304]{2,1,0:T(8,128)(2,1)S(1)}, u32[]{:S(2)}, u32[]{:S(2)}) collective-permute-start(bf16[2,128,2304]{2,1,0:T(8,128)(2,1)S(1)} %get-tuple-element.54), channel_id=1, source_target_pairs={{1,3},{2,0},{3,5},{4,2},{5,7},{6,4},{7,9},{8,6},{9,11},{10,8},{11,... | collective-permute-start | bytes 3538952 | tf_op jit(solution)/shard_map/ppermute | solution.py:495
  67.8 0.0 collective-permute-done.8.relay
  67.8 2.5 %pair_rows.1 = bf16[2,128,2560]{2,1,0:T(8,128)(2,1)S(1)} custom-call(s32[1]{0:T(128)} %bitcast.parity, s32[10,68]{1,0:T(8,128)S(1)} %get-tuple-element.41.lists, s32[10]{0:T(128)S(1)} %get-tuple-element.42.counts, bf16[65,128,128]{2,1,0:T(8,128)(2,1)S(1)} %get-tuple-element.43.blocks, bf16[16,128,2304]{2,1,0:T(8,128)(2,1)S(1)} %get-tuple-element.51.applied, ...), custom_call_target="tpu_custom_call" | custom-call | flops 2000000000 | bytes 10000000 | tf_op jit(solution)/shard_map/pair_rows/pallas_call | solution.py:396
  70.3 1.9 %collective-permute-start.11 = (bf16[2,128,2560]{2,1,0:T(8,128)(2,1)S(1)}, bf16[2,128,2560]{2,1,0:T(8,128)(2,1)S(1)}, u32[]{:S(2)}, u32[]{:S(2)}) collective-permute-start(bf16[2,128,2560]{2,1,0:T(8,128)(2,1)S(1)} %pair_rows.1), channel_id=1, source_target_pairs={{0,2},{2,4},{3,1},{4,6},{5,3},{6,8},{7,5},{8,10},{9,7},{10,12},{11... | collective-permute-start | bytes 3932168 | tf_op jit(solution)/shard_map/ppermute | solution.py:495
  72.2 7.1 %near_rows.1 = (f32[2,128,2304]{2,1,0:T(8,128)S(1)}, bf16[2,128,2304]{2,1,0:T(8,128)(2,1)S(1)}) custom-call(s32[1]{0:T(128)} %bitcast.parity, s32[10,68]{1,0:T(8,128)S(1)} %get-tuple-element.41.lists, s32[10]{0:T(128)S(1)} %get-tuple-element.42.counts, bf16[65,128,128]{2,1,0:T(8,128)(2,1)S(1)} %get-tuple-element.43.blocks, ...), custom_call_target="tpu_custom_call" | custom-call | flops 4000000000 | bytes 20000000 | tf_op jit(solution)/shard_map/near_rows/pallas_call | solution.py:422
  79.3 2.5 %collective-permute-start.9 = (bf16[2,128,2304]{2,1,0:T(8,128)(2,1)S(1)}, bf16[2,128,2304]{2,1,0:T(8,128)(2,1)S(1)}, u32[]{:S(2)}, u32[]{:S(2)}) collective-permute-start(bf16[2,128,2304]{2,1,0:T(8,128)(2,1)S(1)} %get-tuple-element.53), channel_id=1, source_target_pairs={{0,1},{1,0},{2,3},{3,2},{4,5},{5,4},{6,7},{7,6},{8,9},{9,8},{10,11... | collective-permute-start | bytes 3538952 | tf_op jit(solution)/shard_map/ppermute | solution.py:495
  81.8 6.6 %collective-permute-done.10.direct = bf16[2,128,2304]{2,1,0:T(8,128)(2,1)S(1)} collective-permute-done((bf16[2,128,2304]{2,1,0:T(8,128)(2,1)S(1)}, bf16[2,128,2304]{2,1,0:T(8,128)(2,1)S(1)}, u32[]{:S(2)}, u32[]{:S(2)}) %collective-permute-start.10) | collective-permute-done | bytes 1179680 | tf_op jit(solution)/shard_map/ppermute | solution.py:495
  88.4 0.0 collective-permute-done.9.mate
  88.4 1.3 %add_near.1.band = f32[2,128,3328]{2,1,0:T(8,128)S(1)} custom-call(s32[1]{0:T(128)} %bitcast.parity, f32[2,128,2304]{2,1,0:T(8,128)S(1)} %get-tuple-element.52.own, bf16[2,128,2304]{2,1,0:T(8,128)(2,1)S(1)} %collective-permute-done.9.mate, bf16[2,128,2304]{2,1,0:T(8,128)(2,1)S(1)} %collective-permute-done.10.direct), custom_call_target="tpu_custom_call" | custom-call | flops 1000000 | bytes 9000000 | tf_op jit(solution)/shard_map/add_near/pallas_call | solution.py:453
  89.8 8.1 %collective-permute-done.11.pair = bf16[2,128,2560]{2,1,0:T(8,128)(2,1)S(1)} collective-permute-done((bf16[2,128,2560]{2,1,0:T(8,128)(2,1)S(1)}, bf16[2,128,2560]{2,1,0:T(8,128)(2,1)S(1)}, u32[]{:S(2)}, u32[]{:S(2)}) %collective-permute-start.11) | collective-permute-done | bytes 1310752 | tf_op jit(solution)/shard_map/ppermute | solution.py:495
  97.9 1.9 %add_pair.1 = f32[2,128,3328]{2,1,0:T(8,128)} custom-call(s32[1]{0:T(128)} %bitcast.parity, f32[2,128,3328]{2,1,0:T(8,128)S(1)} %add_near.1.band, bf16[2,128,2560]{2,1,0:T(8,128)(2,1)S(1)} %collective-permute-done.11.pair), custom_call_target="tpu_custom_call" | custom-call | tf_op jit(solution)/shard_map/add_pair/pallas_call | solution.py:481
  (3 shorter events, 0.0 us)
Async XLA Ops:
  2.5 20.4 %collective-permute-start = (bf16[1040,128]{1,0:T(8,128)(2,1)}, bf16[1040,128]{1,0:T(8,128)(2,1)S(1)}, u32[]{:S(2)}, u32[]{:S(2)}) collective-permute-start(bf16[1040,128]{1,0:T(8,128)(2,1)} %get-tuple-element.35), channel_id=1, source_target_pairs={{1,3},{2,0},{3,5},{4,2},{5,7},{6,4},{7,9},{8,6},{9,11},{10,8},{11,... | collective-permute-start | bytes 798728 | tf_op jit(solution)/shard_map/ppermute | solution.py:495
  10.8 14.2 %collective-permute-start.1 = (bf16[1040,128]{1,0:T(8,128)(2,1)}, bf16[1040,128]{1,0:T(8,128)(2,1)S(1)}, u32[]{:S(2)}, u32[]{:S(2)}) collective-permute-start(bf16[1040,128]{1,0:T(8,128)(2,1)} %get-tuple-element.36), channel_id=1, source_target_pairs={{0,2},{2,4},{3,1},{4,6},{5,3},{6,8},{7,5},{8,10},{9,7},{10,12},{11... | collective-permute-start | bytes 798728 | tf_op jit(solution)/shard_map/ppermute | solution.py:495
  12.7 13.7 %collective-permute-start.2 = (bf16[1040,128]{1,0:T(8,128)(2,1)}, bf16[1040,128]{1,0:T(8,128)(2,1)S(1)}, u32[]{:S(2)}, u32[]{:S(2)}) collective-permute-start(bf16[1040,128]{1,0:T(8,128)(2,1)} %get-tuple-element.37), channel_id=1, source_target_pairs={{1,2},{2,1},{3,4},{4,3},{5,6},{6,5},{7,8},{8,7},{9,10},{10,9},{11,... | collective-permute-start | bytes 798728 | tf_op jit(solution)/shard_map/ppermute | solution.py:495
  15.6 10.9 %collective-permute-start.3 = (bf16[1040,128]{1,0:T(8,128)(2,1)}, bf16[1040,128]{1,0:T(8,128)(2,1)S(1)}, u32[]{:S(2)}, u32[]{:S(2)}) collective-permute-start(bf16[1040,128]{1,0:T(8,128)(2,1)} %get-tuple-element.38), channel_id=1, source_target_pairs={{0,1},{1,0},{2,3},{3,2},{4,5},{5,4},{6,7},{7,6},{8,9},{9,8},{10,11... | collective-permute-start | bytes 798728 | tf_op jit(solution)/shard_map/ppermute | solution.py:495
  15.6 1.4 %copy-start = (bf16[16,3,128,128]{3,2,1,0:T(8,128)(2,1)S(1)}, bf16[16,3,128,128]{3,2,1,0:T(8,128)(2,1)}, u32[]{:S(2)}) copy-start(bf16[16,3,128,128]{3,2,1,0:T(8,128)(2,1)} %off.5) | copy-start | bytes 4718596
  17.1 1.0 %copy-start.2 = (bf16[16,128,128]{2,1,0:T(8,128)(2,1)S(1)}, bf16[16,128,128]{2,1,0:T(8,128)(2,1)}, u32[]{:S(2)}) copy-start(bf16[16,128,128]{2,1,0:T(8,128)(2,1)} %tent.3) | copy-start | bytes 1572868
  18.1 1.0 %copy-start.3 = (bf16[16,128,128]{2,1,0:T(8,128)(2,1)S(1)}, bf16[16,128,128]{2,1,0:T(8,128)(2,1)}, u32[]{:S(2)}) copy-start(bf16[16,128,128]{2,1,0:T(8,128)(2,1)} %diag.5) | copy-start | bytes 1572868
  19.1 0.7 copy-start.6
  19.8 0.7 copy-start.8
  20.5 5.9 %copy-start.1 = (bf16[16,3,128,128]{3,2,1,0:T(8,128)(2,1)S(1)}, bf16[16,3,128,128]{3,2,1,0:T(8,128)(2,1)}, u32[]{:S(2)}) copy-start(bf16[16,3,128,128]{3,2,1,0:T(8,128)(2,1)} %off.5) | copy-start | bytes 4718596
  20.5 5.9 %copy-start.5 = (s32[4,4]{1,0:T(4,128)S(1)}, s32[4,4]{1,0:T(4,128)}, u32[]{:S(2)}) copy-start(s32[4,4]{1,0:T(4,128)} %send_rows.3) | copy-start | bytes 196
  20.5 5.9 %copy-start.7 = (s32[16,3]{0,1:T(4,128)S(1)}, s32[16,3]{0,1:T(4,128)}, u32[]{:S(2)}) copy-start(s32[16,3]{0,1:T(4,128)} %param.8) | copy-start | bytes 580
  30.5 16.5 %collective-permute-start.4 = (bf16[528,384]{1,0:T(8,128)(2,1)S(1)}, bf16[528,384]{1,0:T(8,128)(2,1)S(1)}, u32[]{:S(2)}, u32[]{:S(2)}) collective-permute-start(bf16[528,384]{1,0:T(8,128)(2,1)S(1)} %get-tuple-element.45), channel_id=1, source_target_pairs={{1,3},{2,0},{3,5},{4,2},{5,7},{6,4},{7,9},{8,6},{9,11},{10,8},{11,... | collective-permute-start | bytes 1216520 | tf_op jit(solution)/shard_map/ppermute | solution.py:495
  34.4 14.6 %collective-permute-start.5 = (bf16[528,384]{1,0:T(8,128)(2,1)S(1)}, bf16[528,384]{1,0:T(8,128)(2,1)S(1)}, u32[]{:S(2)}, u32[]{:S(2)}) collective-permute-start(bf16[528,384]{1,0:T(8,128)(2,1)S(1)} %get-tuple-element.46), channel_id=1, source_target_pairs={{1,2},{2,1},{3,4},{4,3},{5,6},{6,5},{7,8},{8,7},{9,10},{10,9},{11,... | collective-permute-start | bytes 1216520 | tf_op jit(solution)/shard_map/ppermute | solution.py:495
  36.9 15.3 %collective-permute-start.6 = (bf16[528,384]{1,0:T(8,128)(2,1)S(1)}, bf16[528,384]{1,0:T(8,128)(2,1)S(1)}, u32[]{:S(2)}, u32[]{:S(2)}) collective-permute-start(bf16[528,384]{1,0:T(8,128)(2,1)S(1)} %get-tuple-element.47), channel_id=1, source_target_pairs={{0,2},{2,4},{3,1},{4,6},{5,3},{6,8},{7,5},{8,10},{9,7},{10,12},{11... | collective-permute-start | bytes 1216520 | tf_op jit(solution)/shard_map/ppermute | solution.py:495
  38.8 13.3 %collective-permute-start.7 = (bf16[528,384]{1,0:T(8,128)(2,1)S(1)}, bf16[528,384]{1,0:T(8,128)(2,1)S(1)}, u32[]{:S(2)}, u32[]{:S(2)}) collective-permute-start(bf16[528,384]{1,0:T(8,128)(2,1)S(1)} %get-tuple-element.48), channel_id=1, source_target_pairs={{0,1},{1,0},{2,3},{3,2},{4,5},{5,4},{6,7},{7,6},{8,9},{9,8},{10,11... | collective-permute-start | bytes 1216520 | tf_op jit(solution)/shard_map/ppermute | solution.py:495
  44.4 7.8 %copy-start.4 = (bf16[16,128,128]{2,1,0:T(8,128)(2,1)S(1)}, bf16[16,128,128]{2,1,0:T(8,128)(2,1)}, u32[]{:S(2)}) copy-start(bf16[16,128,128]{2,1,0:T(8,128)(2,1)} %diag.5) | copy-start | bytes 1572868
  61.9 5.8 %collective-permute-start.8 = (bf16[2,128,2560]{2,1,0:T(8,128)(2,1)S(1)}, bf16[2,128,2560]{2,1,0:T(8,128)(2,1)S(1)}, u32[]{:S(2)}, u32[]{:S(2)}) collective-permute-start(bf16[2,128,2560]{2,1,0:T(8,128)(2,1)S(1)} %get-tuple-element.50), channel_id=1, source_target_pairs={{0,1},{1,0},{2,3},{3,2},{4,5},{5,4},{6,7},{7,6},{8,9},{9,8},{10,11... | collective-permute-start | bytes 3932168 | tf_op jit(solution)/shard_map/ppermute | solution.py:495
  62.0 26.4 %collective-permute-start.10 = (bf16[2,128,2304]{2,1,0:T(8,128)(2,1)S(1)}, bf16[2,128,2304]{2,1,0:T(8,128)(2,1)S(1)}, u32[]{:S(2)}, u32[]{:S(2)}) collective-permute-start(bf16[2,128,2304]{2,1,0:T(8,128)(2,1)S(1)} %get-tuple-element.54), channel_id=1, source_target_pairs={{1,3},{2,0},{3,5},{4,2},{5,7},{6,4},{7,9},{8,6},{9,11},{10,8},{11,... | collective-permute-start | bytes 3538952 | tf_op jit(solution)/shard_map/ppermute | solution.py:495
  70.3 27.6 %collective-permute-start.11 = (bf16[2,128,2560]{2,1,0:T(8,128)(2,1)S(1)}, bf16[2,128,2560]{2,1,0:T(8,128)(2,1)S(1)}, u32[]{:S(2)}, u32[]{:S(2)}) collective-permute-start(bf16[2,128,2560]{2,1,0:T(8,128)(2,1)S(1)} %pair_rows.1), channel_id=1, source_target_pairs={{0,2},{2,4},{3,1},{4,6},{5,3},{6,8},{7,5},{8,10},{9,7},{10,12},{11... | collective-permute-start | bytes 3932168 | tf_op jit(solution)/shard_map/ppermute | solution.py:495
  79.3 9.1 %collective-permute-start.9 = (bf16[2,128,2304]{2,1,0:T(8,128)(2,1)S(1)}, bf16[2,128,2304]{2,1,0:T(8,128)(2,1)S(1)}, u32[]{:S(2)}, u32[]{:S(2)}) collective-permute-start(bf16[2,128,2304]{2,1,0:T(8,128)(2,1)S(1)} %get-tuple-element.53), channel_id=1, source_target_pairs={{0,1},{1,0},{2,3},{3,2},{4,5},{5,4},{6,7},{7,6},{8,9},{9,8},{10,11... | collective-permute-start | bytes 3538952 | tf_op jit(solution)/shard_map/ppermute | solution.py:495
